TPU v7x, 32 devices: a whole 2x2x4 slice. The times are simulated.
32 devices in a mesh: groups: 1, seq: 32 (over z, y, x, core).
Axes of the slice: x: 2, y: 2, z: 4, core: 2. Of those that a mesh axis runs over, the one named last changes fastest.
Arguments:
- q_gate: bfloat16 [4096, 4096], P(('groups', 'seq')), may hold values from -6 to 6
- values_in: bfloat16 [4096, 4096], P(('groups', 'seq')), may hold values from -6 to 6
- decay_rate: float32 [4096, 16], replicated, as said below
- residue: float32 [4096, 16], replicated, may hold values from -3 to 3
- skip_gain: float32 [4096], replicated, may hold values from 0.5 to 1.5
- out_weight: bfloat16 [4096, 2048], P('seq'), may hold values from -0.09375 to 0.09375
Outputs:
- mixed: bfloat16 [4096, 2048], P(('groups', 'seq'))
Inputs may be any that keep to these rules, and one draw needn't show every extreme that they name: `decay_rate`: every rate is positive and at most about 1/30.
All inputs are finite; a program needn't handle non-finite values.
Results may differ from a plain program's by a relative error of at most 0.0052.
Values may be sent and summed in bfloat16 or wider, within the bound.
No kernel may reach another device: no remote copies, remote signals or barrier semaphores. Data moves between devices by JAX's collectives and lax.ppermute only.
A program may use at most 256 MiB of HBM per device.

v0:
```python
import jax
import jax.numpy as jnp
from jax import lax
from jax.sharding import PartitionSpec as P

ORDER = 16
BLOCK = 32


def entering(value, axis, join, neutral):
    count, mine = (lax.axis_size(axis), lax.axis_index(axis))
    pieces = jax.tree.map(lambda part: lax.all_gather(part, axis), value)
    running = jax.tree.map(
        lambda part, zero: jnp.full_like(part, 0) + jnp.asarray(zero, part.dtype), value, neutral
    )

    def hop(position, running):
        longer = join(running, jax.tree.map(lambda part: part[position], pieces))
        return jax.tree.map(lambda new, old: jnp.where(position < mine, new, old), longer, running)

    return lax.fori_loop(0, count - 1, hop, running)


def on_device(q_gate, values_in, decay_rate, residue, skip_gain, out_weight):
    tok_rows = q_gate.shape[0]
    width = q_gate.shape[1]
    block_count = tok_rows // BLOCK
    rate_modes = decay_rate.T
    mode_scale = jnp.sqrt(-jnp.expm1(-2.0 * rate_modes))
    mode_coef = residue.T * mode_scale
    position = jnp.arange(BLOCK, dtype=jnp.float32)
    tap_values = jnp.sum(
        mode_coef[None] * jnp.exp(-position[:, None, None] * rate_modes[None]), axis=1
    )
    tap_round = tap_values.astype(jnp.bfloat16)
    offsets = jnp.arange(BLOCK)[:, None] - jnp.arange(BLOCK)[None, :]
    selector = (
        (jnp.arange(BLOCK)[:, None, None] == offsets[None])
        .astype(jnp.bfloat16)
        .reshape(BLOCK, BLOCK * BLOCK)
    )
    toeplitz = jnp.dot(tap_round.T, selector, preferred_element_type=jnp.bfloat16).reshape(
        width, BLOCK, BLOCK
    )
    blocked = values_in.reshape(block_count, BLOCK, width)
    local_part = jnp.einsum("dts,nsd->ntd", toeplitz, blocked, preferred_element_type=jnp.float32)
    blocked_wide = blocked.astype(jnp.float32)
    end_weight = jnp.exp(-(BLOCK - 1 - position)[:, None, None] * rate_modes[None])
    block_ends = jnp.einsum(
        "tkd,ntd->nkd", end_weight, blocked_wide, precision=lax.Precision.HIGHEST
    )
    step_decay = jnp.exp(-BLOCK * rate_modes)

    def advance(carry_state, inflow):
        return (step_decay * carry_state + inflow, carry_state)

    end_state, starts_local = lax.scan(advance, jnp.zeros((ORDER, width), jnp.float32), block_ends)
    shard_decay = jnp.exp(-tok_rows * rate_modes)

    def combine_pairs(earlier, later):
        return (earlier[0] * later[0], earlier[1] * later[0] + later[1])

    identity = (jnp.ones_like(shard_decay), jnp.zeros_like(end_state))
    scanned = entering((shard_decay, end_state), "seq", combine_pairs, identity)
    incoming = scanned[1]
    block_index = jnp.arange(block_count, dtype=jnp.float32)
    starts = (
        starts_local
        + jnp.exp(-(BLOCK * block_index)[:, None, None] * rate_modes[None]) * incoming[None]
    )
    reach_table = mode_coef[None] * jnp.exp(-(position + 1.0)[:, None, None] * rate_modes[None])
    correction = jnp.einsum("tkd,nkd->ntd", reach_table, starts, precision=lax.Precision.HIGHEST)
    conv = (local_part + correction).reshape(tok_rows, width)
    gated = (
        q_gate.astype(jnp.float32) * (conv + skip_gain[None] * values_in.astype(jnp.float32))
    ).astype(jnp.bfloat16)
    weights = lax.all_gather(out_weight, "seq", axis=0, tiled=True)
    mixed = jnp.dot(gated, weights, preferred_element_type=jnp.float32)
    return mixed.astype(jnp.bfloat16)


def solution(mesh):
    in_specs = (
        P(("groups", "seq"), None),
        P(("groups", "seq"), None),
        P(),
        P(),
        P(),
        P("seq", None),
    )
    out_specs = P(("groups", "seq"), None)
    return jax.shard_map(
        on_device, mesh=mesh, in_specs=in_specs, out_specs=out_specs, check_vma=False
    )
```

profile of v0, /device:TPU:0, one launch (start us, length us, event | category | flops | bytes accessed | tf_op | source)
XLA Modules:
  0.0 301.1 jit_solution(8403443552745695005)
XLA Ops:
  6.5 1.9 multiply_exponential_fusion
  8.5 0.0 all-gather.10.cloned.1.call-start
  8.6 1.5 copy.31
  10.1 6.2 %copy.34 = bf16[4,32,4096]{1,0,2:T(4,128)(2,1)} copy(bf16[4,32,4096]{2,1,0:T(8,128)(2,1)} %bitcast.53) | data formatting | bytes 2097152 | tf_op jit(solution)/shard_map/reshape | solution.py:45
  16.3 34.1 %fusion.13 = f32[4,16,4096]{1,0,2:T(4,128)} fusion(bf16[4,32,4096]{1,0,2:T(4,128)(2,1)} %copy.34, f32[32]{0:T(128)S(1)} %subtract_negate_fusion, f32[16,4096]{0,1:T(8,128)S(1)} %copy.31), kind=kOutput, calls=%fused_computation.19 | convolution fusion | flops 102760448 | bytes 2359424 | tf_op jit(solution)/shard_map/tkd,ntd->nkd/dot_general | solution.py:49
  50.4 7.5 %copy.36 = f32[4,16,4096]{2,1,0:T(8,128)} copy(f32[4,16,4096]{1,0,2:T(4,128)} %fusion.13) | data formatting | bytes 2097152
  57.9 7.5 %while.27 = (s32[]{:T(128)}, f32[16,4096]{1,0:T(8,128)S(1)}, f32[4,16,4096]{2,1,0:T(8,128)}, f32[16,4096]{1,0:T(8,128)S(1)}, f32[4,16,4096]{2,1,0:T(8,128)}, /*index=5*/s32[]{:T(128)}, s32[]{:T(128)}) while((s32[]{:T(128)}, f32[16,4096]{1,0:T(8,128)S(1)}, f32[4,16,4096]{2,1,0:T(8,128)}, f32[16,4096]{1,0:T(8,128)S(1)}, ...), condition=%wide.region_2.3_spmd.clone, body=%wide.region_1.2_spmd.clone.sunk | while | flops 262147 | bytes 1572968 | solution.py:57
  57.9 0.7 bitcast_dynamic-update-slice_fusion.2
  58.7 1.1 bitcast_add_fusion.5
  59.8 0.7 bitcast_dynamic-update-slice_fusion.2
  60.5 1.2 bitcast_add_fusion.5
  61.7 0.7 bitcast_dynamic-update-slice_fusion.2
  62.5 1.1 bitcast_add_fusion.5
  63.6 0.7 bitcast_dynamic-update-slice_fusion.2
  64.3 1.1 bitcast_add_fusion.5
  65.4 0.7 copy-done
  66.1 0.2 all-gather.6.cloned.1.call-start
  66.4 0.5 all-gather.6.cloned.1.call-update
  66.9 2.0 copy.30
  68.9 25.7 %multiply_reduce_fusion = bf16[32,4096]{0,1:T(8,128)(2,1)} fusion(f32[16,4096]{0,1:T(8,128)S(1)} %copy.31, f32[32]{0:T(128)S(1)} %iota_negate_fusion, f32[16,4096]{0,1:T(8,128)} %copy.30), kind=kLoop, calls=%fused_computation.12 | loop fusion | flops 6160384 | bytes 786560 | tf_op jit(solution)/shard_map/reduce_sum | solution.py:32
  94.6 1.5 copy.32
  96.2 5.6 %fusion.20 = bf16[4096,32,32]{0,2,1:T(8,128)(2,1)} fusion(s32[32,32]{1,0:T(8,128)S(1)} %iota_subtract_fusion, bf16[32,4096]{1,0:T(8,128)(2,1)S(1)} %copy.32), kind=kOutput, calls=%fused_computation.26 | convolution fusion | flops 268468224 | bytes 8654848 | tf_op jit(solution)/shard_map/dot_general | solution.py:42
  101.7 44.1 %copy.33 = bf16[4096,32,32]{2,1,0:T(8,128)(2,1)} copy(bf16[4096,32,32]{0,2,1:T(8,128)(2,1)} %fusion.20) | data formatting | bytes 16777216 | tf_op jit(solution)/shard_map/dot_general | solution.py:42
  145.9 22.8 %fusion.24 = f32[4096,32,4]{1,2,0:T(4,128)} fusion(bf16[4096,32,32]{2,1,0:T(8,128)(2,1)} %copy.33, bf16[4,32,4096]{1,0,2:T(4,128)(2,1)} %copy.34), kind=kOutput, calls=%fused_computation.38 | convolution fusion | flops 33554432 | bytes 11534336 | tf_op jit(solution)/shard_map/dts,nsd->ntd/dot_general | solution.py:46
  168.7 0.6 all-gather.10.cloned.1.call-done
  169.3 39.5 %while.28 = (s32[]{:T(128)}, f32[16,4096]{1,0:T(8,128)S(1)}, s32[]{:T(128)}, f32[32,16,4096]{2,1,0:T(8,128)}, f32[32,16,4096]{2,1,0:T(8,128)}, /*index=5*/s32[]{:T(128)}, s32[]{:T(128)}) while((s32[]{:T(128)}, f32[16,4096]{1,0:T(8,128)S(1)}, s32[]{:T(128)}, f32[32,16,4096]{2,1,0:T(8,128)}, f32[32,16,4096]{2,1,0:T(8,128)}, ...), condition=%wide.region_4.5_spmd.clone, body=%wide.region_3.4_spmd.clone.sunk | while | flops 262148 | bytes 1048685 | solution.py:21
  169.3 1.2 fusion.35
  170.6 1.2 fusion.35
  171.9 1.2 fusion.35
  173.2 1.2 fusion.35
  174.4 1.2 fusion.35
  175.7 1.2 fusion.35
  177.0 1.2 fusion.35
  178.2 1.3 fusion.35
  179.6 1.3 fusion.35
  180.8 1.2 fusion.35
  182.1 1.2 fusion.35
  183.4 1.2 fusion.35
  184.7 1.3 fusion.35
  185.9 1.3 fusion.35
  187.2 1.3 fusion.35
  188.5 1.2 fusion.35
  189.7 1.2 fusion.35
  191.0 1.3 fusion.35
  192.3 1.2 fusion.35
  193.6 1.2 fusion.35
  194.8 1.2 fusion.35
  196.1 1.2 fusion.35
  197.4 1.2 fusion.35
  198.7 1.2 fusion.35
  199.9 1.3 fusion.35
  201.3 1.2 fusion.35
  202.5 1.2 fusion.35
  203.8 1.2 fusion.35
  205.1 1.3 fusion.35
  206.3 1.2 fusion.35
  207.6 1.3 fusion.35
  208.9 2.5 multiply_add_fusion
  211.4 6.9 %copy.37 = f32[4,16,4096]{1,0,2:T(4,128)} copy(f32[4,16,4096]{2,1,0:T(8,128)} %multiply_add_fusion) | data formatting | bytes 2097152 | tf_op jit(solution)/shard_map/add | solution.py:68
  218.3 47.3 %bitcast_add_fusion.2 = f32[4,32,4096]{1,0,2:T(4,128)} fusion(f32[4096,32,4]{1,2,0:T(4,128)} %fusion.24, f32[4,16,4096]{1,0,2:T(4,128)} %copy.37, f32[32]{0:T(128)S(1)} %add_negate_fusion, f32[16,4096]{0,1:T(8,128)S(1)} %copy.31, f32[16,4096]{0,1:T(8,128)} %copy.30), kind=kOutput, calls=%fused_computation.18 | convolution fusion | flops 105381888 | bytes 5767296 | tf_op jit(solution)/shard_map/tkd,nkd->ntd/dot_general | solution.py:72
  265.6 7.1 %copy.38 = f32[4,32,4096]{2,1,0:T(8,128)S(1)} copy(f32[4,32,4096]{1,0,2:T(4,128)} %bitcast_add_fusion.2) | data formatting | bytes 4194304 | tf_op jit(solution)/shard_map/add | solution.py:73
  272.8 2.3 fusion.19
  275.1 10.6 %all-gather.6.cloned.1.call-done = bf16[4096,2048]{1,0:T(8,128)(2,1)} async-done(((bf16[128,2048]{1,0:T(8,128)(2,1)}), bf16[4096,2048]{1,0:T(8,128)(2,1)}) %all-gather.6.cloned.1.call-update) | async-done | bytes 16777232 | tf_op jit(solution)/shard_map/all_gather | solution.py:77
  285.7 8.9 %convolution_convert_fusion = bf16[128,2048]{1,0:T(8,128)(2,1)} fusion(bf16[128,4096]{1,0:T(8,128)(2,1)S(1)} %fusion.19, bf16[4096,2048]{1,0:T(8,128)(2,1)} %all-gather.6.cloned.1.call-done), kind=kOutput, calls=%fused_computation.20 | convolution fusion | flops 2147745792 | bytes 18350080 | tf_op jit(solution)/shard_map/dot_general | solution.py:78
  (17 shorter events, 0.1 us)
Async XLA Ops:
  6.5 162.2 %all-gather.8.cloned.1.call-start = ((), (), s32[]{:S(2)}) async-start(), calls=%async_computation.1 | async-start | bytes 8650752 | tf_op jit(solution)/shard_map/all_gather | solution.py:12
  8.5 160.9 %all-gather.10.cloned.1.call-start = ((), (), s32[]{:S(2)}) async-start(), calls=%async_computation.2 | async-start | bytes 8650752 | tf_op jit(solution)/shard_map/all_gather | solution.py:12
  65.4 0.7 copy-start
  66.1 219.6 %all-gather.6.cloned.1.call-start = ((), (), s32[]{:S(2)}) async-start(), calls=%async_computation | async-start | bytes 17301504 | tf_op jit(solution)/shard_map/all_gather | solution.py:77
  145.9 63.0 %copy-start.1 = (f32[4096,16]{0,1:T(8,128)S(1)}, f32[4096,16]{0,1:T(8,128)}, u32[]{:S(2)}) copy-start(f32[4096,16]{0,1:T(8,128)} %param.12) | copy-start | bytes 786436
  265.6 7.1 %copy-start.2 = (f32[4096]{0:T(1024)S(1)}, f32[4096]{0:T(1024)}, u32[]{:S(2)}) copy-start(f32[4096]{0:T(1024)} %param.14) | copy-start | bytes 49156
Sparse Core Ops, SparseCore 0:
  10.2 80.1 all-gather.7
  93.3 76.0 all-gather.9
  172.2 113.4 all-gather.5
where the time goes:
time: 303 us; the launch traced here: 301 us
  matrix products  119 us (39%)
  other arithmetic  78.8 us (26%)
  local copies, waits for them, and re-layouts  77.6 us (26%)
  between operations  13.2 us (4%)
  waiting for transfers between devices  11.8 us (4%)
    dot_general x1, matrix products, on_device(): jnp.einsum('tkd,nkd->ntd', reach_table, starts, precision=lax.Precision.H...  47.3 us
    dot_general x1, local copies, waits for them, and re-layouts, on_device(): jnp.dot(tap_round.T, selector, preferred_element_type=jnp.bfloat16)  44.1 us
    select_n x31, other arithmetic, hop(): jnp.where(position < mine, new, old)  38.9 us
    dot_general x1, matrix products, on_device(): jnp.einsum('tkd,ntd->nkd', end_weight, blocked_wide, precision=lax.Precis...  34.1 us
    reduce_sum x1, other arithmetic, on_device(): jnp.sum(mode_coef[None] * jnp.exp(-position[:, None, None] * rate_modes[N...  25.7 us
    dot_general x1, matrix products, on_device(): jnp.einsum('dts,nsd->ntd', toeplitz, blocked, preferred_element_type=jnp....  22.8 us
    all_gather x1, waiting for transfers between devices, on_device(): weights = lax.all_gather(out_weight, 'seq', axis=0, tiled=True)  10.6 us
    dot_general x1, matrix products, on_device(): mixed = jnp.dot(gated, weights, preferred_element_type=jnp.float32)  8.9 us
  transfers between devices with their start and end apart: 3, of which 2 were waited for; matrix products, arithmetic and copies ran while one was open for 88% of the time, Pallas kernels for 0%

commit v1 on v0

v1 whole, which is shorter than its diff:
```python
import functools

import jax
import jax.numpy as jnp
from jax import lax
from jax.experimental import pallas as pl
from jax.experimental.pallas import tpu as pltpu
from jax.sharding import PartitionSpec as P

BLOCK = 32
LANES = 128
TEAM = 4
WEIGHT_PARTS = 4
VMEM_LIMIT = 32 * 1024 * 1024

f32 = jnp.float32
bf16 = jnp.bfloat16


def vmem(count):
    return [pl.BlockSpec(memory_space=pltpu.VMEM)] * count


def smem():
    return pl.BlockSpec(memory_space=pltpu.SMEM)


def call(kernel, out_shape, scratch=(), flops=0, moved=0):
    outs = jax.tree.leaves(out_shape)

    def run(info, *args):
        return pl.pallas_call(
            kernel,
            out_shape=out_shape,
            in_specs=[smem()] + vmem(len(args)),
            out_specs=jax.tree.map(lambda _: pl.BlockSpec(memory_space=pltpu.VMEM), out_shape),
            scratch_shapes=list(scratch),
            compiler_params=pltpu.CompilerParams(vmem_limit_bytes=VMEM_LIMIT),
            cost_estimate=pl.CostEstimate(flops=flops, bytes_accessed=moved, transcendentals=0),
        )(info, *args)

    return run


def split_kernel(team, depth, info_ref, *refs):
    me = info_ref[0]
    sources, outs = refs[: len(refs) // (team + 1)], refs[len(refs) // (team + 1) :]
    runs = sources[0].shape[1] // (team * depth)
    for which, source in enumerate(sources):
        for step in range(team):
            out = outs[which * team + step]
            for run in range(runs):
                at = pl.multiple_of((run * team + (me ^ step)) * depth, depth)
                out[:, run * depth : (run + 1) * depth] = source[:, pl.ds(at, depth)]


def split_channels(info, team, depth, sources):
    rows, width = sources[0].shape
    if depth % LANES == 0:
        share = jax.ShapeDtypeStruct((rows, width // team), sources[0].dtype)
        pieces = call(
            functools.partial(split_kernel, team, depth),
            [share] * (team * len(sources)),
            moved=2 * len(sources) * sources[0].size * sources[0].dtype.itemsize,
        )(info, *sources)
        return [pieces[n * team : (n + 1) * team] for n in range(len(sources))]
    out = []
    for source in sources:
        cut = source.reshape(rows, width // (team * depth), team, depth)
        out.append(
            [
                lax.dynamic_index_in_dim(cut, info[0] ^ step, 2, keepdims=False).reshape(rows, -1)
                for step in range(team)
            ]
        )
    return out


def reach_tables(rate, coef, reach, decay8):
    order = rate.shape[0]
    step = lax.broadcasted_iota(jnp.int32, (8, LANES), 0).astype(f32) + 1.0
    for k in range(order):
        reach[k] = coef[k : k + 1] * jnp.exp(-step * rate[k : k + 1])
        decay8[k] = jnp.exp(jnp.broadcast_to(-8.0 * rate[k : k + 1], (8, LANES)))


def local_kernel(info_ref, *refs):
    values = refs[:TEAM]
    rate_ref, coef_ref, skip_ref, y_ref, end_ref, wide, taps, reach, decay8, start = refs[TEAM:]
    me = info_ref[0]
    order = rate_ref.shape[0]
    rows = values[0].shape[0]
    per = rows // BLOCK
    wide[:, :BLOCK, :] = jnp.zeros((wide.shape[0], BLOCK, LANES), f32)

    @pl.loop(0, rate_ref.shape[1] // LANES)
    def _(tile):
        lanes = pl.ds(pl.multiple_of(tile * LANES, LANES), LANES)
        for step in range(TEAM):
            for b in range(per):
                wide[(me ^ step) * per + b, BLOCK:, :] = values[step][
                    b * BLOCK : (b + 1) * BLOCK, lanes
                ].astype(f32)
        rate, coef, skip = rate_ref[:, lanes], coef_ref[:, lanes], skip_ref[:, lanes]
        lam = jnp.exp(-rate)
        power = coef
        for t in range(BLOCK):
            tap = jnp.sum(power, axis=0, keepdims=True).astype(bf16).astype(f32)
            taps[t] = jnp.broadcast_to(tap, (8, LANES))
            power = power * lam
        reach_tables(rate, coef, reach, decay8)
        lam8 = jnp.exp(-8.0 * rate)

        def block(b, state):
            start[...] = state
            y = [skip * wide[b, BLOCK + 8 * i : BLOCK + 8 * i + 8, :] for i in range(BLOCK // 8)]
            for t in range(BLOCK):
                tap = taps[t]
                for i in range(t // 8, BLOCK // 8):
                    at = BLOCK + 8 * i - t
                    y[i] = y[i] + tap * wide[b, at : at + 8, :]
            for k in range(order):
                term = reach[k] * start[k : k + 1, :]
                decay = decay8[k]
                for i in range(BLOCK // 8):
                    y[i] = y[i] + term
                    if i + 1 < BLOCK // 8:
                        term = term * decay
            for i in range(BLOCK // 8):
                y_ref[tile, pl.ds(pl.multiple_of(b * BLOCK + 8 * i, 8), 8), :] = y[i]
            for i in range(BLOCK // 8):
                at = BLOCK + 8 * i
                inflow = jnp.broadcast_to(wide[b, at : at + 1, :], (order, LANES))
                for t in range(1, 8):
                    inflow = lam * inflow + wide[b, at + t : at + t + 1, :]
                state = lam8 * state + inflow
            return state

        end_ref[:, lanes] = lax.fori_loop(0, TEAM * per, block, jnp.zeros((order, LANES), f32))


def gate_kernel(gaps, info_ref, *refs):
    gates = refs[:TEAM]
    y_ref, rate_ref, coef_ref, near_ref = refs[TEAM : TEAM + 4]
    far = refs[TEAM + 4 : TEAM + 4 + gaps]
    out_ref, reach, decay8, start = refs[TEAM + 4 + gaps :]
    me, high = info_ref[0], info_ref[1]
    order = rate_ref.shape[0]
    rows = gates[0].shape[0]
    span = float(TEAM * rows)

    @pl.loop(0, rate_ref.shape[1] // LANES)
    def _(tile):
        lanes = pl.ds(pl.multiple_of(tile * LANES, LANES), LANES)
        rate, coef = rate_ref[:, lanes], coef_ref[:, lanes]
        reach_tables(rate, coef, reach, decay8)
        state = jnp.zeros((order, LANES), f32)
        for gap in range(gaps):
            state = state + jnp.exp(-2.0 * span * gap * rate) * far[gap][:, lanes]
        after = jnp.exp(-span * rate) * state + near_ref[:, lanes]
        state = jnp.where(high == 1, after, state)
        for step in range(TEAM):
            place = me ^ step
            start[...] = state * jnp.exp(-(rows * place).astype(f32) * rate)
            terms = [reach[k] * start[k : k + 1, :] for k in range(order)]
            goes = place ^ (me & 2)
            for at in range(0, rows, 16):
                halves = []
                for half in range(2):
                    total = list(terms)
                    while len(total) > 1:
                        total = [a + b for a, b in zip(total[::2], total[1::2])]
                    here = pl.multiple_of(place * rows + at + 8 * half, 8)
                    halves.append(total[0] + y_ref[tile, pl.ds(here, 8), :])
                    terms = [term * decay8[k] for k, term in enumerate(terms)]
                conv = jnp.concatenate(halves, axis=0)
                gated = gates[step][at : at + 16, lanes].astype(f32) * conv
                out_ref[tile, pl.ds(pl.multiple_of(goes * rows + at, 16), 16), :] = gated.astype(bf16)


def project_kernel(slots, info_ref, own_ref, other_ref, *refs):
    weights, outs, total = refs[:slots], refs[slots : slots + TEAM], refs[-1]
    core = info_ref[2]
    rows = outs[0].shape[0]
    for slot in range(slots):
        group = info_ref[3 + slot]
        left = jnp.concatenate([own_ref[group], other_ref[group]], axis=1)
        product = jnp.dot(left, weights[slot][...], preferred_element_type=f32)
        if slot == 0:
            total[...] = product
        else:
            total[...] += product
    for step, out in enumerate(outs):
        at = (step // 2) * 2 * rows + (core ^ (step & 1)) * rows
        out[...] = total[pl.ds(pl.multiple_of(at, rows), rows), :].astype(out.dtype)


def finish_kernel(parts, info_ref, *refs):
    core = info_ref[2]
    out_ref = refs[-1]
    half = out_ref.shape[1] // 2
    at = 0
    for part in range(parts):
        mine, his, mine_far, his_far = refs[4 * part : 4 * part + 4]
        wide = mine.shape[1]
        near = pl.ds(pl.multiple_of(core * half + at, LANES), wide)
        away = pl.ds(pl.multiple_of((1 - core) * half + at, LANES), wide)
        out_ref[:, near] = (mine[...] + mine_far[...].astype(f32)).astype(bf16)
        out_ref[:, away] = (his[...].astype(f32) + his_far[...].astype(f32)).astype(bf16)
        at += wide


def on_device(q_gate, values_in, decay_rate, residue, skip_gain, out_weight):
    rows, width = q_gate.shape
    depth, features = out_weight.shape
    order = decay_rate.shape[1]
    count = lax.axis_size("seq")
    heights = count // (2 * TEAM)
    mine = lax.axis_index("seq")
    me, core = mine % TEAM, mine % 2
    y, z = (mine // TEAM) % 2, mine // (2 * TEAM)
    share = width // TEAM
    half = features // 2

    def swap(value, bit):
        return lax.ppermute(value, "seq", [(i, i ^ bit) for i in range(count)])

    def up(value, gap, wrap):
        hop = gap * 2 * TEAM
        pairs = [(i, (i + hop) % count) for i in range(count) if wrap or i + hop < count]
        return lax.ppermute(value, "seq", pairs)

    groups = []
    for gap in range(heights):
        at = (z - gap) % heights
        groups += [at * 2 + y, at * 2 + (1 - y)]
    info = jnp.stack([me, y, core] + groups).astype(jnp.int32)

    keep = lax.dynamic_slice_in_dim(out_weight, core * half, half, 1)
    give = lax.dynamic_slice_in_dim(out_weight, (1 - core) * half, half, 1)
    got = swap(give, 1)
    wide = half // WEIGHT_PARTS
    weights = []
    for part in range(WEIGHT_PARTS):
        cut = slice(part * wide, (part + 1) * wide)
        held = jnp.concatenate([keep[:, cut], got[:, cut]], axis=0)
        slots = [held, swap(held, TEAM)]
        for _ in range(1, heights):
            held = up(held, 1, True)
            slots += [held, swap(held, TEAM)]
        weights.append(slots)

    (values,) = split_channels(info, TEAM, depth, [values_in])
    values = [values[0]] + [swap(values[step], step) for step in range(1, TEAM)]
    (gates,) = split_channels(info, TEAM, depth, [q_gate])
    gates = [gates[0]] + [swap(gates[step], step) for step in range(1, TEAM)]
    (rates,), (residues,) = (
        [split[0]] for split in split_channels(info, TEAM, depth, [decay_rate.T, residue.T])
    )
    coef = residues * jnp.sqrt(-jnp.expm1(-2.0 * rates))
    (skips,) = split_channels(info, TEAM, depth, [skip_gain[None]])
    skip = skips[0]

    tiles = share // LANES
    elements = TEAM * rows * share
    blocks = TEAM * rows // BLOCK
    y_local, end = call(
        local_kernel,
        [
            jax.ShapeDtypeStruct((tiles, TEAM * rows, LANES), f32),
            jax.ShapeDtypeStruct((order, share), f32),
        ],
        [
            pltpu.VMEM((blocks, 2 * BLOCK, LANES), f32),
            pltpu.VMEM((BLOCK, 8, LANES), f32),
            pltpu.VMEM((order, 8, LANES), f32),
            pltpu.VMEM((order, 8, LANES), f32),
            pltpu.VMEM((order, LANES), f32),
        ],
        flops=110 * elements,
        moved=6 * elements,
    )(info, *values, rates, coef, skip)

    near = swap(end, TEAM)
    first, second = jnp.where(y == 0, end, near), jnp.where(y == 0, near, end)
    pair_end = jnp.exp(-float(TEAM * rows) * rates) * first + second
    far = [up(pair_end, gap, False) for gap in range(1, heights)]
    gated = call(
        functools.partial(gate_kernel, heights - 1),
        jax.ShapeDtypeStruct((tiles, TEAM * rows, LANES), bf16),
        [
            pltpu.VMEM((order, 8, LANES), f32),
            pltpu.VMEM((order, 8, LANES), f32),
            pltpu.VMEM((order, LANES), f32),
        ],
        flops=40 * elements,
        moved=8 * elements,
    )(info, *gates, y_local, rates, coef, near, *far)
    other = swap(gated, 1)

    if depth % LANES:
        runs = width // (TEAM * depth)

        def by_group(value):
            value = value.transpose(1, 0, 2).reshape(TEAM * rows, runs, depth)
            return value.transpose(1, 0, 2)

        gated, other = by_group(gated), by_group(other)

    finished = []
    for slots in weights:
        shape = functools.partial(jax.ShapeDtypeStruct, (rows, wide))
        sums = call(
            functools.partial(project_kernel, 2 * heights),
            [shape(f32), shape(f32), shape(bf16), shape(bf16)],
            [pltpu.VMEM((TEAM * rows, wide), f32)],
            flops=TEAM * rows * width * wide,
            moved=TEAM * rows * width + width * wide,
        )(info, gated, other, *slots)
        finished += [sums[0]] + [swap(sums[step], step) for step in range(1, TEAM)]
    return call(
        functools.partial(finish_kernel, WEIGHT_PARTS),
        jax.ShapeDtypeStruct((rows, features), bf16),
        moved=rows * features * 8,
    )(info, *finished)


def solution(mesh):
    in_specs = (
        P(("groups", "seq"), None),
        P(("groups", "seq"), None),
        P(),
        P(),
        P(),
        P("seq", None),
    )
    out_specs = P(("groups", "seq"), None)
    return jax.shard_map(
        on_device, mesh=mesh, in_specs=in_specs, out_specs=out_specs, check_vma=False
    )
```

time: 303 us -> 126 us (0.42)
  matrix products: 119 us -> 0 us
  other arithmetic: 78.8 us -> 0.11 us
  local copies, waits for them, and re-layouts: 77.6 us -> 12.7 us
  starting transfers between devices: 0.27 us -> 49.2 us
  waiting for transfers between devices: 11.8 us -> 38.6 us
  Pallas kernels: 0 us -> 24.7 us
  between operations: 13.2 us -> 0.3 us
    dot_general x5 -> x0, matrix products: 119 us -> none  [the longest x1 47.3 us: on_device(): jnp.einsum('tkd,nkd->ntd', reach_table, starts, precision=lax.Precision.H...]
    ppermute x0 -> x52, starting transfers between devices: none -> 49.2 us  [the longest x37 34.4 us: swap(): return lax.ppermute(value, 'seq', [(i, i ^ bit) for i in range(count)])]
    dot_general x1 -> x0, local copies, waits for them, and re-layouts: 44.1 us -> none  [on_device(): jnp.dot(tap_round.T, selector, preferred_element_type=jnp.bfloat16)]
    select_n x31 -> x0, other arithmetic: 38.9 us -> none  [hop(): jnp.where(position < mine, new, old)]
    ppermute x0 -> x52, waiting for transfers between devices: none -> 38.6 us  [the longest x15 25 us: up(): return lax.ppermute(value, 'seq', pairs)]
    reduce_sum x1 -> x0, other arithmetic: 25.7 us -> none  [on_device(): jnp.sum(mode_coef[None] * jnp.exp(-position[:, None, None] * rate_modes[N...]
    pallas_call x0 -> x11, Pallas kernels: none -> 24.7 us  [run(): pl.pallas_call(kernel, out_shape=out_shape, in_specs=[smem()] + vmem(len(...]
    add x2 -> x0, local copies, waits for them, and re-layouts: 14 us -> none  [the longest x1 7.13 us: on_device(): conv = (local_part + correction).reshape(tok_rows, width)]
  transfers between devices with their start and end apart: 3 -> 52, of which waited for: 2 -> 24; matrix products, arithmetic and copies ran while one was open for 88% -> 3% of each run, Pallas kernels for 0% -> 15%
where the time goes in v1:
time: 126 us
  starting transfers between devices  49.2 us (39%)
  waiting for transfers between devices  38.6 us (31%)
  Pallas kernels  24.7 us (20%)
  local copies, waits for them, and re-layouts  12.7 us (10%)
    ppermute x37, starting transfers between devices, swap(): return lax.ppermute(value, 'seq', [(i, i ^ bit) for i in range(count)])  34.4 us
    ppermute x15, waiting for transfers between devices, up(): return lax.ppermute(value, 'seq', pairs)  25 us
    pallas_call x11, Pallas kernels, run(): pl.pallas_call(kernel, out_shape=out_shape, in_specs=[smem()] + vmem(len(...  24.7 us
    ppermute x15, starting transfers between devices, up(): return lax.ppermute(value, 'seq', pairs)  14.7 us
    ppermute x37, waiting for transfers between devices, swap(): return lax.ppermute(value, 'seq', [(i, i ^ bit) for i in range(count)])  13.6 us
    unnamed x30, local copies, waits for them, and re-layouts  8.39 us
    slice x2, local copies, waits for them, and re-layouts, on_device(): held = jnp.concatenate([keep[:, cut], got[:, cut]], axis=0)  2.56 us
  transfers between devices with their start and end apart: 52, of which 24 were waited for; matrix products, arithmetic and copies ran while one was open for 3% of the time, Pallas kernels for 15%

profile of v1, /device:TPU:0, one launch (start us, length us, event | category | flops | bytes accessed | tf_op | source)
XLA Modules:
  0.0 125.6 jit_solution(9090440822704784168)
XLA Ops:
  0.1 1.2 copy-done
  1.3 0.8 shard_map.65
  2.7 2.6 %collective-permute-start.4 = (bf16[128,1024]{1,0:T(8,128)(2,1)S(1)}, bf16[128,1024]{1,0:T(8,128)(2,1)S(1)}, u32[]{:S(2)}, u32[]{:S(2)}) collective-permute-start(bf16[128,1024]{1,0:T(8,128)(2,1)S(1)} %get-tuple-element.40), channel_id=1, source_target_pairs={{0,2},{1,3},{2,0},{3,1},{4,6},{5,7},{6,4},{7,5},{8,10},{9,11},{10,... | collective-permute-start | bytes 786440 | tf_op jit(solution)/shard_map/ppermute | solution.py:226
  5.3 1.2 copy-done.1
  6.5 1.6 %shard_map.64 = (bf16[128,1024]{1,0:T(8,128)(2,1)S(1)}, bf16[128,1024]{1,0:T(8,128)(2,1)}, bf16[128,1024]{1,0:T(8,128)(2,1)}, bf16[128,1024]{1,0:T(8,128)(2,1)}) custom-call(s32[11]{0:T(128)S(1)} %stack.47.info_ref, bf16[128,4096]{1,0:T(8,128)(2,1)S(1)} %copy-done.1), custom_call_target="tpu_custom_call" | custom-call | bytes 2097152 | tf_op jit(solution)/shard_map/pallas_call | solution.py:32
  8.3 1.9 %collective-permute-start.1 = (bf16[128,1024]{1,0:T(8,128)(2,1)}, bf16[128,1024]{1,0:T(8,128)(2,1)S(1)}, u32[]{:S(2)}, u32[]{:S(2)}) collective-permute-start(bf16[128,1024]{1,0:T(8,128)(2,1)} %get-tuple-element.36), channel_id=1, source_target_pairs={{0,2},{1,3},{2,0},{3,1},{4,6},{5,7},{6,4},{7,5},{8,10},{9,11},{10,... | collective-permute-start | bytes 786440 | tf_op jit(solution)/shard_map/ppermute | solution.py:226
  10.2 1.7 %constant_dynamic-slice_fusion.3 = bf16[128,1024]{1,0:T(8,128)(2,1)} fusion(bf16[128,2048]{1,0:T(8,128)(2,1)} %param.11, s32[]{:T(128)S(6)} %select_n.69), kind=kLoop, calls=%fused_computation.9 | loop fusion | bytes 524292 | tf_op jit(solution)/shard_map/dynamic_slice | solution.py:240
  11.9 1.2 shard_map.67
  13.1 1.4 %shard_map.66 = (f32[16,1024]{1,0:T(8,128)S(1)}, f32[16,1024]{1,0:T(8,128)}, f32[16,1024]{1,0:T(8,128)}, f32[16,1024]{1,0:T(8,128)}, f32[16,1024]{1,0:T(8,128)S(...) custom-call(s32[11]{0:T(128)S(1)} %stack.47.info_ref, f32[16,4096]{1,0:T(8,128)S(1)} %bitcast.14, ...), custom_call_target="tpu_custom_call" | custom-call | bytes 1048576 | tf_op jit(solution)/shard_map/pallas_call | solution.py:32
  16.1 1.4 %collective-permute-done.5.refs_3_ = bf16[128,1024]{1,0:T(8,128)(2,1)S(1)} collective-permute-done((bf16[128,1024]{1,0:T(8,128)(2,1)S(1)}, bf16[128,1024]{1,0:T(8,128)(2,1)S(1)}, u32[]{:S(2)}, u32[]{:S(2)}) %collective-permute-start.5) | collective-permute-done | bytes 262176 | tf_op jit(solution)/shard_map/ppermute | solution.py:226
  17.5 0.7 copy-done.10
  18.2 0.9 copy-done.5
  19.2 0.9 copy-done.7
  20.1 0.9 copy-done.9
  21.1 0.9 copy-done.11
  22.0 10.0 %shard_map.68 = (f32[8,512,128]{2,1,0:T(8,128)S(1)}, f32[16,1024]{1,0:T(8,128)S(1)}) custom-call(s32[11]{0:T(128)S(1)} %stack.47.info_ref, bf16[128,1024]{1,0:T(8,128)(2,1)S(1)} %copy-done.5, bf16[128,1024]{1,0:T(8,128)(2,1)S(1)} %copy-done.7, bf16[128,1024]{1,0:T(8,128)(2,1)S(1)} %copy-done.9, bf16[128,1024]{1,0:T(8,128)(2,1)S(1)} %copy-done.11, ...), custom_call_target="tpu_custom_call" | custom-call | flops 57671680 | bytes 3145728 | tf_op jit(solution)/shard_map/pallas_call | solution.py:32
  32.0 1.7 %collective-permute-start.6 = (f32[16,1024]{1,0:T(8,128)S(1)}, f32[16,1024]{1,0:T(8,128)S(1)}, u32[]{:S(2)}, u32[]{:S(2)}) collective-permute-start(f32[16,1024]{1,0:T(8,128)S(1)} %get-tuple-element.46), channel_id=1, source_target_pairs={{0,4},{1,5},{2,6},{3,7},{4,0},{5,1},{6,2},{7,3},{8,12},{9,13},{10,... | collective-permute-start | bytes 196616 | tf_op jit(solution)/shard_map/ppermute | solution.py:226
  33.6 1.6 %constant_dynamic-slice_fusion.4 = (bf16[128,256]{1,0:T(8,128)(2,1)}, bf16[128,256]{1,0:T(8,128)(2,1)}, bf16[128,256]{1,0:T(8,128)(2,1)S(1)}, bf16[128,256]{1,0:T(8,128)(2,1)S(1)}) fusion(bf16[128,2048]{1,0:T(8,128)(2,1)} %param.11, s32[]{:T(128)S(6)} %add.80, s32[]{:T(128)S(6)} %add.79, s32[]{:T(128)S(6)} %add.78, s32[]{:T(128)S(6)} %select_n.68), kind=kLoop, calls=%fused_computation.10 | loop fusion | bytes 524304 | tf_op jit(solution)/shard_map/slice | solution.py:246
  35.2 1.4 %collective-permute-done.6.refs_7_ = f32[16,1024]{1,0:T(8,128)S(1)} collective-permute-done((f32[16,1024]{1,0:T(8,128)S(1)}, f32[16,1024]{1,0:T(8,128)S(1)}, u32[]{:S(2)}, u32[]{:S(2)}) %collective-permute-start.6) | collective-permute-done | bytes 65568 | tf_op jit(solution)/shard_map/ppermute | solution.py:226
  36.6 3.7 %collective-permute-start.7 = (f32[16,1024]{1,0:T(8,128)S(1)}, f32[16,1024]{1,0:T(8,128)S(1)}, u32[]{:S(2)}, u32[]{:S(2)}) collective-permute-start(f32[16,1024]{1,0:T(8,128)S(1)} %select_add_fusion), channel_id=1, source_target_pairs={{0,8},{1,9},{2,10},{3,11},{4,12},{5,13},{6,14},{7,15},{8,16},{9,17... | collective-permute-start | bytes 196616 | tf_op jit(solution)/shard_map/ppermute | solution.py:231
  40.4 4.5 %collective-permute-start.8 = (f32[16,1024]{1,0:T(8,128)S(1)}, f32[16,1024]{1,0:T(8,128)S(1)}, u32[]{:S(2)}, u32[]{:S(2)}) collective-permute-start(f32[16,1024]{1,0:T(8,128)S(1)} %select_add_fusion), channel_id=1, source_target_pairs={{0,16},{1,17},{2,18},{3,19},{4,20},{5,21},{6,22},{7,23},{8,24},{9,... | collective-permute-start | bytes 196616 | tf_op jit(solution)/shard_map/ppermute | solution.py:231
  44.9 1.3 %collective-permute-start.9 = (f32[16,1024]{1,0:T(8,128)S(1)}, f32[16,1024]{1,0:T(8,128)S(1)}, u32[]{:S(2)}, u32[]{:S(2)}) collective-permute-start(f32[16,1024]{1,0:T(8,128)S(1)} %select_add_fusion), channel_id=1, source_target_pairs={{0,24},{1,25},{2,26},{3,27},{4,28},{5,29},{6,30},{7,31}} | collective-permute-start | bytes 196616 | tf_op jit(solution)/shard_map/ppermute | solution.py:231
  46.2 1.0 fusion
  47.3 0.8 collective-permute-done.9.refs_10_
  48.1 3.3 %shard_map.69.own_ref = bf16[8,512,128]{2,1,0:T(8,128)(2,1)S(1)} custom-call(s32[11]{0:T(128)S(1)} %stack.47.info_ref, bf16[128,1024]{1,0:T(8,128)(2,1)S(1)} %get-tuple-element.34.refs_0_, bf16[128,1024]{1,0:T(8,128)(2,1)S(1)} %collective-permute-done.refs_1_, bf16[128,1024]{1,0:T(8,128)(2,1)S(1)} %collective-permute-done.1.refs_2_, ...), custom_call_target="tpu_custom_call" | custom-call | flops 20971520 | bytes 4194304 | tf_op jit(solution)/shard_map/pallas_call | solution.py:32
  51.6 1.6 %collective-permute-start.42 = (bf16[256,256]{1,0:T(8,128)(2,1)S(1)}, bf16[256,256]{1,0:T(8,128)(2,1)S(1)}, u32[]{:S(2)}, u32[]{:S(2)}) collective-permute-start(bf16[256,256]{1,0:T(8,128)(2,1)S(1)} %pad_maximum_fusion.3.refs_0_), channel_id=1, source_target_pairs={{0,4},{1,5},{2,6},{3,7},{4,0},{5,1},{6,2},{7,3},{8,12},{9,13},{10,... | collective-permute-start | bytes 393224 | tf_op jit(solution)/shard_map/ppermute | solution.py:226
  53.2 3.1 %collective-permute-start.33 = (bf16[256,256]{1,0:T(8,128)(2,1)S(1)}, bf16[256,256]{1,0:T(8,128)(2,1)S(1)}, u32[]{:S(2)}, u32[]{:S(2)}) collective-permute-start(bf16[256,256]{1,0:T(8,128)(2,1)S(1)} %pad_maximum_fusion.2.refs_0_), channel_id=1, source_target_pairs={{0,8},{1,9},{2,10},{3,11},{4,12},{5,13},{6,14},{7,15},{8,16},{9,17... | collective-permute-start | bytes 393224 | tf_op jit(solution)/shard_map/ppermute | solution.py:231
  56.8 3.3 %collective-permute-done.43.refs_2_ = bf16[256,256]{1,0:T(8,128)(2,1)S(1)} collective-permute-done((bf16[256,256]{1,0:T(8,128)(2,1)S(1)}, bf16[256,256]{1,0:T(8,128)(2,1)S(1)}, u32[]{:S(2)}, u32[]{:S(2)}) %collective-permute-start.43) | collective-permute-done | bytes 131104 | tf_op jit(solution)/shard_map/ppermute | solution.py:231
  60.1 1.5 %collective-permute-start.22 = (bf16[256,256]{1,0:T(8,128)(2,1)S(1)}, bf16[256,256]{1,0:T(8,128)(2,1)S(1)}, u32[]{:S(2)}, u32[]{:S(2)}) collective-permute-start(bf16[256,256]{1,0:T(8,128)(2,1)S(1)} %pad_maximum_fusion.1.refs_0_), channel_id=1, source_target_pairs={{0,4},{1,5},{2,6},{3,7},{4,0},{5,1},{6,2},{7,3},{8,12},{9,13},{10,... | collective-permute-start | bytes 393224 | tf_op jit(solution)/shard_map/ppermute | solution.py:226
  61.6 1.1 collective-permute-done.33.refs_2_
  62.7 2.0 %collective-permute-start.45 = (bf16[256,256]{1,0:T(8,128)(2,1)S(1)}, bf16[256,256]{1,0:T(8,128)(2,1)S(1)}, u32[]{:S(2)}, u32[]{:S(2)}) collective-permute-start(bf16[256,256]{1,0:T(8,128)(2,1)S(1)} %collective-permute-done.43.refs_2_), channel_id=1, source_target_pairs={{0,8},{1,9},{2,10},{3,11},{4,12},{5,13},{6,14},{7,15},{8,16},{9,17... | collective-permute-start | bytes 393224 | tf_op jit(solution)/shard_map/ppermute | solution.py:231
  64.7 2.3 %collective-permute-done.23.refs_2_ = bf16[256,256]{1,0:T(8,128)(2,1)S(1)} collective-permute-done((bf16[256,256]{1,0:T(8,128)(2,1)S(1)}, bf16[256,256]{1,0:T(8,128)(2,1)S(1)}, u32[]{:S(2)}, u32[]{:S(2)}) %collective-permute-start.23) | collective-permute-done | bytes 131104 | tf_op jit(solution)/shard_map/ppermute | solution.py:231
  67.0 1.5 %collective-permute-start.44 = (bf16[256,256]{1,0:T(8,128)(2,1)S(1)}, bf16[256,256]{1,0:T(8,128)(2,1)S(1)}, u32[]{:S(2)}, u32[]{:S(2)}) collective-permute-start(bf16[256,256]{1,0:T(8,128)(2,1)S(1)} %collective-permute-done.43.refs_2_), channel_id=1, source_target_pairs={{0,4},{1,5},{2,6},{3,7},{4,0},{5,1},{6,2},{7,3},{8,12},{9,13},{10,... | collective-permute-start | bytes 393224 | tf_op jit(solution)/shard_map/ppermute | solution.py:226
  68.5 2.3 %collective-permute-done.13.refs_2_ = bf16[256,256]{1,0:T(8,128)(2,1)S(1)} collective-permute-done((bf16[256,256]{1,0:T(8,128)(2,1)S(1)}, bf16[256,256]{1,0:T(8,128)(2,1)S(1)}, u32[]{:S(2)}, u32[]{:S(2)}) %collective-permute-start.13) | collective-permute-done | bytes 131104 | tf_op jit(solution)/shard_map/ppermute | solution.py:231
  70.9 1.5 %collective-permute-start.34 = (bf16[256,256]{1,0:T(8,128)(2,1)S(1)}, bf16[256,256]{1,0:T(8,128)(2,1)S(1)}, u32[]{:S(2)}, u32[]{:S(2)}) collective-permute-start(bf16[256,256]{1,0:T(8,128)(2,1)S(1)} %collective-permute-done.33.refs_2_), channel_id=1, source_target_pairs={{0,4},{1,5},{2,6},{3,7},{4,0},{5,1},{6,2},{7,3},{8,12},{9,13},{10,... | collective-permute-start | bytes 393224 | tf_op jit(solution)/shard_map/ppermute | solution.py:226
  72.4 1.3 %collective-permute-done.45.refs_4_ = bf16[256,256]{1,0:T(8,128)(2,1)S(1)} collective-permute-done((bf16[256,256]{1,0:T(8,128)(2,1)S(1)}, bf16[256,256]{1,0:T(8,128)(2,1)S(1)}, u32[]{:S(2)}, u32[]{:S(2)}) %collective-permute-start.45) | collective-permute-done | bytes 131104 | tf_op jit(solution)/shard_map/ppermute | solution.py:231
  73.7 1.5 %collective-permute-start.24 = (bf16[256,256]{1,0:T(8,128)(2,1)S(1)}, bf16[256,256]{1,0:T(8,128)(2,1)S(1)}, u32[]{:S(2)}, u32[]{:S(2)}) collective-permute-start(bf16[256,256]{1,0:T(8,128)(2,1)S(1)} %collective-permute-done.23.refs_2_), channel_id=1, source_target_pairs={{0,4},{1,5},{2,6},{3,7},{4,0},{5,1},{6,2},{7,3},{8,12},{9,13},{10,... | collective-permute-start | bytes 393224 | tf_op jit(solution)/shard_map/ppermute | solution.py:226
  75.4 1.6 %collective-permute-done.34.refs_3_ = bf16[256,256]{1,0:T(8,128)(2,1)S(1)} collective-permute-done((bf16[256,256]{1,0:T(8,128)(2,1)S(1)}, bf16[256,256]{1,0:T(8,128)(2,1)S(1)}, u32[]{:S(2)}, u32[]{:S(2)}) %collective-permute-start.34) | collective-permute-done | bytes 131104 | tf_op jit(solution)/shard_map/ppermute | solution.py:226
  77.1 4.7 %collective-permute-done.25.refs_4_ = bf16[256,256]{1,0:T(8,128)(2,1)S(1)} collective-permute-done((bf16[256,256]{1,0:T(8,128)(2,1)S(1)}, bf16[256,256]{1,0:T(8,128)(2,1)S(1)}, u32[]{:S(2)}, u32[]{:S(2)}) %collective-permute-start.25) | collective-permute-done | bytes 131104 | tf_op jit(solution)/shard_map/ppermute | solution.py:231
  81.8 1.6 %collective-permute-start.46 = (bf16[256,256]{1,0:T(8,128)(2,1)S(1)}, bf16[256,256]{1,0:T(8,128)(2,1)S(1)}, u32[]{:S(2)}, u32[]{:S(2)}) collective-permute-start(bf16[256,256]{1,0:T(8,128)(2,1)S(1)} %collective-permute-done.45.refs_4_), channel_id=1, source_target_pairs={{0,4},{1,5},{2,6},{3,7},{4,0},{5,1},{6,2},{7,3},{8,12},{9,13},{10,... | collective-permute-start | bytes 393224 | tf_op jit(solution)/shard_map/ppermute | solution.py:226
  83.4 1.2 collective-permute-done.15.refs_4_
  84.6 1.6 %collective-permute-start.36 = (bf16[256,256]{1,0:T(8,128)(2,1)S(1)}, bf16[256,256]{1,0:T(8,128)(2,1)S(1)}, u32[]{:S(2)}, u32[]{:S(2)}) collective-permute-start(bf16[256,256]{1,0:T(8,128)(2,1)S(1)} %collective-permute-done.35.refs_4_), channel_id=1, source_target_pairs={{0,4},{1,5},{2,6},{3,7},{4,0},{5,1},{6,2},{7,3},{8,12},{9,13},{10,... | collective-permute-start | bytes 393224 | tf_op jit(solution)/shard_map/ppermute | solution.py:226
  86.2 0.8 collective-permute-done.47.refs_6_
  87.0 1.8 %collective-permute-start.26 = (bf16[256,256]{1,0:T(8,128)(2,1)S(1)}, bf16[256,256]{1,0:T(8,128)(2,1)S(1)}, u32[]{:S(2)}, u32[]{:S(2)}) collective-permute-start(bf16[256,256]{1,0:T(8,128)(2,1)S(1)} %collective-permute-done.25.refs_4_), channel_id=1, source_target_pairs={{0,4},{1,5},{2,6},{3,7},{4,0},{5,1},{6,2},{7,3},{8,12},{9,13},{10,... | collective-permute-start | bytes 393224 | tf_op jit(solution)/shard_map/ppermute | solution.py:226
  88.8 2.3 %collective-permute-done.37.refs_6_ = bf16[256,256]{1,0:T(8,128)(2,1)S(1)} collective-permute-done((bf16[256,256]{1,0:T(8,128)(2,1)S(1)}, bf16[256,256]{1,0:T(8,128)(2,1)S(1)}, u32[]{:S(2)}, u32[]{:S(2)}) %collective-permute-start.37) | collective-permute-done | bytes 131104 | tf_op jit(solution)/shard_map/ppermute | solution.py:231
  91.3 2.6 %collective-permute-done.27.refs_6_ = bf16[256,256]{1,0:T(8,128)(2,1)S(1)} collective-permute-done((bf16[256,256]{1,0:T(8,128)(2,1)S(1)}, bf16[256,256]{1,0:T(8,128)(2,1)S(1)}, u32[]{:S(2)}, u32[]{:S(2)}) %collective-permute-start.27) | collective-permute-done | bytes 131104 | tf_op jit(solution)/shard_map/ppermute | solution.py:231
  93.9 2.0 %collective-permute-start.38 = (bf16[256,256]{1,0:T(8,128)(2,1)S(1)}, bf16[256,256]{1,0:T(8,128)(2,1)S(1)}, u32[]{:S(2)}, u32[]{:S(2)}) collective-permute-start(bf16[256,256]{1,0:T(8,128)(2,1)S(1)} %collective-permute-done.37.refs_6_), channel_id=1, source_target_pairs={{0,4},{1,5},{2,6},{3,7},{4,0},{5,1},{6,2},{7,3},{8,12},{9,13},{10,... | collective-permute-start | bytes 393224 | tf_op jit(solution)/shard_map/ppermute | solution.py:226
  96.0 1.9 %collective-permute-done.17.refs_6_ = bf16[256,256]{1,0:T(8,128)(2,1)S(1)} collective-permute-done((bf16[256,256]{1,0:T(8,128)(2,1)S(1)}, bf16[256,256]{1,0:T(8,128)(2,1)S(1)}, u32[]{:S(2)}, u32[]{:S(2)}) %collective-permute-start.17) | collective-permute-done | bytes 131104 | tf_op jit(solution)/shard_map/ppermute | solution.py:231
  98.0 2.0 %collective-permute-start.14 = (bf16[256,256]{1,0:T(8,128)(2,1)S(1)}, bf16[256,256]{1,0:T(8,128)(2,1)S(1)}, u32[]{:S(2)}, u32[]{:S(2)}) collective-permute-start(bf16[256,256]{1,0:T(8,128)(2,1)S(1)} %collective-permute-done.13.refs_2_), channel_id=1, source_target_pairs={{0,4},{1,5},{2,6},{3,7},{4,0},{5,1},{6,2},{7,3},{8,12},{9,13},{10,... | collective-permute-start | bytes 393224 | tf_op jit(solution)/shard_map/ppermute | solution.py:226
  100.3 2.0 %collective-permute-start.16 = (bf16[256,256]{1,0:T(8,128)(2,1)S(1)}, bf16[256,256]{1,0:T(8,128)(2,1)S(1)}, u32[]{:S(2)}, u32[]{:S(2)}) collective-permute-start(bf16[256,256]{1,0:T(8,128)(2,1)S(1)} %collective-permute-done.15.refs_4_), channel_id=1, source_target_pairs={{0,4},{1,5},{2,6},{3,7},{4,0},{5,1},{6,2},{7,3},{8,12},{9,13},{10,... | collective-permute-start | bytes 393224 | tf_op jit(solution)/shard_map/ppermute | solution.py:226
  102.4 1.3 %shard_map.73 = (f32[128,256]{1,0:T(8,128)S(1)}, f32[128,256]{1,0:T(8,128)S(1)}, bf16[128,256]{1,0:T(8,128)(2,1)S(1)}, bf16[128,256]{1,0:T(8,128)(2,1)S(1)}) custom-call(s32[11]{0:T(128)S(1)} %stack.47.info_ref, bf16[8,512,128]{2,1,0:T(8,128)(2,1)S(1)} %shard_map.69.own_ref, bf16[8,512,128]{2,1,0:T(8,128)(2,1)S(1)} %collective-permute-done.10.other_ref, ...), custom_call_target="tpu_custom_call" | custom-call | flops 536870912 | bytes 3145728 | tf_op jit(solution)/shard_map/pallas_call | solution.py:32
  103.7 1.6 %collective-permute-start.50 = (bf16[128,256]{1,0:T(8,128)(2,1)S(1)}, bf16[128,256]{1,0:T(8,128)(2,1)S(1)}, u32[]{:S(2)}, u32[]{:S(2)}) collective-permute-start(bf16[128,256]{1,0:T(8,128)(2,1)S(1)} %get-tuple-element.61), channel_id=1, source_target_pairs={{0,2},{1,3},{2,0},{3,1},{4,6},{5,7},{6,4},{7,5},{8,10},{9,11},{10,... | collective-permute-start | bytes 196616 | tf_op jit(solution)/shard_map/ppermute | solution.py:226
  105.2 1.3 %shard_map.72 = (f32[128,256]{1,0:T(8,128)S(1)}, f32[128,256]{1,0:T(8,128)S(1)}, bf16[128,256]{1,0:T(8,128)(2,1)S(1)}, bf16[128,256]{1,0:T(8,128)(2,1)S(1)}) custom-call(s32[11]{0:T(128)S(1)} %stack.47.info_ref, bf16[8,512,128]{2,1,0:T(8,128)(2,1)S(1)} %shard_map.69.own_ref, bf16[8,512,128]{2,1,0:T(8,128)(2,1)S(1)} %collective-permute-done.10.other_ref, ...), custom_call_target="tpu_custom_call" | custom-call | flops 536870912 | bytes 3145728 | tf_op jit(solution)/shard_map/pallas_call | solution.py:32
  106.5 1.3 %shard_map.71 = (f32[128,256]{1,0:T(8,128)S(1)}, f32[128,256]{1,0:T(8,128)S(1)}, bf16[128,256]{1,0:T(8,128)(2,1)S(1)}, bf16[128,256]{1,0:T(8,128)(2,1)S(1)}) custom-call(s32[11]{0:T(128)S(1)} %stack.47.info_ref, bf16[8,512,128]{2,1,0:T(8,128)(2,1)S(1)} %shard_map.69.own_ref, bf16[8,512,128]{2,1,0:T(8,128)(2,1)S(1)} %collective-permute-done.10.other_ref, ...), custom_call_target="tpu_custom_call" | custom-call | flops 536870912 | bytes 3145728 | tf_op jit(solution)/shard_map/pallas_call | solution.py:32
  107.9 0.9 collective-permute-done.14.refs_3_
  108.8 1.5 %collective-permute-start.40 = (bf16[128,256]{1,0:T(8,128)(2,1)S(1)}, bf16[128,256]{1,0:T(8,128)(2,1)S(1)}, u32[]{:S(2)}, u32[]{:S(2)}) collective-permute-start(bf16[128,256]{1,0:T(8,128)(2,1)S(1)} %get-tuple-element.57), channel_id=1, source_target_pairs={{0,2},{1,3},{2,0},{3,1},{4,6},{5,7},{6,4},{7,5},{8,10},{9,11},{10,... | collective-permute-start | bytes 196616 | tf_op jit(solution)/shard_map/ppermute | solution.py:226
  110.4 1.4 %collective-permute-done.18.refs_7_ = bf16[256,256]{1,0:T(8,128)(2,1)S(1)} collective-permute-done((bf16[256,256]{1,0:T(8,128)(2,1)S(1)}, bf16[256,256]{1,0:T(8,128)(2,1)S(1)}, u32[]{:S(2)}, u32[]{:S(2)}) %collective-permute-start.18) | collective-permute-done | bytes 131104 | tf_op jit(solution)/shard_map/ppermute | solution.py:226
  111.8 1.5 %collective-permute-start.30 = (bf16[128,256]{1,0:T(8,128)(2,1)S(1)}, bf16[128,256]{1,0:T(8,128)(2,1)S(1)}, u32[]{:S(2)}, u32[]{:S(2)}) collective-permute-start(bf16[128,256]{1,0:T(8,128)(2,1)S(1)} %get-tuple-element.53), channel_id=1, source_target_pairs={{0,2},{1,3},{2,0},{3,1},{4,6},{5,7},{6,4},{7,5},{8,10},{9,11},{10,... | collective-permute-start | bytes 196616 | tf_op jit(solution)/shard_map/ppermute | solution.py:226
  113.4 1.3 %shard_map.70 = (f32[128,256]{1,0:T(8,128)S(1)}, f32[128,256]{1,0:T(8,128)S(1)}, bf16[128,256]{1,0:T(8,128)(2,1)S(1)}, bf16[128,256]{1,0:T(8,128)(2,1)S(1)}) custom-call(s32[11]{0:T(128)S(1)} %stack.47.info_ref, bf16[8,512,128]{2,1,0:T(8,128)(2,1)S(1)} %shard_map.69.own_ref, bf16[8,512,128]{2,1,0:T(8,128)(2,1)S(1)} %collective-permute-done.10.other_ref, ...), custom_call_target="tpu_custom_call" | custom-call | flops 536870912 | bytes 3145728 | tf_op jit(solution)/shard_map/pallas_call | solution.py:32
  115.4 1.5 %collective-permute-start.20 = (bf16[128,256]{1,0:T(8,128)(2,1)S(1)}, bf16[128,256]{1,0:T(8,128)(2,1)S(1)}, u32[]{:S(2)}, u32[]{:S(2)}) collective-permute-start(bf16[128,256]{1,0:T(8,128)(2,1)S(1)} %get-tuple-element.49), channel_id=1, source_target_pairs={{0,2},{1,3},{2,0},{3,1},{4,6},{5,7},{6,4},{7,5},{8,10},{9,11},{10,... | collective-permute-start | bytes 196616 | tf_op jit(solution)/shard_map/ppermute | solution.py:226
  117.6 2.2 %collective-permute-done.20.refs_2_ = bf16[128,256]{1,0:T(8,128)(2,1)S(1)} collective-permute-done((bf16[128,256]{1,0:T(8,128)(2,1)S(1)}, bf16[128,256]{1,0:T(8,128)(2,1)S(1)}, u32[]{:S(2)}, u32[]{:S(2)}) %collective-permute-start.20) | collective-permute-done | bytes 65568 | tf_op jit(solution)/shard_map/ppermute | solution.py:226
  119.8 0.7 collective-permute-start.21
  120.6 3.6 %collective-permute-done.21.refs_3_ = bf16[128,256]{1,0:T(8,128)(2,1)S(1)} collective-permute-done((bf16[128,256]{1,0:T(8,128)(2,1)S(1)}, bf16[128,256]{1,0:T(8,128)(2,1)S(1)}, u32[]{:S(2)}, u32[]{:S(2)}) %collective-permute-start.21) | collective-permute-done | bytes 65568 | tf_op jit(solution)/shard_map/ppermute | solution.py:226
  124.2 1.4 %shard_map.74 = bf16[128,2048]{1,0:T(8,128)(2,1)} custom-call(s32[11]{0:T(128)S(1)} %stack.47.info_ref, f32[128,256]{1,0:T(8,128)S(1)} %get-tuple-element.47.refs_0_, f32[128,256]{1,0:T(8,128)S(1)} %collective-permute-done.19.refs_1_, bf16[128,256]{1,0:T(8,128)(2,1)S(1)} %collective-permute-done.20.refs_2_, ...), custom_call_target="tpu_custom_call" | custom-call | bytes 2097152 | tf_op jit(solution)/shard_map/pallas_call | solution.py:32
  (91 shorter events, 6.1 us)
Async XLA Ops:
  0.0 11.9 %copy-start.12 = (f32[4096]{0:T(1024)S(1)}, f32[4096]{0:T(1024)}, u32[]{:S(2)}) copy-start(f32[4096]{0:T(1024)} %param.10) | copy-start | bytes 49156
  0.1 1.2 copy-start
  1.3 11.8 %copy-start.2 = (f32[4096,16]{0,1:T(8,128)S(1)}, f32[4096,16]{0,1:T(8,128)}, u32[]{:S(2)}) copy-start(f32[4096,16]{0,1:T(8,128)} %param.8) | copy-start | bytes 786436
  1.3 11.8 %copy-start.3 = (f32[4096,16]{0,1:T(8,128)S(1)}, f32[4096,16]{0,1:T(8,128)}, u32[]{:S(2)}) copy-start(f32[4096,16]{0,1:T(8,128)} %param.9) | copy-start | bytes 786436
  2.2 6.1 %copy-start.4 = (bf16[128,1024]{1,0:T(8,128)(2,1)}, bf16[128,1024]{1,0:T(8,128)(2,1)S(1)}, u32[]{:S(2)}) copy-start(bf16[128,1024]{1,0:T(8,128)(2,1)S(1)} %get-tuple-element.38.refs_0_) | copy-start | bytes 786436
  2.2 12.3 %collective-permute-start.3 = (bf16[128,1024]{1,0:T(8,128)(2,1)S(1)}, bf16[128,1024]{1,0:T(8,128)(2,1)S(1)}, u32[]{:S(2)}, u32[]{:S(2)}) collective-permute-start(bf16[128,1024]{1,0:T(8,128)(2,1)S(1)} %get-tuple-element.39), channel_id=1, source_target_pairs={{0,1},{1,0},{2,3},{3,2},{4,5},{5,4},{6,7},{7,6},{8,9},{9,8},{10,11... | collective-permute-start | bytes 786440 | tf_op jit(solution)/shard_map/ppermute | solution.py:226
  2.7 12.5 %collective-permute-start.4 = (bf16[128,1024]{1,0:T(8,128)(2,1)S(1)}, bf16[128,1024]{1,0:T(8,128)(2,1)S(1)}, u32[]{:S(2)}, u32[]{:S(2)}) collective-permute-start(bf16[128,1024]{1,0:T(8,128)(2,1)S(1)} %get-tuple-element.40), channel_id=1, source_target_pairs={{0,2},{1,3},{2,0},{3,1},{4,6},{5,7},{6,4},{7,5},{8,10},{9,11},{10,... | collective-permute-start | bytes 786440 | tf_op jit(solution)/shard_map/ppermute | solution.py:226
  5.2 12.3 %collective-permute-start.5 = (bf16[128,1024]{1,0:T(8,128)(2,1)S(1)}, bf16[128,1024]{1,0:T(8,128)(2,1)S(1)}, u32[]{:S(2)}, u32[]{:S(2)}) collective-permute-start(bf16[128,1024]{1,0:T(8,128)(2,1)S(1)} %get-tuple-element.41), channel_id=1, source_target_pairs={{0,3},{1,2},{2,1},{3,0},{4,7},{5,6},{6,5},{7,4},{8,11},{9,10},{10,... | collective-permute-start | bytes 786440 | tf_op jit(solution)/shard_map/ppermute | solution.py:226
  5.3 1.2 copy-start.1
  8.2 32.2 %collective-permute-start = (bf16[128,1024]{1,0:T(8,128)(2,1)}, bf16[128,1024]{1,0:T(8,128)(2,1)S(1)}, u32[]{:S(2)}, u32[]{:S(2)}) collective-permute-start(bf16[128,1024]{1,0:T(8,128)(2,1)} %get-tuple-element.35), channel_id=1, source_target_pairs={{0,1},{1,0},{2,3},{3,2},{4,5},{5,4},{6,7},{7,6},{8,9},{9,8},{10,11... | collective-permute-start | bytes 786440 | tf_op jit(solution)/shard_map/ppermute | solution.py:226
  8.3 38.9 %collective-permute-start.1 = (bf16[128,1024]{1,0:T(8,128)(2,1)}, bf16[128,1024]{1,0:T(8,128)(2,1)S(1)}, u32[]{:S(2)}, u32[]{:S(2)}) collective-permute-start(bf16[128,1024]{1,0:T(8,128)(2,1)} %get-tuple-element.36), channel_id=1, source_target_pairs={{0,2},{1,3},{2,0},{3,1},{4,6},{5,7},{6,4},{7,5},{8,10},{9,11},{10,... | collective-permute-start | bytes 786440 | tf_op jit(solution)/shard_map/ppermute | solution.py:226
  15.2 32.0 %collective-permute-start.2 = (bf16[128,1024]{1,0:T(8,128)(2,1)}, bf16[128,1024]{1,0:T(8,128)(2,1)S(1)}, u32[]{:S(2)}, u32[]{:S(2)}) collective-permute-start(bf16[128,1024]{1,0:T(8,128)(2,1)} %get-tuple-element.37), channel_id=1, source_target_pairs={{0,3},{1,2},{2,1},{3,0},{4,7},{5,6},{6,5},{7,4},{8,11},{9,10},{10,... | collective-permute-start | bytes 786440 | tf_op jit(solution)/shard_map/ppermute | solution.py:226
  15.9 29.0 %collective-permute-start.11 = (bf16[128,1024]{1,0:T(8,128)(2,1)}, bf16[128,1024]{1,0:T(8,128)(2,1)}, u32[]{:S(2)}, u32[]{:S(2)}) collective-permute-start(bf16[128,1024]{1,0:T(8,128)(2,1)} %constant_dynamic-slice_fusion.3), channel_id=1, source_target_pairs={{0,1},{1,0},{2,3},{3,2},{4,5},{5,4},{6,7},{7,6},{8,9},{9,8},{10,11... | collective-permute-start | bytes 786440 | tf_op jit(solution)/shard_map/ppermute | solution.py:226
  18.2 0.9 copy-start.5
  19.2 0.9 copy-start.7
  20.1 0.9 copy-start.9
  21.1 0.9 copy-start.11
  32.0 4.6 %collective-permute-start.6 = (f32[16,1024]{1,0:T(8,128)S(1)}, f32[16,1024]{1,0:T(8,128)S(1)}, u32[]{:S(2)}, u32[]{:S(2)}) collective-permute-start(f32[16,1024]{1,0:T(8,128)S(1)} %get-tuple-element.46), channel_id=1, source_target_pairs={{0,4},{1,5},{2,6},{3,7},{4,0},{5,1},{6,2},{7,3},{8,12},{9,13},{10,... | collective-permute-start | bytes 196616 | tf_op jit(solution)/shard_map/ppermute | solution.py:226
  36.6 10.5 %collective-permute-start.7 = (f32[16,1024]{1,0:T(8,128)S(1)}, f32[16,1024]{1,0:T(8,128)S(1)}, u32[]{:S(2)}, u32[]{:S(2)}) collective-permute-start(f32[16,1024]{1,0:T(8,128)S(1)} %select_add_fusion), channel_id=1, source_target_pairs={{0,8},{1,9},{2,10},{3,11},{4,12},{5,13},{6,14},{7,15},{8,16},{9,17... | collective-permute-start | bytes 196616 | tf_op jit(solution)/shard_map/ppermute | solution.py:231
  40.4 6.9 %collective-permute-start.8 = (f32[16,1024]{1,0:T(8,128)S(1)}, f32[16,1024]{1,0:T(8,128)S(1)}, u32[]{:S(2)}, u32[]{:S(2)}) collective-permute-start(f32[16,1024]{1,0:T(8,128)S(1)} %select_add_fusion), channel_id=1, source_target_pairs={{0,16},{1,17},{2,18},{3,19},{4,20},{5,21},{6,22},{7,23},{8,24},{9,... | collective-permute-start | bytes 196616 | tf_op jit(solution)/shard_map/ppermute | solution.py:231
  44.9 3.2 %collective-permute-start.9 = (f32[16,1024]{1,0:T(8,128)S(1)}, f32[16,1024]{1,0:T(8,128)S(1)}, u32[]{:S(2)}, u32[]{:S(2)}) collective-permute-start(f32[16,1024]{1,0:T(8,128)S(1)} %select_add_fusion), channel_id=1, source_target_pairs={{0,24},{1,25},{2,26},{3,27},{4,28},{5,29},{6,30},{7,31}} | collective-permute-start | bytes 196616 | tf_op jit(solution)/shard_map/ppermute | solution.py:231
  48.1 3.4 %copy-start.14 = (bf16[128,256]{1,0:T(8,128)(2,1)S(1)}, bf16[128,256]{1,0:T(8,128)(2,1)}, u32[]{:S(2)}) copy-start(bf16[128,256]{1,0:T(8,128)(2,1)} %get-tuple-element.63) | copy-start | bytes 196612
  48.1 5.1 %copy-start.13 = (bf16[128,256]{1,0:T(8,128)(2,1)S(1)}, bf16[128,256]{1,0:T(8,128)(2,1)}, u32[]{:S(2)}) copy-start(bf16[128,256]{1,0:T(8,128)(2,1)} %get-tuple-element.64) | copy-start | bytes 196612
  51.4 51.0 %collective-permute-start.10 = (bf16[8,512,128]{2,1,0:T(8,128)(2,1)S(1)}, bf16[8,512,128]{2,1,0:T(8,128)(2,1)S(1)}, u32[]{:S(2)}, u32[]{:S(2)}) collective-permute-start(bf16[8,512,128]{2,1,0:T(8,128)(2,1)S(1)} %shard_map.69.own_ref), channel_id=1, source_target_pairs={{0,1},{1,0},{2,3},{3,2},{4,5},{5,4},{6,7},{7,6},{8,9},{9,8},{10,11... | collective-permute-start | bytes 3145736 | tf_op jit(solution)/shard_map/ppermute | solution.py:226
  51.5 8.6 %collective-permute-start.43 = (bf16[256,256]{1,0:T(8,128)(2,1)S(1)}, bf16[256,256]{1,0:T(8,128)(2,1)S(1)}, u32[]{:S(2)}, u32[]{:S(2)}) collective-permute-start(bf16[256,256]{1,0:T(8,128)(2,1)S(1)} %pad_maximum_fusion.3.refs_0_), channel_id=1, source_target_pairs={{0,8},{1,9},{2,10},{3,11},{4,12},{5,13},{6,14},{7,15},{8,16},{9,17... | collective-permute-start | bytes 393224 | tf_op jit(solution)/shard_map/ppermute | solution.py:231
  51.6 8.5 %collective-permute-start.42 = (bf16[256,256]{1,0:T(8,128)(2,1)S(1)}, bf16[256,256]{1,0:T(8,128)(2,1)S(1)}, u32[]{:S(2)}, u32[]{:S(2)}) collective-permute-start(bf16[256,256]{1,0:T(8,128)(2,1)S(1)} %pad_maximum_fusion.3.refs_0_), channel_id=1, source_target_pairs={{0,4},{1,5},{2,6},{3,7},{4,0},{5,1},{6,2},{7,3},{8,12},{9,13},{10,... | collective-permute-start | bytes 393224 | tf_op jit(solution)/shard_map/ppermute | solution.py:226
  53.2 9.5 %collective-permute-start.33 = (bf16[256,256]{1,0:T(8,128)(2,1)S(1)}, bf16[256,256]{1,0:T(8,128)(2,1)S(1)}, u32[]{:S(2)}, u32[]{:S(2)}) collective-permute-start(bf16[256,256]{1,0:T(8,128)(2,1)S(1)} %pad_maximum_fusion.2.refs_0_), channel_id=1, source_target_pairs={{0,8},{1,9},{2,10},{3,11},{4,12},{5,13},{6,14},{7,15},{8,16},{9,17... | collective-permute-start | bytes 393224 | tf_op jit(solution)/shard_map/ppermute | solution.py:231
  56.3 6.4 %collective-permute-start.32 = (bf16[256,256]{1,0:T(8,128)(2,1)S(1)}, bf16[256,256]{1,0:T(8,128)(2,1)S(1)}, u32[]{:S(2)}, u32[]{:S(2)}) collective-permute-start(bf16[256,256]{1,0:T(8,128)(2,1)S(1)} %pad_maximum_fusion.2.refs_0_), channel_id=1, source_target_pairs={{0,4},{1,5},{2,6},{3,7},{4,0},{5,1},{6,2},{7,3},{8,12},{9,13},{10,... | collective-permute-start | bytes 393224 | tf_op jit(solution)/shard_map/ppermute | solution.py:226
  60.1 6.9 %collective-permute-start.23 = (bf16[256,256]{1,0:T(8,128)(2,1)S(1)}, bf16[256,256]{1,0:T(8,128)(2,1)S(1)}, u32[]{:S(2)}, u32[]{:S(2)}) collective-permute-start(bf16[256,256]{1,0:T(8,128)(2,1)S(1)} %pad_maximum_fusion.1.refs_0_), channel_id=1, source_target_pairs={{0,8},{1,9},{2,10},{3,11},{4,12},{5,13},{6,14},{7,15},{8,16},{9,17... | collective-permute-start | bytes 393224 | tf_op jit(solution)/shard_map/ppermute | solution.py:231
  60.1 8.4 %collective-permute-start.22 = (bf16[256,256]{1,0:T(8,128)(2,1)S(1)}, bf16[256,256]{1,0:T(8,128)(2,1)S(1)}, u32[]{:S(2)}, u32[]{:S(2)}) collective-permute-start(bf16[256,256]{1,0:T(8,128)(2,1)S(1)} %pad_maximum_fusion.1.refs_0_), channel_id=1, source_target_pairs={{0,4},{1,5},{2,6},{3,7},{4,0},{5,1},{6,2},{7,3},{8,12},{9,13},{10,... | collective-permute-start | bytes 393224 | tf_op jit(solution)/shard_map/ppermute | solution.py:226
  62.7 8.2 %collective-permute-start.13 = (bf16[256,256]{1,0:T(8,128)(2,1)S(1)}, bf16[256,256]{1,0:T(8,128)(2,1)S(1)}, u32[]{:S(2)}, u32[]{:S(2)}) collective-permute-start(bf16[256,256]{1,0:T(8,128)(2,1)S(1)} %pad_maximum_fusion.refs_0_), channel_id=1, source_target_pairs={{0,8},{1,9},{2,10},{3,11},{4,12},{5,13},{6,14},{7,15},{8,16},{9,17... | collective-permute-start | bytes 393224 | tf_op jit(solution)/shard_map/ppermute | solution.py:231
  62.7 11.0 %collective-permute-start.45 = (bf16[256,256]{1,0:T(8,128)(2,1)S(1)}, bf16[256,256]{1,0:T(8,128)(2,1)S(1)}, u32[]{:S(2)}, u32[]{:S(2)}) collective-permute-start(bf16[256,256]{1,0:T(8,128)(2,1)S(1)} %collective-permute-done.43.refs_2_), channel_id=1, source_target_pairs={{0,8},{1,9},{2,10},{3,11},{4,12},{5,13},{6,14},{7,15},{8,16},{9,17... | collective-permute-start | bytes 393224 | tf_op jit(solution)/shard_map/ppermute | solution.py:231
  67.0 6.7 %collective-permute-start.44 = (bf16[256,256]{1,0:T(8,128)(2,1)S(1)}, bf16[256,256]{1,0:T(8,128)(2,1)S(1)}, u32[]{:S(2)}, u32[]{:S(2)}) collective-permute-start(bf16[256,256]{1,0:T(8,128)(2,1)S(1)} %collective-permute-done.43.refs_2_), channel_id=1, source_target_pairs={{0,4},{1,5},{2,6},{3,7},{4,0},{5,1},{6,2},{7,3},{8,12},{9,13},{10,... | collective-permute-start | bytes 393224 | tf_op jit(solution)/shard_map/ppermute | solution.py:226
  68.5 6.9 %collective-permute-start.35 = (bf16[256,256]{1,0:T(8,128)(2,1)S(1)}, bf16[256,256]{1,0:T(8,128)(2,1)S(1)}, u32[]{:S(2)}, u32[]{:S(2)}) collective-permute-start(bf16[256,256]{1,0:T(8,128)(2,1)S(1)} %collective-permute-done.33.refs_2_), channel_id=1, source_target_pairs={{0,8},{1,9},{2,10},{3,11},{4,12},{5,13},{6,14},{7,15},{8,16},{9,17... | collective-permute-start | bytes 393224 | tf_op jit(solution)/shard_map/ppermute | solution.py:231
  70.9 6.2 %collective-permute-start.34 = (bf16[256,256]{1,0:T(8,128)(2,1)S(1)}, bf16[256,256]{1,0:T(8,128)(2,1)S(1)}, u32[]{:S(2)}, u32[]{:S(2)}) collective-permute-start(bf16[256,256]{1,0:T(8,128)(2,1)S(1)} %collective-permute-done.33.refs_2_), channel_id=1, source_target_pairs={{0,4},{1,5},{2,6},{3,7},{4,0},{5,1},{6,2},{7,3},{8,12},{9,13},{10,... | collective-permute-start | bytes 393224 | tf_op jit(solution)/shard_map/ppermute | solution.py:226
  73.7 8.1 %collective-permute-start.25 = (bf16[256,256]{1,0:T(8,128)(2,1)S(1)}, bf16[256,256]{1,0:T(8,128)(2,1)S(1)}, u32[]{:S(2)}, u32[]{:S(2)}) collective-permute-start(bf16[256,256]{1,0:T(8,128)(2,1)S(1)} %collective-permute-done.23.refs_2_), channel_id=1, source_target_pairs={{0,8},{1,9},{2,10},{3,11},{4,12},{5,13},{6,14},{7,15},{8,16},{9,17... | collective-permute-start | bytes 393224 | tf_op jit(solution)/shard_map/ppermute | solution.py:231
  73.7 9.7 %collective-permute-start.24 = (bf16[256,256]{1,0:T(8,128)(2,1)S(1)}, bf16[256,256]{1,0:T(8,128)(2,1)S(1)}, u32[]{:S(2)}, u32[]{:S(2)}) collective-permute-start(bf16[256,256]{1,0:T(8,128)(2,1)S(1)} %collective-permute-done.23.refs_2_), channel_id=1, source_target_pairs={{0,4},{1,5},{2,6},{3,7},{4,0},{5,1},{6,2},{7,3},{8,12},{9,13},{10,... | collective-permute-start | bytes 393224 | tf_op jit(solution)/shard_map/ppermute | solution.py:226
  75.4 9.2 %collective-permute-start.15 = (bf16[256,256]{1,0:T(8,128)(2,1)S(1)}, bf16[256,256]{1,0:T(8,128)(2,1)S(1)}, u32[]{:S(2)}, u32[]{:S(2)}) collective-permute-start(bf16[256,256]{1,0:T(8,128)(2,1)S(1)} %collective-permute-done.13.refs_2_), channel_id=1, source_target_pairs={{0,8},{1,9},{2,10},{3,11},{4,12},{5,13},{6,14},{7,15},{8,16},{9,17... | collective-permute-start | bytes 393224 | tf_op jit(solution)/shard_map/ppermute | solution.py:231
  77.1 9.9 %collective-permute-start.47 = (bf16[256,256]{1,0:T(8,128)(2,1)S(1)}, bf16[256,256]{1,0:T(8,128)(2,1)S(1)}, u32[]{:S(2)}, u32[]{:S(2)}) collective-permute-start(bf16[256,256]{1,0:T(8,128)(2,1)S(1)} %collective-permute-done.45.refs_4_), channel_id=1, source_target_pairs={{0,8},{1,9},{2,10},{3,11},{4,12},{5,13},{6,14},{7,15},{8,16},{9,17... | collective-permute-start | bytes 393224 | tf_op jit(solution)/shard_map/ppermute | solution.py:231
  81.8 5.3 %collective-permute-start.46 = (bf16[256,256]{1,0:T(8,128)(2,1)S(1)}, bf16[256,256]{1,0:T(8,128)(2,1)S(1)}, u32[]{:S(2)}, u32[]{:S(2)}) collective-permute-start(bf16[256,256]{1,0:T(8,128)(2,1)S(1)} %collective-permute-done.45.refs_4_), channel_id=1, source_target_pairs={{0,4},{1,5},{2,6},{3,7},{4,0},{5,1},{6,2},{7,3},{8,12},{9,13},{10,... | collective-permute-start | bytes 393224 | tf_op jit(solution)/shard_map/ppermute | solution.py:226
  83.4 7.8 %collective-permute-start.37 = (bf16[256,256]{1,0:T(8,128)(2,1)S(1)}, bf16[256,256]{1,0:T(8,128)(2,1)S(1)}, u32[]{:S(2)}, u32[]{:S(2)}) collective-permute-start(bf16[256,256]{1,0:T(8,128)(2,1)S(1)} %collective-permute-done.35.refs_4_), channel_id=1, source_target_pairs={{0,8},{1,9},{2,10},{3,11},{4,12},{5,13},{6,14},{7,15},{8,16},{9,17... | collective-permute-start | bytes 393224 | tf_op jit(solution)/shard_map/ppermute | solution.py:231
  84.6 6.6 %collective-permute-start.36 = (bf16[256,256]{1,0:T(8,128)(2,1)S(1)}, bf16[256,256]{1,0:T(8,128)(2,1)S(1)}, u32[]{:S(2)}, u32[]{:S(2)}) collective-permute-start(bf16[256,256]{1,0:T(8,128)(2,1)S(1)} %collective-permute-done.35.refs_4_), channel_id=1, source_target_pairs={{0,4},{1,5},{2,6},{3,7},{4,0},{5,1},{6,2},{7,3},{8,12},{9,13},{10,... | collective-permute-start | bytes 393224 | tf_op jit(solution)/shard_map/ppermute | solution.py:226
  87.0 6.9 %collective-permute-start.27 = (bf16[256,256]{1,0:T(8,128)(2,1)S(1)}, bf16[256,256]{1,0:T(8,128)(2,1)S(1)}, u32[]{:S(2)}, u32[]{:S(2)}) collective-permute-start(bf16[256,256]{1,0:T(8,128)(2,1)S(1)} %collective-permute-done.25.refs_4_), channel_id=1, source_target_pairs={{0,8},{1,9},{2,10},{3,11},{4,12},{5,13},{6,14},{7,15},{8,16},{9,17... | collective-permute-start | bytes 393224 | tf_op jit(solution)/shard_map/ppermute | solution.py:231
  87.0 8.9 %collective-permute-start.26 = (bf16[256,256]{1,0:T(8,128)(2,1)S(1)}, bf16[256,256]{1,0:T(8,128)(2,1)S(1)}, u32[]{:S(2)}, u32[]{:S(2)}) collective-permute-start(bf16[256,256]{1,0:T(8,128)(2,1)S(1)} %collective-permute-done.25.refs_4_), channel_id=1, source_target_pairs={{0,4},{1,5},{2,6},{3,7},{4,0},{5,1},{6,2},{7,3},{8,12},{9,13},{10,... | collective-permute-start | bytes 393224 | tf_op jit(solution)/shard_map/ppermute | solution.py:226
  91.1 6.8 %collective-permute-start.17 = (bf16[256,256]{1,0:T(8,128)(2,1)S(1)}, bf16[256,256]{1,0:T(8,128)(2,1)S(1)}, u32[]{:S(2)}, u32[]{:S(2)}) collective-permute-start(bf16[256,256]{1,0:T(8,128)(2,1)S(1)} %collective-permute-done.15.refs_4_), channel_id=1, source_target_pairs={{0,8},{1,9},{2,10},{3,11},{4,12},{5,13},{6,14},{7,15},{8,16},{9,17... | collective-permute-start | bytes 393224 | tf_op jit(solution)/shard_map/ppermute | solution.py:231
  91.1 6.8 %collective-permute-start.48 = (bf16[256,256]{1,0:T(8,128)(2,1)S(1)}, bf16[256,256]{1,0:T(8,128)(2,1)S(1)}, u32[]{:S(2)}, u32[]{:S(2)}) collective-permute-start(bf16[256,256]{1,0:T(8,128)(2,1)S(1)} %collective-permute-done.47.refs_6_), channel_id=1, source_target_pairs={{0,4},{1,5},{2,6},{3,7},{4,0},{5,1},{6,2},{7,3},{8,12},{9,13},{10,... | collective-permute-start | bytes 393224 | tf_op jit(solution)/shard_map/ppermute | solution.py:226
  93.9 6.4 %collective-permute-start.38 = (bf16[256,256]{1,0:T(8,128)(2,1)S(1)}, bf16[256,256]{1,0:T(8,128)(2,1)S(1)}, u32[]{:S(2)}, u32[]{:S(2)}) collective-permute-start(bf16[256,256]{1,0:T(8,128)(2,1)S(1)} %collective-permute-done.37.refs_6_), channel_id=1, source_target_pairs={{0,4},{1,5},{2,6},{3,7},{4,0},{5,1},{6,2},{7,3},{8,12},{9,13},{10,... | collective-permute-start | bytes 393224 | tf_op jit(solution)/shard_map/ppermute | solution.py:226
  95.9 7.7 %collective-permute-start.28 = (bf16[256,256]{1,0:T(8,128)(2,1)S(1)}, bf16[256,256]{1,0:T(8,128)(2,1)S(1)}, u32[]{:S(2)}, u32[]{:S(2)}) collective-permute-start(bf16[256,256]{1,0:T(8,128)(2,1)S(1)} %collective-permute-done.27.refs_6_), channel_id=1, source_target_pairs={{0,4},{1,5},{2,6},{3,7},{4,0},{5,1},{6,2},{7,3},{8,12},{9,13},{10,... | collective-permute-start | bytes 393224 | tf_op jit(solution)/shard_map/ppermute | solution.py:226
  97.9 9.9 %collective-permute-start.12 = (bf16[256,256]{1,0:T(8,128)(2,1)S(1)}, bf16[256,256]{1,0:T(8,128)(2,1)S(1)}, u32[]{:S(2)}, u32[]{:S(2)}) collective-permute-start(bf16[256,256]{1,0:T(8,128)(2,1)S(1)} %pad_maximum_fusion.refs_0_), channel_id=1, source_target_pairs={{0,4},{1,5},{2,6},{3,7},{4,0},{5,1},{6,2},{7,3},{8,12},{9,13},{10,... | collective-permute-start | bytes 393224 | tf_op jit(solution)/shard_map/ppermute | solution.py:226
  98.0 10.8 %collective-permute-start.14 = (bf16[256,256]{1,0:T(8,128)(2,1)S(1)}, bf16[256,256]{1,0:T(8,128)(2,1)S(1)}, u32[]{:S(2)}, u32[]{:S(2)}) collective-permute-start(bf16[256,256]{1,0:T(8,128)(2,1)S(1)} %collective-permute-done.13.refs_2_), channel_id=1, source_target_pairs={{0,4},{1,5},{2,6},{3,7},{4,0},{5,1},{6,2},{7,3},{8,12},{9,13},{10,... | collective-permute-start | bytes 393224 | tf_op jit(solution)/shard_map/ppermute | solution.py:226
  100.3 10.0 %collective-permute-start.16 = (bf16[256,256]{1,0:T(8,128)(2,1)S(1)}, bf16[256,256]{1,0:T(8,128)(2,1)S(1)}, u32[]{:S(2)}, u32[]{:S(2)}) collective-permute-start(bf16[256,256]{1,0:T(8,128)(2,1)S(1)} %collective-permute-done.15.refs_4_), channel_id=1, source_target_pairs={{0,4},{1,5},{2,6},{3,7},{4,0},{5,1},{6,2},{7,3},{8,12},{9,13},{10,... | collective-permute-start | bytes 393224 | tf_op jit(solution)/shard_map/ppermute | solution.py:226
  102.4 9.4 %collective-permute-start.18 = (bf16[256,256]{1,0:T(8,128)(2,1)S(1)}, bf16[256,256]{1,0:T(8,128)(2,1)S(1)}, u32[]{:S(2)}, u32[]{:S(2)}) collective-permute-start(bf16[256,256]{1,0:T(8,128)(2,1)S(1)} %collective-permute-done.17.refs_6_), channel_id=1, source_target_pairs={{0,4},{1,5},{2,6},{3,7},{4,0},{5,1},{6,2},{7,3},{8,12},{9,13},{10,... | collective-permute-start | bytes 393224 | tf_op jit(solution)/shard_map/ppermute | solution.py:226
  103.7 9.6 %collective-permute-start.50 = (bf16[128,256]{1,0:T(8,128)(2,1)S(1)}, bf16[128,256]{1,0:T(8,128)(2,1)S(1)}, u32[]{:S(2)}, u32[]{:S(2)}) collective-permute-start(bf16[128,256]{1,0:T(8,128)(2,1)S(1)} %get-tuple-element.61), channel_id=1, source_target_pairs={{0,2},{1,3},{2,0},{3,1},{4,6},{5,7},{6,4},{7,5},{8,10},{9,11},{10,... | collective-permute-start | bytes 196616 | tf_op jit(solution)/shard_map/ppermute | solution.py:226
  107.8 6.8 %collective-permute-start.51 = (bf16[128,256]{1,0:T(8,128)(2,1)S(1)}, bf16[128,256]{1,0:T(8,128)(2,1)S(1)}, u32[]{:S(2)}, u32[]{:S(2)}) collective-permute-start(bf16[128,256]{1,0:T(8,128)(2,1)S(1)} %get-tuple-element.62), channel_id=1, source_target_pairs={{0,3},{1,2},{2,1},{3,0},{4,7},{5,6},{6,5},{7,4},{8,11},{9,10},{10,... | collective-permute-start | bytes 196616 | tf_op jit(solution)/shard_map/ppermute | solution.py:226
  108.8 6.5 %collective-permute-start.40 = (bf16[128,256]{1,0:T(8,128)(2,1)S(1)}, bf16[128,256]{1,0:T(8,128)(2,1)S(1)}, u32[]{:S(2)}, u32[]{:S(2)}) collective-permute-start(bf16[128,256]{1,0:T(8,128)(2,1)S(1)} %get-tuple-element.57), channel_id=1, source_target_pairs={{0,2},{1,3},{2,0},{3,1},{4,6},{5,7},{6,4},{7,5},{8,10},{9,11},{10,... | collective-permute-start | bytes 196616 | tf_op jit(solution)/shard_map/ppermute | solution.py:226
  110.4 5.0 %collective-permute-start.41 = (bf16[128,256]{1,0:T(8,128)(2,1)S(1)}, bf16[128,256]{1,0:T(8,128)(2,1)S(1)}, u32[]{:S(2)}, u32[]{:S(2)}) collective-permute-start(bf16[128,256]{1,0:T(8,128)(2,1)S(1)} %get-tuple-element.58), channel_id=1, source_target_pairs={{0,3},{1,2},{2,1},{3,0},{4,7},{5,6},{6,5},{7,4},{8,11},{9,10},{10,... | collective-permute-start | bytes 196616 | tf_op jit(solution)/shard_map/ppermute | solution.py:226
  111.8 5.1 %collective-permute-start.30 = (bf16[128,256]{1,0:T(8,128)(2,1)S(1)}, bf16[128,256]{1,0:T(8,128)(2,1)S(1)}, u32[]{:S(2)}, u32[]{:S(2)}) collective-permute-start(bf16[128,256]{1,0:T(8,128)(2,1)S(1)} %get-tuple-element.53), channel_id=1, source_target_pairs={{0,2},{1,3},{2,0},{3,1},{4,6},{5,7},{6,4},{7,5},{8,10},{9,11},{10,... | collective-permute-start | bytes 196616 | tf_op jit(solution)/shard_map/ppermute | solution.py:226
  113.3 4.3 %collective-permute-start.31 = (bf16[128,256]{1,0:T(8,128)(2,1)S(1)}, bf16[128,256]{1,0:T(8,128)(2,1)S(1)}, u32[]{:S(2)}, u32[]{:S(2)}) collective-permute-start(bf16[128,256]{1,0:T(8,128)(2,1)S(1)} %get-tuple-element.54), channel_id=1, source_target_pairs={{0,3},{1,2},{2,1},{3,0},{4,7},{5,6},{6,5},{7,4},{8,11},{9,10},{10,... | collective-permute-start | bytes 196616 | tf_op jit(solution)/shard_map/ppermute | solution.py:226
  114.7 9.5 %collective-permute-start.49 = (f32[128,256]{1,0:T(8,128)S(1)}, f32[128,256]{1,0:T(8,128)S(1)}, u32[]{:S(2)}, u32[]{:S(2)}) collective-permute-start(f32[128,256]{1,0:T(8,128)S(1)} %get-tuple-element.60), channel_id=1, source_target_pairs={{0,1},{1,0},{2,3},{3,2},{4,5},{5,4},{6,7},{7,6},{8,9},{9,8},{10,11... | collective-permute-start | bytes 393224 | tf_op jit(solution)/shard_map/ppermute | solution.py:226
  115.3 8.9 %collective-permute-start.39 = (f32[128,256]{1,0:T(8,128)S(1)}, f32[128,256]{1,0:T(8,128)S(1)}, u32[]{:S(2)}, u32[]{:S(2)}) collective-permute-start(f32[128,256]{1,0:T(8,128)S(1)} %get-tuple-element.56), channel_id=1, source_target_pairs={{0,1},{1,0},{2,3},{3,2},{4,5},{5,4},{6,7},{7,6},{8,9},{9,8},{10,11... | collective-permute-start | bytes 393224 | tf_op jit(solution)/shard_map/ppermute | solution.py:226
  115.4 4.4 %collective-permute-start.20 = (bf16[128,256]{1,0:T(8,128)(2,1)S(1)}, bf16[128,256]{1,0:T(8,128)(2,1)S(1)}, u32[]{:S(2)}, u32[]{:S(2)}) collective-permute-start(bf16[128,256]{1,0:T(8,128)(2,1)S(1)} %get-tuple-element.49), channel_id=1, source_target_pairs={{0,2},{1,3},{2,0},{3,1},{4,6},{5,7},{6,4},{7,5},{8,10},{9,11},{10,... | collective-permute-start | bytes 196616 | tf_op jit(solution)/shard_map/ppermute | solution.py:226
  116.9 7.3 %collective-permute-start.29 = (f32[128,256]{1,0:T(8,128)S(1)}, f32[128,256]{1,0:T(8,128)S(1)}, u32[]{:S(2)}, u32[]{:S(2)}) collective-permute-start(f32[128,256]{1,0:T(8,128)S(1)} %get-tuple-element.52), channel_id=1, source_target_pairs={{0,1},{1,0},{2,3},{3,2},{4,5},{5,4},{6,7},{7,6},{8,9},{9,8},{10,11... | collective-permute-start | bytes 393224 | tf_op jit(solution)/shard_map/ppermute | solution.py:226
  117.6 6.6 %collective-permute-start.19 = (f32[128,256]{1,0:T(8,128)S(1)}, f32[128,256]{1,0:T(8,128)S(1)}, u32[]{:S(2)}, u32[]{:S(2)}) collective-permute-start(f32[128,256]{1,0:T(8,128)S(1)} %get-tuple-element.48), channel_id=1, source_target_pairs={{0,1},{1,0},{2,3},{3,2},{4,5},{5,4},{6,7},{7,6},{8,9},{9,8},{10,11... | collective-permute-start | bytes 393224 | tf_op jit(solution)/shard_map/ppermute | solution.py:226
  119.8 4.3 %collective-permute-start.21 = (bf16[128,256]{1,0:T(8,128)(2,1)S(1)}, bf16[128,256]{1,0:T(8,128)(2,1)S(1)}, u32[]{:S(2)}, u32[]{:S(2)}) collective-permute-start(bf16[128,256]{1,0:T(8,128)(2,1)S(1)} %get-tuple-element.50), channel_id=1, source_target_pairs={{0,3},{1,2},{2,1},{3,0},{4,7},{5,6},{6,5},{7,4},{8,11},{9,10},{10,... | collective-permute-start | bytes 196616 | tf_op jit(solution)/shard_map/ppermute | solution.py:226
  (3 other events, 2.1 us)

commit v2 on v1

--- a/solution.py
+++ b/solution.py
@@ -10,69 +10,66 @@
 BLOCK = 32
 LANES = 128
 TEAM = 4
-WEIGHT_PARTS = 4
+FIRST = 5
 VMEM_LIMIT = 32 * 1024 * 1024
 
 f32 = jnp.float32
 bf16 = jnp.bfloat16
 
 
-def vmem(count):
-    return [pl.BlockSpec(memory_space=pltpu.VMEM)] * count
-
-
-def smem():
-    return pl.BlockSpec(memory_space=pltpu.SMEM)
-
-
-def call(kernel, out_shape, scratch=(), flops=0, moved=0):
-    outs = jax.tree.leaves(out_shape)
+def call(kernel, out_shape, scratch=(), after=()):
+    def body(*refs):
+        return kernel(*refs[len(after) :])
 
     def run(info, *args):
         return pl.pallas_call(
-            kernel,
+            body,
             out_shape=out_shape,
-            in_specs=[smem()] + vmem(len(args)),
-            out_specs=jax.tree.map(lambda _: pl.BlockSpec(memory_space=pltpu.VMEM), out_shape),
+            in_specs=[pl.BlockSpec(memory_space=pl.ANY)] * len(after)
+            + [pl.BlockSpec(memory_space=pltpu.SMEM)]
+            + [pl.BlockSpec()] * len(args),
             scratch_shapes=list(scratch),
             compiler_params=pltpu.CompilerParams(vmem_limit_bytes=VMEM_LIMIT),
-            cost_estimate=pl.CostEstimate(flops=flops, bytes_accessed=moved, transcendentals=0),
-        )(info, *args)
+            cost_estimate=pl.CostEstimate(flops=0, bytes_accessed=0, transcendentals=0),
+        )(*after, info, *args)
 
     return run
 
 
-def split_kernel(team, depth, info_ref, *refs):
+def split_kernel(team, depth, plan, info_ref, *refs):
     me = info_ref[0]
-    sources, outs = refs[: len(refs) // (team + 1)], refs[len(refs) // (team + 1) :]
-    runs = sources[0].shape[1] // (team * depth)
-    for which, source in enumerate(sources):
-        for step in range(team):
-            out = outs[which * team + step]
-            for run in range(runs):
-                at = pl.multiple_of((run * team + (me ^ step)) * depth, depth)
-                out[:, run * depth : (run + 1) * depth] = source[:, pl.ds(at, depth)]
-
-
-def split_channels(info, team, depth, sources):
-    rows, width = sources[0].shape
+    sources, outs = refs[: len(plan)], list(refs[len(plan) :])
+    for source, (steps, parts) in zip(sources, plan):
+        runs = source.shape[1] // (team * depth)
+        for step in range(steps):
+            for part in range(parts):
+                out = outs.pop(0)
+                for run in range(runs // parts):
+                    whole = part * (runs // parts) + run
+                    at = pl.multiple_of((whole * team + (me ^ step)) * depth, depth)
+                    out[:, run * depth : (run + 1) * depth] = source[:, pl.ds(at, depth)]
+
+
+def split_channels(info, team, depth, sources, plan):
     if depth % LANES == 0:
-        share = jax.ShapeDtypeStruct((rows, width // team), sources[0].dtype)
-        pieces = call(
-            functools.partial(split_kernel, team, depth),
-            [share] * (team * len(sources)),
-            moved=2 * len(sources) * sources[0].size * sources[0].dtype.itemsize,
-        )(info, *sources)
-        return [pieces[n * team : (n + 1) * team] for n in range(len(sources))]
+        shapes = [
+            jax.ShapeDtypeStruct((source.shape[0], source.shape[1] // (team * parts)), source.dtype)
+            for source, (steps, parts) in zip(sources, plan)
+            for _ in range(steps * parts)
+        ]
+        kernel = functools.partial(split_kernel, team, depth, plan)
+        pieces = list(call(kernel, shapes)(info, *sources))
+    else:
+        pieces = []
+        for source, (steps, parts) in zip(sources, plan):
+            rows, width = source.shape
+            cut = source.reshape(rows, width // (team * depth), team, depth)
+            for step in range(steps):
+                share = lax.dynamic_index_in_dim(cut, info[0] ^ step, 2, keepdims=False)
+                pieces += jnp.split(share.reshape(rows, -1), parts, axis=1)
     out = []
-    for source in sources:
-        cut = source.reshape(rows, width // (team * depth), team, depth)
-        out.append(
-            [
-                lax.dynamic_index_in_dim(cut, info[0] ^ step, 2, keepdims=False).reshape(rows, -1)
-                for step in range(team)
-            ]
-        )
+    for steps, parts in plan:
+        out.append([[pieces.pop(0) for _ in range(parts)] for _ in range(steps)])
     return out
 
 
@@ -141,16 +138,16 @@
 
 def gate_kernel(gaps, info_ref, *refs):
     gates = refs[:TEAM]
-    y_ref, rate_ref, coef_ref, near_ref = refs[TEAM : TEAM + 4]
-    far = refs[TEAM + 4 : TEAM + 4 + gaps]
-    out_ref, reach, decay8, start = refs[TEAM + 4 + gaps :]
+    y_refs = refs[TEAM : TEAM + 2]
+    rate_ref, coef_ref, near_ref = refs[TEAM + 2 : TEAM + 5]
+    far = refs[TEAM + 5 : TEAM + 5 + gaps]
+    out_ref, reach, decay8, start = refs[TEAM + 5 + gaps :]
     me, high = info_ref[0], info_ref[1]
     order = rate_ref.shape[0]
     rows = gates[0].shape[0]
     span = float(TEAM * rows)
 
-    @pl.loop(0, rate_ref.shape[1] // LANES)
-    def _(tile):
+    def gate_tile(y_ref, tile, row):
         lanes = pl.ds(pl.multiple_of(tile * LANES, LANES), LANES)
         rate, coef = rate_ref[:, lanes], coef_ref[:, lanes]
         reach_tables(rate, coef, reach, decay8)
@@ -171,28 +168,57 @@
                     while len(total) > 1:
                         total = [a + b for a, b in zip(total[::2], total[1::2])]
                     here = pl.multiple_of(place * rows + at + 8 * half, 8)
-                    halves.append(total[0] + y_ref[tile, pl.ds(here, 8), :])
+                    halves.append(total[0] + y_ref[row, pl.ds(here, 8), :])
                     terms = [term * decay8[k] for k, term in enumerate(terms)]
                 conv = jnp.concatenate(halves, axis=0)
                 gated = gates[step][at : at + 16, lanes].astype(f32) * conv
                 out_ref[tile, pl.ds(pl.multiple_of(goes * rows + at, 16), 16), :] = gated.astype(bf16)
 
-
-def project_kernel(slots, info_ref, own_ref, other_ref, *refs):
-    weights, outs, total = refs[:slots], refs[slots : slots + TEAM], refs[-1]
+    for part, y_ref in enumerate(y_refs):
+        tiles = y_ref.shape[0]
+
+        @pl.loop(0, tiles)
+        def _(row, y_ref=y_ref, first=part * tiles):
+            gate_tile(y_ref, first + row, row)
+
+
+def product(groups, gated_ref, weights):
+    total = None
+    for pair, rows in enumerate(weights):
+        first, second = groups[2 * pair], groups[2 * pair + 1]
+        left = jnp.concatenate([gated_ref[first], gated_ref[second]], axis=1)
+        right = jnp.concatenate([ref[...] for ref in rows], axis=0)
+        term = jnp.dot(left, right, preferred_element_type=f32)
+        total = term if total is None else total + term
+    return total
+
+
+def pairs_of(flat, sizes):
+    flat, out = list(flat), []
+    for size in sizes:
+        out.append([flat.pop(0) for _ in range(size)])
+    return out
+
+
+def own_product_kernel(sizes, info_ref, gated_ref, *refs):
+    groups = [info_ref[3 + slot] for slot in range(2 * len(sizes))]
+    weights, out = pairs_of(refs[:-1], sizes), refs[-1]
+    wide = out.shape[1]
+    step = min(wide, 256)
+    for at in range(0, wide, step):
+        part = [[ref.at[:, at : at + step] for ref in rows] for rows in weights]
+        out[:, at : at + step] = product(groups, gated_ref, part)
+
+
+def project_kernel(sizes, at, info_ref, gated_ref, own_ref, *refs):
+    groups = [info_ref[3 + slot] for slot in range(2 * len(sizes))]
+    weights, outs, total = pairs_of(refs[: sum(sizes)], sizes), refs[sum(sizes) : -1], refs[-1]
     core = info_ref[2]
-    rows = outs[0].shape[0]
-    for slot in range(slots):
-        group = info_ref[3 + slot]
-        left = jnp.concatenate([own_ref[group], other_ref[group]], axis=1)
-        product = jnp.dot(left, weights[slot][...], preferred_element_type=f32)
-        if slot == 0:
-            total[...] = product
-        else:
-            total[...] += product
+    rows, wide = outs[0].shape
+    total[...] = own_ref[:, at : at + wide] + product(groups, gated_ref, weights)
     for step, out in enumerate(outs):
-        at = (step // 2) * 2 * rows + (core ^ (step & 1)) * rows
-        out[...] = total[pl.ds(pl.multiple_of(at, rows), rows), :].astype(out.dtype)
+        start = (step // 2) * 2 * rows + (core ^ (step & 1)) * rows
+        out[...] = total[pl.ds(pl.multiple_of(start, rows), rows), :].astype(out.dtype)
 
 
 def finish_kernel(parts, info_ref, *refs):
@@ -210,6 +236,18 @@
         at += wide
 
 
+def halves_kernel(cut, info_ref, weight_ref, keep_ref, *give_refs):
+    core = info_ref[2]
+    half = keep_ref.shape[1]
+    keep_ref[...] = weight_ref[:, pl.ds(pl.multiple_of(core * half, LANES), half)]
+    at = 0
+    for give_ref in give_refs:
+        wide = give_ref.shape[1]
+        start = pl.multiple_of((1 - core) * half + at, LANES)
+        give_ref[...] = weight_ref[:, pl.ds(start, wide)]
+        at += wide
+
+
 def on_device(q_gate, values_in, decay_rate, residue, skip_gain, out_weight):
     rows, width = q_gate.shape
     depth, features = out_weight.shape
@@ -221,6 +259,7 @@
     y, z = (mine // TEAM) % 2, mine // (2 * TEAM)
     share = width // TEAM
     half = features // 2
+    parts = 2
 
     def swap(value, bit):
         return lax.ppermute(value, "seq", [(i, i ^ bit) for i in range(count)])
@@ -236,50 +275,75 @@
         groups += [at * 2 + y, at * 2 + (1 - y)]
     info = jnp.stack([me, y, core] + groups).astype(jnp.int32)
 
-    keep = lax.dynamic_slice_in_dim(out_weight, core * half, half, 1)
-    give = lax.dynamic_slice_in_dim(out_weight, (1 - core) * half, half, 1)
-    got = swap(give, 1)
-    wide = half // WEIGHT_PARTS
-    weights = []
-    for part in range(WEIGHT_PARTS):
-        cut = slice(part * wide, (part + 1) * wide)
-        held = jnp.concatenate([keep[:, cut], got[:, cut]], axis=0)
-        slots = [held, swap(held, TEAM)]
+    (values,) = split_channels(info, TEAM, depth, [values_in], [(TEAM, parts)])
+    values = [values[0]] + [[swap(part, s) for part in values[s]] for s in range(1, TEAM)]
+
+    cut = half * FIRST // 8
+    keep, give0, give1 = call(
+        functools.partial(halves_kernel, cut),
+        [
+            jax.ShapeDtypeStruct((depth, half), bf16),
+            jax.ShapeDtypeStruct((depth, cut), bf16),
+            jax.ShapeDtypeStruct((depth, half - cut), bf16),
+        ],
+    )(info, out_weight)
+
+    def along_first(held):
+        slots = [[held, swap(held, TEAM)]]
         for _ in range(1, heights):
             held = up(held, 1, True)
-            slots += [held, swap(held, TEAM)]
-        weights.append(slots)
-
-    (values,) = split_channels(info, TEAM, depth, [values_in])
-    values = [values[0]] + [swap(values[step], step) for step in range(1, TEAM)]
-    (gates,) = split_channels(info, TEAM, depth, [q_gate])
-    gates = [gates[0]] + [swap(gates[step], step) for step in range(1, TEAM)]
-    (rates,), (residues,) = (
-        [split[0]] for split in split_channels(info, TEAM, depth, [decay_rate.T, residue.T])
+            slots.append([held, swap(held, TEAM)])
+        return slots
+
+    def across_first(held):
+        held = jnp.concatenate([held, swap(held, TEAM)], axis=0)
+        slots = [[held]]
+        for _ in range(1, heights):
+            held = up(held, 1, True)
+            slots.append([held])
+        return slots
+
+    own_rows = along_first(keep)
+    other_rows = [along_first(swap(give0, 1)), across_first(swap(give1, 1))]
+
+    gates, rates, residues, skip = split_channels(
+        info,
+        TEAM,
+        depth,
+        [q_gate, decay_rate.T, residue.T, skip_gain[None]],
+        [(TEAM, 1), (1, 1), (1, 1), (1, 1)],
     )
+    gates = [gates[0][0]] + [swap(gates[step][0], step) for step in range(1, TEAM)]
+    rates, residues, skip = rates[0][0], residues[0][0], skip[0][0]
     coef = residues * jnp.sqrt(-jnp.expm1(-2.0 * rates))
-    (skips,) = split_channels(info, TEAM, depth, [skip_gain[None]])
-    skip = skips[0]
 
     tiles = share // LANES
-    elements = TEAM * rows * share
     blocks = TEAM * rows // BLOCK
-    y_local, end = call(
-        local_kernel,
-        [
-            jax.ShapeDtypeStruct((tiles, TEAM * rows, LANES), f32),
-            jax.ShapeDtypeStruct((order, share), f32),
-        ],
-        [
-            pltpu.VMEM((blocks, 2 * BLOCK, LANES), f32),
-            pltpu.VMEM((BLOCK, 8, LANES), f32),
-            pltpu.VMEM((order, 8, LANES), f32),
-            pltpu.VMEM((order, 8, LANES), f32),
-            pltpu.VMEM((order, LANES), f32),
-        ],
-        flops=110 * elements,
-        moved=6 * elements,
-    )(info, *values, rates, coef, skip)
+    waits = [
+        [own_rows[1][0]],
+        [own_rows[min(2, heights - 1)][0], other_rows[0][1][0], own_rows[0][1], other_rows[1][0][0]],
+    ]
+    y_local, ends = [], []
+    for part in range(parts):
+        lanes = slice(part * share // parts, (part + 1) * share // parts)
+        y_part, end = call(
+            local_kernel,
+            [
+                jax.ShapeDtypeStruct((tiles // parts, TEAM * rows, LANES), f32),
+                jax.ShapeDtypeStruct((order, share // parts), f32),
+            ],
+            [
+                pltpu.VMEM((blocks, 2 * BLOCK, LANES), f32),
+                pltpu.VMEM((BLOCK, 8, LANES), f32),
+                pltpu.VMEM((order, 8, LANES), f32),
+                pltpu.VMEM((order, 8, LANES), f32),
+                pltpu.VMEM((order, LANES), f32),
+            ],
+            after=waits[part],
+        )(info, *[v[part] for v in values], rates[:, lanes], coef[:, lanes], skip[:, lanes])
+        y_local.append(y_part)
+        ends.append(end)
+    end = jnp.concatenate(ends, axis=1)
 
     near = swap(end, TEAM)
     first, second = jnp.where(y == 0, end, near), jnp.where(y == 0, near, end)
@@ -293,9 +357,13 @@
             pltpu.VMEM((order, 8, LANES), f32),
             pltpu.VMEM((order, LANES), f32),
         ],
-        flops=40 * elements,
-        moved=8 * elements,
-    )(info, *gates, y_local, rates, coef, near, *far)
+        after=[
+            other_rows[0][min(2, heights - 1)][0],
+            other_rows[1][1][0],
+            own_rows[1][1],
+            other_rows[0][1][1],
+        ],
+    )(info, *gates, *y_local, rates, coef, near, *far)
     other = swap(gated, 1)
 
     if depth % LANES:
@@ -307,21 +375,29 @@
 
         gated, other = by_group(gated), by_group(other)
 
-    finished = []
-    for slots in weights:
+    def laid_out(slots):
+        return [len(pair) for pair in slots], [ref for pair in slots for ref in pair]
+
+    sizes, flat = laid_out(own_rows)
+    own = call(
+        functools.partial(own_product_kernel, sizes),
+        jax.ShapeDtypeStruct((TEAM * rows, half), f32),
+    )(info, gated, *flat)
+    finished, at = [], 0
+    for slots in other_rows:
+        sizes, flat = laid_out(slots)
+        wide = flat[0].shape[1]
         shape = functools.partial(jax.ShapeDtypeStruct, (rows, wide))
         sums = call(
-            functools.partial(project_kernel, 2 * heights),
+            functools.partial(project_kernel, sizes, at),
             [shape(f32), shape(f32), shape(bf16), shape(bf16)],
             [pltpu.VMEM((TEAM * rows, wide), f32)],
-            flops=TEAM * rows * width * wide,
-            moved=TEAM * rows * width + width * wide,
-        )(info, gated, other, *slots)
+        )(info, other, own, *flat)
         finished += [sums[0]] + [swap(sums[step], step) for step in range(1, TEAM)]
+        at += wide
     return call(
-        functools.partial(finish_kernel, WEIGHT_PARTS),
+        functools.partial(finish_kernel, len(other_rows)),
         jax.ShapeDtypeStruct((rows, features), bf16),
-        moved=rows * features * 8,
     )(info, *finished)
 
 

time: 126 us -> 114 us (0.905)
  starting transfers between devices: 49.2 us -> 38.1 us
  waiting for transfers between devices: 38.6 us -> 44.5 us
  local copies, waits for them, and re-layouts: 12.7 us -> 7.21 us
    ppermute x37 -> x28, starting transfers between devices: 34.4 us -> 19.9 us  [swap(): return lax.ppermute(value, 'seq', [(i, i ^ bit) for i in range(count)])]
    ppermute x37 -> x28, waiting for transfers between devices: 13.6 us -> 23.3 us  [swap(): return lax.ppermute(value, 'seq', [(i, i ^ bit) for i in range(count)])]
    ppermute x15 -> x12, waiting for transfers between devices: 25 us -> 21.2 us  [up(): return lax.ppermute(value, 'seq', pairs)]
    ppermute x15 -> x12, starting transfers between devices: 14.7 us -> 18.2 us  [up(): return lax.ppermute(value, 'seq', pairs)]
    slice x2 -> x3, local copies, waits for them, and re-layouts: 2.56 us -> 0.01 us  [the longest x1 0.01 us: on_device(): coef[:, lanes]]
    dynamic_slice x1 -> x0, local copies, waits for them, and re-layouts: 1.67 us -> none  [on_device(): give = lax.dynamic_slice_in_dim(out_weight, (1 - core) * half, half, 1)]
    unnamed x30 -> x26, local copies, waits for them, and re-layouts: 8.39 us -> 7.09 us
    pallas_call x11 -> x10, Pallas kernels: 24.7 us -> 23.5 us  [run(): pl.pallas_call(body, out_shape=out_shape, in_specs=[pl.BlockSpec(memory_s...]
  transfers between devices with their start and end apart: 52 -> 40, of which waited for: 24 -> 14; matrix products, arithmetic and copies ran while one was open for 3% -> 0% of each run, Pallas kernels for 15% -> 15%
where the time goes in v2:
time: 114 us
  waiting for transfers between devices  44.5 us (39%)
  starting transfers between devices  38.1 us (33%)
  Pallas kernels  23.5 us (21%)
  local copies, waits for them, and re-layouts  7.21 us (6%)
    pallas_call x10, Pallas kernels, run(): pl.pallas_call(body, out_shape=out_shape, in_specs=[pl.BlockSpec(memory_s...  23.5 us
    ppermute x28, waiting for transfers between devices, swap(): return lax.ppermute(value, 'seq', [(i, i ^ bit) for i in range(count)])  23.3 us
    ppermute x12, waiting for transfers between devices, up(): return lax.ppermute(value, 'seq', pairs)  21.2 us
    ppermute x28, starting transfers between devices, swap(): return lax.ppermute(value, 'seq', [(i, i ^ bit) for i in range(count)])  19.9 us
    ppermute x12, starting transfers between devices, up(): return lax.ppermute(value, 'seq', pairs)  18.2 us
    unnamed x26, local copies, waits for them, and re-layouts  7.09 us
  transfers between devices with their start and end apart: 40, of which 14 were waited for; matrix products, arithmetic and copies ran while one was open for 0% of the time, Pallas kernels for 15%

profile of v2, /device:TPU:0, one launch (start us, length us, event | category | flops | bytes accessed | tf_op | source)
XLA Modules:
  0.0 113.7 jit_solution(14543181402755791843)
XLA Ops:
  0.0 0.1 stack.47.refs_0_.refs_1_.refs_4_
  0.1 1.0 copy-done.2
  1.1 0.6 shard_map.64
  1.7 0.5 collective-permute-start.3
  2.3 1.2 %copy-done = bf16[128,4096]{1,0:T(8,128)(2,1)S(1)} copy-done((bf16[128,4096]{1,0:T(8,128)(2,1)S(1)}, bf16[128,4096]{1,0:T(8,128)(2,1)}, u32[]{:S(2)}) %copy-start) | copy-done | bytes 1048600
  3.5 0.8 shard_map.66
  4.3 0.1 collective-permute-start.17
  4.4 3.0 %collective-permute-start.6 = (bf16[128,1024]{1,0:T(8,128)(2,1)S(1)}, bf16[128,1024]{1,0:T(8,128)(2,1)S(1)}, u32[]{:S(2)}, u32[]{:S(2)}) collective-permute-start(bf16[128,1024]{1,0:T(8,128)(2,1)S(1)} %get-tuple-element.37.refs_2_), channel_id=1, source_target_pairs={{0,8},{1,9},{2,10},{3,11},{4,12},{5,13},{6,14},{7,15},{8,16},{9,17... | collective-permute-start | bytes 786440 | tf_op jit(solution)/shard_map/ppermute | solution.py:270
  7.5 0.5 collective-permute-start.12
  8.0 1.2 %copy-done.1 = bf16[128,4096]{1,0:T(8,128)(2,1)S(1)} copy-done((bf16[128,4096]{1,0:T(8,128)(2,1)S(1)}, bf16[128,4096]{1,0:T(8,128)(2,1)}, u32[]{:S(2)}) %copy-start.1) | copy-done | bytes 1048600
  9.2 0.9 copy-done.5
  10.1 0.9 copy-done.6
  11.1 0.7 copy-done.11
  11.8 1.6 %shard_map.65 = (bf16[128,1024]{1,0:T(8,128)(2,1)S(1)}, bf16[128,1024]{1,0:T(8,128)(2,1)}, bf16[128,1024]{1,0:T(8,128)(2,1)}, bf16[128,1024]{1,0:T(8,128)(2,1)},...) custom-call(s32[11]{0:T(128)S(1)} %stack.47.refs_0_.refs_1_.refs_4_, ...), custom_call_target="tpu_custom_call" | custom-call | tf_op jit(solution)/shard_map/pallas_call | solution.py:25
  13.5 1.6 %collective-permute-start.13 = (bf16[128,512]{1,0:T(8,128)(2,1)S(1)}, bf16[128,512]{1,0:T(8,128)(2,1)S(1)}, u32[]{:S(2)}, u32[]{:S(2)}) collective-permute-start(bf16[128,512]{1,0:T(8,128)(2,1)S(1)} %get-tuple-element.44), channel_id=1, source_target_pairs={{0,2},{1,3},{2,0},{3,1},{4,6},{5,7},{6,4},{7,5},{8,10},{9,11},{10,... | collective-permute-start | bytes 393224 | tf_op jit(solution)/shard_map/ppermute | solution.py:265
  15.1 1.6 %collective-permute-start.16 = (bf16[128,1024]{1,0:T(8,128)(2,1)S(1)}, bf16[128,1024]{1,0:T(8,128)(2,1)S(1)}, u32[]{:S(2)}, u32[]{:S(2)}) collective-permute-start(bf16[128,1024]{1,0:T(8,128)(2,1)S(1)} %get-tuple-element.37.refs_2_), channel_id=1, source_target_pairs={{0,4},{1,5},{2,6},{3,7},{4,0},{5,1},{6,2},{7,3},{8,12},{9,13},{10,... | collective-permute-start | bytes 786440 | tf_op jit(solution)/shard_map/ppermute | solution.py:265
  16.7 3.2 %collective-permute-done.13.refs_4_ = bf16[128,512]{1,0:T(8,128)(2,1)S(1)} collective-permute-done((bf16[128,512]{1,0:T(8,128)(2,1)S(1)}, bf16[128,512]{1,0:T(8,128)(2,1)S(1)}, u32[]{:S(2)}, u32[]{:S(2)}) %collective-permute-start.13) | collective-permute-done | bytes 131104 | tf_op jit(solution)/shard_map/ppermute | solution.py:265
  19.9 1.5 %collective-permute-start.18 = (bf16[128,512]{1,0:T(8,128)(2,1)S(1)}, bf16[128,512]{1,0:T(8,128)(2,1)S(1)}, u32[]{:S(2)}, u32[]{:S(2)}) collective-permute-start(bf16[128,512]{1,0:T(8,128)(2,1)S(1)} %get-tuple-element.52), channel_id=1, source_target_pairs={{0,2},{1,3},{2,0},{3,1},{4,6},{5,7},{6,4},{7,5},{8,10},{9,11},{10,... | collective-permute-start | bytes 393224 | tf_op jit(solution)/shard_map/ppermute | solution.py:265
  21.4 0.3 collective-permute-done.14.refs_5_
  21.8 2.2 %collective-permute-start.19 = (bf16[128,512]{1,0:T(8,128)(2,1)S(1)}, bf16[128,512]{1,0:T(8,128)(2,1)S(1)}, u32[]{:S(2)}, u32[]{:S(2)}) collective-permute-start(bf16[128,512]{1,0:T(8,128)(2,1)S(1)} %get-tuple-element.53), channel_id=1, source_target_pairs={{0,3},{1,2},{2,1},{3,0},{4,7},{5,6},{6,5},{7,4},{8,11},{9,10},{10,... | collective-permute-start | bytes 393224 | tf_op jit(solution)/shard_map/ppermute | solution.py:265
  24.0 1.5 %collective-permute-start.4 = (bf16[128,384]{1,0:T(8,128)(2,1)S(1)}, bf16[128,384]{1,0:T(8,128)(2,1)S(1)}, u32[]{:S(2)}, u32[]{:S(2)}) collective-permute-start(bf16[128,384]{1,0:T(8,128)(2,1)S(1)} %collective-permute-done.3), channel_id=1, source_target_pairs={{0,4},{1,5},{2,6},{3,7},{4,0},{5,1},{6,2},{7,3},{8,12},{9,13},{10,... | collective-permute-start | bytes 294920 | tf_op jit(solution)/shard_map/ppermute | solution.py:265
  25.5 1.6 %collective-permute-start.15 = (bf16[128,1024]{1,0:T(8,128)(2,1)S(1)}, bf16[128,1024]{1,0:T(8,128)(2,1)S(1)}, u32[]{:S(2)}, u32[]{:S(2)}) collective-permute-start(bf16[128,1024]{1,0:T(8,128)(2,1)S(1)} %collective-permute-done.6.refs_0_.refs_4_), channel_id=1, source_target_pairs={{0,8},{1,9},{2,10},{3,11},{4,12},{5,13},{6,14},{7,15},{8,16},{9,17... | collective-permute-start | bytes 786440 | tf_op jit(solution)/shard_map/ppermute | solution.py:270
  27.1 1.5 %collective-permute-done.4 = bf16[128,384]{1,0:T(8,128)(2,1)S(1)} collective-permute-done((bf16[128,384]{1,0:T(8,128)(2,1)S(1)}, bf16[128,384]{1,0:T(8,128)(2,1)S(1)}, u32[]{:S(2)}, u32[]{:S(2)}) %collective-permute-start.4) | collective-permute-done | bytes 98336 | tf_op jit(solution)/shard_map/ppermute | solution.py:265
  28.6 1.6 %collective-permute-start.1 = (bf16[128,640]{1,0:T(8,128)(2,1)S(1)}, bf16[128,640]{1,0:T(8,128)(2,1)S(1)}, u32[]{:S(2)}, u32[]{:S(2)}) collective-permute-start(bf16[128,640]{1,0:T(8,128)(2,1)S(1)} %collective-permute-done.refs_3_), channel_id=1, source_target_pairs={{0,8},{1,9},{2,10},{3,11},{4,12},{5,13},{6,14},{7,15},{8,16},{9,17... | collective-permute-start | bytes 491528 | tf_op jit(solution)/shard_map/ppermute | solution.py:270
  30.2 5.2 %shard_map.67 = (f32[4,512,128]{2,1,0:T(8,128)S(1)}, f32[16,512]{1,0:T(8,128)S(1)}) custom-call(bf16[128,1024]{1,0:T(8,128)(2,1)S(1)} %collective-permute-done.6.refs_0_.refs_4_, s32[11]{0:T(128)S(1)} %stack.47.refs_0_.refs_1_.refs_4_, bf16[128,512]{1,0:T(8,128)(2,1)S(1)} %get-tuple-element.42.refs_2_, bf16[128,512]{1,0:T(8,128)(2,1)S(1)} %collective-permute-done.12.refs_3_, ...), custom_call_target="tpu_custom_call" | custom-call | tf_op jit(solution)/shard_map/pallas_call | solution.py:25
  35.4 0.6 collective-permute-start.10
  36.0 1.7 %collective-permute-done.1.refs_1_.refs_5_ = bf16[128,640]{1,0:T(8,128)(2,1)S(1)} collective-permute-done((bf16[128,640]{1,0:T(8,128)(2,1)S(1)}, bf16[128,640]{1,0:T(8,128)(2,1)S(1)}, u32[]{:S(2)}, u32[]{:S(2)}) %collective-permute-start.1) | collective-permute-done | bytes 163872 | tf_op jit(solution)/shard_map/ppermute | solution.py:270
  37.7 5.2 %shard_map.68 = (f32[4,512,128]{2,1,0:T(8,128)S(1)}, f32[16,512]{1,0:T(8,128)S(1)}) custom-call(bf16[128,1024]{1,0:T(8,128)(2,1)S(1)} %collective-permute-done.15.refs_0_.refs_6_, bf16[128,640]{1,0:T(8,128)(2,1)S(1)} %collective-permute-done.1.refs_1_.refs_5_, bf16[128,1024]{1,0:T(8,128)(2,1)S(1)} %collective-permute-done.16.refs_2_.refs_3_, ...), custom_call_target="tpu_custom_call" | custom-call | tf_op jit(solution)/shard_map/pallas_call | solution.py:25
  42.9 0.6 collective-permute-start.20
  43.5 0.7 collective-permute-start.9
  44.1 1.6 %collective-permute-start.5 = (bf16[256,384]{1,0:T(8,128)(2,1)S(1)}, bf16[256,384]{1,0:T(8,128)(2,1)S(1)}, u32[]{:S(2)}, u32[]{:S(2)}) collective-permute-start(bf16[256,384]{1,0:T(8,128)(2,1)S(1)} %constant_dynamic-update-slice_fusion.refs_3_), channel_id=1, source_target_pairs={{0,8},{1,9},{2,10},{3,11},{4,12},{5,13},{6,14},{7,15},{8,16},{9,17... | collective-permute-start | bytes 589832 | tf_op jit(solution)/shard_map/ppermute | solution.py:270
  45.7 0.7 collective-permute-start.7
  46.5 1.6 %collective-permute-start.2 = (bf16[128,640]{1,0:T(8,128)(2,1)S(1)}, bf16[128,640]{1,0:T(8,128)(2,1)S(1)}, u32[]{:S(2)}, u32[]{:S(2)}) collective-permute-start(bf16[128,640]{1,0:T(8,128)(2,1)S(1)} %collective-permute-done.1.refs_1_.refs_5_), channel_id=1, source_target_pairs={{0,8},{1,9},{2,10},{3,11},{4,12},{5,13},{6,14},{7,15},{8,16},{9,17... | collective-permute-start | bytes 491528 | tf_op jit(solution)/shard_map/ppermute | solution.py:270
  48.1 1.5 %collective-permute-start.8 = (bf16[128,640]{1,0:T(8,128)(2,1)S(1)}, bf16[128,640]{1,0:T(8,128)(2,1)S(1)}, u32[]{:S(2)}, u32[]{:S(2)}) collective-permute-start(bf16[128,640]{1,0:T(8,128)(2,1)S(1)} %collective-permute-done.1.refs_1_.refs_5_), channel_id=1, source_target_pairs={{0,4},{1,5},{2,6},{3,7},{4,0},{5,1},{6,2},{7,3},{8,12},{9,13},{10,... | collective-permute-start | bytes 491528 | tf_op jit(solution)/shard_map/ppermute | solution.py:265
  49.6 2.2 %collective-permute-start.21 = (f32[16,1024]{1,0:T(8,128)S(1)}, f32[16,1024]{1,0:T(8,128)S(1)}, u32[]{:S(2)}, u32[]{:S(2)}) collective-permute-start(f32[16,1024]{1,0:T(8,128)S(1)} %select_add_fusion), channel_id=1, source_target_pairs={{0,8},{1,9},{2,10},{3,11},{4,12},{5,13},{6,14},{7,15},{8,16},{9,17... | collective-permute-start | bytes 196616 | tf_op jit(solution)/shard_map/ppermute | solution.py:270
  51.8 1.6 %collective-permute-done.5.refs_1_.refs_4_ = bf16[256,384]{1,0:T(8,128)(2,1)S(1)} collective-permute-done((bf16[256,384]{1,0:T(8,128)(2,1)S(1)}, bf16[256,384]{1,0:T(8,128)(2,1)S(1)}, u32[]{:S(2)}, u32[]{:S(2)}) %collective-permute-start.5) | collective-permute-done | bytes 196640 | tf_op jit(solution)/shard_map/ppermute | solution.py:270
  53.5 2.8 %collective-permute-start.22 = (f32[16,1024]{1,0:T(8,128)S(1)}, f32[16,1024]{1,0:T(8,128)S(1)}, u32[]{:S(2)}, u32[]{:S(2)}) collective-permute-start(f32[16,1024]{1,0:T(8,128)S(1)} %select_add_fusion), channel_id=1, source_target_pairs={{0,16},{1,17},{2,18},{3,19},{4,20},{5,21},{6,22},{7,23},{8,24},{9,... | collective-permute-start | bytes 196616 | tf_op jit(solution)/shard_map/ppermute | solution.py:270
  56.3 2.3 %collective-permute-start.23 = (f32[16,1024]{1,0:T(8,128)S(1)}, f32[16,1024]{1,0:T(8,128)S(1)}, u32[]{:S(2)}, u32[]{:S(2)}) collective-permute-start(f32[16,1024]{1,0:T(8,128)S(1)} %select_add_fusion), channel_id=1, source_target_pairs={{0,24},{1,25},{2,26},{3,27},{4,28},{5,29},{6,30},{7,31}} | collective-permute-start | bytes 196616 | tf_op jit(solution)/shard_map/ppermute | solution.py:270
  58.6 1.8 %collective-permute-done.23.refs_16_ = f32[16,1024]{1,0:T(8,128)S(1)} collective-permute-done((f32[16,1024]{1,0:T(8,128)S(1)}, f32[16,1024]{1,0:T(8,128)S(1)}, u32[]{:S(2)}, u32[]{:S(2)}) %collective-permute-start.23) | collective-permute-done | bytes 65568 | tf_op jit(solution)/shard_map/ppermute | solution.py:270
  60.5 0.9 copy-done.4
  61.4 4.0 %shard_map.69.refs_1_ = bf16[8,512,128]{2,1,0:T(8,128)(2,1)S(1)} custom-call(bf16[128,640]{1,0:T(8,128)(2,1)S(1)} %collective-permute-done.2.refs_0_.refs_7_, bf16[256,384]{1,0:T(8,128)(2,1)S(1)} %collective-permute-done.5.refs_1_.refs_4_, bf16[128,1024]{1,0:T(8,128)(2,1)S(1)} %collective-permute-done.7.refs_2_.refs_5_, ...), custom_call_target="tpu_custom_call" | custom-call | tf_op jit(solution)/shard_map/pallas_call | solution.py:25
  65.4 0.1 collective-permute-start.24
  65.6 0.5 collective-permute-start.25
  66.1 1.5 %collective-permute-start.35 = (bf16[256,384]{1,0:T(8,128)(2,1)S(1)}, bf16[256,384]{1,0:T(8,128)(2,1)S(1)}, u32[]{:S(2)}, u32[]{:S(2)}) collective-permute-start(bf16[256,384]{1,0:T(8,128)(2,1)S(1)} %collective-permute-done.5.refs_1_.refs_4_), channel_id=1, source_target_pairs={{0,8},{1,9},{2,10},{3,11},{4,12},{5,13},{6,14},{7,15},{8,16},{9,17... | collective-permute-start | bytes 589832 | tf_op jit(solution)/shard_map/ppermute | solution.py:270
  67.6 9.3 %collective-permute-done.26.refs_8_ = bf16[128,1024]{1,0:T(8,128)(2,1)S(1)} collective-permute-done((bf16[128,1024]{1,0:T(8,128)(2,1)S(1)}, bf16[128,1024]{1,0:T(8,128)(2,1)S(1)}, u32[]{:S(2)}, u32[]{:S(2)}) %collective-permute-start.26) | collective-permute-done | bytes 262176 | tf_op jit(solution)/shard_map/ppermute | solution.py:270
  76.9 0.5 collective-permute-start.27
  77.4 3.5 %collective-permute-done.35.refs_5_ = bf16[256,384]{1,0:T(8,128)(2,1)S(1)} collective-permute-done((bf16[256,384]{1,0:T(8,128)(2,1)S(1)}, bf16[256,384]{1,0:T(8,128)(2,1)S(1)}, u32[]{:S(2)}, u32[]{:S(2)}) %collective-permute-start.35) | collective-permute-done | bytes 196640 | tf_op jit(solution)/shard_map/ppermute | solution.py:270
  80.9 0.5 collective-permute-start.28
  81.3 3.3 %collective-permute-done.30.refs_9_ = bf16[128,640]{1,0:T(8,128)(2,1)S(1)} collective-permute-done((bf16[128,640]{1,0:T(8,128)(2,1)S(1)}, bf16[128,640]{1,0:T(8,128)(2,1)S(1)}, u32[]{:S(2)}, u32[]{:S(2)}) %collective-permute-start.30) | collective-permute-done | bytes 163872 | tf_op jit(solution)/shard_map/ppermute | solution.py:270
  84.6 1.5 %collective-permute-start.29 = (bf16[128,640]{1,0:T(8,128)(2,1)S(1)}, bf16[128,640]{1,0:T(8,128)(2,1)S(1)}, u32[]{:S(2)}, u32[]{:S(2)}) collective-permute-start(bf16[128,640]{1,0:T(8,128)(2,1)S(1)} %collective-permute-done.2.refs_0_.refs_7_), channel_id=1, source_target_pairs={{0,4},{1,5},{2,6},{3,7},{4,0},{5,1},{6,2},{7,3},{8,12},{9,13},{10,... | collective-permute-start | bytes 491528 | tf_op jit(solution)/shard_map/ppermute | solution.py:265
  86.2 0.5 collective-permute-start.31
  86.7 1.8 %shard_map.70.refs_2_ = f32[512,1024]{1,0:T(8,128)S(1)} custom-call(s32[11]{0:T(128)S(1)} %stack.47.refs_0_.refs_1_.refs_4_, bf16[8,512,128]{2,1,0:T(8,128)(2,1)S(1)} %shard_map.69.refs_1_, bf16[128,1024]{1,0:T(8,128)(2,1)S(1)} %copy-done.8, bf16[128,1024]{1,0:T(8,128)(2,1)S(1)} %collective-permute-done.16.refs_2_.refs_3_, ...), custom_call_target="tpu_custom_call" | custom-call | tf_op jit(solution)/shard_map/pallas_call | solution.py:25
  88.5 1.1 collective-permute-done.28.refs_4_
  89.6 3.5 %collective-permute-done.29.refs_8_ = bf16[128,640]{1,0:T(8,128)(2,1)S(1)} collective-permute-done((bf16[128,640]{1,0:T(8,128)(2,1)S(1)}, bf16[128,640]{1,0:T(8,128)(2,1)S(1)}, u32[]{:S(2)}, u32[]{:S(2)}) %collective-permute-start.29) | collective-permute-done | bytes 163872 | tf_op jit(solution)/shard_map/ppermute | solution.py:265
  93.1 2.2 %collective-permute-done.31.refs_10_ = bf16[128,640]{1,0:T(8,128)(2,1)S(1)} collective-permute-done((bf16[128,640]{1,0:T(8,128)(2,1)S(1)}, bf16[128,640]{1,0:T(8,128)(2,1)S(1)}, u32[]{:S(2)}, u32[]{:S(2)}) %collective-permute-start.31) | collective-permute-done | bytes 163872 | tf_op jit(solution)/shard_map/ppermute | solution.py:265
  95.3 1.6 %shard_map.71 = (f32[128,640]{1,0:T(8,128)S(1)}, f32[128,640]{1,0:T(8,128)S(1)}, bf16[128,640]{1,0:T(8,128)(2,1)S(1)}, bf16[128,640]{1,0:T(8,128)(2,1)S(1)}) custom-call(s32[11]{0:T(128)S(1)} %stack.47.refs_0_.refs_1_.refs_4_, bf16[8,512,128]{2,1,0:T(8,128)(2,1)S(1)} %collective-permute-done.24.refs_1_, f32[512,1024]{1,0:T(8,128)S(1)} %shard_map.70.refs_2_, ...), custom_call_target="tpu_custom_call" | custom-call | tf_op jit(solution)/shard_map/pallas_call | solution.py:25
  97.0 1.3 %shard_map.72 = (f32[128,384]{1,0:T(8,128)S(1)}, f32[128,384]{1,0:T(8,128)S(1)}, bf16[128,384]{1,0:T(8,128)(2,1)S(1)}, bf16[128,384]{1,0:T(8,128)(2,1)S(1)}) custom-call(s32[11]{0:T(128)S(1)} %stack.47.refs_0_.refs_1_.refs_4_, bf16[8,512,128]{2,1,0:T(8,128)(2,1)S(1)} %collective-permute-done.24.refs_1_, f32[512,1024]{1,0:T(8,128)S(1)} %shard_map.70.refs_2_, ...), custom_call_target="tpu_custom_call" | custom-call | tf_op jit(solution)/shard_map/pallas_call | solution.py:25
  98.3 0.8 collective-permute-start.38
  99.0 0.2 collective-permute-start.37
  99.2 1.3 %collective-permute-start.33 = (bf16[128,640]{1,0:T(8,128)(2,1)S(1)}, bf16[128,640]{1,0:T(8,128)(2,1)S(1)}, u32[]{:S(2)}, u32[]{:S(2)}) collective-permute-start(bf16[128,640]{1,0:T(8,128)(2,1)S(1)} %get-tuple-element.59), channel_id=1, source_target_pairs={{0,2},{1,3},{2,0},{3,1},{4,6},{5,7},{6,4},{7,5},{8,10},{9,11},{10,... | collective-permute-start | bytes 491528 | tf_op jit(solution)/shard_map/ppermute | solution.py:265
  100.6 0.3 collective-permute-start.34
  100.9 3.0 %collective-permute-done.38.refs_7_ = bf16[128,384]{1,0:T(8,128)(2,1)S(1)} collective-permute-done((bf16[128,384]{1,0:T(8,128)(2,1)S(1)}, bf16[128,384]{1,0:T(8,128)(2,1)S(1)}, u32[]{:S(2)}, u32[]{:S(2)}) %collective-permute-start.38) | collective-permute-done | bytes 98336 | tf_op jit(solution)/shard_map/ppermute | solution.py:265
  103.9 8.3 %collective-permute-done.39.refs_8_ = bf16[128,384]{1,0:T(8,128)(2,1)S(1)} collective-permute-done((bf16[128,384]{1,0:T(8,128)(2,1)S(1)}, bf16[128,384]{1,0:T(8,128)(2,1)S(1)}, u32[]{:S(2)}, u32[]{:S(2)}) %collective-permute-start.39) | collective-permute-done | bytes 98336 | tf_op jit(solution)/shard_map/ppermute | solution.py:265
  112.3 1.4 %shard_map.73 = bf16[128,2048]{1,0:T(8,128)(2,1)} custom-call(s32[11]{0:T(128)S(1)} %stack.47.refs_0_.refs_1_.refs_4_, f32[128,640]{1,0:T(8,128)S(1)} %get-tuple-element.57.refs_1_, f32[128,640]{1,0:T(8,128)S(1)} %collective-permute-done.32.refs_2_, bf16[128,640]{1,0:T(8,128)(2,1)S(1)} %collective-permute-done.33.refs_3_, ...), custom_call_target="tpu_custom_call" | custom-call | tf_op jit(solution)/shard_map/pallas_call | solution.py:25
  (60 shorter events, 0.4 us)
Async XLA Ops:
  0.1 1.0 copy-start.2
  1.7 33.6 %copy-start.7 = (bf16[128,1024]{1,0:T(8,128)(2,1)}, bf16[128,1024]{1,0:T(8,128)(2,1)S(1)}, u32[]{:S(2)}) copy-start(bf16[128,1024]{1,0:T(8,128)(2,1)S(1)} %get-tuple-element.37.refs_2_) | copy-start | bytes 786436
  1.7 11.8 %collective-permute-start.3 = (bf16[128,384]{1,0:T(8,128)(2,1)S(1)}, bf16[128,384]{1,0:T(8,128)(2,1)S(1)}, u32[]{:S(2)}, u32[]{:S(2)}) collective-permute-start(bf16[128,384]{1,0:T(8,128)(2,1)S(1)} %get-tuple-element.36), channel_id=1, source_target_pairs={{0,1},{1,0},{2,3},{3,2},{4,5},{5,4},{6,7},{7,6},{8,9},{9,8},{10,11... | collective-permute-start | bytes 294920 | tf_op jit(solution)/shard_map/ppermute | solution.py:265
  2.3 1.2 %copy-start = (bf16[128,4096]{1,0:T(8,128)(2,1)S(1)}, bf16[128,4096]{1,0:T(8,128)(2,1)}, u32[]{:S(2)}) copy-start(bf16[128,4096]{1,0:T(8,128)(2,1)} %refs_1_.5) | copy-start | bytes 3145732
  4.3 10.8 %collective-permute-start.17 = (bf16[128,512]{1,0:T(8,128)(2,1)S(1)}, bf16[128,512]{1,0:T(8,128)(2,1)S(1)}, u32[]{:S(2)}, u32[]{:S(2)}) collective-permute-start(bf16[128,512]{1,0:T(8,128)(2,1)S(1)} %get-tuple-element.51), channel_id=1, source_target_pairs={{0,1},{1,0},{2,3},{3,2},{4,5},{5,4},{6,7},{7,6},{8,9},{9,8},{10,11... | collective-permute-start | bytes 393224 | tf_op jit(solution)/shard_map/ppermute | solution.py:265
  4.4 21.1 %collective-permute-start.6 = (bf16[128,1024]{1,0:T(8,128)(2,1)S(1)}, bf16[128,1024]{1,0:T(8,128)(2,1)S(1)}, u32[]{:S(2)}, u32[]{:S(2)}) collective-permute-start(bf16[128,1024]{1,0:T(8,128)(2,1)S(1)} %get-tuple-element.37.refs_2_), channel_id=1, source_target_pairs={{0,8},{1,9},{2,10},{3,11},{4,12},{5,13},{6,14},{7,15},{8,16},{9,17... | collective-permute-start | bytes 786440 | tf_op jit(solution)/shard_map/ppermute | solution.py:270
  7.4 16.5 %collective-permute-start = (bf16[128,640]{1,0:T(8,128)(2,1)S(1)}, bf16[128,640]{1,0:T(8,128)(2,1)S(1)}, u32[]{:S(2)}, u32[]{:S(2)}) collective-permute-start(bf16[128,640]{1,0:T(8,128)(2,1)S(1)} %get-tuple-element.35), channel_id=1, source_target_pairs={{0,1},{1,0},{2,3},{3,2},{4,5},{5,4},{6,7},{7,6},{8,9},{9,8},{10,11... | collective-permute-start | bytes 491528 | tf_op jit(solution)/shard_map/ppermute | solution.py:265
  7.5 7.6 %collective-permute-start.12 = (bf16[128,512]{1,0:T(8,128)(2,1)S(1)}, bf16[128,512]{1,0:T(8,128)(2,1)S(1)}, u32[]{:S(2)}, u32[]{:S(2)}) collective-permute-start(bf16[128,512]{1,0:T(8,128)(2,1)S(1)} %get-tuple-element.43), channel_id=1, source_target_pairs={{0,1},{1,0},{2,3},{3,2},{4,5},{5,4},{6,7},{7,6},{8,9},{9,8},{10,11... | collective-permute-start | bytes 393224 | tf_op jit(solution)/shard_map/ppermute | solution.py:265
  8.0 1.2 %copy-start.1 = (bf16[128,4096]{1,0:T(8,128)(2,1)S(1)}, bf16[128,4096]{1,0:T(8,128)(2,1)}, u32[]{:S(2)}) copy-start(bf16[128,4096]{1,0:T(8,128)(2,1)} %refs_1_.4) | copy-start | bytes 3145732
  9.2 0.9 copy-start.5
  10.1 0.9 copy-start.6
  11.1 0.7 copy-start.11
  13.4 29.4 %copy-start.3 = (bf16[128,1024]{1,0:T(8,128)(2,1)}, bf16[128,1024]{1,0:T(8,128)(2,1)S(1)}, u32[]{:S(2)}) copy-start(bf16[128,1024]{1,0:T(8,128)(2,1)S(1)} %get-tuple-element.38.refs_5_) | copy-start | bytes 786436
  13.5 6.4 %collective-permute-start.13 = (bf16[128,512]{1,0:T(8,128)(2,1)S(1)}, bf16[128,512]{1,0:T(8,128)(2,1)S(1)}, u32[]{:S(2)}, u32[]{:S(2)}) collective-permute-start(bf16[128,512]{1,0:T(8,128)(2,1)S(1)} %get-tuple-element.44), channel_id=1, source_target_pairs={{0,2},{1,3},{2,0},{3,1},{4,6},{5,7},{6,4},{7,5},{8,10},{9,11},{10,... | collective-permute-start | bytes 393224 | tf_op jit(solution)/shard_map/ppermute | solution.py:265
  15.1 6.7 %collective-permute-start.14 = (bf16[128,512]{1,0:T(8,128)(2,1)S(1)}, bf16[128,512]{1,0:T(8,128)(2,1)S(1)}, u32[]{:S(2)}, u32[]{:S(2)}) collective-permute-start(bf16[128,512]{1,0:T(8,128)(2,1)S(1)} %get-tuple-element.45), channel_id=1, source_target_pairs={{0,3},{1,2},{2,1},{3,0},{4,7},{5,6},{6,5},{7,4},{8,11},{9,10},{10,... | collective-permute-start | bytes 393224 | tf_op jit(solution)/shard_map/ppermute | solution.py:265
  15.1 20.9 %collective-permute-start.16 = (bf16[128,1024]{1,0:T(8,128)(2,1)S(1)}, bf16[128,1024]{1,0:T(8,128)(2,1)S(1)}, u32[]{:S(2)}, u32[]{:S(2)}) collective-permute-start(bf16[128,1024]{1,0:T(8,128)(2,1)S(1)} %get-tuple-element.37.refs_2_), channel_id=1, source_target_pairs={{0,4},{1,5},{2,6},{3,7},{4,0},{5,1},{6,2},{7,3},{8,12},{9,13},{10,... | collective-permute-start | bytes 786440 | tf_op jit(solution)/shard_map/ppermute | solution.py:265
  19.9 15.5 %collective-permute-start.18 = (bf16[128,512]{1,0:T(8,128)(2,1)S(1)}, bf16[128,512]{1,0:T(8,128)(2,1)S(1)}, u32[]{:S(2)}, u32[]{:S(2)}) collective-permute-start(bf16[128,512]{1,0:T(8,128)(2,1)S(1)} %get-tuple-element.52), channel_id=1, source_target_pairs={{0,2},{1,3},{2,0},{3,1},{4,6},{5,7},{6,4},{7,5},{8,10},{9,11},{10,... | collective-permute-start | bytes 393224 | tf_op jit(solution)/shard_map/ppermute | solution.py:265
  21.8 14.2 %collective-permute-start.19 = (bf16[128,512]{1,0:T(8,128)(2,1)S(1)}, bf16[128,512]{1,0:T(8,128)(2,1)S(1)}, u32[]{:S(2)}, u32[]{:S(2)}) collective-permute-start(bf16[128,512]{1,0:T(8,128)(2,1)S(1)} %get-tuple-element.53), channel_id=1, source_target_pairs={{0,3},{1,2},{2,1},{3,0},{4,7},{5,6},{6,5},{7,4},{8,11},{9,10},{10,... | collective-permute-start | bytes 393224 | tf_op jit(solution)/shard_map/ppermute | solution.py:265
  24.0 13.7 %copy-start.9 = (bf16[128,640]{1,0:T(8,128)(2,1)}, bf16[128,640]{1,0:T(8,128)(2,1)S(1)}, u32[]{:S(2)}) copy-start(bf16[128,640]{1,0:T(8,128)(2,1)S(1)} %collective-permute-done.refs_3_) | copy-start | bytes 491524
  24.0 4.6 %collective-permute-start.4 = (bf16[128,384]{1,0:T(8,128)(2,1)S(1)}, bf16[128,384]{1,0:T(8,128)(2,1)S(1)}, u32[]{:S(2)}, u32[]{:S(2)}) collective-permute-start(bf16[128,384]{1,0:T(8,128)(2,1)S(1)} %collective-permute-done.3), channel_id=1, source_target_pairs={{0,4},{1,5},{2,6},{3,7},{4,0},{5,1},{6,2},{7,3},{8,12},{9,13},{10,... | collective-permute-start | bytes 294920 | tf_op jit(solution)/shard_map/ppermute | solution.py:265
  25.5 12.2 %collective-permute-start.15 = (bf16[128,1024]{1,0:T(8,128)(2,1)S(1)}, bf16[128,1024]{1,0:T(8,128)(2,1)S(1)}, u32[]{:S(2)}, u32[]{:S(2)}) collective-permute-start(bf16[128,1024]{1,0:T(8,128)(2,1)S(1)} %collective-permute-done.6.refs_0_.refs_4_), channel_id=1, source_target_pairs={{0,8},{1,9},{2,10},{3,11},{4,12},{5,13},{6,14},{7,15},{8,16},{9,17... | collective-permute-start | bytes 786440 | tf_op jit(solution)/shard_map/ppermute | solution.py:270
  28.6 9.1 %collective-permute-start.1 = (bf16[128,640]{1,0:T(8,128)(2,1)S(1)}, bf16[128,640]{1,0:T(8,128)(2,1)S(1)}, u32[]{:S(2)}, u32[]{:S(2)}) collective-permute-start(bf16[128,640]{1,0:T(8,128)(2,1)S(1)} %collective-permute-done.refs_3_), channel_id=1, source_target_pairs={{0,8},{1,9},{2,10},{3,11},{4,12},{5,13},{6,14},{7,15},{8,16},{9,17... | collective-permute-start | bytes 491528 | tf_op jit(solution)/shard_map/ppermute | solution.py:270
  35.4 10.3 %collective-permute-start.10 = (bf16[128,1024]{1,0:T(8,128)(2,1)}, bf16[128,1024]{1,0:T(8,128)(2,1)}, u32[]{:S(2)}, u32[]{:S(2)}) collective-permute-start(bf16[128,1024]{1,0:T(8,128)(2,1)} %get-tuple-element.40), channel_id=1, source_target_pairs={{0,2},{1,3},{2,0},{3,1},{4,6},{5,7},{6,4},{7,5},{8,10},{9,11},{10,... | collective-permute-start | bytes 786440 | tf_op jit(solution)/shard_map/ppermute | solution.py:265
  36.0 10.5 %collective-permute-start.11 = (bf16[128,1024]{1,0:T(8,128)(2,1)}, bf16[128,1024]{1,0:T(8,128)(2,1)}, u32[]{:S(2)}, u32[]{:S(2)}) collective-permute-start(bf16[128,1024]{1,0:T(8,128)(2,1)} %get-tuple-element.41), channel_id=1, source_target_pairs={{0,3},{1,2},{2,1},{3,0},{4,7},{5,6},{6,5},{7,4},{8,11},{9,10},{10,... | collective-permute-start | bytes 786440 | tf_op jit(solution)/shard_map/ppermute | solution.py:265
  42.9 5.2 %collective-permute-start.20 = (f32[16,1024]{1,0:T(8,128)S(1)}, f32[16,1024]{1,0:T(8,128)S(1)}, u32[]{:S(2)}, u32[]{:S(2)}) collective-permute-start(f32[16,1024]{1,0:T(8,128)S(1)} %constant_dynamic-update-slice_fusion.2), channel_id=1, source_target_pairs={{0,4},{1,5},{2,6},{3,7},{4,0},{5,1},{6,2},{7,3},{8,12},{9,13},{10,... | collective-permute-start | bytes 196616 | tf_op jit(solution)/shard_map/ppermute | solution.py:265
  43.5 6.2 %collective-permute-start.9 = (bf16[128,1024]{1,0:T(8,128)(2,1)}, bf16[128,1024]{1,0:T(8,128)(2,1)}, u32[]{:S(2)}, u32[]{:S(2)}) collective-permute-start(bf16[128,1024]{1,0:T(8,128)(2,1)} %get-tuple-element.39), channel_id=1, source_target_pairs={{0,1},{1,0},{2,3},{3,2},{4,5},{5,4},{6,7},{7,6},{8,9},{9,8},{10,11... | collective-permute-start | bytes 786440 | tf_op jit(solution)/shard_map/ppermute | solution.py:265
  44.1 9.3 %collective-permute-start.5 = (bf16[256,384]{1,0:T(8,128)(2,1)S(1)}, bf16[256,384]{1,0:T(8,128)(2,1)S(1)}, u32[]{:S(2)}, u32[]{:S(2)}) collective-permute-start(bf16[256,384]{1,0:T(8,128)(2,1)S(1)} %constant_dynamic-update-slice_fusion.refs_3_), channel_id=1, source_target_pairs={{0,8},{1,9},{2,10},{3,11},{4,12},{5,13},{6,14},{7,15},{8,16},{9,17... | collective-permute-start | bytes 589832 | tf_op jit(solution)/shard_map/ppermute | solution.py:270
  45.7 12.9 %collective-permute-start.7 = (bf16[128,1024]{1,0:T(8,128)(2,1)S(1)}, bf16[128,1024]{1,0:T(8,128)(2,1)S(1)}, u32[]{:S(2)}, u32[]{:S(2)}) collective-permute-start(bf16[128,1024]{1,0:T(8,128)(2,1)S(1)} %collective-permute-done.6.refs_0_.refs_4_), channel_id=1, source_target_pairs={{0,4},{1,5},{2,6},{3,7},{4,0},{5,1},{6,2},{7,3},{8,12},{9,13},{10,... | collective-permute-start | bytes 786440 | tf_op jit(solution)/shard_map/ppermute | solution.py:265
  46.5 9.8 %collective-permute-start.2 = (bf16[128,640]{1,0:T(8,128)(2,1)S(1)}, bf16[128,640]{1,0:T(8,128)(2,1)S(1)}, u32[]{:S(2)}, u32[]{:S(2)}) collective-permute-start(bf16[128,640]{1,0:T(8,128)(2,1)S(1)} %collective-permute-done.1.refs_1_.refs_5_), channel_id=1, source_target_pairs={{0,8},{1,9},{2,10},{3,11},{4,12},{5,13},{6,14},{7,15},{8,16},{9,17... | collective-permute-start | bytes 491528 | tf_op jit(solution)/shard_map/ppermute | solution.py:270
  48.1 10.5 %collective-permute-start.8 = (bf16[128,640]{1,0:T(8,128)(2,1)S(1)}, bf16[128,640]{1,0:T(8,128)(2,1)S(1)}, u32[]{:S(2)}, u32[]{:S(2)}) collective-permute-start(bf16[128,640]{1,0:T(8,128)(2,1)S(1)} %collective-permute-done.1.refs_1_.refs_5_), channel_id=1, source_target_pairs={{0,4},{1,5},{2,6},{3,7},{4,0},{5,1},{6,2},{7,3},{8,12},{9,13},{10,... | collective-permute-start | bytes 491528 | tf_op jit(solution)/shard_map/ppermute | solution.py:265
  49.6 9.0 %collective-permute-start.21 = (f32[16,1024]{1,0:T(8,128)S(1)}, f32[16,1024]{1,0:T(8,128)S(1)}, u32[]{:S(2)}, u32[]{:S(2)}) collective-permute-start(f32[16,1024]{1,0:T(8,128)S(1)} %select_add_fusion), channel_id=1, source_target_pairs={{0,8},{1,9},{2,10},{3,11},{4,12},{5,13},{6,14},{7,15},{8,16},{9,17... | collective-permute-start | bytes 196616 | tf_op jit(solution)/shard_map/ppermute | solution.py:270
  53.5 5.2 %collective-permute-start.22 = (f32[16,1024]{1,0:T(8,128)S(1)}, f32[16,1024]{1,0:T(8,128)S(1)}, u32[]{:S(2)}, u32[]{:S(2)}) collective-permute-start(f32[16,1024]{1,0:T(8,128)S(1)} %select_add_fusion), channel_id=1, source_target_pairs={{0,16},{1,17},{2,18},{3,19},{4,20},{5,21},{6,22},{7,23},{8,24},{9,... | collective-permute-start | bytes 196616 | tf_op jit(solution)/shard_map/ppermute | solution.py:270
  56.3 4.2 %collective-permute-start.23 = (f32[16,1024]{1,0:T(8,128)S(1)}, f32[16,1024]{1,0:T(8,128)S(1)}, u32[]{:S(2)}, u32[]{:S(2)}) collective-permute-start(f32[16,1024]{1,0:T(8,128)S(1)} %select_add_fusion), channel_id=1, source_target_pairs={{0,24},{1,25},{2,26},{3,27},{4,28},{5,29},{6,30},{7,31}} | collective-permute-start | bytes 196616 | tf_op jit(solution)/shard_map/ppermute | solution.py:270
  60.5 0.9 copy-start.4
  61.4 19.4 %copy-start.10 = (bf16[128,640]{1,0:T(8,128)(2,1)S(1)}, bf16[128,640]{1,0:T(8,128)(2,1)}, u32[]{:S(2)}) copy-start(bf16[128,640]{1,0:T(8,128)(2,1)} %copy-done.9) | copy-start | bytes 491524
  61.4 25.2 %copy-start.8 = (bf16[128,1024]{1,0:T(8,128)(2,1)S(1)}, bf16[128,1024]{1,0:T(8,128)(2,1)}, u32[]{:S(2)}) copy-start(bf16[128,1024]{1,0:T(8,128)(2,1)} %copy-done.7) | copy-start | bytes 786436
  65.4 29.8 %collective-permute-start.24 = (bf16[8,512,128]{2,1,0:T(8,128)(2,1)S(1)}, bf16[8,512,128]{2,1,0:T(8,128)(2,1)S(1)}, u32[]{:S(2)}, u32[]{:S(2)}) collective-permute-start(bf16[8,512,128]{2,1,0:T(8,128)(2,1)S(1)} %shard_map.69.refs_1_), channel_id=1, source_target_pairs={{0,1},{1,0},{2,3},{3,2},{4,5},{5,4},{6,7},{7,6},{8,9},{9,8},{10,11... | collective-permute-start | bytes 3145736 | tf_op jit(solution)/shard_map/ppermute | solution.py:265
  65.5 11.4 %collective-permute-start.26 = (bf16[128,1024]{1,0:T(8,128)(2,1)S(1)}, bf16[128,1024]{1,0:T(8,128)(2,1)S(1)}, u32[]{:S(2)}, u32[]{:S(2)}) collective-permute-start(bf16[128,1024]{1,0:T(8,128)(2,1)S(1)} %collective-permute-done.15.refs_0_.refs_6_), channel_id=1, source_target_pairs={{0,8},{1,9},{2,10},{3,11},{4,12},{5,13},{6,14},{7,15},{8,16},{9,17... | collective-permute-start | bytes 786440 | tf_op jit(solution)/shard_map/ppermute | solution.py:270
  65.6 20.6 %collective-permute-start.25 = (bf16[128,1024]{1,0:T(8,128)(2,1)S(1)}, bf16[128,1024]{1,0:T(8,128)(2,1)S(1)}, u32[]{:S(2)}, u32[]{:S(2)}) collective-permute-start(bf16[128,1024]{1,0:T(8,128)(2,1)S(1)} %collective-permute-done.15.refs_0_.refs_6_), channel_id=1, source_target_pairs={{0,4},{1,5},{2,6},{3,7},{4,0},{5,1},{6,2},{7,3},{8,12},{9,13},{10,... | collective-permute-start | bytes 786440 | tf_op jit(solution)/shard_map/ppermute | solution.py:265
  66.1 14.7 %collective-permute-start.35 = (bf16[256,384]{1,0:T(8,128)(2,1)S(1)}, bf16[256,384]{1,0:T(8,128)(2,1)S(1)}, u32[]{:S(2)}, u32[]{:S(2)}) collective-permute-start(bf16[256,384]{1,0:T(8,128)(2,1)S(1)} %collective-permute-done.5.refs_1_.refs_4_), channel_id=1, source_target_pairs={{0,8},{1,9},{2,10},{3,11},{4,12},{5,13},{6,14},{7,15},{8,16},{9,17... | collective-permute-start | bytes 589832 | tf_op jit(solution)/shard_map/ppermute | solution.py:270
  76.9 9.8 %collective-permute-start.27 = (bf16[128,1024]{1,0:T(8,128)(2,1)S(1)}, bf16[128,1024]{1,0:T(8,128)(2,1)S(1)}, u32[]{:S(2)}, u32[]{:S(2)}) collective-permute-start(bf16[128,1024]{1,0:T(8,128)(2,1)S(1)} %collective-permute-done.26.refs_8_), channel_id=1, source_target_pairs={{0,4},{1,5},{2,6},{3,7},{4,0},{5,1},{6,2},{7,3},{8,12},{9,13},{10,... | collective-permute-start | bytes 786440 | tf_op jit(solution)/shard_map/ppermute | solution.py:265
  77.4 7.2 %collective-permute-start.30 = (bf16[128,640]{1,0:T(8,128)(2,1)S(1)}, bf16[128,640]{1,0:T(8,128)(2,1)S(1)}, u32[]{:S(2)}, u32[]{:S(2)}) collective-permute-start(bf16[128,640]{1,0:T(8,128)(2,1)S(1)} %collective-permute-done.2.refs_0_.refs_7_), channel_id=1, source_target_pairs={{0,8},{1,9},{2,10},{3,11},{4,12},{5,13},{6,14},{7,15},{8,16},{9,17... | collective-permute-start | bytes 491528 | tf_op jit(solution)/shard_map/ppermute | solution.py:270
  80.9 8.7 %collective-permute-start.28 = (bf16[128,640]{1,0:T(8,128)(2,1)S(1)}, bf16[128,640]{1,0:T(8,128)(2,1)S(1)}, u32[]{:S(2)}, u32[]{:S(2)}) collective-permute-start(bf16[128,640]{1,0:T(8,128)(2,1)S(1)} %copy-done.10), channel_id=1, source_target_pairs={{0,4},{1,5},{2,6},{3,7},{4,0},{5,1},{6,2},{7,3},{8,12},{9,13},{10,... | collective-permute-start | bytes 491528 | tf_op jit(solution)/shard_map/ppermute | solution.py:265
  84.6 8.5 %collective-permute-start.29 = (bf16[128,640]{1,0:T(8,128)(2,1)S(1)}, bf16[128,640]{1,0:T(8,128)(2,1)S(1)}, u32[]{:S(2)}, u32[]{:S(2)}) collective-permute-start(bf16[128,640]{1,0:T(8,128)(2,1)S(1)} %collective-permute-done.2.refs_0_.refs_7_), channel_id=1, source_target_pairs={{0,4},{1,5},{2,6},{3,7},{4,0},{5,1},{6,2},{7,3},{8,12},{9,13},{10,... | collective-permute-start | bytes 491528 | tf_op jit(solution)/shard_map/ppermute | solution.py:265
  86.2 9.1 %collective-permute-start.31 = (bf16[128,640]{1,0:T(8,128)(2,1)S(1)}, bf16[128,640]{1,0:T(8,128)(2,1)S(1)}, u32[]{:S(2)}, u32[]{:S(2)}) collective-permute-start(bf16[128,640]{1,0:T(8,128)(2,1)S(1)} %collective-permute-done.30.refs_9_), channel_id=1, source_target_pairs={{0,4},{1,5},{2,6},{3,7},{4,0},{5,1},{6,2},{7,3},{8,12},{9,13},{10,... | collective-permute-start | bytes 491528 | tf_op jit(solution)/shard_map/ppermute | solution.py:265
  86.7 10.3 %collective-permute-start.36 = (bf16[256,384]{1,0:T(8,128)(2,1)S(1)}, bf16[256,384]{1,0:T(8,128)(2,1)S(1)}, u32[]{:S(2)}, u32[]{:S(2)}) collective-permute-start(bf16[256,384]{1,0:T(8,128)(2,1)S(1)} %collective-permute-done.35.refs_5_), channel_id=1, source_target_pairs={{0,8},{1,9},{2,10},{3,11},{4,12},{5,13},{6,14},{7,15},{8,16},{9,17... | collective-permute-start | bytes 589832 | tf_op jit(solution)/shard_map/ppermute | solution.py:270
  96.9 15.4 %collective-permute-start.32 = (f32[128,640]{1,0:T(8,128)S(1)}, f32[128,640]{1,0:T(8,128)S(1)}, u32[]{:S(2)}, u32[]{:S(2)}) collective-permute-start(f32[128,640]{1,0:T(8,128)S(1)} %get-tuple-element.58), channel_id=1, source_target_pairs={{0,1},{1,0},{2,3},{3,2},{4,5},{5,4},{6,7},{7,6},{8,9},{9,8},{10,11... | collective-permute-start | bytes 983048 | tf_op jit(solution)/shard_map/ppermute | solution.py:265
  98.3 5.7 %collective-permute-start.38 = (bf16[128,384]{1,0:T(8,128)(2,1)S(1)}, bf16[128,384]{1,0:T(8,128)(2,1)S(1)}, u32[]{:S(2)}, u32[]{:S(2)}) collective-permute-start(bf16[128,384]{1,0:T(8,128)(2,1)S(1)} %get-tuple-element.63), channel_id=1, source_target_pairs={{0,2},{1,3},{2,0},{3,1},{4,6},{5,7},{6,4},{7,5},{8,10},{9,11},{10,... | collective-permute-start | bytes 294920 | tf_op jit(solution)/shard_map/ppermute | solution.py:265
  99.0 13.2 %collective-permute-start.37 = (f32[128,384]{1,0:T(8,128)S(1)}, f32[128,384]{1,0:T(8,128)S(1)}, u32[]{:S(2)}, u32[]{:S(2)}) collective-permute-start(f32[128,384]{1,0:T(8,128)S(1)} %get-tuple-element.62), channel_id=1, source_target_pairs={{0,1},{1,0},{2,3},{3,2},{4,5},{5,4},{6,7},{7,6},{8,9},{9,8},{10,11... | collective-permute-start | bytes 589832 | tf_op jit(solution)/shard_map/ppermute | solution.py:265
  99.2 13.0 %collective-permute-start.33 = (bf16[128,640]{1,0:T(8,128)(2,1)S(1)}, bf16[128,640]{1,0:T(8,128)(2,1)S(1)}, u32[]{:S(2)}, u32[]{:S(2)}) collective-permute-start(bf16[128,640]{1,0:T(8,128)(2,1)S(1)} %get-tuple-element.59), channel_id=1, source_target_pairs={{0,2},{1,3},{2,0},{3,1},{4,6},{5,7},{6,4},{7,5},{8,10},{9,11},{10,... | collective-permute-start | bytes 491528 | tf_op jit(solution)/shard_map/ppermute | solution.py:265
  100.6 11.7 %collective-permute-start.34 = (bf16[128,640]{1,0:T(8,128)(2,1)S(1)}, bf16[128,640]{1,0:T(8,128)(2,1)S(1)}, u32[]{:S(2)}, u32[]{:S(2)}) collective-permute-start(bf16[128,640]{1,0:T(8,128)(2,1)S(1)} %get-tuple-element.60), channel_id=1, source_target_pairs={{0,3},{1,2},{2,1},{3,0},{4,7},{5,6},{6,5},{7,4},{8,11},{9,10},{10,... | collective-permute-start | bytes 491528 | tf_op jit(solution)/shard_map/ppermute | solution.py:265
  103.9 8.3 %collective-permute-start.39 = (bf16[128,384]{1,0:T(8,128)(2,1)S(1)}, bf16[128,384]{1,0:T(8,128)(2,1)S(1)}, u32[]{:S(2)}, u32[]{:S(2)}) collective-permute-start(bf16[128,384]{1,0:T(8,128)(2,1)S(1)} %get-tuple-element.64), channel_id=1, source_target_pairs={{0,3},{1,2},{2,1},{3,0},{4,7},{5,6},{6,5},{7,4},{8,11},{9,10},{10,... | collective-permute-start | bytes 294920 | tf_op jit(solution)/shard_map/ppermute | solution.py:265

commit v3 on v0

v3 whole, which is shorter than its diff:
```python
import functools

import jax
import jax.numpy as jnp
from jax import lax
from jax.experimental import pallas as pl
from jax.experimental.pallas import tpu as pltpu
from jax.sharding import PartitionSpec as P

BLOCK = 32
LANES = 128
TEAM = 4
LAST_PARTS = 2
VMEM_LIMIT = 32 * 1024 * 1024

f32 = jnp.float32
bf16 = jnp.bfloat16


def call(kernel, out_shape, scratch=(), after=()):
    def body(*refs):
        return kernel(*refs[len(after) :])

    def run(info, *args):
        return pl.pallas_call(
            body,
            out_shape=out_shape,
            in_specs=[pl.BlockSpec(memory_space=pl.ANY)] * len(after)
            + [pl.BlockSpec(memory_space=pltpu.SMEM)]
            + [pl.BlockSpec()] * len(args),
            scratch_shapes=list(scratch),
            compiler_params=pltpu.CompilerParams(vmem_limit_bytes=VMEM_LIMIT),
            cost_estimate=pl.CostEstimate(flops=0, bytes_accessed=0, transcendentals=0),
        )(*after, info, *args)

    return run


def halves_kernel(info_ref, weight_ref, give_ref, held_ref, sems):
    core = info_ref[2]
    depth, half = give_ref.shape
    copies = []
    for which, out in enumerate((give_ref, held_ref.at[:depth])):
        at = pl.multiple_of((core ^ (1 - which)) * half, LANES)
        copies.append(
            pltpu.make_async_copy(weight_ref.at[:, pl.ds(at, half)], out, sems.at[which])
        )
        copies[-1].start()
    for copy in copies:
        copy.wait()


def halves_of(info, weight):
    depth, half = weight.shape[0], weight.shape[1] // 2
    return pl.pallas_call(
        halves_kernel,
        out_shape=[
            jax.ShapeDtypeStruct((depth, half), weight.dtype),
            jax.ShapeDtypeStruct((2 * depth, half), weight.dtype),
        ],
        in_specs=[
            pl.BlockSpec(memory_space=pltpu.SMEM),
            pl.BlockSpec(memory_space=pltpu.HBM),
        ],
        out_specs=[pl.BlockSpec(memory_space=pltpu.VMEM)] * 2,
        scratch_shapes=[pltpu.SemaphoreType.DMA((2,))],
    )(info, weight)


CHUNKS = 4


def deal_kernel(team, depth, plan, info_ref, *refs):
    me = info_ref[0]
    count = len(plan)
    sources, held, sems = refs[:count], refs[-1 - count : -1], refs[-1]
    outs = list(refs[count : -1 - count])
    copies = []
    for source, whole in zip(sources, held):
        wide = source.shape[1] // CHUNKS
        for chunk in range(CHUNKS):
            cols = slice(chunk * wide, (chunk + 1) * wide)
            sem = sems.at[len(copies)]
            copies.append(pltpu.make_async_copy(source.at[:, cols], whole.at[:, cols], sem))
            copies[-1].start()
    for source, whole, steps in zip(sources, held, plan):
        rows = source.shape[0]
        runs = source.shape[1] // (team * depth)
        mine = [outs.pop(0) for _ in range(min(steps, 3))]
        for run in range(runs):
            if run % (runs // CHUNKS) == 0:
                copies.pop(0).wait()
            for step in range(steps):
                here = slice(rows * (step == 3), rows * (step == 3) + rows)
                at = pl.multiple_of((run * team + (me ^ step)) * depth, depth)
                mine[min(step, 2)][here, run * depth : (run + 1) * depth] = whole[:, pl.ds(at, depth)]


def deal(info, team, depth, sources, plan):
    pieces = []
    if depth % LANES == 0:
        shapes = []
        for source, steps in zip(sources, plan):
            rows, share = source.shape[0], source.shape[1] // team
            for deep in [rows, rows, 2 * rows][:steps]:
                shapes.append(jax.ShapeDtypeStruct((deep, share), source.dtype))
        pieces = list(
            pl.pallas_call(
                functools.partial(deal_kernel, team, depth, plan),
                out_shape=shapes,
                in_specs=[pl.BlockSpec(memory_space=pltpu.SMEM)]
                + [pl.BlockSpec(memory_space=pltpu.HBM)] * len(sources),
                out_specs=[pl.BlockSpec(memory_space=pltpu.VMEM)] * len(shapes),
                scratch_shapes=[pltpu.VMEM(source.shape, source.dtype) for source in sources]
                + [pltpu.SemaphoreType.DMA((CHUNKS * len(sources),))],
                compiler_params=pltpu.CompilerParams(vmem_limit_bytes=VMEM_LIMIT),
            )(info, *sources)
        )
    else:
        for source, steps in zip(sources, plan):
            rows, width = source.shape
            cut = source.reshape(rows, width // (team * depth), team, depth)
            shares = []
            for step in range(steps):
                share = lax.dynamic_index_in_dim(cut, info[0] ^ step, 2, keepdims=False)
                shares.append(share.reshape(rows, -1))
            if steps == team:
                shares[2:] = [jnp.concatenate(shares[2:], axis=0)]
            pieces += shares
    return [[pieces.pop(0) for _ in range(min(steps, 3))] for steps in plan]


def by_step(parts):
    rows = parts[0].shape[0]
    return [parts[0], parts[1], parts[2].at[:rows], parts[3].at[rows:]]


def spread(values, me, lanes, wide, above):
    per = values[0].shape[0] // BLOCK
    for step in range(TEAM):
        for b in range(per):
            rows = values[step][b * BLOCK : (b + 1) * BLOCK, lanes].astype(f32)
            wide[(me ^ step) * per + b, above:, :] = rows


def tile_lanes(info_ref, slot):
    return pl.ds(pl.multiple_of(info_ref[3 + slot] * LANES, LANES), LANES)


def state_kernel(info_ref, *refs):
    values = by_step(refs[:TEAM])
    rate_ref, starts_ref, end_ref, wide = refs[TEAM:]
    order = rate_ref.shape[0]
    me = info_ref[0]

    @pl.loop(0, starts_ref.shape[0])
    def _(slot):
        lanes = tile_lanes(info_ref, slot)
        spread(values, me, lanes, wide, 0)
        rate = rate_ref[:, lanes]
        lam, lam8 = jnp.exp(-rate), jnp.exp(-8.0 * rate)

        def block(b, state):
            starts_ref[slot, b] = state
            for at in range(0, BLOCK, 8):
                inflow = jnp.broadcast_to(wide[b, at : at + 1, :], (order, LANES))
                for t in range(1, 8):
                    inflow = lam * inflow + wide[b, at + t : at + t + 1, :]
                state = lam8 * state + inflow
            return state

        end_ref[:, lanes] = lax.fori_loop(0, wide.shape[0], block, jnp.zeros((order, LANES), f32))


def taps_kernel(base, info_ref, *refs):
    values = by_step(refs[:TEAM])
    rate_ref, coef_ref, skip_ref, y_ref, wide, taps = refs[TEAM:]
    me = info_ref[0]
    wide[:, :BLOCK, :] = jnp.zeros((wide.shape[0], BLOCK, LANES), f32)

    @pl.loop(0, y_ref.shape[0])
    def _(slot):
        lanes = tile_lanes(info_ref, base + slot)
        spread(values, me, lanes, wide, BLOCK)
        skip = skip_ref[:, lanes]
        lam = jnp.exp(-rate_ref[:, lanes])
        power = coef_ref[:, lanes]
        for t in range(BLOCK):
            tap = jnp.sum(power, axis=0, keepdims=True).astype(bf16).astype(f32)
            taps[t] = jnp.broadcast_to(tap, (8, LANES))
            power = power * lam

        @pl.loop(0, wide.shape[0])
        def _(b):
            y = [skip * wide[b, BLOCK + 8 * i : BLOCK + 8 * i + 8, :] for i in range(BLOCK // 8)]
            for t in range(BLOCK):
                tap = taps[t]
                for i in range(t // 8, BLOCK // 8):
                    at = BLOCK + 8 * i - t
                    y[i] = y[i] + tap * wide[b, at : at + 8, :]
            for i in range(BLOCK // 8):
                y_ref[slot, pl.ds(pl.multiple_of(b * BLOCK + 8 * i, 8), 8), :] = y[i]


def gate_kernel(base, reaches, info_ref, *refs):
    gaps = len(reaches)
    gates = by_step(refs[:TEAM])
    y_ref, starts_ref, rate_ref, coef_ref, near_ref = refs[TEAM : TEAM + 5]
    far = refs[TEAM + 5 : TEAM + 5 + gaps]
    out_ref, reach, decay8, start = refs[TEAM + 5 + gaps :]
    me, high = info_ref[0], info_ref[1]
    order = rate_ref.shape[0]
    rows = gates[0].shape[0]
    per = rows // BLOCK
    span = float(TEAM * rows)
    ahead = lax.broadcasted_iota(jnp.int32, (8, LANES), 0).astype(f32) + 1.0

    @pl.loop(0, y_ref.shape[0])
    def _(slot):
        lanes = tile_lanes(info_ref, base + slot)
        rate, coef = rate_ref[:, lanes], coef_ref[:, lanes]
        for k in range(order):
            reach[k] = coef[k : k + 1] * jnp.exp(-ahead * rate[k : k + 1])
            decay8[k] = jnp.exp(jnp.broadcast_to(-8.0 * rate[k : k + 1], (8, LANES)))
        state = jnp.zeros((order, LANES), f32)
        for gap, ref in zip(reaches, far):
            state = state + jnp.exp(-2.0 * span * gap * rate) * ref[:, lanes]
        after = jnp.exp(-span * rate) * state + near_ref[:, lanes]
        state = jnp.where(high == 1, after, state)
        over = jnp.exp(-float(BLOCK) * rate)
        for step in range(TEAM):
            place = me ^ step
            goes = place ^ (me & 2)
            entering = state * jnp.exp(-(rows * place).astype(f32) * rate)
            for b in range(per):
                start[b] = starts_ref[base + slot, place * per + b] + entering
                entering = entering * over
            for b in range(per):
                y = []
                for i in range(BLOCK // 8):
                    here = pl.multiple_of(place * rows + b * BLOCK + 8 * i, 8)
                    y.append(y_ref[slot, pl.ds(here, 8), :])
                for k in range(order):
                    term = reach[k] * start[b, k : k + 1, :]
                    decay = decay8[k]
                    for i in range(BLOCK // 8):
                        y[i] = y[i] + term
                        if i + 1 < BLOCK // 8:
                            term = term * decay
                for i in range(0, BLOCK // 8, 2):
                    at = b * BLOCK + 8 * i
                    conv = jnp.concatenate(y[i : i + 2], axis=0)
                    gated = gates[step][at : at + 16, lanes].astype(f32) * conv
                    to = pl.ds(pl.multiple_of(goes * rows + at, 16), 16)
                    out_ref[slot, to, :] = gated.astype(bf16)


def gated_columns(gated, halves, per, group):
    own, other = (gated[2 * (group // per) + i][group % per] for i in range(2))
    return jnp.concatenate([own, other], axis=1)


def early_kernel(halves, in_slots, info_ref, *refs):
    gated, weights, out = refs[: 2 * halves], refs[2 * halves : -1], refs[-1]
    per = gated[0].shape[0]
    wide = out.shape[1]
    step = min(wide, 256)
    for slot, weight in enumerate(weights):
        if in_slots:
            left = gated_columns(gated, halves, per, slot)
        else:
            left = jnp.concatenate([ref[info_ref[3 + slot]] for ref in gated], axis=1)
        for col in range(0, wide, step):
            cols = slice(col, col + step)
            term = jnp.dot(left, weight[:, cols], preferred_element_type=f32)
            out[:, cols] = term if slot == 0 else out[:, cols] + term


def project_kernel(halves, in_slots, slots, at, info_ref, *refs):
    gated, (early_ref, near_ref, away_ref) = refs[: 2 * halves], refs[2 * halves : 2 * halves + 3]
    outs, total = refs[2 * halves + 3 : -1], refs[-1]
    core = info_ref[2]
    per = gated[0].shape[0]
    rows, wide = outs[0].shape
    step = min(wide, 256)
    lefts = []
    for slot in (slots - 2, slots - 1):
        if in_slots:
            lefts.append(gated_columns(gated, halves, per, slot))
        else:
            lefts.append(jnp.concatenate([ref[info_ref[3 + slot]] for ref in gated], axis=1))
    for col in range(0, wide, step):
        term = early_ref[:, at + col : at + col + step]
        term += jnp.dot(lefts[0], near_ref[:, at + col : at + col + step], preferred_element_type=f32)
        term += jnp.dot(lefts[1], away_ref[:, col : col + step], preferred_element_type=f32)
        total[:, col : col + step] = term
    for step, out in enumerate(outs):
        start = (step // 2) * 2 * rows + (core ^ (step & 1)) * rows
        out[...] = total[pl.ds(pl.multiple_of(start, rows), rows), :].astype(out.dtype)


def finish_kernel(parts, info_ref, *refs):
    core = info_ref[2]
    out_ref = refs[-1]
    half = out_ref.shape[1] // 2
    at = 0
    for part in range(parts):
        mine, his, mine_far, his_far = refs[4 * part : 4 * part + 4]
        wide = mine.shape[1]
        near = pl.ds(pl.multiple_of(core * half + at, LANES), wide)
        away = pl.ds(pl.multiple_of((1 - core) * half + at, LANES), wide)
        out_ref[:, near] = (mine[...] + mine_far[...].astype(f32)).astype(bf16)
        out_ref[:, away] = (his[...].astype(f32) + his_far[...].astype(f32)).astype(bf16)
        at += wide


def on_device(q_gate, values_in, decay_rate, residue, skip_gain, out_weight):
    rows, width = q_gate.shape
    depth, features = out_weight.shape
    order = decay_rate.shape[1]
    count = lax.axis_size("seq")
    heights = count // (2 * TEAM)
    mine = lax.axis_index("seq")
    me, core = mine % TEAM, mine % 2
    y, z = (mine // TEAM) % 2, mine // (2 * TEAM)
    share = width // TEAM
    half = features // 2

    def swap(value, bit):
        return lax.ppermute(value, "seq", [(i, i ^ bit) for i in range(count)])

    def up(value, gap, wrap):
        hop = gap * 2 * TEAM
        pairs = [(i, (i + hop) % count) for i in range(count) if wrap or i + hop < count]
        return lax.ppermute(value, "seq", pairs)

    in_slots = depth % LANES == 0
    groups = []
    for gap in range(heights):
        at = (z - gap) % heights
        groups += [at * 2 + y, at * 2 + (1 - y)]
    tiles = share // LANES
    order_of = groups if in_slots else list(range(tiles))
    info = jnp.stack([jnp.int32(n) for n in [me, y, core] + order_of])
    group_info = info if in_slots else jnp.stack([jnp.int32(n) for n in [me, y, core] + groups])

    def share_out(shares):
        across = swap(shares[2], 2)
        return [shares[0], swap(shares[1], 1), across, swap(across, 1)]

    def share_out(shares):
        across = swap(shares[2], 2)
        return [shares[0], swap(shares[1], 1), across, swap(across, 1)]

    def tied(value, *others):
        return lax.optimization_barrier((value, *others))[0]

    give, held = halves_of(info, out_weight)
    held = lax.dynamic_update_slice(held, swap(give, 1), (depth, 0))
    last = heights - 1
    weights, weights_away = [held], []
    for gap in range(last):
        weights_away.append(swap(weights[gap], TEAM))
        weights.append(up(weights[gap], 1, True))
    wide = half // LAST_PARTS
    finals = [
        swap(weights[last][:, part * wide : (part + 1) * wide], TEAM) for part in range(LAST_PARTS)
    ]

    (values,) = deal(info, TEAM, depth, [values_in], [TEAM])
    values = share_out(values)
    gates, rates, residues, skip = deal(
        info, TEAM, depth, [q_gate, decay_rate.T, residue.T, skip_gain[None]], [TEAM, 1, 1, 1]
    )
    gates[2] = tied(gates[2], values[2])
    gates = share_out(gates)
    rates, residues, skip = rates[0], residues[0], skip[0]
    coef = residues * jnp.sqrt(-jnp.expm1(-2.0 * rates))

    blocks = TEAM * rows // BLOCK
    starts, end = call(
        state_kernel,
        [
            jax.ShapeDtypeStruct((tiles, blocks, order, LANES), f32),
            jax.ShapeDtypeStruct((order, share), f32),
        ],
        [pltpu.VMEM((blocks, BLOCK, LANES), f32)],
        after=[weights[min(1, last)], weights_away[0]],
    )(info, *values, rates)

    pieces = 4
    some = tiles // pieces
    local = [
        call(
            functools.partial(taps_kernel, part * some),
            jax.ShapeDtypeStruct((some, TEAM * rows, LANES), f32),
            [pltpu.VMEM((blocks, 2 * BLOCK, LANES), f32), pltpu.VMEM((BLOCK, 8, LANES), f32)],
            after=[end],
        )(info, *values, rates, coef, skip)
        for part in range(pieces)
    ]

    near = swap(end, TEAM)
    first, second = jnp.where(y == 0, end, near), jnp.where(y == 0, near, end)
    span = float(TEAM * rows)
    held = jnp.exp(-span * rates) * first + second
    far, gap, part = [], 1, 0
    while gap < heights:
        held = tied(held, local[min(part, pieces - 1)])
        far.append((gap - 1, up(held, gap, False)))
        held = held + jnp.exp(-2.0 * span * gap * rates) * far[-1][1]
        gap, part = gap * 2, part + 1

    tables = [pltpu.VMEM((order, 8, LANES), f32)] * 2
    gated = [
        call(
            functools.partial(gate_kernel, part * some, [lag for lag, _ in far]),
            jax.ShapeDtypeStruct((some, TEAM * rows, LANES), bf16),
            tables + [pltpu.VMEM((rows // BLOCK, order, LANES), f32)],
            after=[weights_away[min(1, last - 1)], weights[min(2, last)]] if part == 0 else [],
        )(info, *gates, local[part], starts, rates, coef, near, *[state for _, state in far])
        for part in range(pieces)
    ]
    if in_slots:
        gated = [ref for part in gated for ref in (part, swap(part, 1))]
    else:
        gated = jnp.concatenate(gated, axis=0).transpose(1, 0, 2)
        gated = gated.reshape(TEAM * rows, width // (TEAM * depth), depth).transpose(1, 0, 2)
        gated = [gated, swap(gated, 1)]
    halves = len(gated) // 2

    blocks_early = [ref for gap in range(last) for ref in (weights[gap], weights_away[gap])]
    early = call(
        functools.partial(early_kernel, halves, in_slots),
        jax.ShapeDtypeStruct((TEAM * rows, half), f32),
    )(group_info, *gated, *blocks_early)
    finished = []
    for part, final in enumerate(finals):
        shape = functools.partial(jax.ShapeDtypeStruct, (rows, wide))
        sums = call(
            functools.partial(project_kernel, halves, in_slots, 2 * heights, part * wide),
            [shape(f32), shape(f32), shape(bf16), shape(bf16)],
            [pltpu.VMEM((TEAM * rows, wide), f32)],
        )(group_info, *gated, early, weights[last], final)
        finished += [sums[0]] + [swap(sums[step], step) for step in range(1, TEAM)]
    return call(
        functools.partial(finish_kernel, LAST_PARTS),
        jax.ShapeDtypeStruct((rows, features), bf16),
    )(info, *finished)


def solution(mesh):
    in_specs = (
        P(("groups", "seq"), None),
        P(("groups", "seq"), None),
        P(),
        P(),
        P(),
        P("seq", None),
    )
    out_specs = P(("groups", "seq"), None)
    return jax.shard_map(
        on_device, mesh=mesh, in_specs=in_specs, out_specs=out_specs, check_vma=False
    )
```

time: 303 us -> 99.6 us (0.33)
  matrix products: 119 us -> 0 us
  other arithmetic: 78.8 us -> 0.96 us
  local copies, waits for them, and re-layouts: 77.6 us -> 4.07 us
  Pallas kernels: 0 us -> 30.3 us
  starting transfers between devices: 0.27 us -> 29.7 us
  waiting for transfers between devices: 11.8 us -> 34.1 us
  between operations: 13.2 us -> 0.26 us
    dot_general x5 -> x0, matrix products: 119 us -> none  [the longest x1 47.3 us: on_device(): jnp.einsum('tkd,nkd->ntd', reach_table, starts, precision=lax.Precision.H...]
    dot_general x1 -> x0, local copies, waits for them, and re-layouts: 44.1 us -> none  [on_device(): jnp.dot(tap_round.T, selector, preferred_element_type=jnp.bfloat16)]
    select_n x31 -> x0, other arithmetic: 38.9 us -> none  [hop(): jnp.where(position < mine, new, old)]
    ppermute x0 -> x28, waiting for transfers between devices: none -> 34.1 us  [the longest x23 26.2 us: swap(): return lax.ppermute(value, 'seq', [(i, i ^ bit) for i in range(count)])]
    pallas_call x0 -> x16, Pallas kernels: none -> 30.3 us  [the longest x13 24.3 us: run(): pl.pallas_call(body, out_shape=out_shape, in_specs=[pl.BlockSpec(memory_s...]
    ppermute x0 -> x28, starting transfers between devices: none -> 29.7 us  [the longest x23 18.5 us: swap(): return lax.ppermute(value, 'seq', [(i, i ^ bit) for i in range(count)])]
    reduce_sum x1 -> x0, other arithmetic: 25.7 us -> none  [on_device(): jnp.sum(mode_coef[None] * jnp.exp(-position[:, None, None] * rate_modes[N...]
    add x2 -> x0, local copies, waits for them, and re-layouts: 14 us -> none  [the longest x1 7.13 us: on_device(): conv = (local_part + correction).reshape(tok_rows, width)]
  transfers between devices with their start and end apart: 3 -> 28, of which waited for: 2 -> 12; matrix products, arithmetic and copies ran while one was open for 88% -> 2% of each run, Pallas kernels for 0% -> 26%
where the time goes in v3:
time: 99.6 us; the launch traced here: 99.3 us
  waiting for transfers between devices  34.1 us (34%)
  Pallas kernels  30.3 us (30%)
  starting transfers between devices  29.7 us (30%)
  local copies, waits for them, and re-layouts  4.07 us (4%)
    ppermute x23, waiting for transfers between devices, swap(): return lax.ppermute(value, 'seq', [(i, i ^ bit) for i in range(count)])  26.2 us
    pallas_call x13, Pallas kernels, run(): pl.pallas_call(body, out_shape=out_shape, in_specs=[pl.BlockSpec(memory_s...  24.3 us
    ppermute x23, starting transfers between devices, swap(): return lax.ppermute(value, 'seq', [(i, i ^ bit) for i in range(count)])  18.5 us
    ppermute x5, starting transfers between devices, up(): return lax.ppermute(value, 'seq', pairs)  11.1 us
    ppermute x5, waiting for transfers between devices, up(): return lax.ppermute(value, 'seq', pairs)  7.94 us
    pallas_call x2, Pallas kernels, deal(): pl.pallas_call(functools.partial(deal_kernel, team, depth, plan), out_sha...  3.23 us
    pallas_call x1, Pallas kernels, halves_of(): pl.pallas_call(halves_kernel, out_shape=[jax.ShapeDtypeStruct((depth, hal...  2.72 us
    unnamed x26, local copies, waits for them, and re-layouts  2.69 us
  transfers between devices with their start and end apart: 28, of which 12 were waited for; matrix products, arithmetic and copies ran while one was open for 2% of the time, Pallas kernels for 26%

profile of v3, /device:TPU:0, one launch (start us, length us, event | category | flops | bytes accessed | tf_op | source)
XLA Modules:
  0.0 99.3 jit_solution(761912001820314725)
XLA Ops:
  0.0 0.6 stack.47.info_ref.refs_2_.refs_1_.refs_0_
  0.6 2.7 %shard_map.64 = (bf16[128,1024]{1,0:T(8,128)(2,1)}, bf16[256,1024]{1,0:T(8,128)(2,1)}) custom-call(s32[11]{0:T(128)} %stack.47.info_ref.refs_2_.refs_1_.refs_0_, bf16[128,2048]{1,0:T(8,128)(2,1)} %weight_ref.1), custom_call_target="tpu_custom_call" | custom-call | tf_op jit(solution)/shard_map/pallas_call | solution.py:55
  3.4 0.6 collective-permute-start
  4.0 1.2 %copy-done.2 = bf16[128,4096]{1,0:T(8,128)(2,1)S(1)} copy-done((bf16[128,4096]{1,0:T(8,128)(2,1)S(1)}, bf16[128,4096]{1,0:T(8,128)(2,1)}, u32[]{:S(2)}) %copy-start.2) | copy-done | bytes 1048600
  5.2 0.6 copy-done.7
  5.8 0.9 shard_map.66
  6.8 2.6 %collective-permute-start.5 = (bf16[256,1024]{1,0:T(8,128)(2,1)S(1)}, bf16[256,1024]{1,0:T(8,128)(2,1)S(1)}, u32[]{:S(2)}, u32[]{:S(2)}) collective-permute-start(bf16[256,1024]{1,0:T(8,128)(2,1)S(1)} %get-tuple-element.34), channel_id=1, source_target_pairs={{0,2},{1,3},{2,0},{3,1},{4,6},{5,7},{6,4},{7,5},{8,10},{9,11},{10,... | collective-permute-start | bytes 1572872 | tf_op jit(solution)/shard_map/ppermute | solution.py:330
  9.4 0.7 constant_dynamic-update-slice_fusion.refs_9_
  10.1 1.6 %collective-permute-start.1 = (bf16[256,1024]{1,0:T(8,128)(2,1)}, bf16[256,1024]{1,0:T(8,128)(2,1)}, u32[]{:S(2)}, u32[]{:S(2)}) collective-permute-start(bf16[256,1024]{1,0:T(8,128)(2,1)} %constant_dynamic-update-slice_fusion.refs_9_), channel_id=1, source_target_pairs={{0,8},{1,9},{2,10},{3,11},{4,12},{5,13},{6,14},{7,15},{8,16},{9,17... | collective-permute-start | bytes 1572872 | tf_op jit(solution)/shard_map/ppermute | solution.py:335
  11.7 1.5 %collective-permute-start.8 = (bf16[256,1024]{1,0:T(8,128)(2,1)}, bf16[256,1024]{1,0:T(8,128)(2,1)S(1)}, u32[]{:S(2)}, u32[]{:S(2)}) collective-permute-start(bf16[256,1024]{1,0:T(8,128)(2,1)} %constant_dynamic-update-slice_fusion.refs_9_), channel_id=1, source_target_pairs={{0,4},{1,5},{2,6},{3,7},{4,0},{5,1},{6,2},{7,3},{8,12},{9,13},{10,... | collective-permute-start | bytes 1572872 | tf_op jit(solution)/shard_map/ppermute | solution.py:330
  13.2 8.8 %collective-permute-done.5.refs_5_.refs_4_ = bf16[256,1024]{1,0:T(8,128)(2,1)S(1)} collective-permute-done((bf16[256,1024]{1,0:T(8,128)(2,1)S(1)}, bf16[256,1024]{1,0:T(8,128)(2,1)S(1)}, u32[]{:S(2)}, u32[]{:S(2)}) %collective-permute-start.5) | collective-permute-done | bytes 524320 | tf_op jit(solution)/shard_map/ppermute | solution.py:330
  21.9 0.0 collective-permute-start.10
  22.0 2.3 %shard_map.65 = (bf16[128,1024]{1,0:T(8,128)(2,1)S(1)}, bf16[128,1024]{1,0:T(8,128)(2,1)S(1)}, bf16[256,1024]{1,0:T(8,128)(2,1)}, f32[16,1024]{1,0:T(8,128)S(1)}...) custom-call(s32[11]{0:T(128)S(1)} %copy-done.8, bf16[128,4096]{1,0:T(8,128)(2,1)S(1)} %copy-done.3, ...), custom_call_target="tpu_custom_call" | custom-call | tf_op jit(solution)/shard_map/pallas_call | solution.py:108
  24.3 1.8 %collective-permute-start.6 = (bf16[256,1024]{1,0:T(8,128)(2,1)}, bf16[256,1024]{1,0:T(8,128)(2,1)S(1)}, u32[]{:S(2)}, u32[]{:S(2)}) collective-permute-start(bf16[256,1024]{1,0:T(8,128)(2,1)} %get-tuple-element.35), channel_id=1, source_target_pairs={{0,2},{1,3},{2,0},{3,1},{4,6},{5,7},{6,4},{7,5},{8,10},{9,11},{10,... | collective-permute-start | bytes 1572872 | tf_op jit(solution)/shard_map/ppermute | solution.py:330
  26.1 0.2 collective-permute-done.1.refs_0_.refs_11_
  26.3 1.4 %collective-permute-start.3 = (bf16[256,1024]{1,0:T(8,128)(2,1)}, bf16[256,1024]{1,0:T(8,128)(2,1)}, u32[]{:S(2)}, u32[]{:S(2)}) collective-permute-start(bf16[256,1024]{1,0:T(8,128)(2,1)} %collective-permute-done.1.refs_0_.refs_11_), channel_id=1, source_target_pairs={{0,8},{1,9},{2,10},{3,11},{4,12},{5,13},{6,14},{7,15},{8,16},{9,17... | collective-permute-start | bytes 1572872 | tf_op jit(solution)/shard_map/ppermute | solution.py:335
  27.7 0.0 collective-permute-start.9
  27.7 1.5 %collective-permute-done.9.refs_4_.refs_3_ = bf16[128,1024]{1,0:T(8,128)(2,1)S(1)} collective-permute-done((bf16[128,1024]{1,0:T(8,128)(2,1)S(1)}, bf16[128,1024]{1,0:T(8,128)(2,1)S(1)}, u32[]{:S(2)}, u32[]{:S(2)}) %collective-permute-start.9) | collective-permute-done | bytes 262176 | tf_op jit(solution)/shard_map/ppermute | solution.py:330
  29.2 0.0 collective-permute-done.8.refs_1_.refs_10_
  29.2 5.0 %shard_map.67 = (f32[8,16,16,128]{3,2,1,0:T(8,128)S(1)}, f32[16,1024]{1,0:T(8,128)}) custom-call(bf16[256,1024]{1,0:T(8,128)(2,1)} %collective-permute-done.1.refs_0_.refs_11_, bf16[256,1024]{1,0:T(8,128)(2,1)S(1)} %collective-permute-done.8.refs_1_.refs_10_, s32[11]{0:T(128)S(1)} %copy-done.8, bf16[128,1024]{1,0:T(8,128)(2,1)S(1)} %get-tuple-element.36.refs_3_.refs_2_, ...), custom_call_target="tpu_custom_call" | custom-call | tf_op jit(solution)/shard_map/pallas_call | solution.py:25
  34.2 0.8 copy-done
  35.0 1.5 %collective-permute-start.11 = (f32[16,1024]{1,0:T(8,128)}, f32[16,1024]{1,0:T(8,128)S(1)}, u32[]{:S(2)}, u32[]{:S(2)}) collective-permute-start(f32[16,1024]{1,0:T(8,128)} %get-tuple-element.39.refs_0_), channel_id=1, source_target_pairs={{0,4},{1,5},{2,6},{3,7},{4,0},{5,1},{6,2},{7,3},{8,12},{9,13},{10,... | collective-permute-start | bytes 196616 | tf_op jit(solution)/shard_map/ppermute | solution.py:330
  36.6 0.5 collective-permute-start.2
  37.1 1.8 %collective-permute-done.6.refs_5_.refs_3_ = bf16[256,1024]{1,0:T(8,128)(2,1)S(1)} collective-permute-done((bf16[256,1024]{1,0:T(8,128)(2,1)}, bf16[256,1024]{1,0:T(8,128)(2,1)S(1)}, u32[]{:S(2)}, u32[]{:S(2)}) %collective-permute-start.6) | collective-permute-done | bytes 524320 | tf_op jit(solution)/shard_map/ppermute | solution.py:330
  38.9 3.4 %collective-permute-done.3.refs_1_.refs_13_ = bf16[256,1024]{1,0:T(8,128)(2,1)} collective-permute-done((bf16[256,1024]{1,0:T(8,128)(2,1)}, bf16[256,1024]{1,0:T(8,128)(2,1)}, u32[]{:S(2)}, u32[]{:S(2)}) %collective-permute-start.3) | collective-permute-done | bytes 524320 | tf_op jit(solution)/shard_map/ppermute | solution.py:335
  42.3 0.9 select_add_fusion
  43.3 2.0 %shard_map.68.refs_7_ = f32[2,512,128]{2,1,0:T(8,128)S(1)} custom-call(f32[16,1024]{1,0:T(8,128)} %get-tuple-element.39.refs_0_, s32[11]{0:T(128)S(1)} %copy-done.8, bf16[128,1024]{1,0:T(8,128)(2,1)S(1)} %get-tuple-element.36.refs_3_.refs_2_, bf16[128,1024]{1,0:T(8,128)(2,1)S(1)} %collective-permute-done.9.refs_4_.refs_3_, ...), custom_call_target="tpu_custom_call" | custom-call | tf_op jit(solution)/shard_map/pallas_call | solution.py:25
  45.2 3.2 %collective-permute-start.12 = (f32[16,1024]{1,0:T(8,128)S(1)}, f32[16,1024]{1,0:T(8,128)S(1)}, u32[]{:S(2)}, u32[]{:S(2)}) collective-permute-start(f32[16,1024]{1,0:T(8,128)S(1)} %get-tuple-element.43), channel_id=1, source_target_pairs={{0,8},{1,9},{2,10},{3,11},{4,12},{5,13},{6,14},{7,15},{8,16},{9,17... | collective-permute-start | bytes 196616 | tf_op jit(solution)/shard_map/ppermute | solution.py:335
  48.4 0.1 collective-permute-start.4
  48.5 2.0 %shard_map.69.refs_5_ = f32[2,512,128]{2,1,0:T(8,128)S(1)} custom-call(f32[16,1024]{1,0:T(8,128)} %get-tuple-element.39.refs_0_, s32[11]{0:T(128)S(1)} %copy-done.8, bf16[128,1024]{1,0:T(8,128)(2,1)S(1)} %get-tuple-element.36.refs_3_.refs_2_, bf16[128,1024]{1,0:T(8,128)(2,1)S(1)} %collective-permute-done.9.refs_4_.refs_3_, ...), custom_call_target="tpu_custom_call" | custom-call | tf_op jit(solution)/shard_map/pallas_call | solution.py:25
  50.5 4.3 %collective-permute-done.12.refs_12_.refs_10_ = f32[16,1024]{1,0:T(8,128)S(1)} collective-permute-done((f32[16,1024]{1,0:T(8,128)S(1)}, f32[16,1024]{1,0:T(8,128)S(1)}, u32[]{:S(2)}, u32[]{:S(2)}) %collective-permute-start.12) | collective-permute-done | bytes 65568 | tf_op jit(solution)/shard_map/ppermute | solution.py:335
  54.8 5.0 %collective-permute-start.13 = (f32[16,1024]{1,0:T(8,128)S(1)}, f32[16,1024]{1,0:T(8,128)S(1)}, u32[]{:S(2)}, u32[]{:S(2)}) collective-permute-start(f32[16,1024]{1,0:T(8,128)S(1)} %multiply_add_fusion), channel_id=1, source_target_pairs={{0,16},{1,17},{2,18},{3,19},{4,20},{5,21},{6,22},{7,23},{8,24},{9,... | collective-permute-start | bytes 196616 | tf_op jit(solution)/shard_map/ppermute | solution.py:335
  59.8 2.0 %shard_map.74.refs_5_ = f32[2,512,128]{2,1,0:T(8,128)S(1)} custom-call(f32[16,1024]{1,0:T(8,128)} %get-tuple-element.39.refs_0_, s32[11]{0:T(128)S(1)} %copy-done.8, bf16[128,1024]{1,0:T(8,128)(2,1)S(1)} %get-tuple-element.36.refs_3_.refs_2_, bf16[128,1024]{1,0:T(8,128)(2,1)S(1)} %collective-permute-done.9.refs_4_.refs_3_, ...), custom_call_target="tpu_custom_call" | custom-call | tf_op jit(solution)/shard_map/pallas_call | solution.py:25
  61.8 0.0 collective-permute-done.4.refs_4_.refs_2_
  61.8 1.6 %collective-permute-start.18 = (bf16[256,1024]{1,0:T(8,128)(2,1)}, bf16[256,1024]{1,0:T(8,128)(2,1)S(1)}, u32[]{:S(2)}, u32[]{:S(2)}) collective-permute-start(bf16[256,1024]{1,0:T(8,128)(2,1)} %collective-permute-done.3.refs_1_.refs_13_), channel_id=1, source_target_pairs={{0,4},{1,5},{2,6},{3,7},{4,0},{5,1},{6,2},{7,3},{8,12},{9,13},{10,... | collective-permute-start | bytes 1572872 | tf_op jit(solution)/shard_map/ppermute | solution.py:330
  63.4 0.0 collective-permute-done.13.refs_13_.refs_11_
  63.4 1.2 %shard_map.75.refs_7_ = bf16[2,512,128]{2,1,0:T(8,128)(2,1)S(1)} custom-call(s32[11]{0:T(128)S(1)} %copy-done.8, bf16[128,1024]{1,0:T(8,128)(2,1)S(1)} %get-tuple-element.31.refs_3_.refs_1_, bf16[128,1024]{1,0:T(8,128)(2,1)S(1)} %collective-permute-done.4.refs_4_.refs_2_, bf16[256,1024]{1,0:T(8,128)(2,1)S(1)} %collective-permute-done.6.refs_5_.refs_3_, ...), custom_call_target="tpu_custom_call" | custom-call | tf_op jit(solution)/shard_map/pallas_call | solution.py:25
  64.6 0.1 collective-permute-start.17
  64.7 2.0 %shard_map.72.refs_5_ = f32[2,512,128]{2,1,0:T(8,128)S(1)} custom-call(f32[16,1024]{1,0:T(8,128)} %get-tuple-element.39.refs_0_, s32[11]{0:T(128)S(1)} %copy-done.8, bf16[128,1024]{1,0:T(8,128)(2,1)S(1)} %get-tuple-element.36.refs_3_.refs_2_, bf16[128,1024]{1,0:T(8,128)(2,1)S(1)} %collective-permute-done.9.refs_4_.refs_3_, ...), custom_call_target="tpu_custom_call" | custom-call | tf_op jit(solution)/shard_map/pallas_call | solution.py:25
  66.7 1.3 %shard_map.73.refs_5_ = bf16[2,512,128]{2,1,0:T(8,128)(2,1)S(1)} custom-call(s32[11]{0:T(128)S(1)} %copy-done.8, bf16[128,1024]{1,0:T(8,128)(2,1)S(1)} %get-tuple-element.31.refs_3_.refs_1_, bf16[128,1024]{1,0:T(8,128)(2,1)S(1)} %collective-permute-done.4.refs_4_.refs_2_, bf16[256,1024]{1,0:T(8,128)(2,1)S(1)} %collective-permute-done.6.refs_5_.refs_3_, ...), custom_call_target="tpu_custom_call" | custom-call | tf_op jit(solution)/shard_map/pallas_call | solution.py:25
  67.9 0.6 collective-permute-start.16
  68.5 1.2 %shard_map.71.refs_3_ = bf16[2,512,128]{2,1,0:T(8,128)(2,1)S(1)} custom-call(s32[11]{0:T(128)S(1)} %copy-done.8, bf16[128,1024]{1,0:T(8,128)(2,1)S(1)} %get-tuple-element.31.refs_3_.refs_1_, bf16[128,1024]{1,0:T(8,128)(2,1)S(1)} %collective-permute-done.4.refs_4_.refs_2_, bf16[256,1024]{1,0:T(8,128)(2,1)S(1)} %collective-permute-done.6.refs_5_.refs_3_, ...), custom_call_target="tpu_custom_call" | custom-call | tf_op jit(solution)/shard_map/pallas_call | solution.py:25
  69.8 0.0 copy-start.4
  69.8 0.1 collective-permute-start.15
  69.9 1.2 %shard_map.70.refs_1_ = bf16[2,512,128]{2,1,0:T(8,128)(2,1)S(1)} custom-call(bf16[256,1024]{1,0:T(8,128)(2,1)S(1)} %collective-permute-done.2.refs_0_.refs_12_, bf16[256,1024]{1,0:T(8,128)(2,1)} %collective-permute-done.3.refs_1_.refs_13_, s32[11]{0:T(128)S(1)} %copy-done.8, bf16[128,1024]{1,0:T(8,128)(2,1)S(1)} %get-tuple-element.31.refs_3_.refs_1_, ...), custom_call_target="tpu_custom_call" | custom-call | tf_op jit(solution)/shard_map/pallas_call | solution.py:25
  71.1 0.6 collective-permute-start.14
  71.7 0.6 collective-permute-start.24
  72.3 1.5 %collective-permute-start.20 = (bf16[256,512]{1,0:T(8,128)(2,1)S(1)}, bf16[256,512]{1,0:T(8,128)(2,1)S(1)}, u32[]{:S(2)}, u32[]{:S(2)}) collective-permute-start(bf16[256,512]{1,0:T(8,128)(2,1)S(1)} %get-tuple-element.54), channel_id=1, source_target_pairs={{0,4},{1,5},{2,6},{3,7},{4,0},{5,1},{6,2},{7,3},{8,12},{9,13},{10,... | collective-permute-start | bytes 786440 | tf_op jit(solution)/shard_map/ppermute | solution.py:330
  73.8 0.2 collective-permute-done.18.refs_14_
  74.1 3.0 %shard_map.76.refs_9_ = f32[512,1024]{1,0:T(8,128)S(1)} custom-call(s32[11]{0:T(128)S(1)} %copy-done.8, bf16[2,512,128]{2,1,0:T(8,128)(2,1)S(1)} %shard_map.70.refs_1_, bf16[2,512,128]{2,1,0:T(8,128)(2,1)S(1)} %collective-permute-done.14.refs_2_, bf16[2,512,128]{2,1,0:T(8,128)(2,1)S(1)} %shard_map.71.refs_3_, ...), custom_call_target="tpu_custom_call" | custom-call | tf_op jit(solution)/shard_map/pallas_call | solution.py:25
  77.1 3.9 %collective-permute-done.24.refs_11_ = bf16[256,512]{1,0:T(8,128)(2,1)S(1)} collective-permute-done((bf16[256,512]{1,0:T(8,128)(2,1)S(1)}, bf16[256,512]{1,0:T(8,128)(2,1)S(1)}, u32[]{:S(2)}, u32[]{:S(2)}) %collective-permute-start.24) | collective-permute-done | bytes 262176 | tf_op jit(solution)/shard_map/ppermute | solution.py:330
  81.0 1.0 %shard_map.78 = (f32[128,512]{1,0:T(8,128)S(1)}, f32[128,512]{1,0:T(8,128)S(1)}, bf16[128,512]{1,0:T(8,128)(2,1)S(1)}, bf16[128,512]{1,0:T(8,128)(2,1)S(1)}) custom-call(s32[11]{0:T(128)S(1)} %copy-done.8, bf16[2,512,128]{2,1,0:T(8,128)(2,1)S(1)} %shard_map.70.refs_1_, bf16[2,512,128]{2,1,0:T(8,128)(2,1)S(1)} %collective-permute-done.14.refs_2_, ...), custom_call_target="tpu_custom_call" | custom-call | tf_op jit(solution)/shard_map/pallas_call | solution.py:25
  82.0 0.1 collective-permute-start.25
  82.1 1.4 %collective-permute-start.26 = (bf16[128,512]{1,0:T(8,128)(2,1)S(1)}, bf16[128,512]{1,0:T(8,128)(2,1)S(1)}, u32[]{:S(2)}, u32[]{:S(2)}) collective-permute-start(bf16[128,512]{1,0:T(8,128)(2,1)S(1)} %get-tuple-element.51), channel_id=1, source_target_pairs={{0,2},{1,3},{2,0},{3,1},{4,6},{5,7},{6,4},{7,5},{8,10},{9,11},{10,... | collective-permute-start | bytes 393224 | tf_op jit(solution)/shard_map/ppermute | solution.py:330
  83.5 2.1 %collective-permute-done.20.refs_11_ = bf16[256,512]{1,0:T(8,128)(2,1)S(1)} collective-permute-done((bf16[256,512]{1,0:T(8,128)(2,1)S(1)}, bf16[256,512]{1,0:T(8,128)(2,1)S(1)}, u32[]{:S(2)}, u32[]{:S(2)}) %collective-permute-start.20) | collective-permute-done | bytes 262176 | tf_op jit(solution)/shard_map/ppermute | solution.py:330
  85.7 1.0 %shard_map.77 = (f32[128,512]{1,0:T(8,128)S(1)}, f32[128,512]{1,0:T(8,128)S(1)}, bf16[128,512]{1,0:T(8,128)(2,1)S(1)}, bf16[128,512]{1,0:T(8,128)(2,1)S(1)}) custom-call(s32[11]{0:T(128)S(1)} %copy-done.8, bf16[2,512,128]{2,1,0:T(8,128)(2,1)S(1)} %shard_map.70.refs_1_, bf16[2,512,128]{2,1,0:T(8,128)(2,1)S(1)} %collective-permute-done.14.refs_2_, ...), custom_call_target="tpu_custom_call" | custom-call | tf_op jit(solution)/shard_map/pallas_call | solution.py:25
  86.7 0.1 collective-permute-start.21
  86.8 1.9 %collective-permute-start.27 = (bf16[128,512]{1,0:T(8,128)(2,1)S(1)}, bf16[128,512]{1,0:T(8,128)(2,1)S(1)}, u32[]{:S(2)}, u32[]{:S(2)}) collective-permute-start(bf16[128,512]{1,0:T(8,128)(2,1)S(1)} %get-tuple-element.52), channel_id=1, source_target_pairs={{0,3},{1,2},{2,1},{3,0},{4,7},{5,6},{6,5},{7,4},{8,11},{9,10},{10,... | collective-permute-start | bytes 393224 | tf_op jit(solution)/shard_map/ppermute | solution.py:330
  88.7 0.2 collective-permute-start.22
  88.9 1.2 %collective-permute-start.23 = (bf16[128,512]{1,0:T(8,128)(2,1)S(1)}, bf16[128,512]{1,0:T(8,128)(2,1)S(1)}, u32[]{:S(2)}, u32[]{:S(2)}) collective-permute-start(bf16[128,512]{1,0:T(8,128)(2,1)S(1)} %get-tuple-element.48), channel_id=1, source_target_pairs={{0,3},{1,2},{2,1},{3,0},{4,7},{5,6},{6,5},{7,4},{8,11},{9,10},{10,... | collective-permute-start | bytes 393224 | tf_op jit(solution)/shard_map/ppermute | solution.py:330
  90.1 2.4 %collective-permute-done.27.refs_8_ = bf16[128,512]{1,0:T(8,128)(2,1)S(1)} collective-permute-done((bf16[128,512]{1,0:T(8,128)(2,1)S(1)}, bf16[128,512]{1,0:T(8,128)(2,1)S(1)}, u32[]{:S(2)}, u32[]{:S(2)}) %collective-permute-start.27) | collective-permute-done | bytes 131104 | tf_op jit(solution)/shard_map/ppermute | solution.py:330
  92.5 3.5 %collective-permute-done.22.refs_3_ = bf16[128,512]{1,0:T(8,128)(2,1)S(1)} collective-permute-done((bf16[128,512]{1,0:T(8,128)(2,1)S(1)}, bf16[128,512]{1,0:T(8,128)(2,1)S(1)}, u32[]{:S(2)}, u32[]{:S(2)}) %collective-permute-start.22) | collective-permute-done | bytes 131104 | tf_op jit(solution)/shard_map/ppermute | solution.py:330
  96.0 1.9 %collective-permute-done.23.refs_4_ = bf16[128,512]{1,0:T(8,128)(2,1)S(1)} collective-permute-done((bf16[128,512]{1,0:T(8,128)(2,1)S(1)}, bf16[128,512]{1,0:T(8,128)(2,1)S(1)}, u32[]{:S(2)}, u32[]{:S(2)}) %collective-permute-start.23) | collective-permute-done | bytes 131104 | tf_op jit(solution)/shard_map/ppermute | solution.py:330
  97.9 1.4 %shard_map.79 = bf16[128,2048]{1,0:T(8,128)(2,1)} custom-call(s32[11]{0:T(128)S(1)} %copy-done.8, f32[128,512]{1,0:T(8,128)S(1)} %get-tuple-element.45.refs_1_, f32[128,512]{1,0:T(8,128)S(1)} %collective-permute-done.21.refs_2_, bf16[128,512]{1,0:T(8,128)(2,1)S(1)} %collective-permute-done.22.refs_3_, bf16[128,512]{1,0:T(8,128)(2,1)S(1)} %collective-permute-done.23.refs_4_, ...), custom_call_target="tpu_custom_call" | custom-call | tf_op jit(solution)/shard_map/pallas_call | solution.py:25
  (39 shorter events, 0.1 us)
Async XLA Ops:
  0.0 22.0 %copy-start.5 = (f32[4096,16]{0,1:T(8,128)S(1)}, f32[4096,16]{0,1:T(8,128)}, u32[]{:S(2)}) copy-start(f32[4096,16]{0,1:T(8,128)} %param.8) | copy-start | bytes 786436
  0.0 22.0 %copy-start.6 = (f32[4096,16]{0,1:T(8,128)S(1)}, f32[4096,16]{0,1:T(8,128)}, u32[]{:S(2)}) copy-start(f32[4096,16]{0,1:T(8,128)} %param.9) | copy-start | bytes 786436
  0.0 22.0 %copy-start.10 = (f32[4096]{0:T(1024)S(1)}, f32[4096]{0:T(1024)}, u32[]{:S(2)}) copy-start(f32[4096]{0:T(1024)} %param.10) | copy-start | bytes 49156
  0.6 21.3 %copy-start.8 = (s32[11]{0:T(128)S(1)}, s32[11]{0:T(128)}, u32[]{:S(2)}) copy-start(s32[11]{0:T(128)} %stack.47.info_ref.refs_2_.refs_1_.refs_0_) | copy-start | bytes 136
  3.4 6.0 %collective-permute-start = (bf16[128,1024]{1,0:T(8,128)(2,1)}, bf16[128,1024]{1,0:T(8,128)(2,1)S(1)}, u32[]{:S(2)}, u32[]{:S(2)}) collective-permute-start(bf16[128,1024]{1,0:T(8,128)(2,1)} %get-tuple-element.30), channel_id=1, source_target_pairs={{0,1},{1,0},{2,3},{3,2},{4,5},{5,4},{6,7},{7,6},{8,9},{9,8},{10,11... | collective-permute-start | bytes 786440 | tf_op jit(solution)/shard_map/ppermute | solution.py:330
  4.0 1.2 %copy-start.2 = (bf16[128,4096]{1,0:T(8,128)(2,1)S(1)}, bf16[128,4096]{1,0:T(8,128)(2,1)}, u32[]{:S(2)}) copy-start(bf16[128,4096]{1,0:T(8,128)(2,1)} %refs_0_.3) | copy-start | bytes 3145732
  5.2 0.6 copy-start.7
  5.8 16.1 %copy-start.3 = (bf16[128,4096]{1,0:T(8,128)(2,1)S(1)}, bf16[128,4096]{1,0:T(8,128)(2,1)}, u32[]{:S(2)}) copy-start(bf16[128,4096]{1,0:T(8,128)(2,1)} %refs_0_.2) | copy-start | bytes 3145732
  6.8 15.1 %collective-permute-start.5 = (bf16[256,1024]{1,0:T(8,128)(2,1)S(1)}, bf16[256,1024]{1,0:T(8,128)(2,1)S(1)}, u32[]{:S(2)}, u32[]{:S(2)}) collective-permute-start(bf16[256,1024]{1,0:T(8,128)(2,1)S(1)} %get-tuple-element.34), channel_id=1, source_target_pairs={{0,2},{1,3},{2,0},{3,1},{4,6},{5,7},{6,4},{7,5},{8,10},{9,11},{10,... | collective-permute-start | bytes 1572872 | tf_op jit(solution)/shard_map/ppermute | solution.py:330
  10.1 16.2 %collective-permute-start.1 = (bf16[256,1024]{1,0:T(8,128)(2,1)}, bf16[256,1024]{1,0:T(8,128)(2,1)}, u32[]{:S(2)}, u32[]{:S(2)}) collective-permute-start(bf16[256,1024]{1,0:T(8,128)(2,1)} %constant_dynamic-update-slice_fusion.refs_9_), channel_id=1, source_target_pairs={{0,8},{1,9},{2,10},{3,11},{4,12},{5,13},{6,14},{7,15},{8,16},{9,17... | collective-permute-start | bytes 1572872 | tf_op jit(solution)/shard_map/ppermute | solution.py:335
  11.7 17.6 %collective-permute-start.8 = (bf16[256,1024]{1,0:T(8,128)(2,1)}, bf16[256,1024]{1,0:T(8,128)(2,1)S(1)}, u32[]{:S(2)}, u32[]{:S(2)}) collective-permute-start(bf16[256,1024]{1,0:T(8,128)(2,1)} %constant_dynamic-update-slice_fusion.refs_9_), channel_id=1, source_target_pairs={{0,4},{1,5},{2,6},{3,7},{4,0},{5,1},{6,2},{7,3},{8,12},{9,13},{10,... | collective-permute-start | bytes 1572872 | tf_op jit(solution)/shard_map/ppermute | solution.py:330
  21.9 7.3 %collective-permute-start.10 = (bf16[256,1024]{1,0:T(8,128)(2,1)S(1)}, bf16[256,1024]{1,0:T(8,128)(2,1)S(1)}, u32[]{:S(2)}, u32[]{:S(2)}) collective-permute-start(bf16[256,1024]{1,0:T(8,128)(2,1)S(1)} %collective-permute-done.5.refs_5_.refs_4_), channel_id=1, source_target_pairs={{0,1},{1,0},{2,3},{3,2},{4,5},{5,4},{6,7},{7,6},{8,9},{9,8},{10,11... | collective-permute-start | bytes 1572872 | tf_op jit(solution)/shard_map/ppermute | solution.py:330
  24.3 10.0 %copy-start.9 = (f32[16,1024]{1,0:T(8,128)}, f32[16,1024]{1,0:T(8,128)S(1)}, u32[]{:S(2)}) copy-start(f32[16,1024]{1,0:T(8,128)S(1)} %get-tuple-element.40) | copy-start | bytes 196612
  24.3 10.8 %copy-start.11 = (bf16[128,1024]{1,0:T(8,128)(2,1)}, bf16[128,1024]{1,0:T(8,128)(2,1)S(1)}, u32[]{:S(2)}) copy-start(bf16[128,1024]{1,0:T(8,128)(2,1)S(1)} %get-tuple-element.32) | copy-start | bytes 786436
  24.3 14.6 %collective-permute-start.6 = (bf16[256,1024]{1,0:T(8,128)(2,1)}, bf16[256,1024]{1,0:T(8,128)(2,1)S(1)}, u32[]{:S(2)}, u32[]{:S(2)}) collective-permute-start(bf16[256,1024]{1,0:T(8,128)(2,1)} %get-tuple-element.35), channel_id=1, source_target_pairs={{0,2},{1,3},{2,0},{3,1},{4,6},{5,7},{6,4},{7,5},{8,10},{9,11},{10,... | collective-permute-start | bytes 1572872 | tf_op jit(solution)/shard_map/ppermute | solution.py:330
  26.3 16.0 %collective-permute-start.3 = (bf16[256,1024]{1,0:T(8,128)(2,1)}, bf16[256,1024]{1,0:T(8,128)(2,1)}, u32[]{:S(2)}, u32[]{:S(2)}) collective-permute-start(bf16[256,1024]{1,0:T(8,128)(2,1)} %collective-permute-done.1.refs_0_.refs_11_), channel_id=1, source_target_pairs={{0,8},{1,9},{2,10},{3,11},{4,12},{5,13},{6,14},{7,15},{8,16},{9,17... | collective-permute-start | bytes 1572872 | tf_op jit(solution)/shard_map/ppermute | solution.py:335
  27.7 1.5 %collective-permute-start.9 = (bf16[128,1024]{1,0:T(8,128)(2,1)S(1)}, bf16[128,1024]{1,0:T(8,128)(2,1)S(1)}, u32[]{:S(2)}, u32[]{:S(2)}) collective-permute-start(bf16[128,1024]{1,0:T(8,128)(2,1)S(1)} %get-tuple-element.37), channel_id=1, source_target_pairs={{0,1},{1,0},{2,3},{3,2},{4,5},{5,4},{6,7},{7,6},{8,9},{9,8},{10,11... | collective-permute-start | bytes 786440 | tf_op jit(solution)/shard_map/ppermute | solution.py:330
  34.2 0.8 copy-start
  35.0 7.3 %collective-permute-start.11 = (f32[16,1024]{1,0:T(8,128)}, f32[16,1024]{1,0:T(8,128)S(1)}, u32[]{:S(2)}, u32[]{:S(2)}) collective-permute-start(f32[16,1024]{1,0:T(8,128)} %get-tuple-element.39.refs_0_), channel_id=1, source_target_pairs={{0,4},{1,5},{2,6},{3,7},{4,0},{5,1},{6,2},{7,3},{8,12},{9,13},{10,... | collective-permute-start | bytes 196616 | tf_op jit(solution)/shard_map/ppermute | solution.py:330
  36.6 11.9 %copy-start.12 = (bf16[128,1024]{1,0:T(8,128)(2,1)S(1)}, bf16[128,1024]{1,0:T(8,128)(2,1)}, u32[]{:S(2)}) copy-start(bf16[128,1024]{1,0:T(8,128)(2,1)} %copy-done.11) | copy-start | bytes 786436
  36.6 33.2 %collective-permute-start.2 = (bf16[256,1024]{1,0:T(8,128)(2,1)}, bf16[256,1024]{1,0:T(8,128)(2,1)S(1)}, u32[]{:S(2)}, u32[]{:S(2)}) collective-permute-start(bf16[256,1024]{1,0:T(8,128)(2,1)} %collective-permute-done.1.refs_0_.refs_11_), channel_id=1, source_target_pairs={{0,4},{1,5},{2,6},{3,7},{4,0},{5,1},{6,2},{7,3},{8,12},{9,13},{10,... | collective-permute-start | bytes 1572872 | tf_op jit(solution)/shard_map/ppermute | solution.py:330
  38.9 24.5 %collective-permute-start.7 = (bf16[256,1024]{1,0:T(8,128)(2,1)S(1)}, bf16[256,1024]{1,0:T(8,128)(2,1)S(1)}, u32[]{:S(2)}, u32[]{:S(2)}) collective-permute-start(bf16[256,1024]{1,0:T(8,128)(2,1)S(1)} %collective-permute-done.6.refs_5_.refs_3_), channel_id=1, source_target_pairs={{0,1},{1,0},{2,3},{3,2},{4,5},{5,4},{6,7},{7,6},{8,9},{9,8},{10,11... | collective-permute-start | bytes 1572872 | tf_op jit(solution)/shard_map/ppermute | solution.py:330
  42.3 28.8 %collective-permute-start.19 = (bf16[256,1024]{1,0:T(8,128)(2,1)}, bf16[256,1024]{1,0:T(8,128)(2,1)S(1)}, u32[]{:S(2)}, u32[]{:S(2)}) collective-permute-start(bf16[256,1024]{1,0:T(8,128)(2,1)} %collective-permute-done.3.refs_1_.refs_13_), channel_id=1, source_target_pairs={{0,8},{1,9},{2,10},{3,11},{4,12},{5,13},{6,14},{7,15},{8,16},{9,17... | collective-permute-start | bytes 1572872 | tf_op jit(solution)/shard_map/ppermute | solution.py:335
  45.2 9.6 %collective-permute-start.12 = (f32[16,1024]{1,0:T(8,128)S(1)}, f32[16,1024]{1,0:T(8,128)S(1)}, u32[]{:S(2)}, u32[]{:S(2)}) collective-permute-start(f32[16,1024]{1,0:T(8,128)S(1)} %get-tuple-element.43), channel_id=1, source_target_pairs={{0,8},{1,9},{2,10},{3,11},{4,12},{5,13},{6,14},{7,15},{8,16},{9,17... | collective-permute-start | bytes 196616 | tf_op jit(solution)/shard_map/ppermute | solution.py:335
  48.4 13.3 %collective-permute-start.4 = (bf16[128,1024]{1,0:T(8,128)(2,1)S(1)}, bf16[128,1024]{1,0:T(8,128)(2,1)S(1)}, u32[]{:S(2)}, u32[]{:S(2)}) collective-permute-start(bf16[128,1024]{1,0:T(8,128)(2,1)S(1)} %copy-done.12), channel_id=1, source_target_pairs={{0,1},{1,0},{2,3},{3,2},{4,5},{5,4},{6,7},{7,6},{8,9},{9,8},{10,11... | collective-permute-start | bytes 786440 | tf_op jit(solution)/shard_map/ppermute | solution.py:330
  54.8 8.6 %collective-permute-start.13 = (f32[16,1024]{1,0:T(8,128)S(1)}, f32[16,1024]{1,0:T(8,128)S(1)}, u32[]{:S(2)}, u32[]{:S(2)}) collective-permute-start(f32[16,1024]{1,0:T(8,128)S(1)} %multiply_add_fusion), channel_id=1, source_target_pairs={{0,16},{1,17},{2,18},{3,19},{4,20},{5,21},{6,22},{7,23},{8,24},{9,... | collective-permute-start | bytes 196616 | tf_op jit(solution)/shard_map/ppermute | solution.py:335
  61.8 12.3 %collective-permute-start.18 = (bf16[256,1024]{1,0:T(8,128)(2,1)}, bf16[256,1024]{1,0:T(8,128)(2,1)S(1)}, u32[]{:S(2)}, u32[]{:S(2)}) collective-permute-start(bf16[256,1024]{1,0:T(8,128)(2,1)} %collective-permute-done.3.refs_1_.refs_13_), channel_id=1, source_target_pairs={{0,4},{1,5},{2,6},{3,7},{4,0},{5,1},{6,2},{7,3},{8,12},{9,13},{10,... | collective-permute-start | bytes 1572872 | tf_op jit(solution)/shard_map/ppermute | solution.py:330
  64.6 7.1 %collective-permute-start.17 = (bf16[2,512,128]{2,1,0:T(8,128)(2,1)S(1)}, bf16[2,512,128]{2,1,0:T(8,128)(2,1)S(1)}, u32[]{:S(2)}, u32[]{:S(2)}) collective-permute-start(bf16[2,512,128]{2,1,0:T(8,128)(2,1)S(1)} %shard_map.75.refs_7_), channel_id=1, source_target_pairs={{0,1},{1,0},{2,3},{3,2},{4,5},{5,4},{6,7},{7,6},{8,9},{9,8},{10,11... | collective-permute-start | bytes 786440 | tf_op jit(solution)/shard_map/ppermute | solution.py:330
  67.9 4.4 %collective-permute-start.16 = (bf16[2,512,128]{2,1,0:T(8,128)(2,1)S(1)}, bf16[2,512,128]{2,1,0:T(8,128)(2,1)S(1)}, u32[]{:S(2)}, u32[]{:S(2)}) collective-permute-start(bf16[2,512,128]{2,1,0:T(8,128)(2,1)S(1)} %shard_map.73.refs_5_), channel_id=1, source_target_pairs={{0,1},{1,0},{2,3},{3,2},{4,5},{5,4},{6,7},{7,6},{8,9},{9,8},{10,11... | collective-permute-start | bytes 786440 | tf_op jit(solution)/shard_map/ppermute | solution.py:330
  69.8 4.3 %copy-start.1 = (bf16[256,1024]{1,0:T(8,128)(2,1)S(1)}, bf16[256,1024]{1,0:T(8,128)(2,1)}, u32[]{:S(2)}) copy-start(bf16[256,1024]{1,0:T(8,128)(2,1)} %copy-done) | copy-start | bytes 1572868
  69.8 4.3 %copy-start.4 = (bf16[256,1024]{1,0:T(8,128)(2,1)S(1)}, bf16[256,1024]{1,0:T(8,128)(2,1)}, u32[]{:S(2)}) copy-start(bf16[256,1024]{1,0:T(8,128)(2,1)} %constant_dynamic-update-slice_fusion.refs_9_) | copy-start | bytes 1572868
  69.8 4.1 %collective-permute-start.15 = (bf16[2,512,128]{2,1,0:T(8,128)(2,1)S(1)}, bf16[2,512,128]{2,1,0:T(8,128)(2,1)S(1)}, u32[]{:S(2)}, u32[]{:S(2)}) collective-permute-start(bf16[2,512,128]{2,1,0:T(8,128)(2,1)S(1)} %shard_map.71.refs_3_), channel_id=1, source_target_pairs={{0,1},{1,0},{2,3},{3,2},{4,5},{5,4},{6,7},{7,6},{8,9},{9,8},{10,11... | collective-permute-start | bytes 786440 | tf_op jit(solution)/shard_map/ppermute | solution.py:330
  71.1 2.7 %collective-permute-start.14 = (bf16[2,512,128]{2,1,0:T(8,128)(2,1)S(1)}, bf16[2,512,128]{2,1,0:T(8,128)(2,1)S(1)}, u32[]{:S(2)}, u32[]{:S(2)}) collective-permute-start(bf16[2,512,128]{2,1,0:T(8,128)(2,1)S(1)} %shard_map.70.refs_1_), channel_id=1, source_target_pairs={{0,1},{1,0},{2,3},{3,2},{4,5},{5,4},{6,7},{7,6},{8,9},{9,8},{10,11... | collective-permute-start | bytes 786440 | tf_op jit(solution)/shard_map/ppermute | solution.py:330
  71.7 9.2 %collective-permute-start.24 = (bf16[256,512]{1,0:T(8,128)(2,1)S(1)}, bf16[256,512]{1,0:T(8,128)(2,1)S(1)}, u32[]{:S(2)}, u32[]{:S(2)}) collective-permute-start(bf16[256,512]{1,0:T(8,128)(2,1)S(1)} %get-tuple-element.53), channel_id=1, source_target_pairs={{0,4},{1,5},{2,6},{3,7},{4,0},{5,1},{6,2},{7,3},{8,12},{9,13},{10,... | collective-permute-start | bytes 786440 | tf_op jit(solution)/shard_map/ppermute | solution.py:330
  72.3 13.3 %collective-permute-start.20 = (bf16[256,512]{1,0:T(8,128)(2,1)S(1)}, bf16[256,512]{1,0:T(8,128)(2,1)S(1)}, u32[]{:S(2)}, u32[]{:S(2)}) collective-permute-start(bf16[256,512]{1,0:T(8,128)(2,1)S(1)} %get-tuple-element.54), channel_id=1, source_target_pairs={{0,4},{1,5},{2,6},{3,7},{4,0},{5,1},{6,2},{7,3},{8,12},{9,13},{10,... | collective-permute-start | bytes 786440 | tf_op jit(solution)/shard_map/ppermute | solution.py:330
  82.0 15.9 %collective-permute-start.25 = (f32[128,512]{1,0:T(8,128)S(1)}, f32[128,512]{1,0:T(8,128)S(1)}, u32[]{:S(2)}, u32[]{:S(2)}) collective-permute-start(f32[128,512]{1,0:T(8,128)S(1)} %get-tuple-element.50), channel_id=1, source_target_pairs={{0,1},{1,0},{2,3},{3,2},{4,5},{5,4},{6,7},{7,6},{8,9},{9,8},{10,11... | collective-permute-start | bytes 786440 | tf_op jit(solution)/shard_map/ppermute | solution.py:330
  82.1 6.8 %collective-permute-start.26 = (bf16[128,512]{1,0:T(8,128)(2,1)S(1)}, bf16[128,512]{1,0:T(8,128)(2,1)S(1)}, u32[]{:S(2)}, u32[]{:S(2)}) collective-permute-start(bf16[128,512]{1,0:T(8,128)(2,1)S(1)} %get-tuple-element.51), channel_id=1, source_target_pairs={{0,2},{1,3},{2,0},{3,1},{4,6},{5,7},{6,4},{7,5},{8,10},{9,11},{10,... | collective-permute-start | bytes 393224 | tf_op jit(solution)/shard_map/ppermute | solution.py:330
  86.7 11.2 %collective-permute-start.21 = (f32[128,512]{1,0:T(8,128)S(1)}, f32[128,512]{1,0:T(8,128)S(1)}, u32[]{:S(2)}, u32[]{:S(2)}) collective-permute-start(f32[128,512]{1,0:T(8,128)S(1)} %get-tuple-element.46), channel_id=1, source_target_pairs={{0,1},{1,0},{2,3},{3,2},{4,5},{5,4},{6,7},{7,6},{8,9},{9,8},{10,11... | collective-permute-start | bytes 786440 | tf_op jit(solution)/shard_map/ppermute | solution.py:330
  86.8 5.8 %collective-permute-start.27 = (bf16[128,512]{1,0:T(8,128)(2,1)S(1)}, bf16[128,512]{1,0:T(8,128)(2,1)S(1)}, u32[]{:S(2)}, u32[]{:S(2)}) collective-permute-start(bf16[128,512]{1,0:T(8,128)(2,1)S(1)} %get-tuple-element.52), channel_id=1, source_target_pairs={{0,3},{1,2},{2,1},{3,0},{4,7},{5,6},{6,5},{7,4},{8,11},{9,10},{10,... | collective-permute-start | bytes 393224 | tf_op jit(solution)/shard_map/ppermute | solution.py:330
  88.7 7.3 %collective-permute-start.22 = (bf16[128,512]{1,0:T(8,128)(2,1)S(1)}, bf16[128,512]{1,0:T(8,128)(2,1)S(1)}, u32[]{:S(2)}, u32[]{:S(2)}) collective-permute-start(bf16[128,512]{1,0:T(8,128)(2,1)S(1)} %get-tuple-element.47), channel_id=1, source_target_pairs={{0,2},{1,3},{2,0},{3,1},{4,6},{5,7},{6,4},{7,5},{8,10},{9,11},{10,... | collective-permute-start | bytes 393224 | tf_op jit(solution)/shard_map/ppermute | solution.py:330
  88.9 9.0 %collective-permute-start.23 = (bf16[128,512]{1,0:T(8,128)(2,1)S(1)}, bf16[128,512]{1,0:T(8,128)(2,1)S(1)}, u32[]{:S(2)}, u32[]{:S(2)}) collective-permute-start(bf16[128,512]{1,0:T(8,128)(2,1)S(1)} %get-tuple-element.48), channel_id=1, source_target_pairs={{0,3},{1,2},{2,1},{3,0},{4,7},{5,6},{6,5},{7,4},{8,11},{9,10},{10,... | collective-permute-start | bytes 393224 | tf_op jit(solution)/shard_map/ppermute | solution.py:330

commit v4 on v3

v4 whole, which is shorter than its diff:
```python
import functools

import jax
import jax.numpy as jnp
from jax import lax
from jax.experimental import pallas as pl
from jax.experimental.pallas import tpu as pltpu
from jax.sharding import PartitionSpec as P

BLOCK = 32
LANES = 128
CHUNKS = 8
TEAM = 4
LAST_PARTS = 2
VMEM_LIMIT = 8 * 1024 * 1024

f32 = jnp.float32
bf16 = jnp.bfloat16


def tied(value, *others):
    return lax.optimization_barrier((value, *others))[0]


def call(kernel, out_shape, scratch=(), after=(), micros=0.0):
    def run(info, *args):
        return pl.pallas_call(
            kernel,
            out_shape=out_shape,
            in_specs=[pl.BlockSpec(memory_space=pltpu.SMEM)] + [pl.BlockSpec()] * len(args),
            scratch_shapes=list(scratch),
            compiler_params=pltpu.CompilerParams(vmem_limit_bytes=VMEM_LIMIT),
            cost_estimate=pl.CostEstimate(
                flops=int(micros * 1.1e9), bytes_accessed=int(micros * 3.6e6), transcendentals=0
            ),
        )(tied(info, *after), *args)

    return run


def deal_kernel(team, depth, plan, info_ref, *refs):
    me = info_ref[0]
    count = len(plan)
    sources, held, sems = refs[:count], refs[-1 - count : -1], refs[-1]
    outs = list(refs[count : -1 - count])
    copies = []
    for source, whole in zip(sources, held):
        wide = source.shape[1] // CHUNKS
        for chunk in range(CHUNKS):
            cols = slice(chunk * wide, (chunk + 1) * wide)
            sem = sems.at[len(copies)]
            copies.append(pltpu.make_async_copy(source.at[:, cols], whole.at[:, cols], sem))
            copies[-1].start()
    for source, whole, steps in zip(sources, held, plan):
        runs = source.shape[1] // (team * depth)
        mine = [outs.pop(0) for _ in range(steps)]
        for run in range(runs):
            if run % (runs // CHUNKS) == 0:
                copies.pop(0).wait()
            for step in range(steps):
                at = pl.multiple_of((run * team + (me ^ step)) * depth, depth)
                mine[step][:, run * depth : (run + 1) * depth] = whole[:, pl.ds(at, depth)]


def deal(info, team, depth, sources, plan):
    pieces = []
    if depth % LANES == 0:
        shapes = []
        for source, steps in zip(sources, plan):
            share = (source.shape[0], source.shape[1] // team)
            shapes += [jax.ShapeDtypeStruct(share, source.dtype)] * steps
        pieces = list(
            pl.pallas_call(
                functools.partial(deal_kernel, team, depth, plan),
                out_shape=shapes,
                in_specs=[pl.BlockSpec(memory_space=pltpu.SMEM)]
                + [pl.BlockSpec(memory_space=pltpu.HBM)] * len(sources),
                out_specs=[pl.BlockSpec(memory_space=pltpu.VMEM)] * len(shapes),
                scratch_shapes=[pltpu.VMEM(source.shape, source.dtype) for source in sources]
                + [pltpu.SemaphoreType.DMA((CHUNKS * len(sources),))],
                compiler_params=pltpu.CompilerParams(vmem_limit_bytes=VMEM_LIMIT),
            )(info, *sources)
        )
    else:
        for source, steps in zip(sources, plan):
            rows, width = source.shape
            cut = source.reshape(rows, width // (team * depth), team, depth)
            for step in range(steps):
                share = lax.dynamic_index_in_dim(cut, info[0] ^ step, 2, keepdims=False)
                pieces.append(share.reshape(rows, -1))
    return [[pieces.pop(0) for _ in range(steps)] for steps in plan]


def spread(values, me, lanes, wide, above):
    per = values[0].shape[0] // BLOCK
    for step in range(TEAM):
        for b in range(per):
            rows = values[step][b * BLOCK : (b + 1) * BLOCK, lanes].astype(f32)
            wide[(me ^ step) * per + b, above:, :] = rows


def tile_lanes(info_ref, slot):
    return pl.ds(pl.multiple_of(info_ref[3 + slot] * LANES, LANES), LANES)


def state_kernel(info_ref, *refs):
    values = refs[:TEAM]
    rate_ref, starts_ref, end_ref, wide = refs[TEAM:]
    order = rate_ref.shape[0]
    me = info_ref[0]

    @pl.loop(0, starts_ref.shape[0])
    def _(slot):
        lanes = tile_lanes(info_ref, slot)
        spread(values, me, lanes, wide, 0)
        rate = rate_ref[:, lanes]
        lam, lam8 = jnp.exp(-rate), jnp.exp(-8.0 * rate)

        def block(b, state):
            starts_ref[slot, b] = state
            for at in range(0, BLOCK, 8):
                inflow = jnp.broadcast_to(wide[b, at : at + 1, :], (order, LANES))
                for t in range(1, 8):
                    inflow = lam * inflow + wide[b, at + t : at + t + 1, :]
                state = lam8 * state + inflow
            return state

        zero = jnp.zeros((order, LANES), f32)
        end_ref[:, lanes] = lax.fori_loop(0, wide.shape[0], block, zero, unroll=4)


def taps_kernel(base, info_ref, *refs):
    values = refs[:TEAM]
    rate_ref, coef_ref, skip_ref, y_ref, wide, taps = refs[TEAM:]
    me = info_ref[0]
    wide[:, :BLOCK, :] = jnp.zeros((wide.shape[0], BLOCK, LANES), f32)

    @pl.loop(0, y_ref.shape[0])
    def _(slot):
        lanes = tile_lanes(info_ref, base + slot)
        spread(values, me, lanes, wide, BLOCK)
        skip = skip_ref[:, lanes]
        lam = jnp.exp(-rate_ref[:, lanes])
        power = coef_ref[:, lanes]
        for t in range(BLOCK):
            tap = jnp.sum(power, axis=0, keepdims=True).astype(bf16).astype(f32)
            taps[t] = jnp.broadcast_to(tap, (8, LANES))
            power = power * lam

        @pl.loop(0, wide.shape[0])
        def _(b):
            y = [skip * wide[b, BLOCK + 8 * i : BLOCK + 8 * i + 8, :] for i in range(BLOCK // 8)]
            for t in range(BLOCK):
                tap = taps[t]
                for i in range(t // 8, BLOCK // 8):
                    at = BLOCK + 8 * i - t
                    y[i] = y[i] + tap * wide[b, at : at + 8, :]
            for i in range(BLOCK // 8):
                y_ref[slot, pl.ds(pl.multiple_of(b * BLOCK + 8 * i, 8), 8), :] = y[i]


def gate_kernel(base, reaches, info_ref, *refs):
    gaps = len(reaches)
    gates = refs[:TEAM]
    y_ref, starts_ref, rate_ref, coef_ref, near_ref = refs[TEAM : TEAM + 5]
    far = refs[TEAM + 5 : TEAM + 5 + gaps]
    out_ref, reach, decay8, start = refs[TEAM + 5 + gaps :]
    me, high = info_ref[0], info_ref[1]
    order = rate_ref.shape[0]
    rows = gates[0].shape[0]
    per = rows // BLOCK
    span = float(TEAM * rows)
    ahead = lax.broadcasted_iota(jnp.int32, (8, LANES), 0).astype(f32) + 1.0

    @pl.loop(0, y_ref.shape[0])
    def _(slot):
        lanes = tile_lanes(info_ref, base + slot)
        rate, coef = rate_ref[:, lanes], coef_ref[:, lanes]
        for k in range(order):
            reach[k] = coef[k : k + 1] * jnp.exp(-ahead * rate[k : k + 1])
            decay8[k] = jnp.exp(jnp.broadcast_to(-8.0 * rate[k : k + 1], (8, LANES)))
        state = jnp.zeros((order, LANES), f32)
        for gap, ref in zip(reaches, far):
            state = state + jnp.exp(-2.0 * span * gap * rate) * ref[:, lanes]
        after = jnp.exp(-span * rate) * state + near_ref[:, lanes]
        state = jnp.where(high == 1, after, state)
        over = jnp.exp(-float(BLOCK) * rate)
        for step in range(TEAM):
            place = me ^ step
            goes = place ^ (me & 2)
            entering = state * jnp.exp(-(rows * place).astype(f32) * rate)
            for b in range(per):
                start[b] = starts_ref[base + slot, place * per + b] + entering
                entering = entering * over
            for b in range(per):
                y = []
                for i in range(BLOCK // 8):
                    here = pl.multiple_of(place * rows + b * BLOCK + 8 * i, 8)
                    y.append(y_ref[slot, pl.ds(here, 8), :])
                for k in range(order):
                    term = reach[k] * start[b, k : k + 1, :]
                    decay = decay8[k]
                    for i in range(BLOCK // 8):
                        y[i] = y[i] + term
                        if i + 1 < BLOCK // 8:
                            term = term * decay
                for i in range(0, BLOCK // 8, 2):
                    at = b * BLOCK + 8 * i
                    conv = jnp.concatenate(y[i : i + 2], axis=0)
                    gated = gates[step][at : at + 16, lanes].astype(f32) * conv
                    to = pl.ds(pl.multiple_of(goes * rows + at, 16), 16)
                    out_ref[slot, to, :] = gated.astype(bf16)


def project_kernel(pieces, in_slots, at, info_ref, *refs):
    gated, weights = refs[:pieces], refs[pieces:-3]
    kept_ref, sent_ref, total = refs[-3:]
    core = info_ref[2]
    per = gated[0].shape[0]
    rows, wide = kept_ref.shape[0] // 2, kept_ref.shape[1]
    step = min(wide, 256)
    slots = len(weights)
    for slot in range(0, slots, 2):
        if in_slots:
            left = [gated[n // per][n % per] for n in (slot, slot + 1)]
        else:
            left = [gated[0][info_ref[3 + n]] for n in (slot, slot + 1)]
        left = jnp.concatenate(left, axis=1)
        for col in range(0, wide, step):
            right = []
            for ref in weights[slot : slot + 2]:
                first = col if ref.shape[1] == wide else at + col
                right.append(ref[:, first : first + step])
            term = jnp.dot(left, jnp.concatenate(right, axis=0), preferred_element_type=f32)
            cols = slice(col, col + step)
            total[:, cols] = term if slot == 0 else total[:, cols] + term
    for across in range(2):
        here = slice(across * rows, (across + 1) * rows)
        for which, out in enumerate((kept_ref, sent_ref)):
            start = (2 * across + (core ^ which)) * rows
            out[here, :] = total[pl.ds(pl.multiple_of(start, rows), rows), :].astype(out.dtype)


def join_kernel(info_ref, kept_ref, got_ref, mine_ref, away_ref):
    rows = mine_ref.shape[0]
    mine_ref[...] = kept_ref[:rows, :] + got_ref[:rows, :].astype(f32)
    away_ref[...] = (kept_ref[rows:, :] + got_ref[rows:, :].astype(f32)).astype(bf16)


def finish_kernel(info_ref, *refs):
    out_ref = refs[-1]
    at = 0
    for mine, far in zip(refs[:-1:2], refs[1:-1:2]):
        wide = mine.shape[1]
        out_ref[:, at : at + wide] = (mine[...] + far[...].astype(f32)).astype(bf16)
        at += wide


def on_device(q_gate, values_in, decay_rate, residue, skip_gain, out_weight):
    rows, width = q_gate.shape
    depth, features = out_weight.shape
    order = decay_rate.shape[1]
    count = lax.axis_size("seq")
    heights = count // (2 * TEAM)
    mine = lax.axis_index("seq")
    me, core = mine % TEAM, mine % 2
    y, z = (mine // TEAM) % 2, mine // (2 * TEAM)
    share = width // TEAM

    def swap(value, bit):
        return lax.ppermute(value, "seq", [(i, i ^ bit) for i in range(count)])

    def up(value, gap, wrap):
        hop = gap * 2 * TEAM
        pairs = [(i, (i + hop) % count) for i in range(count) if wrap or i + hop < count]
        return lax.ppermute(value, "seq", pairs)

    in_slots = depth % LANES == 0
    groups = []
    for gap in range(heights):
        at = (z - gap) % heights
        groups += [at * 2 + y, at * 2 + (1 - y)]
    tiles = share // LANES
    order_of = groups if in_slots else list(range(tiles))
    info = jnp.stack([jnp.int32(n) for n in [me, y, core] + order_of])
    group_info = info if in_slots else jnp.stack([jnp.int32(n) for n in [me, y, core] + groups])

    def share_out(shares):
        return [shares[0]] + [swap(shares[step], step) for step in range(1, TEAM)]

    def share_out(shares):
        return [shares[0]] + [swap(shares[step], step) for step in range(1, TEAM)]

    def next_round(block):
        return up(block, 1, True), swap(block, TEAM)

    last = heights - 1
    weights, weights_away = [out_weight], []
    if last > 0:
        above, away = next_round(out_weight)
        weights.append(above)
        weights_away.append(away)

    (values,) = deal(info, TEAM, depth, [values_in], [TEAM])
    values = share_out(values)
    gates, rates, residues, skip = deal(
        info, TEAM, depth, [q_gate, decay_rate.T, residue.T, skip_gain[None]], [TEAM, 1, 1, 1]
    )
    rates, residues, skip = rates[0], residues[0], skip[0]
    coef = residues * jnp.sqrt(-jnp.expm1(-2.0 * rates))
    gates = share_out(gates[:2] + [tied(gate, values[3]) for gate in gates[2:]])

    blocks = TEAM * rows // BLOCK
    starts, end = call(
        state_kernel,
        [
            jax.ShapeDtypeStruct((tiles, blocks, order, LANES), f32),
            jax.ShapeDtypeStruct((order, share), f32),
        ],
        [pltpu.VMEM((blocks, BLOCK, LANES), f32)],
        after=[weights[-1], weights_away[-1]],
        micros=0.5,
    )(info, *values, rates)

    pieces = 4
    some = tiles // pieces
    if len(weights) < heights:
        above, away = next_round(tied(weights[-1], weights_away[-1]))
        weights.append(above)
        weights_away.append(away)
    local = []
    for part in range(pieces):
        local.append(
            call(
                functools.partial(taps_kernel, part * some),
                jax.ShapeDtypeStruct((some, TEAM * rows, LANES), f32),
                [pltpu.VMEM((blocks, 2 * BLOCK, LANES), f32), pltpu.VMEM((BLOCK, 8, LANES), f32)],
                after=[end] if part == 0 else [local[-1]] + ([weights[-1], weights_away[-1]] if part > 1 else []),
                micros=0.3,
            )(info, *values, rates, coef, skip)
        )

    near = swap(end, TEAM)
    end = tied(end, local[0], local[1], *gates)
    first, second = jnp.where(y == 0, end, near), jnp.where(y == 0, near, end)
    span = float(TEAM * rows)
    held = jnp.exp(-span * rates) * first + second
    while len(weights) < heights:
        above, away = next_round(tied(weights[-1], weights_away[-1], held))
        weights.append(above)
        weights_away.append(away)
    far, gap = [], 1
    while gap < heights:
        lags = [n * gap for n in (1, 2, 3) if n * gap < heights]
        far += [(lag - 1, up(held, lag, False)) for lag in lags]
        for lag, (_, state) in zip(lags, far[-len(lags) :]):
            held = held + jnp.exp(-2.0 * span * lag * rates) * state
        gap *= 4
    wide = features // LAST_PARTS
    block = tied(weights[last], weights_away[-1])
    finals = [swap(block[:, part * wide : (part + 1) * wide], TEAM) for part in range(LAST_PARTS)]

    tables = [pltpu.VMEM((order, 8, LANES), f32)] * 2
    gated = [
        call(
            functools.partial(gate_kernel, part * some, [lag for lag, _ in far]),
            jax.ShapeDtypeStruct((some, TEAM * rows, LANES), bf16),
            tables + [pltpu.VMEM((rows // BLOCK, order, LANES), f32)],
            after=[local[-1]] if part < 2 else [weights[last], weights_away[-1]],
            micros=0.5,
        )(info, *gates, local[part], starts, rates, coef, near, *[state for _, state in far])
        for part in range(pieces)
    ]
    if not in_slots:
        gated = jnp.concatenate(gated, axis=0).transpose(1, 0, 2)
        gated = gated.reshape(TEAM * rows, width // (TEAM * depth), depth).transpose(1, 0, 2)
        gated = [gated]

    finished = []
    for part, final in enumerate(finals):
        slots = [ref for pair in zip(weights, weights_away + [final]) for ref in pair]
        kept, sent = call(
            functools.partial(project_kernel, len(gated), in_slots, part * wide),
            [jax.ShapeDtypeStruct((2 * rows, wide), dtype) for dtype in (f32, bf16)],
            [pltpu.VMEM((TEAM * rows, wide), f32)],
            micros=0.5,
        )(group_info, *gated, *slots)
        mine_sum, away_sum = call(
            join_kernel,
            [jax.ShapeDtypeStruct((rows, wide), f32), jax.ShapeDtypeStruct((rows, wide), bf16)],
        )(info, kept, swap(sent, 1))
        finished += [mine_sum, swap(away_sum, 2)]
    return call(finish_kernel, jax.ShapeDtypeStruct((rows, features), bf16))(info, *finished)


def solution(mesh):
    in_specs = (
        P(("groups", "seq"), None),
        P(("groups", "seq"), None),
        P(),
        P(),
        P(),
        P("seq", None),
    )
    out_specs = P(("groups", "seq"), None)
    return jax.shard_map(
        on_device, mesh=mesh, in_specs=in_specs, out_specs=out_specs, check_vma=False
    )
```

time: 99.6 us -> 86.6 us (0.87)
  waiting for transfers between devices: 34.1 us -> 26.2 us
  starting transfers between devices: 29.7 us -> 26.6 us
  Pallas kernels: 30.3 us -> 28.1 us
    ppermute x23 -> x16, waiting for transfers between devices: 26.2 us -> 20.1 us  [swap(): return lax.ppermute(value, 'seq', [(i, i ^ bit) for i in range(count)])]
    ppermute x23 -> x16, starting transfers between devices: 18.5 us -> 13.5 us  [swap(): return lax.ppermute(value, 'seq', [(i, i ^ bit) for i in range(count)])]
    pallas_call x14, Pallas kernels: 27.1 us -> 24.6 us  [run(): pl.pallas_call(kernel, out_shape=out_shape, in_specs=[pl.BlockSpec(memory...]
    ppermute x5 -> x6, starting transfers between devices: 11.1 us -> 13.1 us  [up(): return lax.ppermute(value, 'seq', pairs)]
    ppermute x5 -> x6, waiting for transfers between devices: 7.94 us -> 6.17 us  [up(): return lax.ppermute(value, 'seq', pairs)]
    unnamed x26 -> x16, local copies, waits for them, and re-layouts: 2.69 us -> 3.94 us
  transfers between devices with their start and end apart: 28 -> 22, of which waited for: 12 -> 8; matrix products, arithmetic and copies ran while one was open for 2% -> 0% of each run, Pallas kernels for 26% -> 31%
where the time goes in v4:
time: 86.6 us; the launch traced here: 85.4 us
  Pallas kernels  28.1 us (32%)
  starting transfers between devices  26.6 us (31%)
  waiting for transfers between devices  26.2 us (30%)
  local copies, waits for them, and re-layouts  4.06 us (5%)
    pallas_call x14, Pallas kernels, run(): pl.pallas_call(kernel, out_shape=out_shape, in_specs=[pl.BlockSpec(memory...  24.6 us
    ppermute x16, waiting for transfers between devices, swap(): return lax.ppermute(value, 'seq', [(i, i ^ bit) for i in range(count)])  20.1 us
    ppermute x16, starting transfers between devices, swap(): return lax.ppermute(value, 'seq', [(i, i ^ bit) for i in range(count)])  13.5 us
    ppermute x6, starting transfers between devices, up(): return lax.ppermute(value, 'seq', pairs)  13.1 us
    ppermute x6, waiting for transfers between devices, up(): return lax.ppermute(value, 'seq', pairs)  6.17 us
    unnamed x16, local copies, waits for them, and re-layouts  3.94 us
    pallas_call x2, Pallas kernels, deal(): pl.pallas_call(functools.partial(deal_kernel, team, depth, plan), out_sha...  3.57 us
  transfers between devices with their start and end apart: 22, of which 8 were waited for; matrix products, arithmetic and copies ran while one was open for 0% of the time, Pallas kernels for 31%

profile of v4, /device:TPU:0, one launch (start us, length us, event | category | flops | bytes accessed | tf_op | source)
XLA Modules:
  0.0 85.4 jit_solution(18079659339020608785)
XLA Ops:
  0.0 3.0 %collective-permute-start = (bf16[128,2048]{1,0:T(8,128)(2,1)}, bf16[128,2048]{1,0:T(8,128)(2,1)}, u32[]{:S(2)}, u32[]{:S(2)}) collective-permute-start(bf16[128,2048]{1,0:T(8,128)(2,1)} %refs_4_.3), channel_id=1, source_target_pairs={{0,8},{1,9},{2,10},{3,11},{4,12},{5,13},{6,14},{7,15},{8,16},{9,17... | collective-permute-start | bytes 1572872 | tf_op jit(solution)/shard_map/ppermute | solution.py:276
  3.0 1.5 %collective-permute-start.1 = (bf16[128,2048]{1,0:T(8,128)(2,1)}, bf16[128,2048]{1,0:T(8,128)(2,1)S(1)}, u32[]{:S(2)}, u32[]{:S(2)}) collective-permute-start(bf16[128,2048]{1,0:T(8,128)(2,1)} %refs_4_.3), channel_id=1, source_target_pairs={{0,4},{1,5},{2,6},{3,7},{4,0},{5,1},{6,2},{7,3},{8,12},{9,13},{10,... | collective-permute-start | bytes 1572872 | tf_op jit(solution)/shard_map/ppermute | solution.py:271
  4.5 0.1 stack.47.info_ref
  4.6 1.2 %copy-done.3 = bf16[128,4096]{1,0:T(8,128)(2,1)S(1)} copy-done((bf16[128,4096]{1,0:T(8,128)(2,1)S(1)}, bf16[128,4096]{1,0:T(8,128)(2,1)}, u32[]{:S(2)}) %copy-start.3) | copy-done | bytes 1048600
  5.9 1.1 %shard_map.64 = (bf16[128,1024]{1,0:T(8,128)(2,1)S(1)}, bf16[128,1024]{1,0:T(8,128)(2,1)S(1)}, bf16[128,1024]{1,0:T(8,128)(2,1)S(1)}, bf16[128,1024]{1,0:T(8,128)(2,1)S(1)}) custom-call(s32[11]{0:T(128)S(1)} %stack.47.info_ref, bf16[128,4096]{1,0:T(8,128)(2,1)S(1)} %copy-done.3), custom_call_target="tpu_custom_call" | custom-call | tf_op jit(solution)/shard_map/pallas_call | solution.py:73
  6.9 0.4 collective-permute-start.4
  7.4 1.2 %collective-permute-start.2 = (bf16[128,1024]{1,0:T(8,128)(2,1)S(1)}, bf16[128,1024]{1,0:T(8,128)(2,1)S(1)}, u32[]{:S(2)}, u32[]{:S(2)}) collective-permute-start(bf16[128,1024]{1,0:T(8,128)(2,1)S(1)} %get-tuple-element.41), channel_id=1, source_target_pairs={{0,1},{1,0},{2,3},{3,2},{4,5},{5,4},{6,7},{7,6},{8,9},{9,8},{10,11... | collective-permute-start | bytes 786440 | tf_op jit(solution)/shard_map/ppermute | solution.py:271
  8.6 0.5 collective-permute-start.3
  9.2 0.9 %copy-done.5 = f32[4096,16]{0,1:T(8,128)S(1)} copy-done((f32[4096,16]{0,1:T(8,128)S(1)}, f32[4096,16]{0,1:T(8,128)}, u32[]{:S(2)}) %copy-start.5) | copy-done | bytes 262168
  10.1 0.9 %copy-done.6 = f32[4096,16]{0,1:T(8,128)S(1)} copy-done((f32[4096,16]{0,1:T(8,128)S(1)}, f32[4096,16]{0,1:T(8,128)}, u32[]{:S(2)}) %copy-start.6) | copy-done | bytes 262168
  11.1 2.5 %shard_map.65 = (bf16[128,1024]{1,0:T(8,128)(2,1)S(1)}, bf16[128,1024]{1,0:T(8,128)(2,1)S(1)}, bf16[128,1024]{1,0:T(8,128)(2,1)}, bf16[128,1024]{1,0:T(8,128)(2,...) custom-call(s32[11]{0:T(128)S(1)} %stack.47.info_ref, bf16[128,4096]{1,0:T(8,128)(2,1)S(1)} %copy-done.4, ...), custom_call_target="tpu_custom_call" | custom-call | tf_op jit(solution)/shard_map/pallas_call | solution.py:73
  13.6 2.0 %collective-permute-done.4.refs_3_ = bf16[128,1024]{1,0:T(8,128)(2,1)S(1)} collective-permute-done((bf16[128,1024]{1,0:T(8,128)(2,1)S(1)}, bf16[128,1024]{1,0:T(8,128)(2,1)S(1)}, u32[]{:S(2)}, u32[]{:S(2)}) %collective-permute-start.4) | collective-permute-done | bytes 262176 | tf_op jit(solution)/shard_map/ppermute | solution.py:271
  15.6 0.3 collective-permute-start.7
  15.9 1.4 %collective-permute-done.refs_6_ = bf16[128,2048]{1,0:T(8,128)(2,1)} collective-permute-done((bf16[128,2048]{1,0:T(8,128)(2,1)}, bf16[128,2048]{1,0:T(8,128)(2,1)}, u32[]{:S(2)}, u32[]{:S(2)}) %collective-permute-start) | collective-permute-done | bytes 524320 | tf_op jit(solution)/shard_map/ppermute | solution.py:276
  17.3 1.5 %collective-permute-start.8 = (bf16[128,1024]{1,0:T(8,128)(2,1)}, bf16[128,1024]{1,0:T(8,128)(2,1)S(1)}, u32[]{:S(2)}, u32[]{:S(2)}) collective-permute-start(bf16[128,1024]{1,0:T(8,128)(2,1)} %get-tuple-element.57), channel_id=1, source_target_pairs={{0,2},{1,3},{2,0},{3,1},{4,6},{5,7},{6,4},{7,5},{8,10},{9,11},{10,... | collective-permute-start | bytes 786440 | tf_op jit(solution)/shard_map/ppermute | solution.py:271
  18.8 0.0 collective-permute-done.1.refs_5_
  18.8 0.8 copy-done.1
  19.6 0.0 collective-permute-start.9
  19.6 0.0 collective-permute-done.2.refs_1_
  19.6 0.2 collective-permute-start.5
  19.8 1.5 %collective-permute-done.3.refs_2_ = bf16[128,1024]{1,0:T(8,128)(2,1)S(1)} collective-permute-done((bf16[128,1024]{1,0:T(8,128)(2,1)S(1)}, bf16[128,1024]{1,0:T(8,128)(2,1)S(1)}, u32[]{:S(2)}, u32[]{:S(2)}) %collective-permute-start.3) | collective-permute-done | bytes 262176 | tf_op jit(solution)/shard_map/ppermute | solution.py:271
  21.3 0.5 collective-permute-start.6
  21.8 3.5 %shard_map.66 = (f32[8,16,16,128]{3,2,1,0:T(8,128)S(1)}, f32[16,1024]{1,0:T(8,128)S(1)}) custom-call(s32[11]{0:T(128)S(1)} %stack.47.info_ref, bf16[128,1024]{1,0:T(8,128)(2,1)S(1)} %get-tuple-element.40.refs_0_, bf16[128,1024]{1,0:T(8,128)(2,1)S(1)} %collective-permute-done.2.refs_1_, bf16[128,1024]{1,0:T(8,128)(2,1)S(1)} %collective-permute-done.3.refs_2_, ...), custom_call_target="tpu_custom_call" | custom-call | flops 550000000 | bytes 1800000 | tf_op jit(solution)/shard_map/pallas_call | solution.py:27
  25.3 0.0 collective-permute-done.7.refs_1_
  25.3 1.6 %collective-permute-start.10 = (f32[16,1024]{1,0:T(8,128)S(1)}, f32[16,1024]{1,0:T(8,128)S(1)}, u32[]{:S(2)}, u32[]{:S(2)}) collective-permute-start(f32[16,1024]{1,0:T(8,128)S(1)} %get-tuple-element.61), channel_id=1, source_target_pairs={{0,4},{1,5},{2,6},{3,7},{4,0},{5,1},{6,2},{7,3},{8,12},{9,13},{10,... | collective-permute-start | bytes 196616 | tf_op jit(solution)/shard_map/ppermute | solution.py:271
  26.9 2.0 %shard_map.67.refs_4_ = f32[2,512,128]{2,1,0:T(8,128)S(1)} custom-call(s32[11]{0:T(128)S(1)} %stack.47.info_ref, bf16[128,1024]{1,0:T(8,128)(2,1)S(1)} %get-tuple-element.40.refs_0_, bf16[128,1024]{1,0:T(8,128)(2,1)S(1)} %collective-permute-done.2.refs_1_, bf16[128,1024]{1,0:T(8,128)(2,1)S(1)} %collective-permute-done.3.refs_2_, ...), custom_call_target="tpu_custom_call" | custom-call | flops 330000000 | bytes 1080000 | tf_op jit(solution)/shard_map/pallas_call | solution.py:27
  28.9 2.0 %shard_map.68.refs_4_ = f32[2,512,128]{2,1,0:T(8,128)S(1)} custom-call(s32[11]{0:T(128)S(1)} %stack.47.info_ref, bf16[128,1024]{1,0:T(8,128)(2,1)S(1)} %get-tuple-element.40.refs_0_, bf16[128,1024]{1,0:T(8,128)(2,1)S(1)} %collective-permute-done.2.refs_1_, bf16[128,1024]{1,0:T(8,128)(2,1)S(1)} %collective-permute-done.3.refs_2_, ...), custom_call_target="tpu_custom_call" | custom-call | flops 330000000 | bytes 1080000 | tf_op jit(solution)/shard_map/pallas_call | solution.py:27
  30.9 0.0 collective-permute-done.8.refs_2_
  30.9 1.5 %collective-permute-done.9.refs_3_ = bf16[128,1024]{1,0:T(8,128)(2,1)S(1)} collective-permute-done((bf16[128,1024]{1,0:T(8,128)(2,1)}, bf16[128,1024]{1,0:T(8,128)(2,1)S(1)}, u32[]{:S(2)}, u32[]{:S(2)}) %collective-permute-start.9) | collective-permute-done | bytes 262176 | tf_op jit(solution)/shard_map/ppermute | solution.py:271
  32.4 4.3 %collective-permute-done.10.refs_8_ = f32[16,1024]{1,0:T(8,128)S(1)} collective-permute-done((f32[16,1024]{1,0:T(8,128)S(1)}, f32[16,1024]{1,0:T(8,128)S(1)}, u32[]{:S(2)}, u32[]{:S(2)}) %collective-permute-start.10) | collective-permute-done | bytes 65568 | tf_op jit(solution)/shard_map/ppermute | solution.py:271
  36.8 0.0 collective-permute-done.5.refs_8_
  36.8 0.0 collective-permute-done.6.refs_7_
  36.8 1.6 %collective-permute-start.14 = (bf16[128,2048]{1,0:T(8,128)(2,1)}, bf16[128,2048]{1,0:T(8,128)(2,1)S(1)}, u32[]{:S(2)}, u32[]{:S(2)}) collective-permute-start(bf16[128,2048]{1,0:T(8,128)(2,1)} %collective-permute-done.5.refs_8_), channel_id=1, source_target_pairs={{0,8},{1,9},{2,10},{3,11},{4,12},{5,13},{6,14},{7,15},{8,16},{9,17... | collective-permute-start | bytes 1572872 | tf_op jit(solution)/shard_map/ppermute | solution.py:276
  38.4 0.5 collective-permute-start.15
  39.0 3.4 %collective-permute-start.11 = (f32[16,1024]{1,0:T(8,128)S(1)}, f32[16,1024]{1,0:T(8,128)S(1)}, u32[]{:S(2)}, u32[]{:S(2)}) collective-permute-start(f32[16,1024]{1,0:T(8,128)S(1)} %select_add_fusion), channel_id=1, source_target_pairs={{0,8},{1,9},{2,10},{3,11},{4,12},{5,13},{6,14},{7,15},{8,16},{9,17... | collective-permute-start | bytes 196616 | tf_op jit(solution)/shard_map/ppermute | solution.py:276
  42.4 3.5 %collective-permute-start.12 = (f32[16,1024]{1,0:T(8,128)S(1)}, f32[16,1024]{1,0:T(8,128)S(1)}, u32[]{:S(2)}, u32[]{:S(2)}) collective-permute-start(f32[16,1024]{1,0:T(8,128)S(1)} %select_add_fusion), channel_id=1, source_target_pairs={{0,16},{1,17},{2,18},{3,19},{4,20},{5,21},{6,22},{7,23},{8,24},{9,... | collective-permute-start | bytes 196616 | tf_op jit(solution)/shard_map/ppermute | solution.py:276
  45.9 1.3 %collective-permute-start.13 = (f32[16,1024]{1,0:T(8,128)S(1)}, f32[16,1024]{1,0:T(8,128)S(1)}, u32[]{:S(2)}, u32[]{:S(2)}) collective-permute-start(f32[16,1024]{1,0:T(8,128)S(1)} %select_add_fusion), channel_id=1, source_target_pairs={{0,24},{1,25},{2,26},{3,27},{4,28},{5,29},{6,30},{7,31}} | collective-permute-start | bytes 196616 | tf_op jit(solution)/shard_map/ppermute | solution.py:276
  47.2 4.8 %collective-permute-done.14.refs_10_ = bf16[128,2048]{1,0:T(8,128)(2,1)S(1)} collective-permute-done((bf16[128,2048]{1,0:T(8,128)(2,1)}, bf16[128,2048]{1,0:T(8,128)(2,1)S(1)}, u32[]{:S(2)}, u32[]{:S(2)}) %collective-permute-start.14) | collective-permute-done | bytes 524320 | tf_op jit(solution)/shard_map/ppermute | solution.py:276
  52.0 0.0 collective-permute-done.15.refs_9_
  52.0 1.4 %collective-permute-start.16 = (bf16[128,1024]{1,0:T(8,128)(2,1)S(1)}, bf16[128,1024]{1,0:T(8,128)(2,1)S(1)}, u32[]{:S(2)}, u32[]{:S(2)}) collective-permute-start(bf16[128,1024]{1,0:T(8,128)(2,1)S(1)} %get-tuple-element.74), channel_id=1, source_target_pairs={{0,4},{1,5},{2,6},{3,7},{4,0},{5,1},{6,2},{7,3},{8,12},{9,13},{10,... | collective-permute-start | bytes 786440 | tf_op jit(solution)/shard_map/ppermute | solution.py:271
  53.4 2.0 %shard_map.69.refs_4_ = f32[2,512,128]{2,1,0:T(8,128)S(1)} custom-call(s32[11]{0:T(128)S(1)} %stack.47.info_ref, bf16[128,1024]{1,0:T(8,128)(2,1)S(1)} %get-tuple-element.40.refs_0_, bf16[128,1024]{1,0:T(8,128)(2,1)S(1)} %collective-permute-done.2.refs_1_, bf16[128,1024]{1,0:T(8,128)(2,1)S(1)} %collective-permute-done.3.refs_2_, ...), custom_call_target="tpu_custom_call" | custom-call | flops 330000000 | bytes 1080000 | tf_op jit(solution)/shard_map/pallas_call | solution.py:27
  55.4 0.7 collective-permute-start.19
  56.1 2.0 %shard_map.70.refs_4_ = f32[2,512,128]{2,1,0:T(8,128)S(1)} custom-call(s32[11]{0:T(128)S(1)} %stack.47.info_ref, bf16[128,1024]{1,0:T(8,128)(2,1)S(1)} %get-tuple-element.40.refs_0_, bf16[128,1024]{1,0:T(8,128)(2,1)S(1)} %collective-permute-done.2.refs_1_, bf16[128,1024]{1,0:T(8,128)(2,1)S(1)} %collective-permute-done.3.refs_2_, ...), custom_call_target="tpu_custom_call" | custom-call | flops 330000000 | bytes 1080000 | tf_op jit(solution)/shard_map/pallas_call | solution.py:27
  58.1 0.0 collective-permute-done.11.refs_9_
  58.1 0.0 collective-permute-done.12.refs_10_
  58.1 0.0 collective-permute-done.13.refs_11_
  58.1 1.3 %shard_map.71.refs_0_ = bf16[2,512,128]{2,1,0:T(8,128)(2,1)S(1)} custom-call(s32[11]{0:T(128)S(1)} %stack.47.info_ref, bf16[128,1024]{1,0:T(8,128)(2,1)S(1)} %get-tuple-element.54.refs_0_, bf16[128,1024]{1,0:T(8,128)(2,1)S(1)} %collective-permute-done.7.refs_1_, bf16[128,1024]{1,0:T(8,128)(2,1)S(1)} %collective-permute-done.8.refs_2_, ...), custom_call_target="tpu_custom_call" | custom-call | flops 550000000 | bytes 1800000 | tf_op jit(solution)/shard_map/pallas_call | solution.py:27
  59.4 1.3 %shard_map.72.refs_1_ = bf16[2,512,128]{2,1,0:T(8,128)(2,1)S(1)} custom-call(s32[11]{0:T(128)S(1)} %stack.47.info_ref, bf16[128,1024]{1,0:T(8,128)(2,1)S(1)} %get-tuple-element.54.refs_0_, bf16[128,1024]{1,0:T(8,128)(2,1)S(1)} %collective-permute-done.7.refs_1_, bf16[128,1024]{1,0:T(8,128)(2,1)S(1)} %collective-permute-done.8.refs_2_, ...), custom_call_target="tpu_custom_call" | custom-call | flops 550000000 | bytes 1800000 | tf_op jit(solution)/shard_map/pallas_call | solution.py:27
  60.7 1.3 %shard_map.73.refs_2_ = bf16[2,512,128]{2,1,0:T(8,128)(2,1)S(1)} custom-call(s32[11]{0:T(128)S(1)} %stack.47.info_ref, bf16[128,1024]{1,0:T(8,128)(2,1)S(1)} %get-tuple-element.54.refs_0_, bf16[128,1024]{1,0:T(8,128)(2,1)S(1)} %collective-permute-done.7.refs_1_, bf16[128,1024]{1,0:T(8,128)(2,1)S(1)} %collective-permute-done.8.refs_2_, ...), custom_call_target="tpu_custom_call" | custom-call | flops 550000000 | bytes 1800000 | tf_op jit(solution)/shard_map/pallas_call | solution.py:27
  61.9 0.0 copy-start
  61.9 0.0 copy-start.2
  62.0 1.3 %shard_map.74.refs_3_ = bf16[2,512,128]{2,1,0:T(8,128)(2,1)S(1)} custom-call(s32[11]{0:T(128)S(1)} %stack.47.info_ref, bf16[128,1024]{1,0:T(8,128)(2,1)S(1)} %get-tuple-element.54.refs_0_, bf16[128,1024]{1,0:T(8,128)(2,1)S(1)} %collective-permute-done.7.refs_1_, bf16[128,1024]{1,0:T(8,128)(2,1)S(1)} %collective-permute-done.8.refs_2_, ...), custom_call_target="tpu_custom_call" | custom-call | flops 550000000 | bytes 1800000 | tf_op jit(solution)/shard_map/pallas_call | solution.py:27
  63.2 0.0 collective-permute-done.16.refs_11_
  63.3 2.7 %shard_map.75 = (f32[256,1024]{1,0:T(8,128)S(1)}, bf16[256,1024]{1,0:T(8,128)(2,1)S(1)}) custom-call(s32[11]{0:T(128)S(1)} %stack.47.info_ref, bf16[2,512,128]{2,1,0:T(8,128)(2,1)S(1)} %shard_map.71.refs_0_, bf16[2,512,128]{2,1,0:T(8,128)(2,1)S(1)} %shard_map.72.refs_1_, bf16[2,512,128]{2,1,0:T(8,128)(2,1)S(1)} %shard_map.73.refs_2_, ...), custom_call_target="tpu_custom_call" | custom-call | flops 550000000 | bytes 1800000 | tf_op jit(solution)/shard_map/pallas_call | solution.py:27
  66.0 0.1 collective-permute-start.17
  66.1 2.7 %shard_map.77 = (f32[256,1024]{1,0:T(8,128)S(1)}, bf16[256,1024]{1,0:T(8,128)(2,1)S(1)}) custom-call(s32[11]{0:T(128)S(1)} %stack.47.info_ref, bf16[2,512,128]{2,1,0:T(8,128)(2,1)S(1)} %shard_map.71.refs_0_, bf16[2,512,128]{2,1,0:T(8,128)(2,1)S(1)} %shard_map.72.refs_1_, bf16[2,512,128]{2,1,0:T(8,128)(2,1)S(1)} %shard_map.73.refs_2_, ...), custom_call_target="tpu_custom_call" | custom-call | flops 550000000 | bytes 1800000 | tf_op jit(solution)/shard_map/pallas_call | solution.py:27
  68.8 0.5 collective-permute-start.20
  69.4 0.6 shard_map.76
  70.0 1.6 %collective-permute-start.18 = (bf16[128,1024]{1,0:T(8,128)(2,1)S(1)}, bf16[128,1024]{1,0:T(8,128)(2,1)S(1)}, u32[]{:S(2)}, u32[]{:S(2)}) collective-permute-start(bf16[128,1024]{1,0:T(8,128)(2,1)S(1)} %get-tuple-element.68), channel_id=1, source_target_pairs={{0,2},{1,3},{2,0},{3,1},{4,6},{5,7},{6,4},{7,5},{8,10},{9,11},{10,... | collective-permute-start | bytes 786440 | tf_op jit(solution)/shard_map/ppermute | solution.py:271
  71.7 0.6 shard_map.78
  72.3 0.9 %collective-permute-start.21 = (bf16[128,1024]{1,0:T(8,128)(2,1)S(1)}, bf16[128,1024]{1,0:T(8,128)(2,1)S(1)}, u32[]{:S(2)}, u32[]{:S(2)}) collective-permute-start(bf16[128,1024]{1,0:T(8,128)(2,1)S(1)} %get-tuple-element.72), channel_id=1, source_target_pairs={{0,2},{1,3},{2,0},{3,1},{4,6},{5,7},{6,4},{7,5},{8,10},{9,11},{10,... | collective-permute-start | bytes 786440 | tf_op jit(solution)/shard_map/ppermute | solution.py:271
  73.2 6.0 %collective-permute-done.18.refs_1_ = bf16[128,1024]{1,0:T(8,128)(2,1)S(1)} collective-permute-done((bf16[128,1024]{1,0:T(8,128)(2,1)S(1)}, bf16[128,1024]{1,0:T(8,128)(2,1)S(1)}, u32[]{:S(2)}, u32[]{:S(2)}) %collective-permute-start.18) | collective-permute-done | bytes 262176 | tf_op jit(solution)/shard_map/ppermute | solution.py:271
  79.3 4.7 %collective-permute-done.21.refs_3_ = bf16[128,1024]{1,0:T(8,128)(2,1)S(1)} collective-permute-done((bf16[128,1024]{1,0:T(8,128)(2,1)S(1)}, bf16[128,1024]{1,0:T(8,128)(2,1)S(1)}, u32[]{:S(2)}, u32[]{:S(2)}) %collective-permute-start.21) | collective-permute-done | bytes 262176 | tf_op jit(solution)/shard_map/ppermute | solution.py:271
  84.0 1.4 %shard_map.79 = bf16[128,2048]{1,0:T(8,128)(2,1)} custom-call(s32[11]{0:T(128)S(1)} %stack.47.info_ref, f32[128,1024]{1,0:T(8,128)S(1)} %get-tuple-element.67.refs_0_, bf16[128,1024]{1,0:T(8,128)(2,1)S(1)} %collective-permute-done.18.refs_1_, f32[128,1024]{1,0:T(8,128)S(1)} %get-tuple-element.71.refs_2_, bf16[128,1024]{1,0:T(8,128)(2,1)S(1)} %collective-permute-done.21.refs_3_), custom_call_target="tpu_custom_call" | custom-call | tf_op jit(solution)/shard_map/pallas_call | solution.py:27
  (16 shorter events, 0.1 us)
Async XLA Ops:
  0.0 17.3 %collective-permute-start = (bf16[128,2048]{1,0:T(8,128)(2,1)}, bf16[128,2048]{1,0:T(8,128)(2,1)}, u32[]{:S(2)}, u32[]{:S(2)}) collective-permute-start(bf16[128,2048]{1,0:T(8,128)(2,1)} %refs_4_.3), channel_id=1, source_target_pairs={{0,8},{1,9},{2,10},{3,11},{4,12},{5,13},{6,14},{7,15},{8,16},{9,17... | collective-permute-start | bytes 1572872 | tf_op jit(solution)/shard_map/ppermute | solution.py:276
  3.0 15.8 %collective-permute-start.1 = (bf16[128,2048]{1,0:T(8,128)(2,1)}, bf16[128,2048]{1,0:T(8,128)(2,1)S(1)}, u32[]{:S(2)}, u32[]{:S(2)}) collective-permute-start(bf16[128,2048]{1,0:T(8,128)(2,1)} %refs_4_.3), channel_id=1, source_target_pairs={{0,4},{1,5},{2,6},{3,7},{4,0},{5,1},{6,2},{7,3},{8,12},{9,13},{10,... | collective-permute-start | bytes 1572872 | tf_op jit(solution)/shard_map/ppermute | solution.py:271
  4.5 4.6 %copy-start.7 = (f32[4096]{0:T(1024)S(1)}, f32[4096]{0:T(1024)}, u32[]{:S(2)}) copy-start(f32[4096]{0:T(1024)} %param.10) | copy-start | bytes 49156
  4.6 1.2 %copy-start.3 = (bf16[128,4096]{1,0:T(8,128)(2,1)S(1)}, bf16[128,4096]{1,0:T(8,128)(2,1)}, u32[]{:S(2)}) copy-start(bf16[128,4096]{1,0:T(8,128)(2,1)} %refs_0_.2) | copy-start | bytes 3145732
  5.9 3.3 %copy-start.4 = (bf16[128,4096]{1,0:T(8,128)(2,1)S(1)}, bf16[128,4096]{1,0:T(8,128)(2,1)}, u32[]{:S(2)}) copy-start(bf16[128,4096]{1,0:T(8,128)(2,1)} %refs_0_.3) | copy-start | bytes 3145732
  6.9 8.6 %collective-permute-start.4 = (bf16[128,1024]{1,0:T(8,128)(2,1)S(1)}, bf16[128,1024]{1,0:T(8,128)(2,1)S(1)}, u32[]{:S(2)}, u32[]{:S(2)}) collective-permute-start(bf16[128,1024]{1,0:T(8,128)(2,1)S(1)} %get-tuple-element.43), channel_id=1, source_target_pairs={{0,3},{1,2},{2,1},{3,0},{4,7},{5,6},{6,5},{7,4},{8,11},{9,10},{10,... | collective-permute-start | bytes 786440 | tf_op jit(solution)/shard_map/ppermute | solution.py:271
  7.4 12.2 %collective-permute-start.2 = (bf16[128,1024]{1,0:T(8,128)(2,1)S(1)}, bf16[128,1024]{1,0:T(8,128)(2,1)S(1)}, u32[]{:S(2)}, u32[]{:S(2)}) collective-permute-start(bf16[128,1024]{1,0:T(8,128)(2,1)S(1)} %get-tuple-element.41), channel_id=1, source_target_pairs={{0,1},{1,0},{2,3},{3,2},{4,5},{5,4},{6,7},{7,6},{8,9},{9,8},{10,11... | collective-permute-start | bytes 786440 | tf_op jit(solution)/shard_map/ppermute | solution.py:271
  8.6 12.7 %collective-permute-start.3 = (bf16[128,1024]{1,0:T(8,128)(2,1)S(1)}, bf16[128,1024]{1,0:T(8,128)(2,1)S(1)}, u32[]{:S(2)}, u32[]{:S(2)}) collective-permute-start(bf16[128,1024]{1,0:T(8,128)(2,1)S(1)} %get-tuple-element.42), channel_id=1, source_target_pairs={{0,2},{1,3},{2,0},{3,1},{4,6},{5,7},{6,4},{7,5},{8,10},{9,11},{10,... | collective-permute-start | bytes 786440 | tf_op jit(solution)/shard_map/ppermute | solution.py:271
  9.2 1.0 %copy-start.5 = (f32[4096,16]{0,1:T(8,128)S(1)}, f32[4096,16]{0,1:T(8,128)}, u32[]{:S(2)}) copy-start(f32[4096,16]{0,1:T(8,128)} %param.8) | copy-start | bytes 786436
  10.1 0.9 %copy-start.6 = (f32[4096,16]{0,1:T(8,128)S(1)}, f32[4096,16]{0,1:T(8,128)}, u32[]{:S(2)}) copy-start(f32[4096,16]{0,1:T(8,128)} %param.9) | copy-start | bytes 786436
  15.6 9.7 %collective-permute-start.7 = (bf16[128,1024]{1,0:T(8,128)(2,1)S(1)}, bf16[128,1024]{1,0:T(8,128)(2,1)S(1)}, u32[]{:S(2)}, u32[]{:S(2)}) collective-permute-start(bf16[128,1024]{1,0:T(8,128)(2,1)S(1)} %get-tuple-element.55), channel_id=1, source_target_pairs={{0,1},{1,0},{2,3},{3,2},{4,5},{5,4},{6,7},{7,6},{8,9},{9,8},{10,11... | collective-permute-start | bytes 786440 | tf_op jit(solution)/shard_map/ppermute | solution.py:271
  17.3 13.6 %collective-permute-start.8 = (bf16[128,1024]{1,0:T(8,128)(2,1)}, bf16[128,1024]{1,0:T(8,128)(2,1)S(1)}, u32[]{:S(2)}, u32[]{:S(2)}) collective-permute-start(bf16[128,1024]{1,0:T(8,128)(2,1)} %get-tuple-element.57), channel_id=1, source_target_pairs={{0,2},{1,3},{2,0},{3,1},{4,6},{5,7},{6,4},{7,5},{8,10},{9,11},{10,... | collective-permute-start | bytes 786440 | tf_op jit(solution)/shard_map/ppermute | solution.py:271
  18.8 0.8 copy-start.1
  19.6 12.8 %collective-permute-start.9 = (bf16[128,1024]{1,0:T(8,128)(2,1)}, bf16[128,1024]{1,0:T(8,128)(2,1)S(1)}, u32[]{:S(2)}, u32[]{:S(2)}) collective-permute-start(bf16[128,1024]{1,0:T(8,128)(2,1)} %get-tuple-element.59), channel_id=1, source_target_pairs={{0,3},{1,2},{2,1},{3,0},{4,7},{5,6},{6,5},{7,4},{8,11},{9,10},{10,... | collective-permute-start | bytes 786440 | tf_op jit(solution)/shard_map/ppermute | solution.py:271
  19.6 17.2 %collective-permute-start.5 = (bf16[128,2048]{1,0:T(8,128)(2,1)}, bf16[128,2048]{1,0:T(8,128)(2,1)}, u32[]{:S(2)}, u32[]{:S(2)}) collective-permute-start(bf16[128,2048]{1,0:T(8,128)(2,1)} %collective-permute-done.refs_6_), channel_id=1, source_target_pairs={{0,8},{1,9},{2,10},{3,11},{4,12},{5,13},{6,14},{7,15},{8,16},{9,17... | collective-permute-start | bytes 1572872 | tf_op jit(solution)/shard_map/ppermute | solution.py:276
  21.3 15.5 %collective-permute-start.6 = (bf16[128,2048]{1,0:T(8,128)(2,1)}, bf16[128,2048]{1,0:T(8,128)(2,1)}, u32[]{:S(2)}, u32[]{:S(2)}) collective-permute-start(bf16[128,2048]{1,0:T(8,128)(2,1)} %collective-permute-done.refs_6_), channel_id=1, source_target_pairs={{0,4},{1,5},{2,6},{3,7},{4,0},{5,1},{6,2},{7,3},{8,12},{9,13},{10,... | collective-permute-start | bytes 1572872 | tf_op jit(solution)/shard_map/ppermute | solution.py:271
  25.3 11.4 %collective-permute-start.10 = (f32[16,1024]{1,0:T(8,128)S(1)}, f32[16,1024]{1,0:T(8,128)S(1)}, u32[]{:S(2)}, u32[]{:S(2)}) collective-permute-start(f32[16,1024]{1,0:T(8,128)S(1)} %get-tuple-element.61), channel_id=1, source_target_pairs={{0,4},{1,5},{2,6},{3,7},{4,0},{5,1},{6,2},{7,3},{8,12},{9,13},{10,... | collective-permute-start | bytes 196616 | tf_op jit(solution)/shard_map/ppermute | solution.py:271
  36.8 15.2 %collective-permute-start.14 = (bf16[128,2048]{1,0:T(8,128)(2,1)}, bf16[128,2048]{1,0:T(8,128)(2,1)S(1)}, u32[]{:S(2)}, u32[]{:S(2)}) collective-permute-start(bf16[128,2048]{1,0:T(8,128)(2,1)} %collective-permute-done.5.refs_8_), channel_id=1, source_target_pairs={{0,8},{1,9},{2,10},{3,11},{4,12},{5,13},{6,14},{7,15},{8,16},{9,17... | collective-permute-start | bytes 1572872 | tf_op jit(solution)/shard_map/ppermute | solution.py:276
  38.4 13.5 %collective-permute-start.15 = (bf16[128,2048]{1,0:T(8,128)(2,1)}, bf16[128,2048]{1,0:T(8,128)(2,1)S(1)}, u32[]{:S(2)}, u32[]{:S(2)}) collective-permute-start(bf16[128,2048]{1,0:T(8,128)(2,1)} %collective-permute-done.5.refs_8_), channel_id=1, source_target_pairs={{0,4},{1,5},{2,6},{3,7},{4,0},{5,1},{6,2},{7,3},{8,12},{9,13},{10,... | collective-permute-start | bytes 1572872 | tf_op jit(solution)/shard_map/ppermute | solution.py:271
  39.0 19.1 %collective-permute-start.11 = (f32[16,1024]{1,0:T(8,128)S(1)}, f32[16,1024]{1,0:T(8,128)S(1)}, u32[]{:S(2)}, u32[]{:S(2)}) collective-permute-start(f32[16,1024]{1,0:T(8,128)S(1)} %select_add_fusion), channel_id=1, source_target_pairs={{0,8},{1,9},{2,10},{3,11},{4,12},{5,13},{6,14},{7,15},{8,16},{9,17... | collective-permute-start | bytes 196616 | tf_op jit(solution)/shard_map/ppermute | solution.py:276
  42.4 15.7 %collective-permute-start.12 = (f32[16,1024]{1,0:T(8,128)S(1)}, f32[16,1024]{1,0:T(8,128)S(1)}, u32[]{:S(2)}, u32[]{:S(2)}) collective-permute-start(f32[16,1024]{1,0:T(8,128)S(1)} %select_add_fusion), channel_id=1, source_target_pairs={{0,16},{1,17},{2,18},{3,19},{4,20},{5,21},{6,22},{7,23},{8,24},{9,... | collective-permute-start | bytes 196616 | tf_op jit(solution)/shard_map/ppermute | solution.py:276
  45.9 12.2 %collective-permute-start.13 = (f32[16,1024]{1,0:T(8,128)S(1)}, f32[16,1024]{1,0:T(8,128)S(1)}, u32[]{:S(2)}, u32[]{:S(2)}) collective-permute-start(f32[16,1024]{1,0:T(8,128)S(1)} %select_add_fusion), channel_id=1, source_target_pairs={{0,24},{1,25},{2,26},{3,27},{4,28},{5,29},{6,30},{7,31}} | collective-permute-start | bytes 196616 | tf_op jit(solution)/shard_map/ppermute | solution.py:276
  52.0 11.2 %collective-permute-start.16 = (bf16[128,1024]{1,0:T(8,128)(2,1)S(1)}, bf16[128,1024]{1,0:T(8,128)(2,1)S(1)}, u32[]{:S(2)}, u32[]{:S(2)}) collective-permute-start(bf16[128,1024]{1,0:T(8,128)(2,1)S(1)} %get-tuple-element.74), channel_id=1, source_target_pairs={{0,4},{1,5},{2,6},{3,7},{4,0},{5,1},{6,2},{7,3},{8,12},{9,13},{10,... | collective-permute-start | bytes 786440 | tf_op jit(solution)/shard_map/ppermute | solution.py:271
  55.4 10.7 %collective-permute-start.19 = (bf16[128,1024]{1,0:T(8,128)(2,1)S(1)}, bf16[128,1024]{1,0:T(8,128)(2,1)S(1)}, u32[]{:S(2)}, u32[]{:S(2)}) collective-permute-start(bf16[128,1024]{1,0:T(8,128)(2,1)S(1)} %get-tuple-element.73), channel_id=1, source_target_pairs={{0,4},{1,5},{2,6},{3,7},{4,0},{5,1},{6,2},{7,3},{8,12},{9,13},{10,... | collective-permute-start | bytes 786440 | tf_op jit(solution)/shard_map/ppermute | solution.py:271
  61.9 1.3 %copy-start = (bf16[128,2048]{1,0:T(8,128)(2,1)S(1)}, bf16[128,2048]{1,0:T(8,128)(2,1)}, u32[]{:S(2)}) copy-start(bf16[128,2048]{1,0:T(8,128)(2,1)} %refs_4_.3) | copy-start | bytes 1572868
  61.9 1.3 %copy-start.2 = (bf16[128,2048]{1,0:T(8,128)(2,1)S(1)}, bf16[128,2048]{1,0:T(8,128)(2,1)}, u32[]{:S(2)}) copy-start(bf16[128,2048]{1,0:T(8,128)(2,1)} %copy-done.1) | copy-start | bytes 1572868
  66.0 3.4 %collective-permute-start.17 = (bf16[256,1024]{1,0:T(8,128)(2,1)S(1)}, bf16[256,1024]{1,0:T(8,128)(2,1)S(1)}, u32[]{:S(2)}, u32[]{:S(2)}) collective-permute-start(bf16[256,1024]{1,0:T(8,128)(2,1)S(1)} %get-tuple-element.66), channel_id=1, source_target_pairs={{0,1},{1,0},{2,3},{3,2},{4,5},{5,4},{6,7},{7,6},{8,9},{9,8},{10,11... | collective-permute-start | bytes 1572872 | tf_op jit(solution)/shard_map/ppermute | solution.py:271
  68.8 2.8 %collective-permute-start.20 = (bf16[256,1024]{1,0:T(8,128)(2,1)S(1)}, bf16[256,1024]{1,0:T(8,128)(2,1)S(1)}, u32[]{:S(2)}, u32[]{:S(2)}) collective-permute-start(bf16[256,1024]{1,0:T(8,128)(2,1)S(1)} %get-tuple-element.70), channel_id=1, source_target_pairs={{0,1},{1,0},{2,3},{3,2},{4,5},{5,4},{6,7},{7,6},{8,9},{9,8},{10,11... | collective-permute-start | bytes 1572872 | tf_op jit(solution)/shard_map/ppermute | solution.py:271
  70.0 9.2 %collective-permute-start.18 = (bf16[128,1024]{1,0:T(8,128)(2,1)S(1)}, bf16[128,1024]{1,0:T(8,128)(2,1)S(1)}, u32[]{:S(2)}, u32[]{:S(2)}) collective-permute-start(bf16[128,1024]{1,0:T(8,128)(2,1)S(1)} %get-tuple-element.68), channel_id=1, source_target_pairs={{0,2},{1,3},{2,0},{3,1},{4,6},{5,7},{6,4},{7,5},{8,10},{9,11},{10,... | collective-permute-start | bytes 786440 | tf_op jit(solution)/shard_map/ppermute | solution.py:271
  72.3 11.6 %collective-permute-start.21 = (bf16[128,1024]{1,0:T(8,128)(2,1)S(1)}, bf16[128,1024]{1,0:T(8,128)(2,1)S(1)}, u32[]{:S(2)}, u32[]{:S(2)}) collective-permute-start(bf16[128,1024]{1,0:T(8,128)(2,1)S(1)} %get-tuple-element.72), channel_id=1, source_target_pairs={{0,2},{1,3},{2,0},{3,1},{4,6},{5,7},{6,4},{7,5},{8,10},{9,11},{10,... | collective-permute-start | bytes 786440 | tf_op jit(solution)/shard_map/ppermute | solution.py:271

commit v5 on v4

--- a/solution.py
+++ b/solution.py
@@ -157,6 +157,13 @@
                     y[i] = y[i] + tap * wide[b, at : at + 8, :]
             for i in range(BLOCK // 8):
                 y_ref[slot, pl.ds(pl.multiple_of(b * BLOCK + 8 * i, 8), 8), :] = y[i]
+
+
+def pair_kernel(span, info_ref, end_ref, near_ref, rate_ref, out_ref):
+    high = info_ref[1] == 1
+    first = jnp.where(high, near_ref[...], end_ref[...])
+    second = jnp.where(high, end_ref[...], near_ref[...])
+    out_ref[...] = jnp.exp(-span * rate_ref[...]) * first + second
 
 
 def gate_kernel(base, reaches, info_ref, *refs):
@@ -212,28 +219,36 @@
                     out_ref[slot, to, :] = gated.astype(bf16)
 
 
-def project_kernel(pieces, in_slots, at, info_ref, *refs):
-    gated, weights = refs[:pieces], refs[pieces:-3]
+def product(pieces, in_slots, first, info_ref, gated, weights, into, before):
+    per = gated[0].shape[0]
+    wide = into.shape[1]
+    step = min(wide, 256)
+    for slot in range(0, len(weights), 2):
+        if in_slots:
+            left = [gated[n // per][n % per] for n in (first + slot, first + slot + 1)]
+        else:
+            left = [gated[0][info_ref[3 + n]] for n in (first + slot, first + slot + 1)]
+        left = jnp.concatenate(left, axis=1)
+        for col in range(0, wide, step):
+            right = jnp.concatenate([ref[:, col : col + step] for ref in weights[slot : slot + 2]], axis=0)
+            term = jnp.dot(left, right, preferred_element_type=f32)
+            cols = slice(col, col + step)
+            start = before if slot == 0 else into
+            into[:, cols] = term if start is None else start[:, cols] + term
+
+
+def early_kernel(pieces, in_slots, info_ref, *refs):
+    product(pieces, in_slots, 0, info_ref, refs[:pieces], refs[pieces:-1], refs[-1], None)
+
+
+def project_kernel(pieces, in_slots, slots, at, info_ref, *refs):
+    gated, (early_ref, near_ref, away_ref) = refs[:pieces], refs[pieces : pieces + 3]
     kept_ref, sent_ref, total = refs[-3:]
     core = info_ref[2]
-    per = gated[0].shape[0]
     rows, wide = kept_ref.shape[0] // 2, kept_ref.shape[1]
-    step = min(wide, 256)
-    slots = len(weights)
-    for slot in range(0, slots, 2):
-        if in_slots:
-            left = [gated[n // per][n % per] for n in (slot, slot + 1)]
-        else:
-            left = [gated[0][info_ref[3 + n]] for n in (slot, slot + 1)]
-        left = jnp.concatenate(left, axis=1)
-        for col in range(0, wide, step):
-            right = []
-            for ref in weights[slot : slot + 2]:
-                first = col if ref.shape[1] == wide else at + col
-                right.append(ref[:, first : first + step])
-            term = jnp.dot(left, jnp.concatenate(right, axis=0), preferred_element_type=f32)
-            cols = slice(col, col + step)
-            total[:, cols] = term if slot == 0 else total[:, cols] + term
+    cols = slice(at, at + wide)
+    weights = [near_ref.at[:, cols], away_ref]
+    product(pieces, in_slots, slots - 2, info_ref, gated, weights, total, early_ref.at[:, cols])
     for across in range(2):
         here = slice(across * rows, (across + 1) * rows)
         for which, out in enumerate((kept_ref, sent_ref)):
@@ -325,7 +340,7 @@
     pieces = 4
     some = tiles // pieces
     if len(weights) < heights:
-        above, away = next_round(tied(weights[-1], weights_away[-1]))
+        above, away = next_round(tied(weights[-1], weights_away[-1], rates, values[1]))
         weights.append(above)
         weights_away.append(away)
     local = []
@@ -342,11 +357,12 @@
 
     near = swap(end, TEAM)
     end = tied(end, local[0], local[1], *gates)
-    first, second = jnp.where(y == 0, end, near), jnp.where(y == 0, near, end)
     span = float(TEAM * rows)
-    held = jnp.exp(-span * rates) * first + second
+    held = call(
+        functools.partial(pair_kernel, span), jax.ShapeDtypeStruct((order, share), f32), micros=0.2
+    )(info, end, near, rates)
     while len(weights) < heights:
-        above, away = next_round(tied(weights[-1], weights_away[-1], held))
+        above, away = next_round(tied(weights[-1], weights_away[-1], near, local[1], *gates))
         weights.append(above)
         weights_away.append(away)
     far, gap = [], 1
@@ -357,7 +373,7 @@
             held = held + jnp.exp(-2.0 * span * lag * rates) * state
         gap *= 4
     wide = features // LAST_PARTS
-    block = tied(weights[last], weights_away[-1])
+    block = tied(weights[last], weights_away[-1], local[-1])
     finals = [swap(block[:, part * wide : (part + 1) * wide], TEAM) for part in range(LAST_PARTS)]
 
     tables = [pltpu.VMEM((order, 8, LANES), f32)] * 2
@@ -376,19 +392,24 @@
         gated = gated.reshape(TEAM * rows, width // (TEAM * depth), depth).transpose(1, 0, 2)
         gated = [gated]
 
-    finished = []
+    early = call(
+        functools.partial(early_kernel, len(gated), in_slots),
+        jax.ShapeDtypeStruct((TEAM * rows, features), f32),
+        micros=1.0,
+    )(group_info, *gated, *[ref for pair in zip(weights, weights_away) for ref in pair])
+    finished, joined = [], []
     for part, final in enumerate(finals):
-        slots = [ref for pair in zip(weights, weights_away + [final]) for ref in pair]
         kept, sent = call(
-            functools.partial(project_kernel, len(gated), in_slots, part * wide),
+            functools.partial(project_kernel, len(gated), in_slots, 2 * heights, part * wide),
             [jax.ShapeDtypeStruct((2 * rows, wide), dtype) for dtype in (f32, bf16)],
             [pltpu.VMEM((TEAM * rows, wide), f32)],
-            micros=0.5,
-        )(group_info, *gated, *slots)
+            micros=0.3,
+        )(group_info, *gated, early, weights[last], final)
         mine_sum, away_sum = call(
             join_kernel,
             [jax.ShapeDtypeStruct((rows, wide), f32), jax.ShapeDtypeStruct((rows, wide), bf16)],
         )(info, kept, swap(sent, 1))
+        joined.append(mine_sum)
         finished += [mine_sum, swap(away_sum, 2)]
     return call(finish_kernel, jax.ShapeDtypeStruct((rows, features), bf16))(info, *finished)
 

time: 86.6 us -> 79.5 us (0.918); the launches traced: 85.4 us -> 79.2 us
  waiting for transfers between devices: 26.2 us -> 19.5 us
  local copies, waits for them, and re-layouts: 4.06 us -> 5.19 us
  Pallas kernels: 28.1 us -> 27 us
    ppermute x16, waiting for transfers between devices: 20.1 us -> 15.6 us  [swap(): return lax.ppermute(value, 'seq', [(i, i ^ bit) for i in range(count)])]
    ppermute x6, waiting for transfers between devices: 6.17 us -> 3.93 us  [up(): return lax.ppermute(value, 'seq', pairs)]
    unnamed x16 -> x12, local copies, waits for them, and re-layouts: 3.94 us -> 5.07 us
    pallas_call x14 -> x16, Pallas kernels: 24.6 us -> 24.2 us  [run(): pl.pallas_call(kernel, out_shape=out_shape, in_specs=[pl.BlockSpec(memory...]
  transfers between devices with their start and end apart: 22 -> 22, of which waited for: 8 -> 10; matrix products, arithmetic and copies ran while one was open for 0% -> 0% of each run, Pallas kernels for 31% -> 32%
where the time goes in v5:
time: 79.5 us; the launch traced here: 79.2 us
  starting transfers between devices  27.2 us (34%)
  Pallas kernels  27 us (34%)
  waiting for transfers between devices  19.5 us (25%)
  local copies, waits for them, and re-layouts  5.19 us (7%)
    pallas_call x16, Pallas kernels, run(): pl.pallas_call(kernel, out_shape=out_shape, in_specs=[pl.BlockSpec(memory...  24.2 us
    ppermute x16, waiting for transfers between devices, swap(): return lax.ppermute(value, 'seq', [(i, i ^ bit) for i in range(count)])  15.6 us
    ppermute x16, starting transfers between devices, swap(): return lax.ppermute(value, 'seq', [(i, i ^ bit) for i in range(count)])  13.9 us
    ppermute x6, starting transfers between devices, up(): return lax.ppermute(value, 'seq', pairs)  13.3 us
    unnamed x12, local copies, waits for them, and re-layouts  5.07 us
    ppermute x6, waiting for transfers between devices, up(): return lax.ppermute(value, 'seq', pairs)  3.93 us
    pallas_call x2, Pallas kernels, deal(): pl.pallas_call(functools.partial(deal_kernel, team, depth, plan), out_sha...  2.78 us
  transfers between devices with their start and end apart: 22, of which 10 were waited for; matrix products, arithmetic and copies ran while one was open for 0% of the time, Pallas kernels for 32%

profile of v5, /device:TPU:0, one launch (start us, length us, event | category | flops | bytes accessed | tf_op | source)
XLA Modules:
  0.0 79.2 jit_solution(9841497391234860598)
XLA Ops:
  0.0 3.0 %collective-permute-start = (bf16[128,2048]{1,0:T(8,128)(2,1)}, bf16[128,2048]{1,0:T(8,128)(2,1)S(1)}, u32[]{:S(2)}, u32[]{:S(2)}) collective-permute-start(bf16[128,2048]{1,0:T(8,128)(2,1)} %refs_4_.1), channel_id=1, source_target_pairs={{0,8},{1,9},{2,10},{3,11},{4,12},{5,13},{6,14},{7,15},{8,16},{9,17... | collective-permute-start | bytes 1572872 | tf_op jit(solution)/shard_map/ppermute | solution.py:291
  3.0 1.5 %collective-permute-start.1 = (bf16[128,2048]{1,0:T(8,128)(2,1)}, bf16[128,2048]{1,0:T(8,128)(2,1)S(1)}, u32[]{:S(2)}, u32[]{:S(2)}) collective-permute-start(bf16[128,2048]{1,0:T(8,128)(2,1)} %refs_4_.1), channel_id=1, source_target_pairs={{0,4},{1,5},{2,6},{3,7},{4,0},{5,1},{6,2},{7,3},{8,12},{9,13},{10,... | collective-permute-start | bytes 1572872 | tf_op jit(solution)/shard_map/ppermute | solution.py:286
  4.5 0.1 stack.47.info_ref
  4.6 1.2 %copy-done = bf16[128,4096]{1,0:T(8,128)(2,1)S(1)} copy-done((bf16[128,4096]{1,0:T(8,128)(2,1)S(1)}, bf16[128,4096]{1,0:T(8,128)(2,1)}, u32[]{:S(2)}) %copy-start) | copy-done | bytes 1048600
  5.9 1.1 %shard_map.64 = (bf16[128,1024]{1,0:T(8,128)(2,1)S(1)}, bf16[128,1024]{1,0:T(8,128)(2,1)S(1)}, bf16[128,1024]{1,0:T(8,128)(2,1)S(1)}, bf16[128,1024]{1,0:T(8,128)(2,1)S(1)}) custom-call(s32[11]{0:T(128)S(1)} %stack.47.info_ref, bf16[128,4096]{1,0:T(8,128)(2,1)S(1)} %copy-done), custom_call_target="tpu_custom_call" | custom-call | tf_op jit(solution)/shard_map/pallas_call | solution.py:73
  6.9 0.1 collective-permute-start.2
  7.0 1.6 %collective-permute-start.4 = (bf16[128,1024]{1,0:T(8,128)(2,1)S(1)}, bf16[128,1024]{1,0:T(8,128)(2,1)S(1)}, u32[]{:S(2)}, u32[]{:S(2)}) collective-permute-start(bf16[128,1024]{1,0:T(8,128)(2,1)S(1)} %get-tuple-element.43), channel_id=1, source_target_pairs={{0,3},{1,2},{2,1},{3,0},{4,7},{5,6},{6,5},{7,4},{8,11},{9,10},{10,... | collective-permute-start | bytes 786440 | tf_op jit(solution)/shard_map/ppermute | solution.py:286
  8.6 0.5 collective-permute-start.3
  9.2 1.2 %copy-done.1 = bf16[128,4096]{1,0:T(8,128)(2,1)S(1)} copy-done((bf16[128,4096]{1,0:T(8,128)(2,1)S(1)}, bf16[128,4096]{1,0:T(8,128)(2,1)}, u32[]{:S(2)}) %copy-start.1) | copy-done | bytes 1048600
  10.4 0.9 %copy-done.3 = f32[4096,16]{0,1:T(8,128)S(1)} copy-done((f32[4096,16]{0,1:T(8,128)S(1)}, f32[4096,16]{0,1:T(8,128)}, u32[]{:S(2)}) %copy-start.3) | copy-done | bytes 262168
  11.3 0.9 %copy-done.4 = f32[4096,16]{0,1:T(8,128)S(1)} copy-done((f32[4096,16]{0,1:T(8,128)S(1)}, f32[4096,16]{0,1:T(8,128)}, u32[]{:S(2)}) %copy-start.4) | copy-done | bytes 262168
  12.3 0.7 copy-done.5
  13.0 1.7 %shard_map.65 = (bf16[128,1024]{1,0:T(8,128)(2,1)S(1)}, bf16[128,1024]{1,0:T(8,128)(2,1)S(1)}, bf16[128,1024]{1,0:T(8,128)(2,1)S(1)}, bf16[128,1024]{1,0:T(8,128...) custom-call(s32[11]{0:T(128)S(1)} %stack.47.info_ref, ...), custom_call_target="tpu_custom_call" | custom-call | tf_op jit(solution)/shard_map/pallas_call | solution.py:73
  14.7 0.0 collective-permute-done.2.refs_1_
  14.7 0.1 collective-permute-start.7
  14.8 2.4 %collective-permute-done.refs_6_ = bf16[128,2048]{1,0:T(8,128)(2,1)S(1)} collective-permute-done((bf16[128,2048]{1,0:T(8,128)(2,1)}, bf16[128,2048]{1,0:T(8,128)(2,1)S(1)}, u32[]{:S(2)}, u32[]{:S(2)}) %collective-permute-start) | collective-permute-done | bytes 524320 | tf_op jit(solution)/shard_map/ppermute | solution.py:291
  17.2 1.0 %collective-permute-start.5 = (bf16[128,2048]{1,0:T(8,128)(2,1)S(1)}, bf16[128,2048]{1,0:T(8,128)(2,1)S(1)}, u32[]{:S(2)}, u32[]{:S(2)}) collective-permute-start(bf16[128,2048]{1,0:T(8,128)(2,1)S(1)} %collective-permute-done.refs_6_), channel_id=1, source_target_pairs={{0,8},{1,9},{2,10},{3,11},{4,12},{5,13},{6,14},{7,15},{8,16},{9,17... | collective-permute-start | bytes 1572872 | tf_op jit(solution)/shard_map/ppermute | solution.py:291
  18.2 1.5 %collective-permute-start.6 = (bf16[128,2048]{1,0:T(8,128)(2,1)S(1)}, bf16[128,2048]{1,0:T(8,128)(2,1)S(1)}, u32[]{:S(2)}, u32[]{:S(2)}) collective-permute-start(bf16[128,2048]{1,0:T(8,128)(2,1)S(1)} %collective-permute-done.refs_6_), channel_id=1, source_target_pairs={{0,4},{1,5},{2,6},{3,7},{4,0},{5,1},{6,2},{7,3},{8,12},{9,13},{10,... | collective-permute-start | bytes 1572872 | tf_op jit(solution)/shard_map/ppermute | solution.py:286
  19.7 0.0 collective-permute-done.4.refs_3_
  19.7 1.5 %collective-permute-start.8 = (bf16[128,1024]{1,0:T(8,128)(2,1)S(1)}, bf16[128,1024]{1,0:T(8,128)(2,1)S(1)}, u32[]{:S(2)}, u32[]{:S(2)}) collective-permute-start(bf16[128,1024]{1,0:T(8,128)(2,1)S(1)} %get-tuple-element.57), channel_id=1, source_target_pairs={{0,2},{1,3},{2,0},{3,1},{4,6},{5,7},{6,4},{7,5},{8,10},{9,11},{10,... | collective-permute-start | bytes 786440 | tf_op jit(solution)/shard_map/ppermute | solution.py:286
  21.2 0.7 collective-permute-done.3.refs_2_
  21.9 0.1 collective-permute-start.9
  22.0 3.5 %shard_map.66 = (f32[8,16,16,128]{3,2,1,0:T(8,128)S(1)}, f32[16,1024]{1,0:T(8,128)S(1)}) custom-call(s32[11]{0:T(128)S(1)} %stack.47.info_ref, bf16[128,1024]{1,0:T(8,128)(2,1)S(1)} %get-tuple-element.40.refs_0_, bf16[128,1024]{1,0:T(8,128)(2,1)S(1)} %collective-permute-done.2.refs_1_, bf16[128,1024]{1,0:T(8,128)(2,1)S(1)} %collective-permute-done.3.refs_2_, ...), custom_call_target="tpu_custom_call" | custom-call | flops 550000000 | bytes 1800000 | tf_op jit(solution)/shard_map/pallas_call | solution.py:27
  25.5 0.0 collective-permute-done.7.refs_1_
  25.5 0.6 collective-permute-start.10
  26.1 2.0 %shard_map.67.refs_4_ = f32[2,512,128]{2,1,0:T(8,128)S(1)} custom-call(s32[11]{0:T(128)S(1)} %stack.47.info_ref, bf16[128,1024]{1,0:T(8,128)(2,1)S(1)} %get-tuple-element.40.refs_0_, bf16[128,1024]{1,0:T(8,128)(2,1)S(1)} %collective-permute-done.2.refs_1_, bf16[128,1024]{1,0:T(8,128)(2,1)S(1)} %collective-permute-done.3.refs_2_, ...), custom_call_target="tpu_custom_call" | custom-call | flops 330000000 | bytes 1080000 | tf_op jit(solution)/shard_map/pallas_call | solution.py:27
  28.1 2.0 %shard_map.68.refs_4_ = f32[2,512,128]{2,1,0:T(8,128)S(1)} custom-call(s32[11]{0:T(128)S(1)} %stack.47.info_ref, bf16[128,1024]{1,0:T(8,128)(2,1)S(1)} %get-tuple-element.40.refs_0_, bf16[128,1024]{1,0:T(8,128)(2,1)S(1)} %collective-permute-done.2.refs_1_, bf16[128,1024]{1,0:T(8,128)(2,1)S(1)} %collective-permute-done.3.refs_2_, ...), custom_call_target="tpu_custom_call" | custom-call | flops 330000000 | bytes 1080000 | tf_op jit(solution)/shard_map/pallas_call | solution.py:27
  30.0 1.5 %collective-permute-done.9.refs_3_ = bf16[128,1024]{1,0:T(8,128)(2,1)S(1)} collective-permute-done((bf16[128,1024]{1,0:T(8,128)(2,1)S(1)}, bf16[128,1024]{1,0:T(8,128)(2,1)S(1)}, u32[]{:S(2)}, u32[]{:S(2)}) %collective-permute-start.9) | collective-permute-done | bytes 262176 | tf_op jit(solution)/shard_map/ppermute | solution.py:286
  31.6 0.3 collective-permute-done.10.near_ref.refs_8_
  31.8 0.2 collective-permute-done.5.refs_8_
  32.1 0.0 collective-permute-done.6.refs_7_
  32.1 1.3 %collective-permute-start.14 = (bf16[128,2048]{1,0:T(8,128)(2,1)S(1)}, bf16[128,2048]{1,0:T(8,128)(2,1)S(1)}, u32[]{:S(2)}, u32[]{:S(2)}) collective-permute-start(bf16[128,2048]{1,0:T(8,128)(2,1)S(1)} %collective-permute-done.5.refs_8_), channel_id=1, source_target_pairs={{0,8},{1,9},{2,10},{3,11},{4,12},{5,13},{6,14},{7,15},{8,16},{9,17... | collective-permute-start | bytes 1572872 | tf_op jit(solution)/shard_map/ppermute | solution.py:291
  33.4 1.5 %collective-permute-start.15 = (bf16[128,2048]{1,0:T(8,128)(2,1)S(1)}, bf16[128,2048]{1,0:T(8,128)(2,1)S(1)}, u32[]{:S(2)}, u32[]{:S(2)}) collective-permute-start(bf16[128,2048]{1,0:T(8,128)(2,1)S(1)} %collective-permute-done.5.refs_8_), channel_id=1, source_target_pairs={{0,4},{1,5},{2,6},{3,7},{4,0},{5,1},{6,2},{7,3},{8,12},{9,13},{10,... | collective-permute-start | bytes 1572872 | tf_op jit(solution)/shard_map/ppermute | solution.py:286
  34.9 0.6 shard_map.71
  35.5 2.5 %collective-permute-start.11 = (f32[16,1024]{1,0:T(8,128)S(1)}, f32[16,1024]{1,0:T(8,128)S(1)}, u32[]{:S(2)}, u32[]{:S(2)}) collective-permute-start(f32[16,1024]{1,0:T(8,128)S(1)} %shard_map.71), channel_id=1, source_target_pairs={{0,8},{1,9},{2,10},{3,11},{4,12},{5,13},{6,14},{7,15},{8,16},{9,17... | collective-permute-start | bytes 196616 | tf_op jit(solution)/shard_map/ppermute | solution.py:291
  38.0 4.1 %collective-permute-start.12 = (f32[16,1024]{1,0:T(8,128)S(1)}, f32[16,1024]{1,0:T(8,128)S(1)}, u32[]{:S(2)}, u32[]{:S(2)}) collective-permute-start(f32[16,1024]{1,0:T(8,128)S(1)} %shard_map.71), channel_id=1, source_target_pairs={{0,16},{1,17},{2,18},{3,19},{4,20},{5,21},{6,22},{7,23},{8,24},{9,... | collective-permute-start | bytes 196616 | tf_op jit(solution)/shard_map/ppermute | solution.py:291
  42.2 1.3 %collective-permute-start.13 = (f32[16,1024]{1,0:T(8,128)S(1)}, f32[16,1024]{1,0:T(8,128)S(1)}, u32[]{:S(2)}, u32[]{:S(2)}) collective-permute-start(f32[16,1024]{1,0:T(8,128)S(1)} %shard_map.71), channel_id=1, source_target_pairs={{0,24},{1,25},{2,26},{3,27},{4,28},{5,29},{6,30},{7,31}} | collective-permute-start | bytes 196616 | tf_op jit(solution)/shard_map/ppermute | solution.py:291
  43.5 2.0 %shard_map.69.refs_4_ = f32[2,512,128]{2,1,0:T(8,128)S(1)} custom-call(s32[11]{0:T(128)S(1)} %stack.47.info_ref, bf16[128,1024]{1,0:T(8,128)(2,1)S(1)} %get-tuple-element.40.refs_0_, bf16[128,1024]{1,0:T(8,128)(2,1)S(1)} %collective-permute-done.2.refs_1_, bf16[128,1024]{1,0:T(8,128)(2,1)S(1)} %collective-permute-done.3.refs_2_, ...), custom_call_target="tpu_custom_call" | custom-call | flops 330000000 | bytes 1080000 | tf_op jit(solution)/shard_map/pallas_call | solution.py:27
  45.4 2.0 %shard_map.70.refs_4_ = f32[2,512,128]{2,1,0:T(8,128)S(1)} custom-call(s32[11]{0:T(128)S(1)} %stack.47.info_ref, bf16[128,1024]{1,0:T(8,128)(2,1)S(1)} %get-tuple-element.40.refs_0_, bf16[128,1024]{1,0:T(8,128)(2,1)S(1)} %collective-permute-done.2.refs_1_, bf16[128,1024]{1,0:T(8,128)(2,1)S(1)} %collective-permute-done.3.refs_2_, ...), custom_call_target="tpu_custom_call" | custom-call | flops 330000000 | bytes 1080000 | tf_op jit(solution)/shard_map/pallas_call | solution.py:27
  47.4 0.7 collective-permute-done.14.refs_5_
  48.1 0.9 %collective-permute-start.16 = (bf16[128,1024]{1,0:T(8,128)(2,1)S(1)}, bf16[128,1024]{1,0:T(8,128)(2,1)S(1)}, u32[]{:S(2)}, u32[]{:S(2)}) collective-permute-start(bf16[128,1024]{1,0:T(8,128)(2,1)S(1)} %get-tuple-element.74), channel_id=1, source_target_pairs={{0,4},{1,5},{2,6},{3,7},{4,0},{5,1},{6,2},{7,3},{8,12},{9,13},{10,... | collective-permute-start | bytes 786440 | tf_op jit(solution)/shard_map/ppermute | solution.py:286
  49.0 0.0 collective-permute-done.11.refs_9_
  49.0 0.0 collective-permute-done.12.refs_10_
  49.0 0.6 collective-permute-done.13.refs_11_
  49.6 1.3 %shard_map.72.refs_0_ = bf16[2,512,128]{2,1,0:T(8,128)(2,1)S(1)} custom-call(s32[11]{0:T(128)S(1)} %stack.47.info_ref, bf16[128,1024]{1,0:T(8,128)(2,1)S(1)} %get-tuple-element.54.refs_0_, bf16[128,1024]{1,0:T(8,128)(2,1)S(1)} %collective-permute-done.7.refs_1_, bf16[128,1024]{1,0:T(8,128)(2,1)S(1)} %collective-permute-done.8.refs_2_, ...), custom_call_target="tpu_custom_call" | custom-call | flops 550000000 | bytes 1800000 | tf_op jit(solution)/shard_map/pallas_call | solution.py:27
  50.9 0.0 copy-start.2
  50.9 0.9 %collective-permute-start.19 = (bf16[128,1024]{1,0:T(8,128)(2,1)S(1)}, bf16[128,1024]{1,0:T(8,128)(2,1)S(1)}, u32[]{:S(2)}, u32[]{:S(2)}) collective-permute-start(bf16[128,1024]{1,0:T(8,128)(2,1)S(1)} %get-tuple-element.73), channel_id=1, source_target_pairs={{0,4},{1,5},{2,6},{3,7},{4,0},{5,1},{6,2},{7,3},{8,12},{9,13},{10,... | collective-permute-start | bytes 786440 | tf_op jit(solution)/shard_map/ppermute | solution.py:286
  51.8 1.3 %shard_map.73.refs_1_ = bf16[2,512,128]{2,1,0:T(8,128)(2,1)S(1)} custom-call(s32[11]{0:T(128)S(1)} %stack.47.info_ref, bf16[128,1024]{1,0:T(8,128)(2,1)S(1)} %get-tuple-element.54.refs_0_, bf16[128,1024]{1,0:T(8,128)(2,1)S(1)} %collective-permute-done.7.refs_1_, bf16[128,1024]{1,0:T(8,128)(2,1)S(1)} %collective-permute-done.8.refs_2_, ...), custom_call_target="tpu_custom_call" | custom-call | flops 550000000 | bytes 1800000 | tf_op jit(solution)/shard_map/pallas_call | solution.py:27
  53.0 1.3 %shard_map.74.refs_2_ = bf16[2,512,128]{2,1,0:T(8,128)(2,1)S(1)} custom-call(s32[11]{0:T(128)S(1)} %stack.47.info_ref, bf16[128,1024]{1,0:T(8,128)(2,1)S(1)} %get-tuple-element.54.refs_0_, bf16[128,1024]{1,0:T(8,128)(2,1)S(1)} %collective-permute-done.7.refs_1_, bf16[128,1024]{1,0:T(8,128)(2,1)S(1)} %collective-permute-done.8.refs_2_, ...), custom_call_target="tpu_custom_call" | custom-call | flops 550000000 | bytes 1800000 | tf_op jit(solution)/shard_map/pallas_call | solution.py:27
  54.3 1.3 %shard_map.75.refs_3_ = bf16[2,512,128]{2,1,0:T(8,128)(2,1)S(1)} custom-call(s32[11]{0:T(128)S(1)} %stack.47.info_ref, bf16[128,1024]{1,0:T(8,128)(2,1)S(1)} %get-tuple-element.54.refs_0_, bf16[128,1024]{1,0:T(8,128)(2,1)S(1)} %collective-permute-done.7.refs_1_, bf16[128,1024]{1,0:T(8,128)(2,1)S(1)} %collective-permute-done.8.refs_2_, ...), custom_call_target="tpu_custom_call" | custom-call | flops 550000000 | bytes 1800000 | tf_op jit(solution)/shard_map/pallas_call | solution.py:27
  55.6 2.4 %shard_map.76.refs_4_ = f32[512,2048]{1,0:T(8,128)S(1)} custom-call(s32[11]{0:T(128)S(1)} %stack.47.info_ref, bf16[2,512,128]{2,1,0:T(8,128)(2,1)S(1)} %shard_map.72.refs_0_, bf16[2,512,128]{2,1,0:T(8,128)(2,1)S(1)} %shard_map.73.refs_1_, bf16[2,512,128]{2,1,0:T(8,128)(2,1)S(1)} %shard_map.74.refs_2_, bf16[2,512,128]{2,1,0:T(8,128)(2,1)S(1)} %shard_map.75.refs_3_, ...), custom_call_target="tpu_custom_call" | custom-call | flops 1100000000 | bytes 3600000 | tf_op jit(solution)/shard_map/pallas_call | solution.py:27
  57.9 1.1 %shard_map.77 = (f32[256,1024]{1,0:T(8,128)S(1)}, bf16[256,1024]{1,0:T(8,128)(2,1)S(1)}) custom-call(s32[11]{0:T(128)S(1)} %stack.47.info_ref, bf16[2,512,128]{2,1,0:T(8,128)(2,1)S(1)} %shard_map.72.refs_0_, bf16[2,512,128]{2,1,0:T(8,128)(2,1)S(1)} %shard_map.73.refs_1_, bf16[2,512,128]{2,1,0:T(8,128)(2,1)S(1)} %shard_map.74.refs_2_, ...), custom_call_target="tpu_custom_call" | custom-call | flops 330000000 | bytes 1080000 | tf_op jit(solution)/shard_map/pallas_call | solution.py:27
  59.0 0.1 collective-permute-start.17
  59.1 2.4 %collective-permute-done.19.refs_6_ = bf16[128,1024]{1,0:T(8,128)(2,1)S(1)} collective-permute-done((bf16[128,1024]{1,0:T(8,128)(2,1)S(1)}, bf16[128,1024]{1,0:T(8,128)(2,1)S(1)}, u32[]{:S(2)}, u32[]{:S(2)}) %collective-permute-start.19) | collective-permute-done | bytes 262176 | tf_op jit(solution)/shard_map/ppermute | solution.py:286
  61.5 1.1 %shard_map.79 = (f32[256,1024]{1,0:T(8,128)S(1)}, bf16[256,1024]{1,0:T(8,128)(2,1)S(1)}) custom-call(s32[11]{0:T(128)S(1)} %stack.47.info_ref, bf16[2,512,128]{2,1,0:T(8,128)(2,1)S(1)} %shard_map.72.refs_0_, bf16[2,512,128]{2,1,0:T(8,128)(2,1)S(1)} %shard_map.73.refs_1_, bf16[2,512,128]{2,1,0:T(8,128)(2,1)S(1)} %shard_map.74.refs_2_, ...), custom_call_target="tpu_custom_call" | custom-call | flops 330000000 | bytes 1080000 | tf_op jit(solution)/shard_map/pallas_call | solution.py:27
  62.6 0.1 collective-permute-start.20
  62.7 0.6 shard_map.78
  63.4 1.8 %collective-permute-start.18 = (bf16[128,1024]{1,0:T(8,128)(2,1)S(1)}, bf16[128,1024]{1,0:T(8,128)(2,1)S(1)}, u32[]{:S(2)}, u32[]{:S(2)}) collective-permute-start(bf16[128,1024]{1,0:T(8,128)(2,1)S(1)} %get-tuple-element.68), channel_id=1, source_target_pairs={{0,2},{1,3},{2,0},{3,1},{4,6},{5,7},{6,4},{7,5},{8,10},{9,11},{10,... | collective-permute-start | bytes 786440 | tf_op jit(solution)/shard_map/ppermute | solution.py:286
  65.2 0.0 collective-permute-done.20.got_ref
  65.2 0.6 shard_map.80
  65.8 1.2 %collective-permute-start.21 = (bf16[128,1024]{1,0:T(8,128)(2,1)S(1)}, bf16[128,1024]{1,0:T(8,128)(2,1)S(1)}, u32[]{:S(2)}, u32[]{:S(2)}) collective-permute-start(bf16[128,1024]{1,0:T(8,128)(2,1)S(1)} %get-tuple-element.72), channel_id=1, source_target_pairs={{0,2},{1,3},{2,0},{3,1},{4,6},{5,7},{6,4},{7,5},{8,10},{9,11},{10,... | collective-permute-start | bytes 786440 | tf_op jit(solution)/shard_map/ppermute | solution.py:286
  67.1 5.4 %collective-permute-done.18.refs_1_ = bf16[128,1024]{1,0:T(8,128)(2,1)S(1)} collective-permute-done((bf16[128,1024]{1,0:T(8,128)(2,1)S(1)}, bf16[128,1024]{1,0:T(8,128)(2,1)S(1)}, u32[]{:S(2)}, u32[]{:S(2)}) %collective-permute-start.18) | collective-permute-done | bytes 262176 | tf_op jit(solution)/shard_map/ppermute | solution.py:286
  72.5 5.2 %collective-permute-done.21.refs_3_ = bf16[128,1024]{1,0:T(8,128)(2,1)S(1)} collective-permute-done((bf16[128,1024]{1,0:T(8,128)(2,1)S(1)}, bf16[128,1024]{1,0:T(8,128)(2,1)S(1)}, u32[]{:S(2)}, u32[]{:S(2)}) %collective-permute-start.21) | collective-permute-done | bytes 262176 | tf_op jit(solution)/shard_map/ppermute | solution.py:286
  77.8 1.4 %shard_map.81 = bf16[128,2048]{1,0:T(8,128)(2,1)} custom-call(s32[11]{0:T(128)S(1)} %stack.47.info_ref, f32[128,1024]{1,0:T(8,128)S(1)} %get-tuple-element.67.refs_0_, bf16[128,1024]{1,0:T(8,128)(2,1)S(1)} %collective-permute-done.18.refs_1_, f32[128,1024]{1,0:T(8,128)S(1)} %get-tuple-element.71.refs_2_, bf16[128,1024]{1,0:T(8,128)(2,1)S(1)} %collective-permute-done.21.refs_3_), custom_call_target="tpu_custom_call" | custom-call | tf_op jit(solution)/shard_map/pallas_call | solution.py:27
  (13 shorter events, 0.1 us)
Async XLA Ops:
  0.0 17.2 %collective-permute-start = (bf16[128,2048]{1,0:T(8,128)(2,1)}, bf16[128,2048]{1,0:T(8,128)(2,1)S(1)}, u32[]{:S(2)}, u32[]{:S(2)}) collective-permute-start(bf16[128,2048]{1,0:T(8,128)(2,1)} %refs_4_.1), channel_id=1, source_target_pairs={{0,8},{1,9},{2,10},{3,11},{4,12},{5,13},{6,14},{7,15},{8,16},{9,17... | collective-permute-start | bytes 1572872 | tf_op jit(solution)/shard_map/ppermute | solution.py:291
  3.0 14.2 %collective-permute-start.1 = (bf16[128,2048]{1,0:T(8,128)(2,1)}, bf16[128,2048]{1,0:T(8,128)(2,1)S(1)}, u32[]{:S(2)}, u32[]{:S(2)}) collective-permute-start(bf16[128,2048]{1,0:T(8,128)(2,1)} %refs_4_.1), channel_id=1, source_target_pairs={{0,4},{1,5},{2,6},{3,7},{4,0},{5,1},{6,2},{7,3},{8,12},{9,13},{10,... | collective-permute-start | bytes 1572872 | tf_op jit(solution)/shard_map/ppermute | solution.py:286
  4.6 1.2 %copy-start = (bf16[128,4096]{1,0:T(8,128)(2,1)S(1)}, bf16[128,4096]{1,0:T(8,128)(2,1)}, u32[]{:S(2)}) copy-start(bf16[128,4096]{1,0:T(8,128)(2,1)} %refs_0_.2) | copy-start | bytes 3145732
  6.9 7.8 %collective-permute-start.2 = (bf16[128,1024]{1,0:T(8,128)(2,1)S(1)}, bf16[128,1024]{1,0:T(8,128)(2,1)S(1)}, u32[]{:S(2)}, u32[]{:S(2)}) collective-permute-start(bf16[128,1024]{1,0:T(8,128)(2,1)S(1)} %get-tuple-element.41), channel_id=1, source_target_pairs={{0,1},{1,0},{2,3},{3,2},{4,5},{5,4},{6,7},{7,6},{8,9},{9,8},{10,11... | collective-permute-start | bytes 786440 | tf_op jit(solution)/shard_map/ppermute | solution.py:286
  7.0 12.7 %collective-permute-start.4 = (bf16[128,1024]{1,0:T(8,128)(2,1)S(1)}, bf16[128,1024]{1,0:T(8,128)(2,1)S(1)}, u32[]{:S(2)}, u32[]{:S(2)}) collective-permute-start(bf16[128,1024]{1,0:T(8,128)(2,1)S(1)} %get-tuple-element.43), channel_id=1, source_target_pairs={{0,3},{1,2},{2,1},{3,0},{4,7},{5,6},{6,5},{7,4},{8,11},{9,10},{10,... | collective-permute-start | bytes 786440 | tf_op jit(solution)/shard_map/ppermute | solution.py:286
  8.6 13.2 %collective-permute-start.3 = (bf16[128,1024]{1,0:T(8,128)(2,1)S(1)}, bf16[128,1024]{1,0:T(8,128)(2,1)S(1)}, u32[]{:S(2)}, u32[]{:S(2)}) collective-permute-start(bf16[128,1024]{1,0:T(8,128)(2,1)S(1)} %get-tuple-element.42), channel_id=1, source_target_pairs={{0,2},{1,3},{2,0},{3,1},{4,6},{5,7},{6,4},{7,5},{8,10},{9,11},{10,... | collective-permute-start | bytes 786440 | tf_op jit(solution)/shard_map/ppermute | solution.py:286
  9.2 1.2 %copy-start.1 = (bf16[128,4096]{1,0:T(8,128)(2,1)S(1)}, bf16[128,4096]{1,0:T(8,128)(2,1)}, u32[]{:S(2)}) copy-start(bf16[128,4096]{1,0:T(8,128)(2,1)} %refs_0_.3) | copy-start | bytes 3145732
  10.4 0.9 %copy-start.3 = (f32[4096,16]{0,1:T(8,128)S(1)}, f32[4096,16]{0,1:T(8,128)}, u32[]{:S(2)}) copy-start(f32[4096,16]{0,1:T(8,128)} %param.8) | copy-start | bytes 786436
  11.3 0.9 %copy-start.4 = (f32[4096,16]{0,1:T(8,128)S(1)}, f32[4096,16]{0,1:T(8,128)}, u32[]{:S(2)}) copy-start(f32[4096,16]{0,1:T(8,128)} %param.9) | copy-start | bytes 786436
  12.3 0.7 copy-start.5
  14.7 10.7 %collective-permute-start.7 = (bf16[128,1024]{1,0:T(8,128)(2,1)S(1)}, bf16[128,1024]{1,0:T(8,128)(2,1)S(1)}, u32[]{:S(2)}, u32[]{:S(2)}) collective-permute-start(bf16[128,1024]{1,0:T(8,128)(2,1)S(1)} %get-tuple-element.55), channel_id=1, source_target_pairs={{0,1},{1,0},{2,3},{3,2},{4,5},{5,4},{6,7},{7,6},{8,9},{9,8},{10,11... | collective-permute-start | bytes 786440 | tf_op jit(solution)/shard_map/ppermute | solution.py:286
  17.2 14.9 %collective-permute-start.5 = (bf16[128,2048]{1,0:T(8,128)(2,1)S(1)}, bf16[128,2048]{1,0:T(8,128)(2,1)S(1)}, u32[]{:S(2)}, u32[]{:S(2)}) collective-permute-start(bf16[128,2048]{1,0:T(8,128)(2,1)S(1)} %collective-permute-done.refs_6_), channel_id=1, source_target_pairs={{0,8},{1,9},{2,10},{3,11},{4,12},{5,13},{6,14},{7,15},{8,16},{9,17... | collective-permute-start | bytes 1572872 | tf_op jit(solution)/shard_map/ppermute | solution.py:291
  18.2 13.9 %collective-permute-start.6 = (bf16[128,2048]{1,0:T(8,128)(2,1)S(1)}, bf16[128,2048]{1,0:T(8,128)(2,1)S(1)}, u32[]{:S(2)}, u32[]{:S(2)}) collective-permute-start(bf16[128,2048]{1,0:T(8,128)(2,1)S(1)} %collective-permute-done.refs_6_), channel_id=1, source_target_pairs={{0,4},{1,5},{2,6},{3,7},{4,0},{5,1},{6,2},{7,3},{8,12},{9,13},{10,... | collective-permute-start | bytes 1572872 | tf_op jit(solution)/shard_map/ppermute | solution.py:286
  19.7 10.3 %collective-permute-start.8 = (bf16[128,1024]{1,0:T(8,128)(2,1)S(1)}, bf16[128,1024]{1,0:T(8,128)(2,1)S(1)}, u32[]{:S(2)}, u32[]{:S(2)}) collective-permute-start(bf16[128,1024]{1,0:T(8,128)(2,1)S(1)} %get-tuple-element.57), channel_id=1, source_target_pairs={{0,2},{1,3},{2,0},{3,1},{4,6},{5,7},{6,4},{7,5},{8,10},{9,11},{10,... | collective-permute-start | bytes 786440 | tf_op jit(solution)/shard_map/ppermute | solution.py:286
  21.9 9.7 %collective-permute-start.9 = (bf16[128,1024]{1,0:T(8,128)(2,1)S(1)}, bf16[128,1024]{1,0:T(8,128)(2,1)S(1)}, u32[]{:S(2)}, u32[]{:S(2)}) collective-permute-start(bf16[128,1024]{1,0:T(8,128)(2,1)S(1)} %get-tuple-element.59), channel_id=1, source_target_pairs={{0,3},{1,2},{2,1},{3,0},{4,7},{5,6},{6,5},{7,4},{8,11},{9,10},{10,... | collective-permute-start | bytes 786440 | tf_op jit(solution)/shard_map/ppermute | solution.py:286
  25.5 6.4 %collective-permute-start.10 = (f32[16,1024]{1,0:T(8,128)S(1)}, f32[16,1024]{1,0:T(8,128)S(1)}, u32[]{:S(2)}, u32[]{:S(2)}) collective-permute-start(f32[16,1024]{1,0:T(8,128)S(1)} %get-tuple-element.61.end_ref), channel_id=1, source_target_pairs={{0,4},{1,5},{2,6},{3,7},{4,0},{5,1},{6,2},{7,3},{8,12},{9,13},{10,... | collective-permute-start | bytes 196616 | tf_op jit(solution)/shard_map/ppermute | solution.py:286
  32.1 16.0 %collective-permute-start.14 = (bf16[128,2048]{1,0:T(8,128)(2,1)S(1)}, bf16[128,2048]{1,0:T(8,128)(2,1)S(1)}, u32[]{:S(2)}, u32[]{:S(2)}) collective-permute-start(bf16[128,2048]{1,0:T(8,128)(2,1)S(1)} %collective-permute-done.5.refs_8_), channel_id=1, source_target_pairs={{0,8},{1,9},{2,10},{3,11},{4,12},{5,13},{6,14},{7,15},{8,16},{9,17... | collective-permute-start | bytes 1572872 | tf_op jit(solution)/shard_map/ppermute | solution.py:291
  33.4 14.6 %collective-permute-start.15 = (bf16[128,2048]{1,0:T(8,128)(2,1)S(1)}, bf16[128,2048]{1,0:T(8,128)(2,1)S(1)}, u32[]{:S(2)}, u32[]{:S(2)}) collective-permute-start(bf16[128,2048]{1,0:T(8,128)(2,1)S(1)} %collective-permute-done.5.refs_8_), channel_id=1, source_target_pairs={{0,4},{1,5},{2,6},{3,7},{4,0},{5,1},{6,2},{7,3},{8,12},{9,13},{10,... | collective-permute-start | bytes 1572872 | tf_op jit(solution)/shard_map/ppermute | solution.py:286
  35.5 13.5 %collective-permute-start.11 = (f32[16,1024]{1,0:T(8,128)S(1)}, f32[16,1024]{1,0:T(8,128)S(1)}, u32[]{:S(2)}, u32[]{:S(2)}) collective-permute-start(f32[16,1024]{1,0:T(8,128)S(1)} %shard_map.71), channel_id=1, source_target_pairs={{0,8},{1,9},{2,10},{3,11},{4,12},{5,13},{6,14},{7,15},{8,16},{9,17... | collective-permute-start | bytes 196616 | tf_op jit(solution)/shard_map/ppermute | solution.py:291
  38.0 11.0 %collective-permute-start.12 = (f32[16,1024]{1,0:T(8,128)S(1)}, f32[16,1024]{1,0:T(8,128)S(1)}, u32[]{:S(2)}, u32[]{:S(2)}) collective-permute-start(f32[16,1024]{1,0:T(8,128)S(1)} %shard_map.71), channel_id=1, source_target_pairs={{0,16},{1,17},{2,18},{3,19},{4,20},{5,21},{6,22},{7,23},{8,24},{9,... | collective-permute-start | bytes 196616 | tf_op jit(solution)/shard_map/ppermute | solution.py:291
  42.2 7.5 %collective-permute-start.13 = (f32[16,1024]{1,0:T(8,128)S(1)}, f32[16,1024]{1,0:T(8,128)S(1)}, u32[]{:S(2)}, u32[]{:S(2)}) collective-permute-start(f32[16,1024]{1,0:T(8,128)S(1)} %shard_map.71), channel_id=1, source_target_pairs={{0,24},{1,25},{2,26},{3,27},{4,28},{5,29},{6,30},{7,31}} | collective-permute-start | bytes 196616 | tf_op jit(solution)/shard_map/ppermute | solution.py:291
  48.1 9.8 %collective-permute-start.16 = (bf16[128,1024]{1,0:T(8,128)(2,1)S(1)}, bf16[128,1024]{1,0:T(8,128)(2,1)S(1)}, u32[]{:S(2)}, u32[]{:S(2)}) collective-permute-start(bf16[128,1024]{1,0:T(8,128)(2,1)S(1)} %get-tuple-element.74), channel_id=1, source_target_pairs={{0,4},{1,5},{2,6},{3,7},{4,0},{5,1},{6,2},{7,3},{8,12},{9,13},{10,... | collective-permute-start | bytes 786440 | tf_op jit(solution)/shard_map/ppermute | solution.py:286
  50.9 4.7 %copy-start.2 = (bf16[128,2048]{1,0:T(8,128)(2,1)S(1)}, bf16[128,2048]{1,0:T(8,128)(2,1)}, u32[]{:S(2)}) copy-start(bf16[128,2048]{1,0:T(8,128)(2,1)} %refs_4_.1) | copy-start | bytes 1572868
  50.9 10.6 %collective-permute-start.19 = (bf16[128,1024]{1,0:T(8,128)(2,1)S(1)}, bf16[128,1024]{1,0:T(8,128)(2,1)S(1)}, u32[]{:S(2)}, u32[]{:S(2)}) collective-permute-start(bf16[128,1024]{1,0:T(8,128)(2,1)S(1)} %get-tuple-element.73), channel_id=1, source_target_pairs={{0,4},{1,5},{2,6},{3,7},{4,0},{5,1},{6,2},{7,3},{8,12},{9,13},{10,... | collective-permute-start | bytes 786440 | tf_op jit(solution)/shard_map/ppermute | solution.py:286
  59.0 3.7 %collective-permute-start.17 = (bf16[256,1024]{1,0:T(8,128)(2,1)S(1)}, bf16[256,1024]{1,0:T(8,128)(2,1)S(1)}, u32[]{:S(2)}, u32[]{:S(2)}) collective-permute-start(bf16[256,1024]{1,0:T(8,128)(2,1)S(1)} %get-tuple-element.66), channel_id=1, source_target_pairs={{0,1},{1,0},{2,3},{3,2},{4,5},{5,4},{6,7},{7,6},{8,9},{9,8},{10,11... | collective-permute-start | bytes 1572872 | tf_op jit(solution)/shard_map/ppermute | solution.py:286
  62.6 2.6 %collective-permute-start.20 = (bf16[256,1024]{1,0:T(8,128)(2,1)S(1)}, bf16[256,1024]{1,0:T(8,128)(2,1)S(1)}, u32[]{:S(2)}, u32[]{:S(2)}) collective-permute-start(bf16[256,1024]{1,0:T(8,128)(2,1)S(1)} %get-tuple-element.70), channel_id=1, source_target_pairs={{0,1},{1,0},{2,3},{3,2},{4,5},{5,4},{6,7},{7,6},{8,9},{9,8},{10,11... | collective-permute-start | bytes 1572872 | tf_op jit(solution)/shard_map/ppermute | solution.py:286
  63.4 9.2 %collective-permute-start.18 = (bf16[128,1024]{1,0:T(8,128)(2,1)S(1)}, bf16[128,1024]{1,0:T(8,128)(2,1)S(1)}, u32[]{:S(2)}, u32[]{:S(2)}) collective-permute-start(bf16[128,1024]{1,0:T(8,128)(2,1)S(1)} %get-tuple-element.68), channel_id=1, source_target_pairs={{0,2},{1,3},{2,0},{3,1},{4,6},{5,7},{6,4},{7,5},{8,10},{9,11},{10,... | collective-permute-start | bytes 786440 | tf_op jit(solution)/shard_map/ppermute | solution.py:286
  65.8 11.9 %collective-permute-start.21 = (bf16[128,1024]{1,0:T(8,128)(2,1)S(1)}, bf16[128,1024]{1,0:T(8,128)(2,1)S(1)}, u32[]{:S(2)}, u32[]{:S(2)}) collective-permute-start(bf16[128,1024]{1,0:T(8,128)(2,1)S(1)} %get-tuple-element.72), channel_id=1, source_target_pairs={{0,2},{1,3},{2,0},{3,1},{4,6},{5,7},{6,4},{7,5},{8,10},{9,11},{10,... | collective-permute-start | bytes 786440 | tf_op jit(solution)/shard_map/ppermute | solution.py:286

commit v6 on v5

--- a/solution.py
+++ b/solution.py
@@ -11,7 +11,6 @@
 LANES = 128
 CHUNKS = 8
 TEAM = 4
-LAST_PARTS = 2
 VMEM_LIMIT = 8 * 1024 * 1024
 
 f32 = jnp.float32
@@ -223,32 +222,26 @@
     per = gated[0].shape[0]
     wide = into.shape[1]
     step = min(wide, 256)
-    for slot in range(0, len(weights), 2):
-        if in_slots:
-            left = [gated[n // per][n % per] for n in (first + slot, first + slot + 1)]
-        else:
-            left = [gated[0][info_ref[3 + n]] for n in (first + slot, first + slot + 1)]
-        left = jnp.concatenate(left, axis=1)
-        for col in range(0, wide, step):
-            right = jnp.concatenate([ref[:, col : col + step] for ref in weights[slot : slot + 2]], axis=0)
-            term = jnp.dot(left, right, preferred_element_type=f32)
-            cols = slice(col, col + step)
-            start = before if slot == 0 else into
-            into[:, cols] = term if start is None else start[:, cols] + term
-
-
-def early_kernel(pieces, in_slots, info_ref, *refs):
-    product(pieces, in_slots, 0, info_ref, refs[:pieces], refs[pieces:-1], refs[-1], None)
-
-
-def project_kernel(pieces, in_slots, slots, at, info_ref, *refs):
-    gated, (early_ref, near_ref, away_ref) = refs[:pieces], refs[pieces : pieces + 3]
+    slots = range(first, first + len(weights))
+    if in_slots:
+        left = [gated[slot // per][slot % per] for slot in slots]
+    else:
+        left = [gated[0][info_ref[3 + slot]] for slot in slots]
+    left = jnp.concatenate(left, axis=1)
+    for col in range(0, wide, step):
+        cols = slice(col, col + step)
+        right = jnp.concatenate([ref[:, cols] for ref in weights], axis=0)
+        total = jnp.dot(left, right, preferred_element_type=f32)
+        into[:, cols] = total if before is None else before[:, cols] + total
+
+
+def project_kernel(pieces, in_slots, at, info_ref, *refs):
+    gated, weights = refs[:pieces], refs[pieces:-3]
     kept_ref, sent_ref, total = refs[-3:]
     core = info_ref[2]
     rows, wide = kept_ref.shape[0] // 2, kept_ref.shape[1]
-    cols = slice(at, at + wide)
-    weights = [near_ref.at[:, cols], away_ref]
-    product(pieces, in_slots, slots - 2, info_ref, gated, weights, total, early_ref.at[:, cols])
+    weights = [ref.at[:, at : at + wide] for ref in weights[:-1]] + [weights[-1]]
+    product(pieces, in_slots, 0, info_ref, gated, weights, total, None)
     for across in range(2):
         here = slice(across * rows, (across + 1) * rows)
         for which, out in enumerate((kept_ref, sent_ref)):
@@ -299,9 +292,6 @@
     order_of = groups if in_slots else list(range(tiles))
     info = jnp.stack([jnp.int32(n) for n in [me, y, core] + order_of])
     group_info = info if in_slots else jnp.stack([jnp.int32(n) for n in [me, y, core] + groups])
-
-    def share_out(shares):
-        return [shares[0]] + [swap(shares[step], step) for step in range(1, TEAM)]
 
     def share_out(shares):
         return [shares[0]] + [swap(shares[step], step) for step in range(1, TEAM)]
@@ -372,9 +362,9 @@
         for lag, (_, state) in zip(lags, far[-len(lags) :]):
             held = held + jnp.exp(-2.0 * span * lag * rates) * state
         gap *= 4
-    wide = features // LAST_PARTS
-    block = tied(weights[last], weights_away[-1], local[-1])
-    finals = [swap(block[:, part * wide : (part + 1) * wide], TEAM) for part in range(LAST_PARTS)]
+    wide = features // 2
+    mine, theirs = lax.optimization_barrier((weights[last], weights_away[-1], local[-1]))[:2]
+    finals = [swap(mine[:, :wide], TEAM), up(theirs[:, wide:], 1, True)]
 
     tables = [pltpu.VMEM((order, 8, LANES), f32)] * 2
     gated = [
@@ -392,19 +382,15 @@
         gated = gated.reshape(TEAM * rows, width // (TEAM * depth), depth).transpose(1, 0, 2)
         gated = [gated]
 
-    early = call(
-        functools.partial(early_kernel, len(gated), in_slots),
-        jax.ShapeDtypeStruct((TEAM * rows, features), f32),
-        micros=1.0,
-    )(group_info, *gated, *[ref for pair in zip(weights, weights_away) for ref in pair])
+    slots = [ref for pair in zip(weights, weights_away) for ref in pair] + [weights[last]]
     finished, joined = [], []
     for part, final in enumerate(finals):
         kept, sent = call(
-            functools.partial(project_kernel, len(gated), in_slots, 2 * heights, part * wide),
+            functools.partial(project_kernel, len(gated), in_slots, part * wide),
             [jax.ShapeDtypeStruct((2 * rows, wide), dtype) for dtype in (f32, bf16)],
             [pltpu.VMEM((TEAM * rows, wide), f32)],
-            micros=0.3,
-        )(group_info, *gated, early, weights[last], final)
+            micros=1.0,
+        )(group_info, *gated, *slots, final)
         mine_sum, away_sum = call(
             join_kernel,
             [jax.ShapeDtypeStruct((rows, wide), f32), jax.ShapeDtypeStruct((rows, wide), bf16)],

time: 79.5 us -> 76.6 us (0.964)
  local copies, waits for them, and re-layouts: 5.19 us -> 3.26 us
  Pallas kernels: 27 us -> 26.2 us
    unnamed x12, local copies, waits for them, and re-layouts: 5.07 us -> 3.14 us
    ppermute x16 -> x15, waiting for transfers between devices: 15.6 us -> 13.9 us  [swap(): return lax.ppermute(value, 'seq', [(i, i ^ bit) for i in range(count)])]
    ppermute x6 -> x7, waiting for transfers between devices: 3.93 us -> 5.35 us  [up(): return lax.ppermute(value, 'seq', pairs)]
    ppermute x6 -> x7, starting transfers between devices: 13.3 us -> 14.2 us  [up(): return lax.ppermute(value, 'seq', pairs)]
    pallas_call x16 -> x15, Pallas kernels: 24.2 us -> 23.5 us  [run(): pl.pallas_call(kernel, out_shape=out_shape, in_specs=[pl.BlockSpec(memory...]
    ppermute x16 -> x15, starting transfers between devices: 13.9 us -> 13.2 us  [swap(): return lax.ppermute(value, 'seq', [(i, i ^ bit) for i in range(count)])]
where the time goes in v6:
time: 76.6 us; the launch traced here: 76.4 us
  starting transfers between devices  27.4 us (36%)
  Pallas kernels  26.2 us (34%)
  waiting for transfers between devices  19.2 us (25%)
  local copies, waits for them, and re-layouts  3.26 us (4%)
    pallas_call x15, Pallas kernels, run(): pl.pallas_call(kernel, out_shape=out_shape, in_specs=[pl.BlockSpec(memory...  23.5 us
    ppermute x7, starting transfers between devices, up(): return lax.ppermute(value, 'seq', pairs)  14.2 us
    ppermute x15, waiting for transfers between devices, swap(): return lax.ppermute(value, 'seq', [(i, i ^ bit) for i in range(count)])  13.9 us
    ppermute x15, starting transfers between devices, swap(): return lax.ppermute(value, 'seq', [(i, i ^ bit) for i in range(count)])  13.2 us
    ppermute x7, waiting for transfers between devices, up(): return lax.ppermute(value, 'seq', pairs)  5.35 us
    unnamed x12, local copies, waits for them, and re-layouts  3.14 us
    pallas_call x2, Pallas kernels, deal(): pl.pallas_call(functools.partial(deal_kernel, team, depth, plan), out_sha...  2.78 us
  transfers between devices with their start and end apart: 22, of which 10 were waited for; matrix products, arithmetic and copies ran while one was open for 0% of the time, Pallas kernels for 32%

profile of v6, /device:TPU:0, one launch (start us, length us, event | category | flops | bytes accessed | tf_op | source)
XLA Modules:
  0.0 76.4 jit_solution(2717051421926879588)
XLA Ops:
  0.0 3.0 %collective-permute-start = (bf16[128,2048]{1,0:T(8,128)(2,1)}, bf16[128,2048]{1,0:T(8,128)(2,1)S(1)}, u32[]{:S(2)}, u32[]{:S(2)}) collective-permute-start(bf16[128,2048]{1,0:T(8,128)(2,1)} %refs_4_.3), channel_id=1, source_target_pairs={{0,8},{1,9},{2,10},{3,11},{4,12},{5,13},{6,14},{7,15},{8,16},{9,17... | collective-permute-start | bytes 1572872 | tf_op jit(solution)/shard_map/ppermute | solution.py:284
  3.0 1.5 %collective-permute-start.1 = (bf16[128,2048]{1,0:T(8,128)(2,1)}, bf16[128,2048]{1,0:T(8,128)(2,1)S(1)}, u32[]{:S(2)}, u32[]{:S(2)}) collective-permute-start(bf16[128,2048]{1,0:T(8,128)(2,1)} %refs_4_.3), channel_id=1, source_target_pairs={{0,4},{1,5},{2,6},{3,7},{4,0},{5,1},{6,2},{7,3},{8,12},{9,13},{10,... | collective-permute-start | bytes 1572872 | tf_op jit(solution)/shard_map/ppermute | solution.py:279
  4.5 0.1 stack.47.info_ref
  4.6 1.2 %copy-done.1 = bf16[128,4096]{1,0:T(8,128)(2,1)S(1)} copy-done((bf16[128,4096]{1,0:T(8,128)(2,1)S(1)}, bf16[128,4096]{1,0:T(8,128)(2,1)}, u32[]{:S(2)}) %copy-start.1) | copy-done | bytes 1048600
  5.9 1.1 %shard_map.64 = (bf16[128,1024]{1,0:T(8,128)(2,1)S(1)}, bf16[128,1024]{1,0:T(8,128)(2,1)S(1)}, bf16[128,1024]{1,0:T(8,128)(2,1)S(1)}, bf16[128,1024]{1,0:T(8,128)(2,1)S(1)}) custom-call(s32[11]{0:T(128)S(1)} %stack.47.info_ref, bf16[128,4096]{1,0:T(8,128)(2,1)S(1)} %copy-done.1), custom_call_target="tpu_custom_call" | custom-call | tf_op jit(solution)/shard_map/pallas_call | solution.py:72
  6.9 0.1 collective-permute-start.2
  7.0 1.6 %collective-permute-start.4 = (bf16[128,1024]{1,0:T(8,128)(2,1)S(1)}, bf16[128,1024]{1,0:T(8,128)(2,1)S(1)}, u32[]{:S(2)}, u32[]{:S(2)}) collective-permute-start(bf16[128,1024]{1,0:T(8,128)(2,1)S(1)} %get-tuple-element.44), channel_id=1, source_target_pairs={{0,3},{1,2},{2,1},{3,0},{4,7},{5,6},{6,5},{7,4},{8,11},{9,10},{10,... | collective-permute-start | bytes 786440 | tf_op jit(solution)/shard_map/ppermute | solution.py:279
  8.6 0.5 collective-permute-start.3
  9.2 0.9 %copy-done.3 = f32[4096,16]{0,1:T(8,128)S(1)} copy-done((f32[4096,16]{0,1:T(8,128)S(1)}, f32[4096,16]{0,1:T(8,128)}, u32[]{:S(2)}) %copy-start.3) | copy-done | bytes 262168
  10.1 0.9 %copy-done.4 = f32[4096,16]{0,1:T(8,128)S(1)} copy-done((f32[4096,16]{0,1:T(8,128)S(1)}, f32[4096,16]{0,1:T(8,128)}, u32[]{:S(2)}) %copy-start.4) | copy-done | bytes 262168
  11.1 1.7 %shard_map.65 = (bf16[128,1024]{1,0:T(8,128)(2,1)S(1)}, bf16[128,1024]{1,0:T(8,128)(2,1)S(1)}, bf16[128,1024]{1,0:T(8,128)(2,1)S(1)}, bf16[128,1024]{1,0:T(8,128...) custom-call(s32[11]{0:T(128)S(1)} %stack.47.info_ref, ...), custom_call_target="tpu_custom_call" | custom-call | tf_op jit(solution)/shard_map/pallas_call | solution.py:72
  12.8 0.0 collective-permute-done.2.refs_1_
  12.8 0.1 collective-permute-start.7
  12.9 4.3 %collective-permute-done.refs_6_ = bf16[128,2048]{1,0:T(8,128)(2,1)S(1)} collective-permute-done((bf16[128,2048]{1,0:T(8,128)(2,1)}, bf16[128,2048]{1,0:T(8,128)(2,1)S(1)}, u32[]{:S(2)}, u32[]{:S(2)}) %collective-permute-start) | collective-permute-done | bytes 524320 | tf_op jit(solution)/shard_map/ppermute | solution.py:284
  17.2 0.0 collective-permute-done.1.refs_5_
  17.2 1.0 %collective-permute-start.5 = (bf16[128,2048]{1,0:T(8,128)(2,1)S(1)}, bf16[128,2048]{1,0:T(8,128)(2,1)S(1)}, u32[]{:S(2)}, u32[]{:S(2)}) collective-permute-start(bf16[128,2048]{1,0:T(8,128)(2,1)S(1)} %collective-permute-done.refs_6_), channel_id=1, source_target_pairs={{0,8},{1,9},{2,10},{3,11},{4,12},{5,13},{6,14},{7,15},{8,16},{9,17... | collective-permute-start | bytes 1572872 | tf_op jit(solution)/shard_map/ppermute | solution.py:284
  18.2 1.5 %collective-permute-start.6 = (bf16[128,2048]{1,0:T(8,128)(2,1)S(1)}, bf16[128,2048]{1,0:T(8,128)(2,1)S(1)}, u32[]{:S(2)}, u32[]{:S(2)}) collective-permute-start(bf16[128,2048]{1,0:T(8,128)(2,1)S(1)} %collective-permute-done.refs_6_), channel_id=1, source_target_pairs={{0,4},{1,5},{2,6},{3,7},{4,0},{5,1},{6,2},{7,3},{8,12},{9,13},{10,... | collective-permute-start | bytes 1572872 | tf_op jit(solution)/shard_map/ppermute | solution.py:279
  19.7 0.0 collective-permute-done.4.refs_3_
  19.7 1.5 %collective-permute-start.8 = (bf16[128,1024]{1,0:T(8,128)(2,1)S(1)}, bf16[128,1024]{1,0:T(8,128)(2,1)S(1)}, u32[]{:S(2)}, u32[]{:S(2)}) collective-permute-start(bf16[128,1024]{1,0:T(8,128)(2,1)S(1)} %get-tuple-element.58), channel_id=1, source_target_pairs={{0,2},{1,3},{2,0},{3,1},{4,6},{5,7},{6,4},{7,5},{8,10},{9,11},{10,... | collective-permute-start | bytes 786440 | tf_op jit(solution)/shard_map/ppermute | solution.py:279
  21.2 0.7 collective-permute-done.3.refs_2_
  21.9 0.1 collective-permute-start.9
  22.0 3.5 %shard_map.66 = (f32[8,16,16,128]{3,2,1,0:T(8,128)S(1)}, f32[16,1024]{1,0:T(8,128)S(1)}) custom-call(s32[11]{0:T(128)S(1)} %stack.47.info_ref, bf16[128,1024]{1,0:T(8,128)(2,1)S(1)} %get-tuple-element.41.refs_0_, bf16[128,1024]{1,0:T(8,128)(2,1)S(1)} %collective-permute-done.2.refs_1_, bf16[128,1024]{1,0:T(8,128)(2,1)S(1)} %collective-permute-done.3.refs_2_, ...), custom_call_target="tpu_custom_call" | custom-call | flops 550000000 | bytes 1800000 | tf_op jit(solution)/shard_map/pallas_call | solution.py:26
  25.5 0.0 collective-permute-done.7.refs_1_
  25.5 0.6 collective-permute-start.10
  26.1 2.0 %shard_map.67.refs_4_ = f32[2,512,128]{2,1,0:T(8,128)S(1)} custom-call(s32[11]{0:T(128)S(1)} %stack.47.info_ref, bf16[128,1024]{1,0:T(8,128)(2,1)S(1)} %get-tuple-element.41.refs_0_, bf16[128,1024]{1,0:T(8,128)(2,1)S(1)} %collective-permute-done.2.refs_1_, bf16[128,1024]{1,0:T(8,128)(2,1)S(1)} %collective-permute-done.3.refs_2_, ...), custom_call_target="tpu_custom_call" | custom-call | flops 330000000 | bytes 1080000 | tf_op jit(solution)/shard_map/pallas_call | solution.py:26
  28.1 2.0 %shard_map.68.refs_4_ = f32[2,512,128]{2,1,0:T(8,128)S(1)} custom-call(s32[11]{0:T(128)S(1)} %stack.47.info_ref, bf16[128,1024]{1,0:T(8,128)(2,1)S(1)} %get-tuple-element.41.refs_0_, bf16[128,1024]{1,0:T(8,128)(2,1)S(1)} %collective-permute-done.2.refs_1_, bf16[128,1024]{1,0:T(8,128)(2,1)S(1)} %collective-permute-done.3.refs_2_, ...), custom_call_target="tpu_custom_call" | custom-call | flops 330000000 | bytes 1080000 | tf_op jit(solution)/shard_map/pallas_call | solution.py:26
  30.0 0.0 collective-permute-done.8.refs_2_
  30.0 1.5 %collective-permute-done.9.refs_3_ = bf16[128,1024]{1,0:T(8,128)(2,1)S(1)} collective-permute-done((bf16[128,1024]{1,0:T(8,128)(2,1)S(1)}, bf16[128,1024]{1,0:T(8,128)(2,1)S(1)}, u32[]{:S(2)}, u32[]{:S(2)}) %collective-permute-start.9) | collective-permute-done | bytes 262176 | tf_op jit(solution)/shard_map/ppermute | solution.py:279
  31.6 0.2 collective-permute-done.10.near_ref.refs_8_
  31.8 0.3 collective-permute-done.5.refs_8_
  32.1 0.0 collective-permute-done.6.refs_7_
  32.1 1.3 %collective-permute-start.14 = (bf16[128,2048]{1,0:T(8,128)(2,1)S(1)}, bf16[128,2048]{1,0:T(8,128)(2,1)S(1)}, u32[]{:S(2)}, u32[]{:S(2)}) collective-permute-start(bf16[128,2048]{1,0:T(8,128)(2,1)S(1)} %collective-permute-done.5.refs_8_), channel_id=1, source_target_pairs={{0,8},{1,9},{2,10},{3,11},{4,12},{5,13},{6,14},{7,15},{8,16},{9,17... | collective-permute-start | bytes 1572872 | tf_op jit(solution)/shard_map/ppermute | solution.py:284
  33.4 1.5 %collective-permute-start.15 = (bf16[128,2048]{1,0:T(8,128)(2,1)S(1)}, bf16[128,2048]{1,0:T(8,128)(2,1)S(1)}, u32[]{:S(2)}, u32[]{:S(2)}) collective-permute-start(bf16[128,2048]{1,0:T(8,128)(2,1)S(1)} %collective-permute-done.5.refs_8_), channel_id=1, source_target_pairs={{0,4},{1,5},{2,6},{3,7},{4,0},{5,1},{6,2},{7,3},{8,12},{9,13},{10,... | collective-permute-start | bytes 1572872 | tf_op jit(solution)/shard_map/ppermute | solution.py:279
  34.9 0.6 shard_map.71
  35.5 2.5 %collective-permute-start.11 = (f32[16,1024]{1,0:T(8,128)S(1)}, f32[16,1024]{1,0:T(8,128)S(1)}, u32[]{:S(2)}, u32[]{:S(2)}) collective-permute-start(f32[16,1024]{1,0:T(8,128)S(1)} %shard_map.71), channel_id=1, source_target_pairs={{0,8},{1,9},{2,10},{3,11},{4,12},{5,13},{6,14},{7,15},{8,16},{9,17... | collective-permute-start | bytes 196616 | tf_op jit(solution)/shard_map/ppermute | solution.py:284
  38.0 4.1 %collective-permute-start.12 = (f32[16,1024]{1,0:T(8,128)S(1)}, f32[16,1024]{1,0:T(8,128)S(1)}, u32[]{:S(2)}, u32[]{:S(2)}) collective-permute-start(f32[16,1024]{1,0:T(8,128)S(1)} %shard_map.71), channel_id=1, source_target_pairs={{0,16},{1,17},{2,18},{3,19},{4,20},{5,21},{6,22},{7,23},{8,24},{9,... | collective-permute-start | bytes 196616 | tf_op jit(solution)/shard_map/ppermute | solution.py:284
  42.2 1.3 %collective-permute-start.13 = (f32[16,1024]{1,0:T(8,128)S(1)}, f32[16,1024]{1,0:T(8,128)S(1)}, u32[]{:S(2)}, u32[]{:S(2)}) collective-permute-start(f32[16,1024]{1,0:T(8,128)S(1)} %shard_map.71), channel_id=1, source_target_pairs={{0,24},{1,25},{2,26},{3,27},{4,28},{5,29},{6,30},{7,31}} | collective-permute-start | bytes 196616 | tf_op jit(solution)/shard_map/ppermute | solution.py:284
  43.5 2.0 %shard_map.69.refs_4_ = f32[2,512,128]{2,1,0:T(8,128)S(1)} custom-call(s32[11]{0:T(128)S(1)} %stack.47.info_ref, bf16[128,1024]{1,0:T(8,128)(2,1)S(1)} %get-tuple-element.41.refs_0_, bf16[128,1024]{1,0:T(8,128)(2,1)S(1)} %collective-permute-done.2.refs_1_, bf16[128,1024]{1,0:T(8,128)(2,1)S(1)} %collective-permute-done.3.refs_2_, ...), custom_call_target="tpu_custom_call" | custom-call | flops 330000000 | bytes 1080000 | tf_op jit(solution)/shard_map/pallas_call | solution.py:26
  45.4 2.0 %shard_map.70.refs_4_ = f32[2,512,128]{2,1,0:T(8,128)S(1)} custom-call(s32[11]{0:T(128)S(1)} %stack.47.info_ref, bf16[128,1024]{1,0:T(8,128)(2,1)S(1)} %get-tuple-element.41.refs_0_, bf16[128,1024]{1,0:T(8,128)(2,1)S(1)} %collective-permute-done.2.refs_1_, bf16[128,1024]{1,0:T(8,128)(2,1)S(1)} %collective-permute-done.3.refs_2_, ...), custom_call_target="tpu_custom_call" | custom-call | flops 330000000 | bytes 1080000 | tf_op jit(solution)/shard_map/pallas_call | solution.py:26
  47.4 0.7 collective-permute-done.14.refs_10_
  48.1 0.0 collective-permute-done.15.refs_9_
  48.1 0.9 %collective-permute-start.16 = (bf16[128,1024]{1,0:T(8,128)(2,1)S(1)}, bf16[128,1024]{1,0:T(8,128)(2,1)S(1)}, u32[]{:S(2)}, u32[]{:S(2)}) collective-permute-start(bf16[128,1024]{1,0:T(8,128)(2,1)S(1)} %slice.6), channel_id=1, source_target_pairs={{0,4},{1,5},{2,6},{3,7},{4,0},{5,1},{6,2},{7,3},{8,12},{9,13},{10,... | collective-permute-start | bytes 786440 | tf_op jit(solution)/shard_map/ppermute | solution.py:279
  49.0 0.9 %collective-permute-start.19 = (bf16[128,1024]{1,0:T(8,128)(2,1)S(1)}, bf16[128,1024]{1,0:T(8,128)(2,1)S(1)}, u32[]{:S(2)}, u32[]{:S(2)}) collective-permute-start(bf16[128,1024]{1,0:T(8,128)(2,1)S(1)} %slice.7), channel_id=1, source_target_pairs={{0,8},{1,9},{2,10},{3,11},{4,12},{5,13},{6,14},{7,15},{8,16},{9,17... | collective-permute-start | bytes 786440 | tf_op jit(solution)/shard_map/ppermute | solution.py:284
  49.9 0.0 collective-permute-done.11.refs_9_
  49.9 0.0 collective-permute-done.12.refs_10_
  49.9 0.1 collective-permute-done.13.refs_11_
  50.0 1.3 %shard_map.72.refs_0_ = bf16[2,512,128]{2,1,0:T(8,128)(2,1)S(1)} custom-call(s32[11]{0:T(128)S(1)} %stack.47.info_ref, bf16[128,1024]{1,0:T(8,128)(2,1)S(1)} %get-tuple-element.55.refs_0_, bf16[128,1024]{1,0:T(8,128)(2,1)S(1)} %collective-permute-done.7.refs_1_, bf16[128,1024]{1,0:T(8,128)(2,1)S(1)} %collective-permute-done.8.refs_2_, ...), custom_call_target="tpu_custom_call" | custom-call | flops 550000000 | bytes 1800000 | tf_op jit(solution)/shard_map/pallas_call | solution.py:26
  51.2 1.3 %shard_map.73.refs_1_ = bf16[2,512,128]{2,1,0:T(8,128)(2,1)S(1)} custom-call(s32[11]{0:T(128)S(1)} %stack.47.info_ref, bf16[128,1024]{1,0:T(8,128)(2,1)S(1)} %get-tuple-element.55.refs_0_, bf16[128,1024]{1,0:T(8,128)(2,1)S(1)} %collective-permute-done.7.refs_1_, bf16[128,1024]{1,0:T(8,128)(2,1)S(1)} %collective-permute-done.8.refs_2_, ...), custom_call_target="tpu_custom_call" | custom-call | flops 550000000 | bytes 1800000 | tf_op jit(solution)/shard_map/pallas_call | solution.py:26
  52.5 1.3 %shard_map.74.refs_2_ = bf16[2,512,128]{2,1,0:T(8,128)(2,1)S(1)} custom-call(s32[11]{0:T(128)S(1)} %stack.47.info_ref, bf16[128,1024]{1,0:T(8,128)(2,1)S(1)} %get-tuple-element.55.refs_0_, bf16[128,1024]{1,0:T(8,128)(2,1)S(1)} %collective-permute-done.7.refs_1_, bf16[128,1024]{1,0:T(8,128)(2,1)S(1)} %collective-permute-done.8.refs_2_, ...), custom_call_target="tpu_custom_call" | custom-call | flops 550000000 | bytes 1800000 | tf_op jit(solution)/shard_map/pallas_call | solution.py:26
  53.8 0.0 copy-start
  53.8 1.3 %shard_map.75.refs_3_ = bf16[2,512,128]{2,1,0:T(8,128)(2,1)S(1)} custom-call(s32[11]{0:T(128)S(1)} %stack.47.info_ref, bf16[128,1024]{1,0:T(8,128)(2,1)S(1)} %get-tuple-element.55.refs_0_, bf16[128,1024]{1,0:T(8,128)(2,1)S(1)} %collective-permute-done.7.refs_1_, bf16[128,1024]{1,0:T(8,128)(2,1)S(1)} %collective-permute-done.8.refs_2_, ...), custom_call_target="tpu_custom_call" | custom-call | flops 550000000 | bytes 1800000 | tf_op jit(solution)/shard_map/pallas_call | solution.py:26
  55.0 0.9 %collective-permute-done.16.refs_11_ = bf16[128,1024]{1,0:T(8,128)(2,1)S(1)} collective-permute-done((bf16[128,1024]{1,0:T(8,128)(2,1)S(1)}, bf16[128,1024]{1,0:T(8,128)(2,1)S(1)}, u32[]{:S(2)}, u32[]{:S(2)}) %collective-permute-start.16) | collective-permute-done | bytes 262176 | tf_op jit(solution)/shard_map/ppermute | solution.py:279
  55.9 1.9 %shard_map.76 = (f32[256,1024]{1,0:T(8,128)S(1)}, bf16[256,1024]{1,0:T(8,128)(2,1)S(1)}) custom-call(s32[11]{0:T(128)S(1)} %stack.47.info_ref, bf16[2,512,128]{2,1,0:T(8,128)(2,1)S(1)} %shard_map.72.refs_0_, bf16[2,512,128]{2,1,0:T(8,128)(2,1)S(1)} %shard_map.73.refs_1_, bf16[2,512,128]{2,1,0:T(8,128)(2,1)S(1)} %shard_map.74.refs_2_, ...), custom_call_target="tpu_custom_call" | custom-call | flops 1100000000 | bytes 3600000 | tf_op jit(solution)/shard_map/pallas_call | solution.py:26
  57.8 0.1 collective-permute-start.17
  57.9 1.9 %shard_map.78 = (f32[256,1024]{1,0:T(8,128)S(1)}, bf16[256,1024]{1,0:T(8,128)(2,1)S(1)}) custom-call(s32[11]{0:T(128)S(1)} %stack.47.info_ref, bf16[2,512,128]{2,1,0:T(8,128)(2,1)S(1)} %shard_map.72.refs_0_, bf16[2,512,128]{2,1,0:T(8,128)(2,1)S(1)} %shard_map.73.refs_1_, bf16[2,512,128]{2,1,0:T(8,128)(2,1)S(1)} %shard_map.74.refs_2_, ...), custom_call_target="tpu_custom_call" | custom-call | flops 1100000000 | bytes 3600000 | tf_op jit(solution)/shard_map/pallas_call | solution.py:26
  59.8 0.6 collective-permute-start.20
  60.4 0.0 collective-permute-done.17.got_ref
  60.4 0.6 shard_map.77
  61.0 1.8 %collective-permute-start.18 = (bf16[128,1024]{1,0:T(8,128)(2,1)S(1)}, bf16[128,1024]{1,0:T(8,128)(2,1)S(1)}, u32[]{:S(2)}, u32[]{:S(2)}) collective-permute-start(bf16[128,1024]{1,0:T(8,128)(2,1)S(1)} %get-tuple-element.69), channel_id=1, source_target_pairs={{0,2},{1,3},{2,0},{3,1},{4,6},{5,7},{6,4},{7,5},{8,10},{9,11},{10,... | collective-permute-start | bytes 786440 | tf_op jit(solution)/shard_map/ppermute | solution.py:279
  62.9 0.6 shard_map.79
  63.5 0.9 %collective-permute-start.21 = (bf16[128,1024]{1,0:T(8,128)(2,1)S(1)}, bf16[128,1024]{1,0:T(8,128)(2,1)S(1)}, u32[]{:S(2)}, u32[]{:S(2)}) collective-permute-start(bf16[128,1024]{1,0:T(8,128)(2,1)S(1)} %get-tuple-element.74), channel_id=1, source_target_pairs={{0,2},{1,3},{2,0},{3,1},{4,6},{5,7},{6,4},{7,5},{8,10},{9,11},{10,... | collective-permute-start | bytes 786440 | tf_op jit(solution)/shard_map/ppermute | solution.py:279
  64.4 5.8 %collective-permute-done.18.refs_1_ = bf16[128,1024]{1,0:T(8,128)(2,1)S(1)} collective-permute-done((bf16[128,1024]{1,0:T(8,128)(2,1)S(1)}, bf16[128,1024]{1,0:T(8,128)(2,1)S(1)}, u32[]{:S(2)}, u32[]{:S(2)}) %collective-permute-start.18) | collective-permute-done | bytes 262176 | tf_op jit(solution)/shard_map/ppermute | solution.py:279
  70.2 4.7 %collective-permute-done.21.refs_3_ = bf16[128,1024]{1,0:T(8,128)(2,1)S(1)} collective-permute-done((bf16[128,1024]{1,0:T(8,128)(2,1)S(1)}, bf16[128,1024]{1,0:T(8,128)(2,1)S(1)}, u32[]{:S(2)}, u32[]{:S(2)}) %collective-permute-start.21) | collective-permute-done | bytes 262176 | tf_op jit(solution)/shard_map/ppermute | solution.py:279
  75.0 1.4 %shard_map.80 = bf16[128,2048]{1,0:T(8,128)(2,1)} custom-call(s32[11]{0:T(128)S(1)} %stack.47.info_ref, f32[128,1024]{1,0:T(8,128)S(1)} %get-tuple-element.68.refs_0_, bf16[128,1024]{1,0:T(8,128)(2,1)S(1)} %collective-permute-done.18.refs_1_, f32[128,1024]{1,0:T(8,128)S(1)} %get-tuple-element.73.refs_2_, bf16[128,1024]{1,0:T(8,128)(2,1)S(1)} %collective-permute-done.21.refs_3_), custom_call_target="tpu_custom_call" | custom-call | tf_op jit(solution)/shard_map/pallas_call | solution.py:26
  (13 shorter events, 0.1 us)
Async XLA Ops:
  0.0 17.2 %collective-permute-start = (bf16[128,2048]{1,0:T(8,128)(2,1)}, bf16[128,2048]{1,0:T(8,128)(2,1)S(1)}, u32[]{:S(2)}, u32[]{:S(2)}) collective-permute-start(bf16[128,2048]{1,0:T(8,128)(2,1)} %refs_4_.3), channel_id=1, source_target_pairs={{0,8},{1,9},{2,10},{3,11},{4,12},{5,13},{6,14},{7,15},{8,16},{9,17... | collective-permute-start | bytes 1572872 | tf_op jit(solution)/shard_map/ppermute | solution.py:284
  3.0 14.2 %collective-permute-start.1 = (bf16[128,2048]{1,0:T(8,128)(2,1)}, bf16[128,2048]{1,0:T(8,128)(2,1)S(1)}, u32[]{:S(2)}, u32[]{:S(2)}) collective-permute-start(bf16[128,2048]{1,0:T(8,128)(2,1)} %refs_4_.3), channel_id=1, source_target_pairs={{0,4},{1,5},{2,6},{3,7},{4,0},{5,1},{6,2},{7,3},{8,12},{9,13},{10,... | collective-permute-start | bytes 1572872 | tf_op jit(solution)/shard_map/ppermute | solution.py:279
  4.5 4.6 %copy-start.5 = (f32[4096]{0:T(1024)S(1)}, f32[4096]{0:T(1024)}, u32[]{:S(2)}) copy-start(f32[4096]{0:T(1024)} %param.10) | copy-start | bytes 49156
  4.6 1.2 %copy-start.1 = (bf16[128,4096]{1,0:T(8,128)(2,1)S(1)}, bf16[128,4096]{1,0:T(8,128)(2,1)}, u32[]{:S(2)}) copy-start(bf16[128,4096]{1,0:T(8,128)(2,1)} %refs_0_.2) | copy-start | bytes 3145732
  5.9 3.3 %copy-start.2 = (bf16[128,4096]{1,0:T(8,128)(2,1)S(1)}, bf16[128,4096]{1,0:T(8,128)(2,1)}, u32[]{:S(2)}) copy-start(bf16[128,4096]{1,0:T(8,128)(2,1)} %refs_0_.3) | copy-start | bytes 3145732
  6.9 5.8 %collective-permute-start.2 = (bf16[128,1024]{1,0:T(8,128)(2,1)S(1)}, bf16[128,1024]{1,0:T(8,128)(2,1)S(1)}, u32[]{:S(2)}, u32[]{:S(2)}) collective-permute-start(bf16[128,1024]{1,0:T(8,128)(2,1)S(1)} %get-tuple-element.42), channel_id=1, source_target_pairs={{0,1},{1,0},{2,3},{3,2},{4,5},{5,4},{6,7},{7,6},{8,9},{9,8},{10,11... | collective-permute-start | bytes 786440 | tf_op jit(solution)/shard_map/ppermute | solution.py:279
  7.0 12.7 %collective-permute-start.4 = (bf16[128,1024]{1,0:T(8,128)(2,1)S(1)}, bf16[128,1024]{1,0:T(8,128)(2,1)S(1)}, u32[]{:S(2)}, u32[]{:S(2)}) collective-permute-start(bf16[128,1024]{1,0:T(8,128)(2,1)S(1)} %get-tuple-element.44), channel_id=1, source_target_pairs={{0,3},{1,2},{2,1},{3,0},{4,7},{5,6},{6,5},{7,4},{8,11},{9,10},{10,... | collective-permute-start | bytes 786440 | tf_op jit(solution)/shard_map/ppermute | solution.py:279
  8.6 13.2 %collective-permute-start.3 = (bf16[128,1024]{1,0:T(8,128)(2,1)S(1)}, bf16[128,1024]{1,0:T(8,128)(2,1)S(1)}, u32[]{:S(2)}, u32[]{:S(2)}) collective-permute-start(bf16[128,1024]{1,0:T(8,128)(2,1)S(1)} %get-tuple-element.43), channel_id=1, source_target_pairs={{0,2},{1,3},{2,0},{3,1},{4,6},{5,7},{6,4},{7,5},{8,10},{9,11},{10,... | collective-permute-start | bytes 786440 | tf_op jit(solution)/shard_map/ppermute | solution.py:279
  9.2 1.0 %copy-start.3 = (f32[4096,16]{0,1:T(8,128)S(1)}, f32[4096,16]{0,1:T(8,128)}, u32[]{:S(2)}) copy-start(f32[4096,16]{0,1:T(8,128)} %param.8) | copy-start | bytes 786436
  10.1 0.9 %copy-start.4 = (f32[4096,16]{0,1:T(8,128)S(1)}, f32[4096,16]{0,1:T(8,128)}, u32[]{:S(2)}) copy-start(f32[4096,16]{0,1:T(8,128)} %param.9) | copy-start | bytes 786436
  12.8 12.7 %collective-permute-start.7 = (bf16[128,1024]{1,0:T(8,128)(2,1)S(1)}, bf16[128,1024]{1,0:T(8,128)(2,1)S(1)}, u32[]{:S(2)}, u32[]{:S(2)}) collective-permute-start(bf16[128,1024]{1,0:T(8,128)(2,1)S(1)} %get-tuple-element.56), channel_id=1, source_target_pairs={{0,1},{1,0},{2,3},{3,2},{4,5},{5,4},{6,7},{7,6},{8,9},{9,8},{10,11... | collective-permute-start | bytes 786440 | tf_op jit(solution)/shard_map/ppermute | solution.py:279
  17.2 14.9 %collective-permute-start.5 = (bf16[128,2048]{1,0:T(8,128)(2,1)S(1)}, bf16[128,2048]{1,0:T(8,128)(2,1)S(1)}, u32[]{:S(2)}, u32[]{:S(2)}) collective-permute-start(bf16[128,2048]{1,0:T(8,128)(2,1)S(1)} %collective-permute-done.refs_6_), channel_id=1, source_target_pairs={{0,8},{1,9},{2,10},{3,11},{4,12},{5,13},{6,14},{7,15},{8,16},{9,17... | collective-permute-start | bytes 1572872 | tf_op jit(solution)/shard_map/ppermute | solution.py:284
  18.2 13.9 %collective-permute-start.6 = (bf16[128,2048]{1,0:T(8,128)(2,1)S(1)}, bf16[128,2048]{1,0:T(8,128)(2,1)S(1)}, u32[]{:S(2)}, u32[]{:S(2)}) collective-permute-start(bf16[128,2048]{1,0:T(8,128)(2,1)S(1)} %collective-permute-done.refs_6_), channel_id=1, source_target_pairs={{0,4},{1,5},{2,6},{3,7},{4,0},{5,1},{6,2},{7,3},{8,12},{9,13},{10,... | collective-permute-start | bytes 1572872 | tf_op jit(solution)/shard_map/ppermute | solution.py:279
  19.7 10.3 %collective-permute-start.8 = (bf16[128,1024]{1,0:T(8,128)(2,1)S(1)}, bf16[128,1024]{1,0:T(8,128)(2,1)S(1)}, u32[]{:S(2)}, u32[]{:S(2)}) collective-permute-start(bf16[128,1024]{1,0:T(8,128)(2,1)S(1)} %get-tuple-element.58), channel_id=1, source_target_pairs={{0,2},{1,3},{2,0},{3,1},{4,6},{5,7},{6,4},{7,5},{8,10},{9,11},{10,... | collective-permute-start | bytes 786440 | tf_op jit(solution)/shard_map/ppermute | solution.py:279
  21.9 9.7 %collective-permute-start.9 = (bf16[128,1024]{1,0:T(8,128)(2,1)S(1)}, bf16[128,1024]{1,0:T(8,128)(2,1)S(1)}, u32[]{:S(2)}, u32[]{:S(2)}) collective-permute-start(bf16[128,1024]{1,0:T(8,128)(2,1)S(1)} %get-tuple-element.60), channel_id=1, source_target_pairs={{0,3},{1,2},{2,1},{3,0},{4,7},{5,6},{6,5},{7,4},{8,11},{9,10},{10,... | collective-permute-start | bytes 786440 | tf_op jit(solution)/shard_map/ppermute | solution.py:279
  25.5 6.3 %collective-permute-start.10 = (f32[16,1024]{1,0:T(8,128)S(1)}, f32[16,1024]{1,0:T(8,128)S(1)}, u32[]{:S(2)}, u32[]{:S(2)}) collective-permute-start(f32[16,1024]{1,0:T(8,128)S(1)} %get-tuple-element.62.end_ref), channel_id=1, source_target_pairs={{0,4},{1,5},{2,6},{3,7},{4,0},{5,1},{6,2},{7,3},{8,12},{9,13},{10,... | collective-permute-start | bytes 196616 | tf_op jit(solution)/shard_map/ppermute | solution.py:279
  32.1 16.0 %collective-permute-start.14 = (bf16[128,2048]{1,0:T(8,128)(2,1)S(1)}, bf16[128,2048]{1,0:T(8,128)(2,1)S(1)}, u32[]{:S(2)}, u32[]{:S(2)}) collective-permute-start(bf16[128,2048]{1,0:T(8,128)(2,1)S(1)} %collective-permute-done.5.refs_8_), channel_id=1, source_target_pairs={{0,8},{1,9},{2,10},{3,11},{4,12},{5,13},{6,14},{7,15},{8,16},{9,17... | collective-permute-start | bytes 1572872 | tf_op jit(solution)/shard_map/ppermute | solution.py:284
  33.4 14.7 %collective-permute-start.15 = (bf16[128,2048]{1,0:T(8,128)(2,1)S(1)}, bf16[128,2048]{1,0:T(8,128)(2,1)S(1)}, u32[]{:S(2)}, u32[]{:S(2)}) collective-permute-start(bf16[128,2048]{1,0:T(8,128)(2,1)S(1)} %collective-permute-done.5.refs_8_), channel_id=1, source_target_pairs={{0,4},{1,5},{2,6},{3,7},{4,0},{5,1},{6,2},{7,3},{8,12},{9,13},{10,... | collective-permute-start | bytes 1572872 | tf_op jit(solution)/shard_map/ppermute | solution.py:279
  35.5 14.4 %collective-permute-start.11 = (f32[16,1024]{1,0:T(8,128)S(1)}, f32[16,1024]{1,0:T(8,128)S(1)}, u32[]{:S(2)}, u32[]{:S(2)}) collective-permute-start(f32[16,1024]{1,0:T(8,128)S(1)} %shard_map.71), channel_id=1, source_target_pairs={{0,8},{1,9},{2,10},{3,11},{4,12},{5,13},{6,14},{7,15},{8,16},{9,17... | collective-permute-start | bytes 196616 | tf_op jit(solution)/shard_map/ppermute | solution.py:284
  38.0 11.9 %collective-permute-start.12 = (f32[16,1024]{1,0:T(8,128)S(1)}, f32[16,1024]{1,0:T(8,128)S(1)}, u32[]{:S(2)}, u32[]{:S(2)}) collective-permute-start(f32[16,1024]{1,0:T(8,128)S(1)} %shard_map.71), channel_id=1, source_target_pairs={{0,16},{1,17},{2,18},{3,19},{4,20},{5,21},{6,22},{7,23},{8,24},{9,... | collective-permute-start | bytes 196616 | tf_op jit(solution)/shard_map/ppermute | solution.py:284
  42.2 7.8 %collective-permute-start.13 = (f32[16,1024]{1,0:T(8,128)S(1)}, f32[16,1024]{1,0:T(8,128)S(1)}, u32[]{:S(2)}, u32[]{:S(2)}) collective-permute-start(f32[16,1024]{1,0:T(8,128)S(1)} %shard_map.71), channel_id=1, source_target_pairs={{0,24},{1,25},{2,26},{3,27},{4,28},{5,29},{6,30},{7,31}} | collective-permute-start | bytes 196616 | tf_op jit(solution)/shard_map/ppermute | solution.py:284
  48.1 7.8 %collective-permute-start.16 = (bf16[128,1024]{1,0:T(8,128)(2,1)S(1)}, bf16[128,1024]{1,0:T(8,128)(2,1)S(1)}, u32[]{:S(2)}, u32[]{:S(2)}) collective-permute-start(bf16[128,1024]{1,0:T(8,128)(2,1)S(1)} %slice.6), channel_id=1, source_target_pairs={{0,4},{1,5},{2,6},{3,7},{4,0},{5,1},{6,2},{7,3},{8,12},{9,13},{10,... | collective-permute-start | bytes 786440 | tf_op jit(solution)/shard_map/ppermute | solution.py:279
  49.0 8.9 %collective-permute-start.19 = (bf16[128,1024]{1,0:T(8,128)(2,1)S(1)}, bf16[128,1024]{1,0:T(8,128)(2,1)S(1)}, u32[]{:S(2)}, u32[]{:S(2)}) collective-permute-start(bf16[128,1024]{1,0:T(8,128)(2,1)S(1)} %slice.7), channel_id=1, source_target_pairs={{0,8},{1,9},{2,10},{3,11},{4,12},{5,13},{6,14},{7,15},{8,16},{9,17... | collective-permute-start | bytes 786440 | tf_op jit(solution)/shard_map/ppermute | solution.py:284
  53.8 2.2 %copy-start = (bf16[128,2048]{1,0:T(8,128)(2,1)S(1)}, bf16[128,2048]{1,0:T(8,128)(2,1)}, u32[]{:S(2)}) copy-start(bf16[128,2048]{1,0:T(8,128)(2,1)} %refs_4_.3) | copy-start | bytes 1572868
  57.8 2.6 %collective-permute-start.17 = (bf16[256,1024]{1,0:T(8,128)(2,1)S(1)}, bf16[256,1024]{1,0:T(8,128)(2,1)S(1)}, u32[]{:S(2)}, u32[]{:S(2)}) collective-permute-start(bf16[256,1024]{1,0:T(8,128)(2,1)S(1)} %get-tuple-element.67), channel_id=1, source_target_pairs={{0,1},{1,0},{2,3},{3,2},{4,5},{5,4},{6,7},{7,6},{8,9},{9,8},{10,11... | collective-permute-start | bytes 1572872 | tf_op jit(solution)/shard_map/ppermute | solution.py:279
  59.8 3.0 %collective-permute-start.20 = (bf16[256,1024]{1,0:T(8,128)(2,1)S(1)}, bf16[256,1024]{1,0:T(8,128)(2,1)S(1)}, u32[]{:S(2)}, u32[]{:S(2)}) collective-permute-start(bf16[256,1024]{1,0:T(8,128)(2,1)S(1)} %get-tuple-element.72), channel_id=1, source_target_pairs={{0,1},{1,0},{2,3},{3,2},{4,5},{5,4},{6,7},{7,6},{8,9},{9,8},{10,11... | collective-permute-start | bytes 1572872 | tf_op jit(solution)/shard_map/ppermute | solution.py:279
  61.0 9.2 %collective-permute-start.18 = (bf16[128,1024]{1,0:T(8,128)(2,1)S(1)}, bf16[128,1024]{1,0:T(8,128)(2,1)S(1)}, u32[]{:S(2)}, u32[]{:S(2)}) collective-permute-start(bf16[128,1024]{1,0:T(8,128)(2,1)S(1)} %get-tuple-element.69), channel_id=1, source_target_pairs={{0,2},{1,3},{2,0},{3,1},{4,6},{5,7},{6,4},{7,5},{8,10},{9,11},{10,... | collective-permute-start | bytes 786440 | tf_op jit(solution)/shard_map/ppermute | solution.py:279
  63.5 11.5 %collective-permute-start.21 = (bf16[128,1024]{1,0:T(8,128)(2,1)S(1)}, bf16[128,1024]{1,0:T(8,128)(2,1)S(1)}, u32[]{:S(2)}, u32[]{:S(2)}) collective-permute-start(bf16[128,1024]{1,0:T(8,128)(2,1)S(1)} %get-tuple-element.74), channel_id=1, source_target_pairs={{0,2},{1,3},{2,0},{3,1},{4,6},{5,7},{6,4},{7,5},{8,10},{9,11},{10,... | collective-permute-start | bytes 786440 | tf_op jit(solution)/shard_map/ppermute | solution.py:279

commit v7 on v6

--- a/solution.py
+++ b/solution.py
@@ -255,13 +255,27 @@
     away_ref[...] = (kept_ref[rows:, :] + got_ref[rows:, :].astype(f32)).astype(bf16)
 
 
-def finish_kernel(info_ref, *refs):
-    out_ref = refs[-1]
-    at = 0
-    for mine, far in zip(refs[:-1:2], refs[1:-1:2]):
-        wide = mine.shape[1]
-        out_ref[:, at : at + wide] = (mine[...] + far[...].astype(f32)).astype(bf16)
-        at += wide
+def finish_kernel(at, info_ref, mine_ref, far_ref, *refs):
+    out_ref, rounded, sem = refs[-3:]
+    rounded[...] = (mine_ref[...] + far_ref[...].astype(f32)).astype(bf16)
+    copy = pltpu.make_async_copy(rounded, out_ref.at[:, at : at + rounded.shape[1]], sem)
+    copy.start()
+    copy.wait()
+
+
+def finish(info, at, features, mine, far, before):
+    anywhere = pl.BlockSpec(memory_space=pl.ANY)
+    return pl.pallas_call(
+        functools.partial(finish_kernel, at),
+        out_shape=jax.ShapeDtypeStruct((mine.shape[0], features), bf16),
+        in_specs=[pl.BlockSpec(memory_space=pltpu.SMEM)]
+        + [pl.BlockSpec()] * 2
+        + [anywhere] * len(before),
+        out_specs=anywhere,
+        input_output_aliases={3: 0} if before else {},
+        scratch_shapes=[pltpu.VMEM(mine.shape, bf16), pltpu.SemaphoreType.DMA],
+        compiler_params=pltpu.CompilerParams(vmem_limit_bytes=VMEM_LIMIT),
+    )(info, mine, far, *before)
 
 
 def on_device(q_gate, values_in, decay_rate, residue, skip_gain, out_weight):
@@ -397,7 +411,11 @@
         )(info, kept, swap(sent, 1))
         joined.append(mine_sum)
         finished += [mine_sum, swap(away_sum, 2)]
-    return call(finish_kernel, jax.ShapeDtypeStruct((rows, features), bf16))(info, *finished)
+    out = []
+    for part in range(2):
+        sums = finished[2 * part : 2 * part + 2]
+        out = [finish(info, part * wide, features, *sums, out)]
+    return out[0]
 
 
 def solution(mesh):

time: 76.6 us -> 76.5 us (level)
  waiting for transfers between devices: 19.2 us -> 17.9 us
  Pallas kernels: 26.2 us -> 27.4 us
    pallas_call x0 -> x2, Pallas kernels: none -> 2.59 us  [finish(): pl.pallas_call(functools.partial(finish_kernel, at), out_shape=jax.ShapeD...]
    pallas_call x15 -> x14, Pallas kernels: 23.5 us -> 22 us  [run(): pl.pallas_call(kernel, out_shape=out_shape, in_specs=[pl.BlockSpec(memory...]
    ppermute x15, waiting for transfers between devices: 13.9 us -> 12.6 us  [swap(): return lax.ppermute(value, 'seq', [(i, i ^ bit) for i in range(count)])]
  transfers between devices with their start and end apart: 22 -> 22, of which waited for: 10 -> 10; matrix products, arithmetic and copies ran while one was open for 0% -> 0% of each run, Pallas kernels for 32% -> 34%
where the time goes in v7:
time: 76.5 us; the launch traced here: 76.3 us
  starting transfers between devices  27.4 us (36%)
  Pallas kernels  27.4 us (36%)
  waiting for transfers between devices  17.9 us (23%)
  local copies, waits for them, and re-layouts  3.26 us (4%)
    pallas_call x14, Pallas kernels, run(): pl.pallas_call(kernel, out_shape=out_shape, in_specs=[pl.BlockSpec(memory...  22 us
    ppermute x7, starting transfers between devices, up(): return lax.ppermute(value, 'seq', pairs)  14.2 us
    ppermute x15, starting transfers between devices, swap(): return lax.ppermute(value, 'seq', [(i, i ^ bit) for i in range(count)])  13.2 us
    ppermute x15, waiting for transfers between devices, swap(): return lax.ppermute(value, 'seq', [(i, i ^ bit) for i in range(count)])  12.6 us
    ppermute x7, waiting for transfers between devices, up(): return lax.ppermute(value, 'seq', pairs)  5.35 us
    unnamed x12, local copies, waits for them, and re-layouts  3.14 us
    pallas_call x2, Pallas kernels, deal(): pl.pallas_call(functools.partial(deal_kernel, team, depth, plan), out_sha...  2.78 us
    pallas_call x2, Pallas kernels, finish(): pl.pallas_call(functools.partial(finish_kernel, at), out_shape=jax.ShapeD...  2.59 us
  transfers between devices with their start and end apart: 22, of which 10 were waited for; matrix products, arithmetic and copies ran while one was open for 0% of the time, Pallas kernels for 34%

profile of v7, /device:TPU:0, one launch (start us, length us, event | category | flops | bytes accessed | tf_op | source)
XLA Modules:
  0.0 76.3 jit_solution(4517468925723221424)
XLA Ops:
  0.0 3.0 %collective-permute-start = (bf16[128,2048]{1,0:T(8,128)(2,1)}, bf16[128,2048]{1,0:T(8,128)(2,1)S(1)}, u32[]{:S(2)}, u32[]{:S(2)}) collective-permute-start(bf16[128,2048]{1,0:T(8,128)(2,1)} %refs_4_.3), channel_id=1, source_target_pairs={{0,8},{1,9},{2,10},{3,11},{4,12},{5,13},{6,14},{7,15},{8,16},{9,17... | collective-permute-start | bytes 1572872 | tf_op jit(solution)/shard_map/ppermute | solution.py:298
  3.0 1.5 %collective-permute-start.1 = (bf16[128,2048]{1,0:T(8,128)(2,1)}, bf16[128,2048]{1,0:T(8,128)(2,1)S(1)}, u32[]{:S(2)}, u32[]{:S(2)}) collective-permute-start(bf16[128,2048]{1,0:T(8,128)(2,1)} %refs_4_.3), channel_id=1, source_target_pairs={{0,4},{1,5},{2,6},{3,7},{4,0},{5,1},{6,2},{7,3},{8,12},{9,13},{10,... | collective-permute-start | bytes 1572872 | tf_op jit(solution)/shard_map/ppermute | solution.py:293
  4.5 0.1 stack.47.info_ref
  4.6 1.2 %copy-done.1 = bf16[128,4096]{1,0:T(8,128)(2,1)S(1)} copy-done((bf16[128,4096]{1,0:T(8,128)(2,1)S(1)}, bf16[128,4096]{1,0:T(8,128)(2,1)}, u32[]{:S(2)}) %copy-start.1) | copy-done | bytes 1048600
  5.9 1.1 %shard_map.64 = (bf16[128,1024]{1,0:T(8,128)(2,1)S(1)}, bf16[128,1024]{1,0:T(8,128)(2,1)S(1)}, bf16[128,1024]{1,0:T(8,128)(2,1)S(1)}, bf16[128,1024]{1,0:T(8,128)(2,1)S(1)}) custom-call(s32[11]{0:T(128)S(1)} %stack.47.info_ref, bf16[128,4096]{1,0:T(8,128)(2,1)S(1)} %copy-done.1), custom_call_target="tpu_custom_call" | custom-call | tf_op jit(solution)/shard_map/pallas_call | solution.py:72
  6.9 0.1 collective-permute-start.2
  7.0 1.6 %collective-permute-start.4 = (bf16[128,1024]{1,0:T(8,128)(2,1)S(1)}, bf16[128,1024]{1,0:T(8,128)(2,1)S(1)}, u32[]{:S(2)}, u32[]{:S(2)}) collective-permute-start(bf16[128,1024]{1,0:T(8,128)(2,1)S(1)} %get-tuple-element.44), channel_id=1, source_target_pairs={{0,3},{1,2},{2,1},{3,0},{4,7},{5,6},{6,5},{7,4},{8,11},{9,10},{10,... | collective-permute-start | bytes 786440 | tf_op jit(solution)/shard_map/ppermute | solution.py:293
  8.6 0.5 collective-permute-start.3
  9.2 0.9 %copy-done.3 = f32[4096,16]{0,1:T(8,128)S(1)} copy-done((f32[4096,16]{0,1:T(8,128)S(1)}, f32[4096,16]{0,1:T(8,128)}, u32[]{:S(2)}) %copy-start.3) | copy-done | bytes 262168
  10.1 0.9 %copy-done.4 = f32[4096,16]{0,1:T(8,128)S(1)} copy-done((f32[4096,16]{0,1:T(8,128)S(1)}, f32[4096,16]{0,1:T(8,128)}, u32[]{:S(2)}) %copy-start.4) | copy-done | bytes 262168
  11.1 1.7 %shard_map.65 = (bf16[128,1024]{1,0:T(8,128)(2,1)S(1)}, bf16[128,1024]{1,0:T(8,128)(2,1)S(1)}, bf16[128,1024]{1,0:T(8,128)(2,1)S(1)}, bf16[128,1024]{1,0:T(8,128...) custom-call(s32[11]{0:T(128)S(1)} %stack.47.info_ref, ...), custom_call_target="tpu_custom_call" | custom-call | tf_op jit(solution)/shard_map/pallas_call | solution.py:72
  12.8 0.0 collective-permute-done.2.refs_1_
  12.8 0.1 collective-permute-start.7
  12.9 4.3 %collective-permute-done.refs_6_ = bf16[128,2048]{1,0:T(8,128)(2,1)S(1)} collective-permute-done((bf16[128,2048]{1,0:T(8,128)(2,1)}, bf16[128,2048]{1,0:T(8,128)(2,1)S(1)}, u32[]{:S(2)}, u32[]{:S(2)}) %collective-permute-start) | collective-permute-done | bytes 524320 | tf_op jit(solution)/shard_map/ppermute | solution.py:298
  17.2 0.0 collective-permute-done.1.refs_5_
  17.2 1.0 %collective-permute-start.5 = (bf16[128,2048]{1,0:T(8,128)(2,1)S(1)}, bf16[128,2048]{1,0:T(8,128)(2,1)S(1)}, u32[]{:S(2)}, u32[]{:S(2)}) collective-permute-start(bf16[128,2048]{1,0:T(8,128)(2,1)S(1)} %collective-permute-done.refs_6_), channel_id=1, source_target_pairs={{0,8},{1,9},{2,10},{3,11},{4,12},{5,13},{6,14},{7,15},{8,16},{9,17... | collective-permute-start | bytes 1572872 | tf_op jit(solution)/shard_map/ppermute | solution.py:298
  18.2 1.5 %collective-permute-start.6 = (bf16[128,2048]{1,0:T(8,128)(2,1)S(1)}, bf16[128,2048]{1,0:T(8,128)(2,1)S(1)}, u32[]{:S(2)}, u32[]{:S(2)}) collective-permute-start(bf16[128,2048]{1,0:T(8,128)(2,1)S(1)} %collective-permute-done.refs_6_), channel_id=1, source_target_pairs={{0,4},{1,5},{2,6},{3,7},{4,0},{5,1},{6,2},{7,3},{8,12},{9,13},{10,... | collective-permute-start | bytes 1572872 | tf_op jit(solution)/shard_map/ppermute | solution.py:293
  19.7 0.0 collective-permute-done.4.refs_3_
  19.7 1.5 %collective-permute-start.8 = (bf16[128,1024]{1,0:T(8,128)(2,1)S(1)}, bf16[128,1024]{1,0:T(8,128)(2,1)S(1)}, u32[]{:S(2)}, u32[]{:S(2)}) collective-permute-start(bf16[128,1024]{1,0:T(8,128)(2,1)S(1)} %get-tuple-element.58), channel_id=1, source_target_pairs={{0,2},{1,3},{2,0},{3,1},{4,6},{5,7},{6,4},{7,5},{8,10},{9,11},{10,... | collective-permute-start | bytes 786440 | tf_op jit(solution)/shard_map/ppermute | solution.py:293
  21.2 0.7 collective-permute-done.3.refs_2_
  21.9 0.1 collective-permute-start.9
  22.0 3.5 %shard_map.66 = (f32[8,16,16,128]{3,2,1,0:T(8,128)S(1)}, f32[16,1024]{1,0:T(8,128)S(1)}) custom-call(s32[11]{0:T(128)S(1)} %stack.47.info_ref, bf16[128,1024]{1,0:T(8,128)(2,1)S(1)} %get-tuple-element.41.refs_0_, bf16[128,1024]{1,0:T(8,128)(2,1)S(1)} %collective-permute-done.2.refs_1_, bf16[128,1024]{1,0:T(8,128)(2,1)S(1)} %collective-permute-done.3.refs_2_, ...), custom_call_target="tpu_custom_call" | custom-call | flops 550000000 | bytes 1800000 | tf_op jit(solution)/shard_map/pallas_call | solution.py:26
  25.5 0.0 collective-permute-done.7.refs_1_
  25.5 0.6 collective-permute-start.10
  26.1 2.0 %shard_map.67.refs_4_ = f32[2,512,128]{2,1,0:T(8,128)S(1)} custom-call(s32[11]{0:T(128)S(1)} %stack.47.info_ref, bf16[128,1024]{1,0:T(8,128)(2,1)S(1)} %get-tuple-element.41.refs_0_, bf16[128,1024]{1,0:T(8,128)(2,1)S(1)} %collective-permute-done.2.refs_1_, bf16[128,1024]{1,0:T(8,128)(2,1)S(1)} %collective-permute-done.3.refs_2_, ...), custom_call_target="tpu_custom_call" | custom-call | flops 330000000 | bytes 1080000 | tf_op jit(solution)/shard_map/pallas_call | solution.py:26
  28.1 2.0 %shard_map.68.refs_4_ = f32[2,512,128]{2,1,0:T(8,128)S(1)} custom-call(s32[11]{0:T(128)S(1)} %stack.47.info_ref, bf16[128,1024]{1,0:T(8,128)(2,1)S(1)} %get-tuple-element.41.refs_0_, bf16[128,1024]{1,0:T(8,128)(2,1)S(1)} %collective-permute-done.2.refs_1_, bf16[128,1024]{1,0:T(8,128)(2,1)S(1)} %collective-permute-done.3.refs_2_, ...), custom_call_target="tpu_custom_call" | custom-call | flops 330000000 | bytes 1080000 | tf_op jit(solution)/shard_map/pallas_call | solution.py:26
  30.0 0.0 collective-permute-done.8.refs_2_
  30.0 1.5 %collective-permute-done.9.refs_3_ = bf16[128,1024]{1,0:T(8,128)(2,1)S(1)} collective-permute-done((bf16[128,1024]{1,0:T(8,128)(2,1)S(1)}, bf16[128,1024]{1,0:T(8,128)(2,1)S(1)}, u32[]{:S(2)}, u32[]{:S(2)}) %collective-permute-start.9) | collective-permute-done | bytes 262176 | tf_op jit(solution)/shard_map/ppermute | solution.py:293
  31.6 0.2 collective-permute-done.10.near_ref.refs_8_
  31.8 0.3 collective-permute-done.5.refs_8_
  32.1 0.0 collective-permute-done.6.refs_7_
  32.1 1.3 %collective-permute-start.14 = (bf16[128,2048]{1,0:T(8,128)(2,1)S(1)}, bf16[128,2048]{1,0:T(8,128)(2,1)S(1)}, u32[]{:S(2)}, u32[]{:S(2)}) collective-permute-start(bf16[128,2048]{1,0:T(8,128)(2,1)S(1)} %collective-permute-done.5.refs_8_), channel_id=1, source_target_pairs={{0,8},{1,9},{2,10},{3,11},{4,12},{5,13},{6,14},{7,15},{8,16},{9,17... | collective-permute-start | bytes 1572872 | tf_op jit(solution)/shard_map/ppermute | solution.py:298
  33.4 1.5 %collective-permute-start.15 = (bf16[128,2048]{1,0:T(8,128)(2,1)S(1)}, bf16[128,2048]{1,0:T(8,128)(2,1)S(1)}, u32[]{:S(2)}, u32[]{:S(2)}) collective-permute-start(bf16[128,2048]{1,0:T(8,128)(2,1)S(1)} %collective-permute-done.5.refs_8_), channel_id=1, source_target_pairs={{0,4},{1,5},{2,6},{3,7},{4,0},{5,1},{6,2},{7,3},{8,12},{9,13},{10,... | collective-permute-start | bytes 1572872 | tf_op jit(solution)/shard_map/ppermute | solution.py:293
  34.9 0.6 shard_map.71
  35.5 2.5 %collective-permute-start.11 = (f32[16,1024]{1,0:T(8,128)S(1)}, f32[16,1024]{1,0:T(8,128)S(1)}, u32[]{:S(2)}, u32[]{:S(2)}) collective-permute-start(f32[16,1024]{1,0:T(8,128)S(1)} %shard_map.71), channel_id=1, source_target_pairs={{0,8},{1,9},{2,10},{3,11},{4,12},{5,13},{6,14},{7,15},{8,16},{9,17... | collective-permute-start | bytes 196616 | tf_op jit(solution)/shard_map/ppermute | solution.py:298
  38.0 4.1 %collective-permute-start.12 = (f32[16,1024]{1,0:T(8,128)S(1)}, f32[16,1024]{1,0:T(8,128)S(1)}, u32[]{:S(2)}, u32[]{:S(2)}) collective-permute-start(f32[16,1024]{1,0:T(8,128)S(1)} %shard_map.71), channel_id=1, source_target_pairs={{0,16},{1,17},{2,18},{3,19},{4,20},{5,21},{6,22},{7,23},{8,24},{9,... | collective-permute-start | bytes 196616 | tf_op jit(solution)/shard_map/ppermute | solution.py:298
  42.2 1.3 %collective-permute-start.13 = (f32[16,1024]{1,0:T(8,128)S(1)}, f32[16,1024]{1,0:T(8,128)S(1)}, u32[]{:S(2)}, u32[]{:S(2)}) collective-permute-start(f32[16,1024]{1,0:T(8,128)S(1)} %shard_map.71), channel_id=1, source_target_pairs={{0,24},{1,25},{2,26},{3,27},{4,28},{5,29},{6,30},{7,31}} | collective-permute-start | bytes 196616 | tf_op jit(solution)/shard_map/ppermute | solution.py:298
  43.5 2.0 %shard_map.69.refs_4_ = f32[2,512,128]{2,1,0:T(8,128)S(1)} custom-call(s32[11]{0:T(128)S(1)} %stack.47.info_ref, bf16[128,1024]{1,0:T(8,128)(2,1)S(1)} %get-tuple-element.41.refs_0_, bf16[128,1024]{1,0:T(8,128)(2,1)S(1)} %collective-permute-done.2.refs_1_, bf16[128,1024]{1,0:T(8,128)(2,1)S(1)} %collective-permute-done.3.refs_2_, ...), custom_call_target="tpu_custom_call" | custom-call | flops 330000000 | bytes 1080000 | tf_op jit(solution)/shard_map/pallas_call | solution.py:26
  45.4 2.0 %shard_map.70.refs_4_ = f32[2,512,128]{2,1,0:T(8,128)S(1)} custom-call(s32[11]{0:T(128)S(1)} %stack.47.info_ref, bf16[128,1024]{1,0:T(8,128)(2,1)S(1)} %get-tuple-element.41.refs_0_, bf16[128,1024]{1,0:T(8,128)(2,1)S(1)} %collective-permute-done.2.refs_1_, bf16[128,1024]{1,0:T(8,128)(2,1)S(1)} %collective-permute-done.3.refs_2_, ...), custom_call_target="tpu_custom_call" | custom-call | flops 330000000 | bytes 1080000 | tf_op jit(solution)/shard_map/pallas_call | solution.py:26
  47.4 0.7 collective-permute-done.14.refs_10_
  48.1 0.0 collective-permute-done.15.refs_9_
  48.1 0.9 %collective-permute-start.19 = (bf16[128,1024]{1,0:T(8,128)(2,1)S(1)}, bf16[128,1024]{1,0:T(8,128)(2,1)S(1)}, u32[]{:S(2)}, u32[]{:S(2)}) collective-permute-start(bf16[128,1024]{1,0:T(8,128)(2,1)S(1)} %slice.7), channel_id=1, source_target_pairs={{0,4},{1,5},{2,6},{3,7},{4,0},{5,1},{6,2},{7,3},{8,12},{9,13},{10,... | collective-permute-start | bytes 786440 | tf_op jit(solution)/shard_map/ppermute | solution.py:293
  49.0 0.9 %collective-permute-start.16 = (bf16[128,1024]{1,0:T(8,128)(2,1)S(1)}, bf16[128,1024]{1,0:T(8,128)(2,1)S(1)}, u32[]{:S(2)}, u32[]{:S(2)}) collective-permute-start(bf16[128,1024]{1,0:T(8,128)(2,1)S(1)} %slice.6), channel_id=1, source_target_pairs={{0,8},{1,9},{2,10},{3,11},{4,12},{5,13},{6,14},{7,15},{8,16},{9,17... | collective-permute-start | bytes 786440 | tf_op jit(solution)/shard_map/ppermute | solution.py:298
  49.9 0.0 collective-permute-done.12.refs_10_
  49.9 0.1 collective-permute-done.13.refs_11_
  50.0 1.3 %shard_map.72.refs_0_ = bf16[2,512,128]{2,1,0:T(8,128)(2,1)S(1)} custom-call(s32[11]{0:T(128)S(1)} %stack.47.info_ref, bf16[128,1024]{1,0:T(8,128)(2,1)S(1)} %get-tuple-element.55.refs_0_, bf16[128,1024]{1,0:T(8,128)(2,1)S(1)} %collective-permute-done.7.refs_1_, bf16[128,1024]{1,0:T(8,128)(2,1)S(1)} %collective-permute-done.8.refs_2_, ...), custom_call_target="tpu_custom_call" | custom-call | flops 550000000 | bytes 1800000 | tf_op jit(solution)/shard_map/pallas_call | solution.py:26
  51.2 1.3 %shard_map.73.refs_1_ = bf16[2,512,128]{2,1,0:T(8,128)(2,1)S(1)} custom-call(s32[11]{0:T(128)S(1)} %stack.47.info_ref, bf16[128,1024]{1,0:T(8,128)(2,1)S(1)} %get-tuple-element.55.refs_0_, bf16[128,1024]{1,0:T(8,128)(2,1)S(1)} %collective-permute-done.7.refs_1_, bf16[128,1024]{1,0:T(8,128)(2,1)S(1)} %collective-permute-done.8.refs_2_, ...), custom_call_target="tpu_custom_call" | custom-call | flops 550000000 | bytes 1800000 | tf_op jit(solution)/shard_map/pallas_call | solution.py:26
  52.5 1.3 %shard_map.74.refs_2_ = bf16[2,512,128]{2,1,0:T(8,128)(2,1)S(1)} custom-call(s32[11]{0:T(128)S(1)} %stack.47.info_ref, bf16[128,1024]{1,0:T(8,128)(2,1)S(1)} %get-tuple-element.55.refs_0_, bf16[128,1024]{1,0:T(8,128)(2,1)S(1)} %collective-permute-done.7.refs_1_, bf16[128,1024]{1,0:T(8,128)(2,1)S(1)} %collective-permute-done.8.refs_2_, ...), custom_call_target="tpu_custom_call" | custom-call | flops 550000000 | bytes 1800000 | tf_op jit(solution)/shard_map/pallas_call | solution.py:26
  53.8 0.0 copy-start
  53.8 1.3 %shard_map.75.refs_3_ = bf16[2,512,128]{2,1,0:T(8,128)(2,1)S(1)} custom-call(s32[11]{0:T(128)S(1)} %stack.47.info_ref, bf16[128,1024]{1,0:T(8,128)(2,1)S(1)} %get-tuple-element.55.refs_0_, bf16[128,1024]{1,0:T(8,128)(2,1)S(1)} %collective-permute-done.7.refs_1_, bf16[128,1024]{1,0:T(8,128)(2,1)S(1)} %collective-permute-done.8.refs_2_, ...), custom_call_target="tpu_custom_call" | custom-call | flops 550000000 | bytes 1800000 | tf_op jit(solution)/shard_map/pallas_call | solution.py:26
  55.0 0.9 %collective-permute-done.19.refs_11_ = bf16[128,1024]{1,0:T(8,128)(2,1)S(1)} collective-permute-done((bf16[128,1024]{1,0:T(8,128)(2,1)S(1)}, bf16[128,1024]{1,0:T(8,128)(2,1)S(1)}, u32[]{:S(2)}, u32[]{:S(2)}) %collective-permute-start.19) | collective-permute-done | bytes 262176 | tf_op jit(solution)/shard_map/ppermute | solution.py:293
  55.9 1.9 %shard_map.78 = (f32[256,1024]{1,0:T(8,128)S(1)}, bf16[256,1024]{1,0:T(8,128)(2,1)S(1)}) custom-call(s32[11]{0:T(128)S(1)} %stack.47.info_ref, bf16[2,512,128]{2,1,0:T(8,128)(2,1)S(1)} %shard_map.72.refs_0_, bf16[2,512,128]{2,1,0:T(8,128)(2,1)S(1)} %shard_map.73.refs_1_, bf16[2,512,128]{2,1,0:T(8,128)(2,1)S(1)} %shard_map.74.refs_2_, ...), custom_call_target="tpu_custom_call" | custom-call | flops 1100000000 | bytes 3600000 | tf_op jit(solution)/shard_map/pallas_call | solution.py:26
  57.8 0.1 collective-permute-start.20
  57.9 1.9 %shard_map.76 = (f32[256,1024]{1,0:T(8,128)S(1)}, bf16[256,1024]{1,0:T(8,128)(2,1)S(1)}) custom-call(s32[11]{0:T(128)S(1)} %stack.47.info_ref, bf16[2,512,128]{2,1,0:T(8,128)(2,1)S(1)} %shard_map.72.refs_0_, bf16[2,512,128]{2,1,0:T(8,128)(2,1)S(1)} %shard_map.73.refs_1_, bf16[2,512,128]{2,1,0:T(8,128)(2,1)S(1)} %shard_map.74.refs_2_, ...), custom_call_target="tpu_custom_call" | custom-call | flops 1100000000 | bytes 3600000 | tf_op jit(solution)/shard_map/pallas_call | solution.py:26
  59.8 0.6 collective-permute-start.17
  60.4 0.0 collective-permute-done.20.got_ref
  60.4 0.6 shard_map.79
  61.0 1.8 %collective-permute-start.21 = (bf16[128,1024]{1,0:T(8,128)(2,1)S(1)}, bf16[128,1024]{1,0:T(8,128)(2,1)S(1)}, u32[]{:S(2)}, u32[]{:S(2)}) collective-permute-start(bf16[128,1024]{1,0:T(8,128)(2,1)S(1)} %get-tuple-element.74), channel_id=1, source_target_pairs={{0,2},{1,3},{2,0},{3,1},{4,6},{5,7},{6,4},{7,5},{8,10},{9,11},{10,... | collective-permute-start | bytes 786440 | tf_op jit(solution)/shard_map/ppermute | solution.py:293
  62.9 0.6 shard_map.77
  63.5 0.9 %collective-permute-start.18 = (bf16[128,1024]{1,0:T(8,128)(2,1)S(1)}, bf16[128,1024]{1,0:T(8,128)(2,1)S(1)}, u32[]{:S(2)}, u32[]{:S(2)}) collective-permute-start(bf16[128,1024]{1,0:T(8,128)(2,1)S(1)} %get-tuple-element.69), channel_id=1, source_target_pairs={{0,2},{1,3},{2,0},{3,1},{4,6},{5,7},{6,4},{7,5},{8,10},{9,11},{10,... | collective-permute-start | bytes 786440 | tf_op jit(solution)/shard_map/ppermute | solution.py:293
  64.4 5.8 %collective-permute-done.21.far_ref = bf16[128,1024]{1,0:T(8,128)(2,1)S(1)} collective-permute-done((bf16[128,1024]{1,0:T(8,128)(2,1)S(1)}, bf16[128,1024]{1,0:T(8,128)(2,1)S(1)}, u32[]{:S(2)}, u32[]{:S(2)}) %collective-permute-start.21) | collective-permute-done | bytes 262176 | tf_op jit(solution)/shard_map/ppermute | solution.py:293
  70.2 1.3 %shard_map.80.refs_0_ = bf16[128,2048]{1,0:T(8,128)(2,1)} custom-call(s32[11]{0:T(128)S(1)} %stack.47.info_ref, f32[128,1024]{1,0:T(8,128)S(1)} %get-tuple-element.73.mine_ref, bf16[128,1024]{1,0:T(8,128)(2,1)S(1)} %collective-permute-done.21.far_ref), custom_call_target="tpu_custom_call" | custom-call | tf_op jit(solution)/shard_map/pallas_call | solution.py:268
  71.6 3.4 %collective-permute-done.18.far_ref = bf16[128,1024]{1,0:T(8,128)(2,1)S(1)} collective-permute-done((bf16[128,1024]{1,0:T(8,128)(2,1)S(1)}, bf16[128,1024]{1,0:T(8,128)(2,1)S(1)}, u32[]{:S(2)}, u32[]{:S(2)}) %collective-permute-start.18) | collective-permute-done | bytes 262176 | tf_op jit(solution)/shard_map/ppermute | solution.py:293
  75.0 1.3 %shard_map.81 = bf16[128,2048]{1,0:T(8,128)(2,1)} custom-call(s32[11]{0:T(128)S(1)} %stack.47.info_ref, f32[128,1024]{1,0:T(8,128)S(1)} %get-tuple-element.68.mine_ref, bf16[128,1024]{1,0:T(8,128)(2,1)S(1)} %collective-permute-done.18.far_ref, bf16[128,2048]{1,0:T(8,128)(2,1)} %shard_map.80.refs_0_), custom_call_target="tpu_custom_call", output_to_operand_aliasing={{}: (3, {})} | custom-call | tf_op jit(solution)/shard_map/pallas_call | solution.py:268
  (14 shorter events, 0.1 us)
Async XLA Ops:
  0.0 17.2 %collective-permute-start = (bf16[128,2048]{1,0:T(8,128)(2,1)}, bf16[128,2048]{1,0:T(8,128)(2,1)S(1)}, u32[]{:S(2)}, u32[]{:S(2)}) collective-permute-start(bf16[128,2048]{1,0:T(8,128)(2,1)} %refs_4_.3), channel_id=1, source_target_pairs={{0,8},{1,9},{2,10},{3,11},{4,12},{5,13},{6,14},{7,15},{8,16},{9,17... | collective-permute-start | bytes 1572872 | tf_op jit(solution)/shard_map/ppermute | solution.py:298
  3.0 14.2 %collective-permute-start.1 = (bf16[128,2048]{1,0:T(8,128)(2,1)}, bf16[128,2048]{1,0:T(8,128)(2,1)S(1)}, u32[]{:S(2)}, u32[]{:S(2)}) collective-permute-start(bf16[128,2048]{1,0:T(8,128)(2,1)} %refs_4_.3), channel_id=1, source_target_pairs={{0,4},{1,5},{2,6},{3,7},{4,0},{5,1},{6,2},{7,3},{8,12},{9,13},{10,... | collective-permute-start | bytes 1572872 | tf_op jit(solution)/shard_map/ppermute | solution.py:293
  4.5 4.6 %copy-start.5 = (f32[4096]{0:T(1024)S(1)}, f32[4096]{0:T(1024)}, u32[]{:S(2)}) copy-start(f32[4096]{0:T(1024)} %param.10) | copy-start | bytes 49156
  4.6 1.2 %copy-start.1 = (bf16[128,4096]{1,0:T(8,128)(2,1)S(1)}, bf16[128,4096]{1,0:T(8,128)(2,1)}, u32[]{:S(2)}) copy-start(bf16[128,4096]{1,0:T(8,128)(2,1)} %refs_0_.2) | copy-start | bytes 3145732
  5.9 3.3 %copy-start.2 = (bf16[128,4096]{1,0:T(8,128)(2,1)S(1)}, bf16[128,4096]{1,0:T(8,128)(2,1)}, u32[]{:S(2)}) copy-start(bf16[128,4096]{1,0:T(8,128)(2,1)} %refs_0_.3) | copy-start | bytes 3145732
  6.9 5.8 %collective-permute-start.2 = (bf16[128,1024]{1,0:T(8,128)(2,1)S(1)}, bf16[128,1024]{1,0:T(8,128)(2,1)S(1)}, u32[]{:S(2)}, u32[]{:S(2)}) collective-permute-start(bf16[128,1024]{1,0:T(8,128)(2,1)S(1)} %get-tuple-element.42), channel_id=1, source_target_pairs={{0,1},{1,0},{2,3},{3,2},{4,5},{5,4},{6,7},{7,6},{8,9},{9,8},{10,11... | collective-permute-start | bytes 786440 | tf_op jit(solution)/shard_map/ppermute | solution.py:293
  7.0 12.7 %collective-permute-start.4 = (bf16[128,1024]{1,0:T(8,128)(2,1)S(1)}, bf16[128,1024]{1,0:T(8,128)(2,1)S(1)}, u32[]{:S(2)}, u32[]{:S(2)}) collective-permute-start(bf16[128,1024]{1,0:T(8,128)(2,1)S(1)} %get-tuple-element.44), channel_id=1, source_target_pairs={{0,3},{1,2},{2,1},{3,0},{4,7},{5,6},{6,5},{7,4},{8,11},{9,10},{10,... | collective-permute-start | bytes 786440 | tf_op jit(solution)/shard_map/ppermute | solution.py:293
  8.6 13.2 %collective-permute-start.3 = (bf16[128,1024]{1,0:T(8,128)(2,1)S(1)}, bf16[128,1024]{1,0:T(8,128)(2,1)S(1)}, u32[]{:S(2)}, u32[]{:S(2)}) collective-permute-start(bf16[128,1024]{1,0:T(8,128)(2,1)S(1)} %get-tuple-element.43), channel_id=1, source_target_pairs={{0,2},{1,3},{2,0},{3,1},{4,6},{5,7},{6,4},{7,5},{8,10},{9,11},{10,... | collective-permute-start | bytes 786440 | tf_op jit(solution)/shard_map/ppermute | solution.py:293
  9.2 1.0 %copy-start.3 = (f32[4096,16]{0,1:T(8,128)S(1)}, f32[4096,16]{0,1:T(8,128)}, u32[]{:S(2)}) copy-start(f32[4096,16]{0,1:T(8,128)} %param.8) | copy-start | bytes 786436
  10.1 0.9 %copy-start.4 = (f32[4096,16]{0,1:T(8,128)S(1)}, f32[4096,16]{0,1:T(8,128)}, u32[]{:S(2)}) copy-start(f32[4096,16]{0,1:T(8,128)} %param.9) | copy-start | bytes 786436
  12.8 12.7 %collective-permute-start.7 = (bf16[128,1024]{1,0:T(8,128)(2,1)S(1)}, bf16[128,1024]{1,0:T(8,128)(2,1)S(1)}, u32[]{:S(2)}, u32[]{:S(2)}) collective-permute-start(bf16[128,1024]{1,0:T(8,128)(2,1)S(1)} %get-tuple-element.56), channel_id=1, source_target_pairs={{0,1},{1,0},{2,3},{3,2},{4,5},{5,4},{6,7},{7,6},{8,9},{9,8},{10,11... | collective-permute-start | bytes 786440 | tf_op jit(solution)/shard_map/ppermute | solution.py:293
  17.2 14.9 %collective-permute-start.5 = (bf16[128,2048]{1,0:T(8,128)(2,1)S(1)}, bf16[128,2048]{1,0:T(8,128)(2,1)S(1)}, u32[]{:S(2)}, u32[]{:S(2)}) collective-permute-start(bf16[128,2048]{1,0:T(8,128)(2,1)S(1)} %collective-permute-done.refs_6_), channel_id=1, source_target_pairs={{0,8},{1,9},{2,10},{3,11},{4,12},{5,13},{6,14},{7,15},{8,16},{9,17... | collective-permute-start | bytes 1572872 | tf_op jit(solution)/shard_map/ppermute | solution.py:298
  18.2 13.9 %collective-permute-start.6 = (bf16[128,2048]{1,0:T(8,128)(2,1)S(1)}, bf16[128,2048]{1,0:T(8,128)(2,1)S(1)}, u32[]{:S(2)}, u32[]{:S(2)}) collective-permute-start(bf16[128,2048]{1,0:T(8,128)(2,1)S(1)} %collective-permute-done.refs_6_), channel_id=1, source_target_pairs={{0,4},{1,5},{2,6},{3,7},{4,0},{5,1},{6,2},{7,3},{8,12},{9,13},{10,... | collective-permute-start | bytes 1572872 | tf_op jit(solution)/shard_map/ppermute | solution.py:293
  19.7 10.3 %collective-permute-start.8 = (bf16[128,1024]{1,0:T(8,128)(2,1)S(1)}, bf16[128,1024]{1,0:T(8,128)(2,1)S(1)}, u32[]{:S(2)}, u32[]{:S(2)}) collective-permute-start(bf16[128,1024]{1,0:T(8,128)(2,1)S(1)} %get-tuple-element.58), channel_id=1, source_target_pairs={{0,2},{1,3},{2,0},{3,1},{4,6},{5,7},{6,4},{7,5},{8,10},{9,11},{10,... | collective-permute-start | bytes 786440 | tf_op jit(solution)/shard_map/ppermute | solution.py:293
  21.9 9.7 %collective-permute-start.9 = (bf16[128,1024]{1,0:T(8,128)(2,1)S(1)}, bf16[128,1024]{1,0:T(8,128)(2,1)S(1)}, u32[]{:S(2)}, u32[]{:S(2)}) collective-permute-start(bf16[128,1024]{1,0:T(8,128)(2,1)S(1)} %get-tuple-element.60), channel_id=1, source_target_pairs={{0,3},{1,2},{2,1},{3,0},{4,7},{5,6},{6,5},{7,4},{8,11},{9,10},{10,... | collective-permute-start | bytes 786440 | tf_op jit(solution)/shard_map/ppermute | solution.py:293
  25.5 6.3 %collective-permute-start.10 = (f32[16,1024]{1,0:T(8,128)S(1)}, f32[16,1024]{1,0:T(8,128)S(1)}, u32[]{:S(2)}, u32[]{:S(2)}) collective-permute-start(f32[16,1024]{1,0:T(8,128)S(1)} %get-tuple-element.62.end_ref), channel_id=1, source_target_pairs={{0,4},{1,5},{2,6},{3,7},{4,0},{5,1},{6,2},{7,3},{8,12},{9,13},{10,... | collective-permute-start | bytes 196616 | tf_op jit(solution)/shard_map/ppermute | solution.py:293
  32.1 16.0 %collective-permute-start.14 = (bf16[128,2048]{1,0:T(8,128)(2,1)S(1)}, bf16[128,2048]{1,0:T(8,128)(2,1)S(1)}, u32[]{:S(2)}, u32[]{:S(2)}) collective-permute-start(bf16[128,2048]{1,0:T(8,128)(2,1)S(1)} %collective-permute-done.5.refs_8_), channel_id=1, source_target_pairs={{0,8},{1,9},{2,10},{3,11},{4,12},{5,13},{6,14},{7,15},{8,16},{9,17... | collective-permute-start | bytes 1572872 | tf_op jit(solution)/shard_map/ppermute | solution.py:298
  33.4 14.7 %collective-permute-start.15 = (bf16[128,2048]{1,0:T(8,128)(2,1)S(1)}, bf16[128,2048]{1,0:T(8,128)(2,1)S(1)}, u32[]{:S(2)}, u32[]{:S(2)}) collective-permute-start(bf16[128,2048]{1,0:T(8,128)(2,1)S(1)} %collective-permute-done.5.refs_8_), channel_id=1, source_target_pairs={{0,4},{1,5},{2,6},{3,7},{4,0},{5,1},{6,2},{7,3},{8,12},{9,13},{10,... | collective-permute-start | bytes 1572872 | tf_op jit(solution)/shard_map/ppermute | solution.py:293
  35.5 14.4 %collective-permute-start.11 = (f32[16,1024]{1,0:T(8,128)S(1)}, f32[16,1024]{1,0:T(8,128)S(1)}, u32[]{:S(2)}, u32[]{:S(2)}) collective-permute-start(f32[16,1024]{1,0:T(8,128)S(1)} %shard_map.71), channel_id=1, source_target_pairs={{0,8},{1,9},{2,10},{3,11},{4,12},{5,13},{6,14},{7,15},{8,16},{9,17... | collective-permute-start | bytes 196616 | tf_op jit(solution)/shard_map/ppermute | solution.py:298
  38.0 11.9 %collective-permute-start.12 = (f32[16,1024]{1,0:T(8,128)S(1)}, f32[16,1024]{1,0:T(8,128)S(1)}, u32[]{:S(2)}, u32[]{:S(2)}) collective-permute-start(f32[16,1024]{1,0:T(8,128)S(1)} %shard_map.71), channel_id=1, source_target_pairs={{0,16},{1,17},{2,18},{3,19},{4,20},{5,21},{6,22},{7,23},{8,24},{9,... | collective-permute-start | bytes 196616 | tf_op jit(solution)/shard_map/ppermute | solution.py:298
  42.2 7.8 %collective-permute-start.13 = (f32[16,1024]{1,0:T(8,128)S(1)}, f32[16,1024]{1,0:T(8,128)S(1)}, u32[]{:S(2)}, u32[]{:S(2)}) collective-permute-start(f32[16,1024]{1,0:T(8,128)S(1)} %shard_map.71), channel_id=1, source_target_pairs={{0,24},{1,25},{2,26},{3,27},{4,28},{5,29},{6,30},{7,31}} | collective-permute-start | bytes 196616 | tf_op jit(solution)/shard_map/ppermute | solution.py:298
  48.1 7.8 %collective-permute-start.19 = (bf16[128,1024]{1,0:T(8,128)(2,1)S(1)}, bf16[128,1024]{1,0:T(8,128)(2,1)S(1)}, u32[]{:S(2)}, u32[]{:S(2)}) collective-permute-start(bf16[128,1024]{1,0:T(8,128)(2,1)S(1)} %slice.7), channel_id=1, source_target_pairs={{0,4},{1,5},{2,6},{3,7},{4,0},{5,1},{6,2},{7,3},{8,12},{9,13},{10,... | collective-permute-start | bytes 786440 | tf_op jit(solution)/shard_map/ppermute | solution.py:293
  49.0 8.9 %collective-permute-start.16 = (bf16[128,1024]{1,0:T(8,128)(2,1)S(1)}, bf16[128,1024]{1,0:T(8,128)(2,1)S(1)}, u32[]{:S(2)}, u32[]{:S(2)}) collective-permute-start(bf16[128,1024]{1,0:T(8,128)(2,1)S(1)} %slice.6), channel_id=1, source_target_pairs={{0,8},{1,9},{2,10},{3,11},{4,12},{5,13},{6,14},{7,15},{8,16},{9,17... | collective-permute-start | bytes 786440 | tf_op jit(solution)/shard_map/ppermute | solution.py:298
  53.8 2.2 %copy-start = (bf16[128,2048]{1,0:T(8,128)(2,1)S(1)}, bf16[128,2048]{1,0:T(8,128)(2,1)}, u32[]{:S(2)}) copy-start(bf16[128,2048]{1,0:T(8,128)(2,1)} %refs_4_.3) | copy-start | bytes 1572868
  57.8 2.6 %collective-permute-start.20 = (bf16[256,1024]{1,0:T(8,128)(2,1)S(1)}, bf16[256,1024]{1,0:T(8,128)(2,1)S(1)}, u32[]{:S(2)}, u32[]{:S(2)}) collective-permute-start(bf16[256,1024]{1,0:T(8,128)(2,1)S(1)} %get-tuple-element.72), channel_id=1, source_target_pairs={{0,1},{1,0},{2,3},{3,2},{4,5},{5,4},{6,7},{7,6},{8,9},{9,8},{10,11... | collective-permute-start | bytes 1572872 | tf_op jit(solution)/shard_map/ppermute | solution.py:293
  59.8 3.0 %collective-permute-start.17 = (bf16[256,1024]{1,0:T(8,128)(2,1)S(1)}, bf16[256,1024]{1,0:T(8,128)(2,1)S(1)}, u32[]{:S(2)}, u32[]{:S(2)}) collective-permute-start(bf16[256,1024]{1,0:T(8,128)(2,1)S(1)} %get-tuple-element.67), channel_id=1, source_target_pairs={{0,1},{1,0},{2,3},{3,2},{4,5},{5,4},{6,7},{7,6},{8,9},{9,8},{10,11... | collective-permute-start | bytes 1572872 | tf_op jit(solution)/shard_map/ppermute | solution.py:293
  61.0 9.2 %collective-permute-start.21 = (bf16[128,1024]{1,0:T(8,128)(2,1)S(1)}, bf16[128,1024]{1,0:T(8,128)(2,1)S(1)}, u32[]{:S(2)}, u32[]{:S(2)}) collective-permute-start(bf16[128,1024]{1,0:T(8,128)(2,1)S(1)} %get-tuple-element.74), channel_id=1, source_target_pairs={{0,2},{1,3},{2,0},{3,1},{4,6},{5,7},{6,4},{7,5},{8,10},{9,11},{10,... | collective-permute-start | bytes 786440 | tf_op jit(solution)/shard_map/ppermute | solution.py:293
  63.5 11.5 %collective-permute-start.18 = (bf16[128,1024]{1,0:T(8,128)(2,1)S(1)}, bf16[128,1024]{1,0:T(8,128)(2,1)S(1)}, u32[]{:S(2)}, u32[]{:S(2)}) collective-permute-start(bf16[128,1024]{1,0:T(8,128)(2,1)S(1)} %get-tuple-element.69), channel_id=1, source_target_pairs={{0,2},{1,3},{2,0},{3,1},{4,6},{5,7},{6,4},{7,5},{8,10},{9,11},{10,... | collective-permute-start | bytes 786440 | tf_op jit(solution)/shard_map/ppermute | solution.py:293

commit v8 on v7

--- a/solution.py
+++ b/solution.py
@@ -221,7 +221,7 @@
 def product(pieces, in_slots, first, info_ref, gated, weights, into, before):
     per = gated[0].shape[0]
     wide = into.shape[1]
-    step = min(wide, 256)
+    step = min(wide, 512)
     slots = range(first, first + len(weights))
     if in_slots:
         left = [gated[slot // per][slot % per] for slot in slots]

time: 76.5 us -> 76.5 us (level)
  no operation moved by 1% of the time
where the time goes in v8:
time: 76.5 us; the launch traced here: 76.3 us
  starting transfers between devices  27.4 us (36%)
  Pallas kernels  27.4 us (36%)
  waiting for transfers between devices  17.9 us (23%)
  local copies, waits for them, and re-layouts  3.26 us (4%)
    pallas_call x14, Pallas kernels, run(): pl.pallas_call(kernel, out_shape=out_shape, in_specs=[pl.BlockSpec(memory...  22 us
    ppermute x7, starting transfers between devices, up(): return lax.ppermute(value, 'seq', pairs)  14.2 us
    ppermute x15, starting transfers between devices, swap(): return lax.ppermute(value, 'seq', [(i, i ^ bit) for i in range(count)])  13.2 us
    ppermute x15, waiting for transfers between devices, swap(): return lax.ppermute(value, 'seq', [(i, i ^ bit) for i in range(count)])  12.6 us
    ppermute x7, waiting for transfers between devices, up(): return lax.ppermute(value, 'seq', pairs)  5.35 us
    unnamed x12, local copies, waits for them, and re-layouts  3.14 us
    pallas_call x2, Pallas kernels, deal(): pl.pallas_call(functools.partial(deal_kernel, team, depth, plan), out_sha...  2.78 us
    pallas_call x2, Pallas kernels, finish(): pl.pallas_call(functools.partial(finish_kernel, at), out_shape=jax.ShapeD...  2.59 us
  transfers between devices with their start and end apart: 22, of which 10 were waited for; matrix products, arithmetic and copies ran while one was open for 0% of the time, Pallas kernels for 34%

profile of v8, /device:TPU:0, one launch (start us, length us, event | category | flops | bytes accessed | tf_op | source)
XLA Modules:
  0.0 76.3 jit_solution(4517468925723221424)
XLA Ops:
  0.0 3.0 %collective-permute-start = (bf16[128,2048]{1,0:T(8,128)(2,1)}, bf16[128,2048]{1,0:T(8,128)(2,1)S(1)}, u32[]{:S(2)}, u32[]{:S(2)}) collective-permute-start(bf16[128,2048]{1,0:T(8,128)(2,1)} %refs_4_.3), channel_id=1, source_target_pairs={{0,8},{1,9},{2,10},{3,11},{4,12},{5,13},{6,14},{7,15},{8,16},{9,17... | collective-permute-start | bytes 1572872 | tf_op jit(solution)/shard_map/ppermute | solution.py:298
  3.0 1.5 %collective-permute-start.1 = (bf16[128,2048]{1,0:T(8,128)(2,1)}, bf16[128,2048]{1,0:T(8,128)(2,1)S(1)}, u32[]{:S(2)}, u32[]{:S(2)}) collective-permute-start(bf16[128,2048]{1,0:T(8,128)(2,1)} %refs_4_.3), channel_id=1, source_target_pairs={{0,4},{1,5},{2,6},{3,7},{4,0},{5,1},{6,2},{7,3},{8,12},{9,13},{10,... | collective-permute-start | bytes 1572872 | tf_op jit(solution)/shard_map/ppermute | solution.py:293
  4.5 0.1 stack.47.info_ref
  4.6 1.2 %copy-done.1 = bf16[128,4096]{1,0:T(8,128)(2,1)S(1)} copy-done((bf16[128,4096]{1,0:T(8,128)(2,1)S(1)}, bf16[128,4096]{1,0:T(8,128)(2,1)}, u32[]{:S(2)}) %copy-start.1) | copy-done | bytes 1048600
  5.9 1.1 %shard_map.64 = (bf16[128,1024]{1,0:T(8,128)(2,1)S(1)}, bf16[128,1024]{1,0:T(8,128)(2,1)S(1)}, bf16[128,1024]{1,0:T(8,128)(2,1)S(1)}, bf16[128,1024]{1,0:T(8,128)(2,1)S(1)}) custom-call(s32[11]{0:T(128)S(1)} %stack.47.info_ref, bf16[128,4096]{1,0:T(8,128)(2,1)S(1)} %copy-done.1), custom_call_target="tpu_custom_call" | custom-call | tf_op jit(solution)/shard_map/pallas_call | solution.py:72
  6.9 0.1 collective-permute-start.2
  7.0 1.6 %collective-permute-start.4 = (bf16[128,1024]{1,0:T(8,128)(2,1)S(1)}, bf16[128,1024]{1,0:T(8,128)(2,1)S(1)}, u32[]{:S(2)}, u32[]{:S(2)}) collective-permute-start(bf16[128,1024]{1,0:T(8,128)(2,1)S(1)} %get-tuple-element.44), channel_id=1, source_target_pairs={{0,3},{1,2},{2,1},{3,0},{4,7},{5,6},{6,5},{7,4},{8,11},{9,10},{10,... | collective-permute-start | bytes 786440 | tf_op jit(solution)/shard_map/ppermute | solution.py:293
  8.6 0.5 collective-permute-start.3
  9.2 0.9 %copy-done.3 = f32[4096,16]{0,1:T(8,128)S(1)} copy-done((f32[4096,16]{0,1:T(8,128)S(1)}, f32[4096,16]{0,1:T(8,128)}, u32[]{:S(2)}) %copy-start.3) | copy-done | bytes 262168
  10.1 0.9 %copy-done.4 = f32[4096,16]{0,1:T(8,128)S(1)} copy-done((f32[4096,16]{0,1:T(8,128)S(1)}, f32[4096,16]{0,1:T(8,128)}, u32[]{:S(2)}) %copy-start.4) | copy-done | bytes 262168
  11.1 1.7 %shard_map.65 = (bf16[128,1024]{1,0:T(8,128)(2,1)S(1)}, bf16[128,1024]{1,0:T(8,128)(2,1)S(1)}, bf16[128,1024]{1,0:T(8,128)(2,1)S(1)}, bf16[128,1024]{1,0:T(8,128...) custom-call(s32[11]{0:T(128)S(1)} %stack.47.info_ref, ...), custom_call_target="tpu_custom_call" | custom-call | tf_op jit(solution)/shard_map/pallas_call | solution.py:72
  12.8 0.0 collective-permute-done.2.refs_1_
  12.8 0.1 collective-permute-start.7
  12.9 4.3 %collective-permute-done.refs_6_ = bf16[128,2048]{1,0:T(8,128)(2,1)S(1)} collective-permute-done((bf16[128,2048]{1,0:T(8,128)(2,1)}, bf16[128,2048]{1,0:T(8,128)(2,1)S(1)}, u32[]{:S(2)}, u32[]{:S(2)}) %collective-permute-start) | collective-permute-done | bytes 524320 | tf_op jit(solution)/shard_map/ppermute | solution.py:298
  17.2 0.0 collective-permute-done.1.refs_5_
  17.2 1.0 %collective-permute-start.5 = (bf16[128,2048]{1,0:T(8,128)(2,1)S(1)}, bf16[128,2048]{1,0:T(8,128)(2,1)S(1)}, u32[]{:S(2)}, u32[]{:S(2)}) collective-permute-start(bf16[128,2048]{1,0:T(8,128)(2,1)S(1)} %collective-permute-done.refs_6_), channel_id=1, source_target_pairs={{0,8},{1,9},{2,10},{3,11},{4,12},{5,13},{6,14},{7,15},{8,16},{9,17... | collective-permute-start | bytes 1572872 | tf_op jit(solution)/shard_map/ppermute | solution.py:298
  18.2 1.5 %collective-permute-start.6 = (bf16[128,2048]{1,0:T(8,128)(2,1)S(1)}, bf16[128,2048]{1,0:T(8,128)(2,1)S(1)}, u32[]{:S(2)}, u32[]{:S(2)}) collective-permute-start(bf16[128,2048]{1,0:T(8,128)(2,1)S(1)} %collective-permute-done.refs_6_), channel_id=1, source_target_pairs={{0,4},{1,5},{2,6},{3,7},{4,0},{5,1},{6,2},{7,3},{8,12},{9,13},{10,... | collective-permute-start | bytes 1572872 | tf_op jit(solution)/shard_map/ppermute | solution.py:293
  19.7 0.0 collective-permute-done.4.refs_3_
  19.7 1.5 %collective-permute-start.8 = (bf16[128,1024]{1,0:T(8,128)(2,1)S(1)}, bf16[128,1024]{1,0:T(8,128)(2,1)S(1)}, u32[]{:S(2)}, u32[]{:S(2)}) collective-permute-start(bf16[128,1024]{1,0:T(8,128)(2,1)S(1)} %get-tuple-element.58), channel_id=1, source_target_pairs={{0,2},{1,3},{2,0},{3,1},{4,6},{5,7},{6,4},{7,5},{8,10},{9,11},{10,... | collective-permute-start | bytes 786440 | tf_op jit(solution)/shard_map/ppermute | solution.py:293
  21.2 0.7 collective-permute-done.3.refs_2_
  21.9 0.1 collective-permute-start.9
  22.0 3.5 %shard_map.66 = (f32[8,16,16,128]{3,2,1,0:T(8,128)S(1)}, f32[16,1024]{1,0:T(8,128)S(1)}) custom-call(s32[11]{0:T(128)S(1)} %stack.47.info_ref, bf16[128,1024]{1,0:T(8,128)(2,1)S(1)} %get-tuple-element.41.refs_0_, bf16[128,1024]{1,0:T(8,128)(2,1)S(1)} %collective-permute-done.2.refs_1_, bf16[128,1024]{1,0:T(8,128)(2,1)S(1)} %collective-permute-done.3.refs_2_, ...), custom_call_target="tpu_custom_call" | custom-call | flops 550000000 | bytes 1800000 | tf_op jit(solution)/shard_map/pallas_call | solution.py:26
  25.5 0.0 collective-permute-done.7.refs_1_
  25.5 0.6 collective-permute-start.10
  26.1 2.0 %shard_map.67.refs_4_ = f32[2,512,128]{2,1,0:T(8,128)S(1)} custom-call(s32[11]{0:T(128)S(1)} %stack.47.info_ref, bf16[128,1024]{1,0:T(8,128)(2,1)S(1)} %get-tuple-element.41.refs_0_, bf16[128,1024]{1,0:T(8,128)(2,1)S(1)} %collective-permute-done.2.refs_1_, bf16[128,1024]{1,0:T(8,128)(2,1)S(1)} %collective-permute-done.3.refs_2_, ...), custom_call_target="tpu_custom_call" | custom-call | flops 330000000 | bytes 1080000 | tf_op jit(solution)/shard_map/pallas_call | solution.py:26
  28.1 2.0 %shard_map.68.refs_4_ = f32[2,512,128]{2,1,0:T(8,128)S(1)} custom-call(s32[11]{0:T(128)S(1)} %stack.47.info_ref, bf16[128,1024]{1,0:T(8,128)(2,1)S(1)} %get-tuple-element.41.refs_0_, bf16[128,1024]{1,0:T(8,128)(2,1)S(1)} %collective-permute-done.2.refs_1_, bf16[128,1024]{1,0:T(8,128)(2,1)S(1)} %collective-permute-done.3.refs_2_, ...), custom_call_target="tpu_custom_call" | custom-call | flops 330000000 | bytes 1080000 | tf_op jit(solution)/shard_map/pallas_call | solution.py:26
  30.0 0.0 collective-permute-done.8.refs_2_
  30.0 1.5 %collective-permute-done.9.refs_3_ = bf16[128,1024]{1,0:T(8,128)(2,1)S(1)} collective-permute-done((bf16[128,1024]{1,0:T(8,128)(2,1)S(1)}, bf16[128,1024]{1,0:T(8,128)(2,1)S(1)}, u32[]{:S(2)}, u32[]{:S(2)}) %collective-permute-start.9) | collective-permute-done | bytes 262176 | tf_op jit(solution)/shard_map/ppermute | solution.py:293
  31.6 0.2 collective-permute-done.10.near_ref.refs_8_
  31.8 0.3 collective-permute-done.5.refs_8_
  32.1 0.0 collective-permute-done.6.refs_7_
  32.1 1.3 %collective-permute-start.14 = (bf16[128,2048]{1,0:T(8,128)(2,1)S(1)}, bf16[128,2048]{1,0:T(8,128)(2,1)S(1)}, u32[]{:S(2)}, u32[]{:S(2)}) collective-permute-start(bf16[128,2048]{1,0:T(8,128)(2,1)S(1)} %collective-permute-done.5.refs_8_), channel_id=1, source_target_pairs={{0,8},{1,9},{2,10},{3,11},{4,12},{5,13},{6,14},{7,15},{8,16},{9,17... | collective-permute-start | bytes 1572872 | tf_op jit(solution)/shard_map/ppermute | solution.py:298
  33.4 1.5 %collective-permute-start.15 = (bf16[128,2048]{1,0:T(8,128)(2,1)S(1)}, bf16[128,2048]{1,0:T(8,128)(2,1)S(1)}, u32[]{:S(2)}, u32[]{:S(2)}) collective-permute-start(bf16[128,2048]{1,0:T(8,128)(2,1)S(1)} %collective-permute-done.5.refs_8_), channel_id=1, source_target_pairs={{0,4},{1,5},{2,6},{3,7},{4,0},{5,1},{6,2},{7,3},{8,12},{9,13},{10,... | collective-permute-start | bytes 1572872 | tf_op jit(solution)/shard_map/ppermute | solution.py:293
  34.9 0.6 shard_map.71
  35.5 2.5 %collective-permute-start.11 = (f32[16,1024]{1,0:T(8,128)S(1)}, f32[16,1024]{1,0:T(8,128)S(1)}, u32[]{:S(2)}, u32[]{:S(2)}) collective-permute-start(f32[16,1024]{1,0:T(8,128)S(1)} %shard_map.71), channel_id=1, source_target_pairs={{0,8},{1,9},{2,10},{3,11},{4,12},{5,13},{6,14},{7,15},{8,16},{9,17... | collective-permute-start | bytes 196616 | tf_op jit(solution)/shard_map/ppermute | solution.py:298
  38.0 4.1 %collective-permute-start.12 = (f32[16,1024]{1,0:T(8,128)S(1)}, f32[16,1024]{1,0:T(8,128)S(1)}, u32[]{:S(2)}, u32[]{:S(2)}) collective-permute-start(f32[16,1024]{1,0:T(8,128)S(1)} %shard_map.71), channel_id=1, source_target_pairs={{0,16},{1,17},{2,18},{3,19},{4,20},{5,21},{6,22},{7,23},{8,24},{9,... | collective-permute-start | bytes 196616 | tf_op jit(solution)/shard_map/ppermute | solution.py:298
  42.2 1.3 %collective-permute-start.13 = (f32[16,1024]{1,0:T(8,128)S(1)}, f32[16,1024]{1,0:T(8,128)S(1)}, u32[]{:S(2)}, u32[]{:S(2)}) collective-permute-start(f32[16,1024]{1,0:T(8,128)S(1)} %shard_map.71), channel_id=1, source_target_pairs={{0,24},{1,25},{2,26},{3,27},{4,28},{5,29},{6,30},{7,31}} | collective-permute-start | bytes 196616 | tf_op jit(solution)/shard_map/ppermute | solution.py:298
  43.5 2.0 %shard_map.69.refs_4_ = f32[2,512,128]{2,1,0:T(8,128)S(1)} custom-call(s32[11]{0:T(128)S(1)} %stack.47.info_ref, bf16[128,1024]{1,0:T(8,128)(2,1)S(1)} %get-tuple-element.41.refs_0_, bf16[128,1024]{1,0:T(8,128)(2,1)S(1)} %collective-permute-done.2.refs_1_, bf16[128,1024]{1,0:T(8,128)(2,1)S(1)} %collective-permute-done.3.refs_2_, ...), custom_call_target="tpu_custom_call" | custom-call | flops 330000000 | bytes 1080000 | tf_op jit(solution)/shard_map/pallas_call | solution.py:26
  45.4 2.0 %shard_map.70.refs_4_ = f32[2,512,128]{2,1,0:T(8,128)S(1)} custom-call(s32[11]{0:T(128)S(1)} %stack.47.info_ref, bf16[128,1024]{1,0:T(8,128)(2,1)S(1)} %get-tuple-element.41.refs_0_, bf16[128,1024]{1,0:T(8,128)(2,1)S(1)} %collective-permute-done.2.refs_1_, bf16[128,1024]{1,0:T(8,128)(2,1)S(1)} %collective-permute-done.3.refs_2_, ...), custom_call_target="tpu_custom_call" | custom-call | flops 330000000 | bytes 1080000 | tf_op jit(solution)/shard_map/pallas_call | solution.py:26
  47.4 0.7 collective-permute-done.14.refs_10_
  48.1 0.0 collective-permute-done.15.refs_9_
  48.1 0.9 %collective-permute-start.19 = (bf16[128,1024]{1,0:T(8,128)(2,1)S(1)}, bf16[128,1024]{1,0:T(8,128)(2,1)S(1)}, u32[]{:S(2)}, u32[]{:S(2)}) collective-permute-start(bf16[128,1024]{1,0:T(8,128)(2,1)S(1)} %slice.7), channel_id=1, source_target_pairs={{0,4},{1,5},{2,6},{3,7},{4,0},{5,1},{6,2},{7,3},{8,12},{9,13},{10,... | collective-permute-start | bytes 786440 | tf_op jit(solution)/shard_map/ppermute | solution.py:293
  49.0 0.9 %collective-permute-start.16 = (bf16[128,1024]{1,0:T(8,128)(2,1)S(1)}, bf16[128,1024]{1,0:T(8,128)(2,1)S(1)}, u32[]{:S(2)}, u32[]{:S(2)}) collective-permute-start(bf16[128,1024]{1,0:T(8,128)(2,1)S(1)} %slice.6), channel_id=1, source_target_pairs={{0,8},{1,9},{2,10},{3,11},{4,12},{5,13},{6,14},{7,15},{8,16},{9,17... | collective-permute-start | bytes 786440 | tf_op jit(solution)/shard_map/ppermute | solution.py:298
  49.9 0.0 collective-permute-done.12.refs_10_
  49.9 0.1 collective-permute-done.13.refs_11_
  50.0 1.3 %shard_map.72.refs_0_ = bf16[2,512,128]{2,1,0:T(8,128)(2,1)S(1)} custom-call(s32[11]{0:T(128)S(1)} %stack.47.info_ref, bf16[128,1024]{1,0:T(8,128)(2,1)S(1)} %get-tuple-element.55.refs_0_, bf16[128,1024]{1,0:T(8,128)(2,1)S(1)} %collective-permute-done.7.refs_1_, bf16[128,1024]{1,0:T(8,128)(2,1)S(1)} %collective-permute-done.8.refs_2_, ...), custom_call_target="tpu_custom_call" | custom-call | flops 550000000 | bytes 1800000 | tf_op jit(solution)/shard_map/pallas_call | solution.py:26
  51.2 1.3 %shard_map.73.refs_1_ = bf16[2,512,128]{2,1,0:T(8,128)(2,1)S(1)} custom-call(s32[11]{0:T(128)S(1)} %stack.47.info_ref, bf16[128,1024]{1,0:T(8,128)(2,1)S(1)} %get-tuple-element.55.refs_0_, bf16[128,1024]{1,0:T(8,128)(2,1)S(1)} %collective-permute-done.7.refs_1_, bf16[128,1024]{1,0:T(8,128)(2,1)S(1)} %collective-permute-done.8.refs_2_, ...), custom_call_target="tpu_custom_call" | custom-call | flops 550000000 | bytes 1800000 | tf_op jit(solution)/shard_map/pallas_call | solution.py:26
  52.5 1.3 %shard_map.74.refs_2_ = bf16[2,512,128]{2,1,0:T(8,128)(2,1)S(1)} custom-call(s32[11]{0:T(128)S(1)} %stack.47.info_ref, bf16[128,1024]{1,0:T(8,128)(2,1)S(1)} %get-tuple-element.55.refs_0_, bf16[128,1024]{1,0:T(8,128)(2,1)S(1)} %collective-permute-done.7.refs_1_, bf16[128,1024]{1,0:T(8,128)(2,1)S(1)} %collective-permute-done.8.refs_2_, ...), custom_call_target="tpu_custom_call" | custom-call | flops 550000000 | bytes 1800000 | tf_op jit(solution)/shard_map/pallas_call | solution.py:26
  53.8 0.0 copy-start
  53.8 1.3 %shard_map.75.refs_3_ = bf16[2,512,128]{2,1,0:T(8,128)(2,1)S(1)} custom-call(s32[11]{0:T(128)S(1)} %stack.47.info_ref, bf16[128,1024]{1,0:T(8,128)(2,1)S(1)} %get-tuple-element.55.refs_0_, bf16[128,1024]{1,0:T(8,128)(2,1)S(1)} %collective-permute-done.7.refs_1_, bf16[128,1024]{1,0:T(8,128)(2,1)S(1)} %collective-permute-done.8.refs_2_, ...), custom_call_target="tpu_custom_call" | custom-call | flops 550000000 | bytes 1800000 | tf_op jit(solution)/shard_map/pallas_call | solution.py:26
  55.0 0.9 %collective-permute-done.19.refs_11_ = bf16[128,1024]{1,0:T(8,128)(2,1)S(1)} collective-permute-done((bf16[128,1024]{1,0:T(8,128)(2,1)S(1)}, bf16[128,1024]{1,0:T(8,128)(2,1)S(1)}, u32[]{:S(2)}, u32[]{:S(2)}) %collective-permute-start.19) | collective-permute-done | bytes 262176 | tf_op jit(solution)/shard_map/ppermute | solution.py:293
  55.9 1.9 %shard_map.78 = (f32[256,1024]{1,0:T(8,128)S(1)}, bf16[256,1024]{1,0:T(8,128)(2,1)S(1)}) custom-call(s32[11]{0:T(128)S(1)} %stack.47.info_ref, bf16[2,512,128]{2,1,0:T(8,128)(2,1)S(1)} %shard_map.72.refs_0_, bf16[2,512,128]{2,1,0:T(8,128)(2,1)S(1)} %shard_map.73.refs_1_, bf16[2,512,128]{2,1,0:T(8,128)(2,1)S(1)} %shard_map.74.refs_2_, ...), custom_call_target="tpu_custom_call" | custom-call | flops 1100000000 | bytes 3600000 | tf_op jit(solution)/shard_map/pallas_call | solution.py:26
  57.8 0.1 collective-permute-start.20
  57.9 1.9 %shard_map.76 = (f32[256,1024]{1,0:T(8,128)S(1)}, bf16[256,1024]{1,0:T(8,128)(2,1)S(1)}) custom-call(s32[11]{0:T(128)S(1)} %stack.47.info_ref, bf16[2,512,128]{2,1,0:T(8,128)(2,1)S(1)} %shard_map.72.refs_0_, bf16[2,512,128]{2,1,0:T(8,128)(2,1)S(1)} %shard_map.73.refs_1_, bf16[2,512,128]{2,1,0:T(8,128)(2,1)S(1)} %shard_map.74.refs_2_, ...), custom_call_target="tpu_custom_call" | custom-call | flops 1100000000 | bytes 3600000 | tf_op jit(solution)/shard_map/pallas_call | solution.py:26
  59.8 0.6 collective-permute-start.17
  60.4 0.0 collective-permute-done.20.got_ref
  60.4 0.6 shard_map.79
  61.0 1.8 %collective-permute-start.21 = (bf16[128,1024]{1,0:T(8,128)(2,1)S(1)}, bf16[128,1024]{1,0:T(8,128)(2,1)S(1)}, u32[]{:S(2)}, u32[]{:S(2)}) collective-permute-start(bf16[128,1024]{1,0:T(8,128)(2,1)S(1)} %get-tuple-element.74), channel_id=1, source_target_pairs={{0,2},{1,3},{2,0},{3,1},{4,6},{5,7},{6,4},{7,5},{8,10},{9,11},{10,... | collective-permute-start | bytes 786440 | tf_op jit(solution)/shard_map/ppermute | solution.py:293
  62.9 0.6 shard_map.77
  63.5 0.9 %collective-permute-start.18 = (bf16[128,1024]{1,0:T(8,128)(2,1)S(1)}, bf16[128,1024]{1,0:T(8,128)(2,1)S(1)}, u32[]{:S(2)}, u32[]{:S(2)}) collective-permute-start(bf16[128,1024]{1,0:T(8,128)(2,1)S(1)} %get-tuple-element.69), channel_id=1, source_target_pairs={{0,2},{1,3},{2,0},{3,1},{4,6},{5,7},{6,4},{7,5},{8,10},{9,11},{10,... | collective-permute-start | bytes 786440 | tf_op jit(solution)/shard_map/ppermute | solution.py:293
  64.4 5.8 %collective-permute-done.21.far_ref = bf16[128,1024]{1,0:T(8,128)(2,1)S(1)} collective-permute-done((bf16[128,1024]{1,0:T(8,128)(2,1)S(1)}, bf16[128,1024]{1,0:T(8,128)(2,1)S(1)}, u32[]{:S(2)}, u32[]{:S(2)}) %collective-permute-start.21) | collective-permute-done | bytes 262176 | tf_op jit(solution)/shard_map/ppermute | solution.py:293
  70.2 1.3 %shard_map.80.refs_0_ = bf16[128,2048]{1,0:T(8,128)(2,1)} custom-call(s32[11]{0:T(128)S(1)} %stack.47.info_ref, f32[128,1024]{1,0:T(8,128)S(1)} %get-tuple-element.73.mine_ref, bf16[128,1024]{1,0:T(8,128)(2,1)S(1)} %collective-permute-done.21.far_ref), custom_call_target="tpu_custom_call" | custom-call | tf_op jit(solution)/shard_map/pallas_call | solution.py:268
  71.6 3.4 %collective-permute-done.18.far_ref = bf16[128,1024]{1,0:T(8,128)(2,1)S(1)} collective-permute-done((bf16[128,1024]{1,0:T(8,128)(2,1)S(1)}, bf16[128,1024]{1,0:T(8,128)(2,1)S(1)}, u32[]{:S(2)}, u32[]{:S(2)}) %collective-permute-start.18) | collective-permute-done | bytes 262176 | tf_op jit(solution)/shard_map/ppermute | solution.py:293
  75.0 1.3 %shard_map.81 = bf16[128,2048]{1,0:T(8,128)(2,1)} custom-call(s32[11]{0:T(128)S(1)} %stack.47.info_ref, f32[128,1024]{1,0:T(8,128)S(1)} %get-tuple-element.68.mine_ref, bf16[128,1024]{1,0:T(8,128)(2,1)S(1)} %collective-permute-done.18.far_ref, bf16[128,2048]{1,0:T(8,128)(2,1)} %shard_map.80.refs_0_), custom_call_target="tpu_custom_call", output_to_operand_aliasing={{}: (3, {})} | custom-call | tf_op jit(solution)/shard_map/pallas_call | solution.py:268
  (14 shorter events, 0.1 us)
Async XLA Ops:
  0.0 17.2 %collective-permute-start = (bf16[128,2048]{1,0:T(8,128)(2,1)}, bf16[128,2048]{1,0:T(8,128)(2,1)S(1)}, u32[]{:S(2)}, u32[]{:S(2)}) collective-permute-start(bf16[128,2048]{1,0:T(8,128)(2,1)} %refs_4_.3), channel_id=1, source_target_pairs={{0,8},{1,9},{2,10},{3,11},{4,12},{5,13},{6,14},{7,15},{8,16},{9,17... | collective-permute-start | bytes 1572872 | tf_op jit(solution)/shard_map/ppermute | solution.py:298
  3.0 14.2 %collective-permute-start.1 = (bf16[128,2048]{1,0:T(8,128)(2,1)}, bf16[128,2048]{1,0:T(8,128)(2,1)S(1)}, u32[]{:S(2)}, u32[]{:S(2)}) collective-permute-start(bf16[128,2048]{1,0:T(8,128)(2,1)} %refs_4_.3), channel_id=1, source_target_pairs={{0,4},{1,5},{2,6},{3,7},{4,0},{5,1},{6,2},{7,3},{8,12},{9,13},{10,... | collective-permute-start | bytes 1572872 | tf_op jit(solution)/shard_map/ppermute | solution.py:293
  4.5 4.6 %copy-start.5 = (f32[4096]{0:T(1024)S(1)}, f32[4096]{0:T(1024)}, u32[]{:S(2)}) copy-start(f32[4096]{0:T(1024)} %param.10) | copy-start | bytes 49156
  4.6 1.2 %copy-start.1 = (bf16[128,4096]{1,0:T(8,128)(2,1)S(1)}, bf16[128,4096]{1,0:T(8,128)(2,1)}, u32[]{:S(2)}) copy-start(bf16[128,4096]{1,0:T(8,128)(2,1)} %refs_0_.2) | copy-start | bytes 3145732
  5.9 3.3 %copy-start.2 = (bf16[128,4096]{1,0:T(8,128)(2,1)S(1)}, bf16[128,4096]{1,0:T(8,128)(2,1)}, u32[]{:S(2)}) copy-start(bf16[128,4096]{1,0:T(8,128)(2,1)} %refs_0_.3) | copy-start | bytes 3145732
  6.9 5.8 %collective-permute-start.2 = (bf16[128,1024]{1,0:T(8,128)(2,1)S(1)}, bf16[128,1024]{1,0:T(8,128)(2,1)S(1)}, u32[]{:S(2)}, u32[]{:S(2)}) collective-permute-start(bf16[128,1024]{1,0:T(8,128)(2,1)S(1)} %get-tuple-element.42), channel_id=1, source_target_pairs={{0,1},{1,0},{2,3},{3,2},{4,5},{5,4},{6,7},{7,6},{8,9},{9,8},{10,11... | collective-permute-start | bytes 786440 | tf_op jit(solution)/shard_map/ppermute | solution.py:293
  7.0 12.7 %collective-permute-start.4 = (bf16[128,1024]{1,0:T(8,128)(2,1)S(1)}, bf16[128,1024]{1,0:T(8,128)(2,1)S(1)}, u32[]{:S(2)}, u32[]{:S(2)}) collective-permute-start(bf16[128,1024]{1,0:T(8,128)(2,1)S(1)} %get-tuple-element.44), channel_id=1, source_target_pairs={{0,3},{1,2},{2,1},{3,0},{4,7},{5,6},{6,5},{7,4},{8,11},{9,10},{10,... | collective-permute-start | bytes 786440 | tf_op jit(solution)/shard_map/ppermute | solution.py:293
  8.6 13.2 %collective-permute-start.3 = (bf16[128,1024]{1,0:T(8,128)(2,1)S(1)}, bf16[128,1024]{1,0:T(8,128)(2,1)S(1)}, u32[]{:S(2)}, u32[]{:S(2)}) collective-permute-start(bf16[128,1024]{1,0:T(8,128)(2,1)S(1)} %get-tuple-element.43), channel_id=1, source_target_pairs={{0,2},{1,3},{2,0},{3,1},{4,6},{5,7},{6,4},{7,5},{8,10},{9,11},{10,... | collective-permute-start | bytes 786440 | tf_op jit(solution)/shard_map/ppermute | solution.py:293
  9.2 1.0 %copy-start.3 = (f32[4096,16]{0,1:T(8,128)S(1)}, f32[4096,16]{0,1:T(8,128)}, u32[]{:S(2)}) copy-start(f32[4096,16]{0,1:T(8,128)} %param.8) | copy-start | bytes 786436
  10.1 0.9 %copy-start.4 = (f32[4096,16]{0,1:T(8,128)S(1)}, f32[4096,16]{0,1:T(8,128)}, u32[]{:S(2)}) copy-start(f32[4096,16]{0,1:T(8,128)} %param.9) | copy-start | bytes 786436
  12.8 12.7 %collective-permute-start.7 = (bf16[128,1024]{1,0:T(8,128)(2,1)S(1)}, bf16[128,1024]{1,0:T(8,128)(2,1)S(1)}, u32[]{:S(2)}, u32[]{:S(2)}) collective-permute-start(bf16[128,1024]{1,0:T(8,128)(2,1)S(1)} %get-tuple-element.56), channel_id=1, source_target_pairs={{0,1},{1,0},{2,3},{3,2},{4,5},{5,4},{6,7},{7,6},{8,9},{9,8},{10,11... | collective-permute-start | bytes 786440 | tf_op jit(solution)/shard_map/ppermute | solution.py:293
  17.2 14.9 %collective-permute-start.5 = (bf16[128,2048]{1,0:T(8,128)(2,1)S(1)}, bf16[128,2048]{1,0:T(8,128)(2,1)S(1)}, u32[]{:S(2)}, u32[]{:S(2)}) collective-permute-start(bf16[128,2048]{1,0:T(8,128)(2,1)S(1)} %collective-permute-done.refs_6_), channel_id=1, source_target_pairs={{0,8},{1,9},{2,10},{3,11},{4,12},{5,13},{6,14},{7,15},{8,16},{9,17... | collective-permute-start | bytes 1572872 | tf_op jit(solution)/shard_map/ppermute | solution.py:298
  18.2 13.9 %collective-permute-start.6 = (bf16[128,2048]{1,0:T(8,128)(2,1)S(1)}, bf16[128,2048]{1,0:T(8,128)(2,1)S(1)}, u32[]{:S(2)}, u32[]{:S(2)}) collective-permute-start(bf16[128,2048]{1,0:T(8,128)(2,1)S(1)} %collective-permute-done.refs_6_), channel_id=1, source_target_pairs={{0,4},{1,5},{2,6},{3,7},{4,0},{5,1},{6,2},{7,3},{8,12},{9,13},{10,... | collective-permute-start | bytes 1572872 | tf_op jit(solution)/shard_map/ppermute | solution.py:293
  19.7 10.3 %collective-permute-start.8 = (bf16[128,1024]{1,0:T(8,128)(2,1)S(1)}, bf16[128,1024]{1,0:T(8,128)(2,1)S(1)}, u32[]{:S(2)}, u32[]{:S(2)}) collective-permute-start(bf16[128,1024]{1,0:T(8,128)(2,1)S(1)} %get-tuple-element.58), channel_id=1, source_target_pairs={{0,2},{1,3},{2,0},{3,1},{4,6},{5,7},{6,4},{7,5},{8,10},{9,11},{10,... | collective-permute-start | bytes 786440 | tf_op jit(solution)/shard_map/ppermute | solution.py:293
  21.9 9.7 %collective-permute-start.9 = (bf16[128,1024]{1,0:T(8,128)(2,1)S(1)}, bf16[128,1024]{1,0:T(8,128)(2,1)S(1)}, u32[]{:S(2)}, u32[]{:S(2)}) collective-permute-start(bf16[128,1024]{1,0:T(8,128)(2,1)S(1)} %get-tuple-element.60), channel_id=1, source_target_pairs={{0,3},{1,2},{2,1},{3,0},{4,7},{5,6},{6,5},{7,4},{8,11},{9,10},{10,... | collective-permute-start | bytes 786440 | tf_op jit(solution)/shard_map/ppermute | solution.py:293
  25.5 6.3 %collective-permute-start.10 = (f32[16,1024]{1,0:T(8,128)S(1)}, f32[16,1024]{1,0:T(8,128)S(1)}, u32[]{:S(2)}, u32[]{:S(2)}) collective-permute-start(f32[16,1024]{1,0:T(8,128)S(1)} %get-tuple-element.62.end_ref), channel_id=1, source_target_pairs={{0,4},{1,5},{2,6},{3,7},{4,0},{5,1},{6,2},{7,3},{8,12},{9,13},{10,... | collective-permute-start | bytes 196616 | tf_op jit(solution)/shard_map/ppermute | solution.py:293
  32.1 16.0 %collective-permute-start.14 = (bf16[128,2048]{1,0:T(8,128)(2,1)S(1)}, bf16[128,2048]{1,0:T(8,128)(2,1)S(1)}, u32[]{:S(2)}, u32[]{:S(2)}) collective-permute-start(bf16[128,2048]{1,0:T(8,128)(2,1)S(1)} %collective-permute-done.5.refs_8_), channel_id=1, source_target_pairs={{0,8},{1,9},{2,10},{3,11},{4,12},{5,13},{6,14},{7,15},{8,16},{9,17... | collective-permute-start | bytes 1572872 | tf_op jit(solution)/shard_map/ppermute | solution.py:298
  33.4 14.7 %collective-permute-start.15 = (bf16[128,2048]{1,0:T(8,128)(2,1)S(1)}, bf16[128,2048]{1,0:T(8,128)(2,1)S(1)}, u32[]{:S(2)}, u32[]{:S(2)}) collective-permute-start(bf16[128,2048]{1,0:T(8,128)(2,1)S(1)} %collective-permute-done.5.refs_8_), channel_id=1, source_target_pairs={{0,4},{1,5},{2,6},{3,7},{4,0},{5,1},{6,2},{7,3},{8,12},{9,13},{10,... | collective-permute-start | bytes 1572872 | tf_op jit(solution)/shard_map/ppermute | solution.py:293
  35.5 14.4 %collective-permute-start.11 = (f32[16,1024]{1,0:T(8,128)S(1)}, f32[16,1024]{1,0:T(8,128)S(1)}, u32[]{:S(2)}, u32[]{:S(2)}) collective-permute-start(f32[16,1024]{1,0:T(8,128)S(1)} %shard_map.71), channel_id=1, source_target_pairs={{0,8},{1,9},{2,10},{3,11},{4,12},{5,13},{6,14},{7,15},{8,16},{9,17... | collective-permute-start | bytes 196616 | tf_op jit(solution)/shard_map/ppermute | solution.py:298
  38.0 11.9 %collective-permute-start.12 = (f32[16,1024]{1,0:T(8,128)S(1)}, f32[16,1024]{1,0:T(8,128)S(1)}, u32[]{:S(2)}, u32[]{:S(2)}) collective-permute-start(f32[16,1024]{1,0:T(8,128)S(1)} %shard_map.71), channel_id=1, source_target_pairs={{0,16},{1,17},{2,18},{3,19},{4,20},{5,21},{6,22},{7,23},{8,24},{9,... | collective-permute-start | bytes 196616 | tf_op jit(solution)/shard_map/ppermute | solution.py:298
  42.2 7.8 %collective-permute-start.13 = (f32[16,1024]{1,0:T(8,128)S(1)}, f32[16,1024]{1,0:T(8,128)S(1)}, u32[]{:S(2)}, u32[]{:S(2)}) collective-permute-start(f32[16,1024]{1,0:T(8,128)S(1)} %shard_map.71), channel_id=1, source_target_pairs={{0,24},{1,25},{2,26},{3,27},{4,28},{5,29},{6,30},{7,31}} | collective-permute-start | bytes 196616 | tf_op jit(solution)/shard_map/ppermute | solution.py:298
  48.1 7.8 %collective-permute-start.19 = (bf16[128,1024]{1,0:T(8,128)(2,1)S(1)}, bf16[128,1024]{1,0:T(8,128)(2,1)S(1)}, u32[]{:S(2)}, u32[]{:S(2)}) collective-permute-start(bf16[128,1024]{1,0:T(8,128)(2,1)S(1)} %slice.7), channel_id=1, source_target_pairs={{0,4},{1,5},{2,6},{3,7},{4,0},{5,1},{6,2},{7,3},{8,12},{9,13},{10,... | collective-permute-start | bytes 786440 | tf_op jit(solution)/shard_map/ppermute | solution.py:293
  49.0 8.9 %collective-permute-start.16 = (bf16[128,1024]{1,0:T(8,128)(2,1)S(1)}, bf16[128,1024]{1,0:T(8,128)(2,1)S(1)}, u32[]{:S(2)}, u32[]{:S(2)}) collective-permute-start(bf16[128,1024]{1,0:T(8,128)(2,1)S(1)} %slice.6), channel_id=1, source_target_pairs={{0,8},{1,9},{2,10},{3,11},{4,12},{5,13},{6,14},{7,15},{8,16},{9,17... | collective-permute-start | bytes 786440 | tf_op jit(solution)/shard_map/ppermute | solution.py:298
  53.8 2.2 %copy-start = (bf16[128,2048]{1,0:T(8,128)(2,1)S(1)}, bf16[128,2048]{1,0:T(8,128)(2,1)}, u32[]{:S(2)}) copy-start(bf16[128,2048]{1,0:T(8,128)(2,1)} %refs_4_.3) | copy-start | bytes 1572868
  57.8 2.6 %collective-permute-start.20 = (bf16[256,1024]{1,0:T(8,128)(2,1)S(1)}, bf16[256,1024]{1,0:T(8,128)(2,1)S(1)}, u32[]{:S(2)}, u32[]{:S(2)}) collective-permute-start(bf16[256,1024]{1,0:T(8,128)(2,1)S(1)} %get-tuple-element.72), channel_id=1, source_target_pairs={{0,1},{1,0},{2,3},{3,2},{4,5},{5,4},{6,7},{7,6},{8,9},{9,8},{10,11... | collective-permute-start | bytes 1572872 | tf_op jit(solution)/shard_map/ppermute | solution.py:293
  59.8 3.0 %collective-permute-start.17 = (bf16[256,1024]{1,0:T(8,128)(2,1)S(1)}, bf16[256,1024]{1,0:T(8,128)(2,1)S(1)}, u32[]{:S(2)}, u32[]{:S(2)}) collective-permute-start(bf16[256,1024]{1,0:T(8,128)(2,1)S(1)} %get-tuple-element.67), channel_id=1, source_target_pairs={{0,1},{1,0},{2,3},{3,2},{4,5},{5,4},{6,7},{7,6},{8,9},{9,8},{10,11... | collective-permute-start | bytes 1572872 | tf_op jit(solution)/shard_map/ppermute | solution.py:293
  61.0 9.2 %collective-permute-start.21 = (bf16[128,1024]{1,0:T(8,128)(2,1)S(1)}, bf16[128,1024]{1,0:T(8,128)(2,1)S(1)}, u32[]{:S(2)}, u32[]{:S(2)}) collective-permute-start(bf16[128,1024]{1,0:T(8,128)(2,1)S(1)} %get-tuple-element.74), channel_id=1, source_target_pairs={{0,2},{1,3},{2,0},{3,1},{4,6},{5,7},{6,4},{7,5},{8,10},{9,11},{10,... | collective-permute-start | bytes 786440 | tf_op jit(solution)/shard_map/ppermute | solution.py:293
  63.5 11.5 %collective-permute-start.18 = (bf16[128,1024]{1,0:T(8,128)(2,1)S(1)}, bf16[128,1024]{1,0:T(8,128)(2,1)S(1)}, u32[]{:S(2)}, u32[]{:S(2)}) collective-permute-start(bf16[128,1024]{1,0:T(8,128)(2,1)S(1)} %get-tuple-element.69), channel_id=1, source_target_pairs={{0,2},{1,3},{2,0},{3,1},{4,6},{5,7},{6,4},{7,5},{8,10},{9,11},{10,... | collective-permute-start | bytes 786440 | tf_op jit(solution)/shard_map/ppermute | solution.py:293
